TPU v7x, 32 devices: a whole 2x2x4 slice. The times are simulated.
32 devices in a mesh: grp: 4 (over y, x), emb: 8 (over z, core).
Axes of the slice: x: 2, y: 2, z: 4, core: 2. Of those that a mesh axis runs over, the one named last changes fastest.
Arguments:
- pooled: bfloat16 [384, 256, 192], P(('grp', 'emb')), may hold values from -6 to 6
- upstream: bfloat16 [384, 256, 192], P(('grp', 'emb')), may hold values from -6 to 6
- ids_now: int32 [384, 256], P(('grp', 'emb')), may hold values from 0 to 127
- ids_next: int32 [384, 256], P(('grp', 'emb')), may hold values from 0 to 127
- tables: bfloat16 [256, 128, 192], P('emb'), may hold values from -6 to 6
- w_fm: bfloat16 [256, 128], replicated, may hold values from -0.02734375 to 0.02734375
- w_proj: bfloat16 [128, 192], replicated, may hold values from -0.5 to 0.5
- w_lcb: bfloat16 [256, 256], replicated, may hold values from -0.375 to 0.375
- gain: float32 [192], replicated, may hold values from 0.5 to 1.5
Outputs:
- next_rows: bfloat16 [384, 256, 192], P(('grp', 'emb'))
- table_grad: float32 [256, 128, 192], P('emb', 'grp')
- grad_fm: float32 [256, 128], replicated
- grad_proj: float32 [128, 192], replicated
- grad_lcb: float32 [256, 256], replicated
- grad_gain: float32 [192], replicated
All inputs are finite; a program needn't handle non-finite values.
Results may differ from a plain program's by a relative error of at most 0.017.
Values may be sent and summed in bfloat16 or wider, within the bound.
No kernel may reach another device: no remote copies, remote signals or barrier semaphores. Data moves between devices by JAX's collectives and lax.ppermute only.
A program may use at most 64 MiB of HBM per device.

v0:
```python
import jax
import jax.numpy as jnp
from jax import lax
from jax.sharding import PartitionSpec as P


def product(form, left, right):
    return jnp.einsum(form, left, right, preferred_element_type=jnp.float32)


def layer_backward(embeds, cotangent, w_fm, w_proj, w_lcb, gain):
    fm_proj = product("bfc,fj->bcj", embeds, w_fm).astype(jnp.bfloat16)
    fm_rows = product("bfc,bcj->bfj", embeds, fm_proj).astype(jnp.bfloat16)
    projected = product("bfj,jc->bfc", fm_rows, w_proj)
    compressed = product("fi,bfc->bic", w_lcb, embeds)
    summed = embeds.astype(jnp.float32) + projected + compressed
    centre = jnp.mean(summed, axis=2, keepdims=True)
    spread = jnp.mean((summed - centre) ** 2, axis=2, keepdims=True)
    inverse = lax.rsqrt(spread + 1e-05)
    normed = (summed - centre) * inverse
    upper = cotangent.astype(jnp.float32)
    scaled = upper * gain
    grad_sum = inverse * (
        scaled
        - jnp.mean(scaled, axis=2, keepdims=True)
        - normed * jnp.mean(scaled * normed, axis=2, keepdims=True)
    )
    grad_sum = grad_sum.astype(jnp.bfloat16)
    grad_gain = jnp.sum(upper * normed, axis=(0, 1))
    grad_proj = product("bfj,bfc->jc", fm_rows, grad_sum)
    grad_rows = product("bfc,jc->bfj", grad_sum, w_proj).astype(jnp.bfloat16)
    grad_p = product("bfc,bfj->bcj", embeds, grad_rows).astype(jnp.bfloat16)
    grad_fm = product("bfc,bcj->fj", embeds, grad_p)
    grad_lcb = product("bfc,bic->fi", embeds, grad_sum)
    grad_in = (
        grad_sum.astype(jnp.float32)
        + product("bfj,bcj->bfc", grad_rows, fm_proj)
        + product("fj,bcj->bfc", w_fm, grad_p)
        + product("fi,bic->bfc", w_lcb, grad_sum)
    )
    return (grad_in.astype(jnp.bfloat16), (grad_fm, grad_proj, grad_lcb, grad_gain))


def local(pooled, upstream, ids_now, ids_next, tables, w_fm, w_proj, w_lcb, gain):
    samples = pooled.shape[0] * lax.axis_size("grp") * lax.axis_size("emb")
    now_seen, next_seen = (
        lax.all_to_all(ids_now, "emb", split_axis=1, concat_axis=0, tiled=True),
        lax.all_to_all(ids_next, "emb", split_axis=1, concat_axis=0, tiled=True),
    )
    local_features = tables.shape[0]
    row_count = tables.shape[1]
    feature_pos = jnp.arange(local_features)[None, :]
    fetched = tables[feature_pos, next_seen]
    next_rows = lax.all_to_all(fetched, "emb", split_axis=0, concat_axis=1, tiled=True)
    grad_in, partials = layer_backward(pooled, upstream, w_fm, w_proj, w_lcb, gain)
    grad_fm, grad_proj, grad_lcb, grad_gain = partials
    row_index = jnp.arange(row_count)
    indicator = (now_seen.T[:, None, :] == row_index[None, :, None]).astype(jnp.bfloat16)
    table_terms = product(
        "frs,sfc->frc",
        indicator,
        lax.all_to_all(grad_in, "emb", split_axis=1, concat_axis=0, tiled=True),
    )
    table_grad = lax.psum_scatter(
        table_terms.astype(jnp.bfloat16), "grp", scatter_dimension=1, tiled=True
    ).astype(jnp.float32)
    total_fm, total_proj, total_lcb, total_gain = lax.psum(
        (grad_fm, grad_proj, grad_lcb, grad_gain), ("grp", "emb")
    )
    factor = 1.0 / samples
    return (
        next_rows,
        table_grad,
        total_fm * factor,
        total_proj * factor,
        total_lcb * factor,
        total_gain * factor,
    )


def solution(mesh):
    return jax.shard_map(
        local,
        mesh=mesh,
        in_specs=(
            P(("grp", "emb"), None, None),
            P(("grp", "emb"), None, None),
            P(("grp", "emb"), None),
            P(("grp", "emb"), None),
            P("emb", None, None),
            P(),
            P(),
            P(),
            P(),
        ),
        out_specs=(P(("grp", "emb"), None, None), P("emb", "grp", None), P(), P(), P(), P()),
        check_vma=False,
    )
```

profile of v0, /device:TPU:0, one launch (start us, length us, event | category | flops | bytes accessed | tf_op | source)
XLA Modules:
  0.0 216.3 jit_solution(10154466792405514569)
XLA Ops:
  8.0 0.9 all_to_all.62
  9.6 6.3 %all-to-all-start.2 = ((s32[8,1,384]{2,1,0:T(1,128)}), s32[8,1,384]{2,1,0:T(1,128)S(1)}, u32[]{:S(2)}, u32[]{:S(2)}) async-start(s32[8,1,384]{2,1,0:T(1,128)} %reshape.85), calls=%async_computation.2 | async-start | bytes 24576 | tf_op jit(solution)/shard_map/all_to_all | solution.py:47
  16.0 1.7 convolution_convert_fusion.4
  19.8 1.0 copy-done.3
  20.8 1.1 fusion.7
  25.6 1.6 fusion.8
  27.2 4.4 %copy.53 = bf16[12,256,192]{2,0,1:T(8,128)(2,1)} copy(bf16[12,256,192]{1,2,0:T(8,128)(2,1)} %fusion.8) | data formatting | bytes 2359296 | tf_op jit(solution)/shard_map/convert_element_type | solution.py:41
  31.6 5.1 %all-to-all-start.3 = ((bf16[12,256,192]{2,0,1:T(8,128)(2,1)}), bf16[12,256,192]{2,0,1:T(8,128)(2,1)}, u32[]{:S(2)}, u32[]{:S(2)}) async-start(bf16[12,256,192]{2,0,1:T(8,128)(2,1)} %copy.53), calls=%async_computation.3 | async-start | bytes 4194304 | tf_op jit(solution)/shard_map/all_to_all | solution.py:62
  36.8 2.1 convolution_bitcast_fusion.1
  38.9 1.1 convolution_bitcast_fusion.2
  40.0 1.2 convolution_bitcast_fusion
  42.6 45.8 %all-to-all-done.3 = bf16[12,256,192]{2,0,1:T(8,128)(2,1)} async-done(((bf16[12,256,192]{2,0,1:T(8,128)(2,1)}), bf16[12,256,192]{2,0,1:T(8,128)(2,1)}, u32[]{:S(2)}, u32[]{:S(2)}) %all-to-all-start.3) | async-done | bytes 1179680 | tf_op jit(solution)/shard_map/all_to_all | solution.py:62
  88.4 2.2 %copy.55 = bf16[8,12,32,192]{3,2,1,0:T(8,128)(2,1)S(1)} copy(bf16[8,12,32,192]{3,1,2,0:T(8,128)(2,1)} %bitcast.17) | data formatting | bytes 2359296 | tf_op jit(solution)/shard_map/all_to_all | solution.py:62
  90.6 3.8 %convolution_convert_fusion = bf16[32,128,192]{2,1,0:T(8,128)(2,1)} fusion(bf16[96,32,192]{2,1,0:T(8,128)(2,1)S(1)} %bitcast.85, s32[32,96]{1,0:T(8,128)S(1)} %copy.51), kind=kOutput, calls=%fused_computation.17 | convolution fusion | flops 152174592 | bytes 2764800 | tf_op jit(solution)/shard_map/frs,sfc->frc/dot_general | solution.py:8
  95.9 3.3 %all-to-all-start = ((s32[8,1,384]{2,1,0:T(1,128)}), s32[8,1,384]{2,1,0:T(1,128)S(1)}, u32[]{:S(2)}, u32[]{:S(2)}) async-start(s32[8,1,384]{2,1,0:T(1,128)} %reshape.83), calls=%async_computation | async-start | bytes 24576 | tf_op jit(solution)/shard_map/all_to_all | solution.py:48
  99.3 3.3 %copy.48 = bf16[32,128,192]{2,1,0:T(8,128)(2,1)S(1)} copy(bf16[32,128,192]{1,2,0:T(8,128)(2,1)} %param.13) | data formatting | bytes 3145728 | tf_op args[4]
  102.6 2.2 %all-to-all-done = s32[8,1,384]{2,1,0:T(1,128)S(1)} async-done(((s32[8,1,384]{2,1,0:T(1,128)}), s32[8,1,384]{2,1,0:T(1,128)S(1)}, u32[]{:S(2)}, u32[]{:S(2)}) %all-to-all-start) | async-done | bytes 12320 | tf_op jit(solution)/shard_map/all_to_all | solution.py:48
  105.7 30.6 %gather_fusion = bf16[3072,192]{1,0:T(8,128)(2,1)} fusion(bf16[32,128,192]{2,1,0:T(8,128)(2,1)S(1)} %copy.48, s32[3072]{0:T(1024)S(1)} %reshape.71), kind=kCustom, calls=%fused_computation | custom fusion | bytes 2383872 | tf_op jit(solution)/shard_map/gather | solution.py:53
  136.4 3.6 %all-to-all-start.1 = ((bf16[96,32,192]{2,1,0:T(8,128)(2,1)}), bf16[96,32,192]{2,1,0:T(8,128)(2,1)S(1)}, u32[]{:S(2)}, u32[]{:S(2)}) async-start(bf16[96,32,192]{2,1,0:T(8,128)(2,1)} %bitcast.88), calls=%async_computation.1 | async-start | bytes 3145728 | tf_op jit(solution)/shard_map/all_to_all | solution.py:54
  140.0 60.4 %psum.31 = f32[192]{0:T(256)S(1)} all-reduce(f32[192]{0:T(256)S(1)} %get-tuple-element.30), channel_id=1, replica_groups=mesh['grp'=4,'emb'=8] {'grp','emb'}, use_global_device_ids=true, to_apply=%region_9.0 | all-reduce | flops 192 | bytes 1536 | tf_op jit(solution)/shard_map/psum | solution.py:67
  200.9 1.0 broadcast_multiply_fusion
  202.7 0.9 broadcast_multiply_fusion.1
  205.2 1.5 copy.58
  206.7 2.1 convert_element_type.52
  (59 shorter events, 13.2 us)
Async XLA Ops:
  8.0 10.1 %copy-start = (bf16[256,256]{1,0:T(8,128)(2,1)S(1)}, bf16[256,256]{1,0:T(8,128)(2,1)}, u32[]{:S(2)}) copy-start(bf16[256,256]{1,0:T(8,128)(2,1)} %param.16) | copy-start | bytes 393220
  8.0 9.7 %copy-start.1 = (bf16[12,256,192]{1,2,0:T(8,128)(2,1)S(1)}, bf16[12,256,192]{1,2,0:T(8,128)(2,1)}, u32[]{:S(2)}) copy-start(bf16[12,256,192]{1,2,0:T(8,128)(2,1)} %param.9) | copy-start | bytes 3538948
  9.6 22.0 %all-to-all-start.2 = ((s32[8,1,384]{2,1,0:T(1,128)}), s32[8,1,384]{2,1,0:T(1,128)S(1)}, u32[]{:S(2)}, u32[]{:S(2)}) async-start(s32[8,1,384]{2,1,0:T(1,128)} %reshape.85), calls=%async_computation.2 | async-start | bytes 24576 | tf_op jit(solution)/shard_map/all_to_all | solution.py:47
  18.1 0.8 copy-start.5
  19.5 1.3 copy-start.3
  19.5 1.3 copy-start.8
  23.9 1.3 copy-start.4
  24.4 0.8 copy-start.2
  31.6 56.8 %all-to-all-start.3 = ((bf16[12,256,192]{2,0,1:T(8,128)(2,1)}), bf16[12,256,192]{2,0,1:T(8,128)(2,1)}, u32[]{:S(2)}, u32[]{:S(2)}) async-start(bf16[12,256,192]{2,0,1:T(8,128)(2,1)} %copy.53), calls=%async_computation.3 | async-start | bytes 4194304 | tf_op jit(solution)/shard_map/all_to_all | solution.py:62
  36.7 164.2 %all-reduce.3.cloned.1.call-start = ((), (), s32[]{:S(2)}) async-start(), calls=%async_computation.6 | async-start | bytes 983040 | tf_op jit(solution)/shard_map/psum | solution.py:67
  41.2 165.5 %reduce-scatter.2.cloned.1.call-start = ((), (), s32[]{:S(2)}) async-start(), calls=%async_computation.5 | async-start | bytes 2621440 | tf_op jit(solution)/shard_map/reduce_scatter | solution.py:64
  94.4 0.7 copy-start.7
  95.9 8.9 %all-to-all-start = ((s32[8,1,384]{2,1,0:T(1,128)}), s32[8,1,384]{2,1,0:T(1,128)S(1)}, u32[]{:S(2)}, u32[]{:S(2)}) async-start(s32[8,1,384]{2,1,0:T(1,128)} %reshape.83), calls=%async_computation | async-start | bytes 24576 | tf_op jit(solution)/shard_map/all_to_all | solution.py:48
  136.4 68.7 %all-to-all-start.1 = ((bf16[96,32,192]{2,1,0:T(8,128)(2,1)}), bf16[96,32,192]{2,1,0:T(8,128)(2,1)S(1)}, u32[]{:S(2)}, u32[]{:S(2)}) async-start(bf16[96,32,192]{2,1,0:T(8,128)(2,1)} %bitcast.88), calls=%async_computation.1 | async-start | bytes 3145728 | tf_op jit(solution)/shard_map/all_to_all | solution.py:54
  200.9 3.5 %copy-start.6 = (f32[128,192]{0,1:T(8,128)S(1)}, f32[128,192]{0,1:T(8,128)}, u32[]{:S(2)}) copy-start(f32[128,192]{0,1:T(8,128)} %get-tuple-element.34) | copy-start | bytes 294916
Sparse Core Ops, SparseCore 0:
  44.8 144.9 all-reduce.2
Sparse Core Ops, SparseCore 1:
  94.5 34.0 reduce-scatter.1
where the time goes:
time: 217 us; the launch traced here: 216 us
  blocking collectives  60.4 us (28%)
  local copies, waits for them, and re-layouts  49.8 us (23%)
  waiting for transfers between devices  48.1 us (22%)
  starting transfers between devices  18.4 us (8%)
  between operations  15.8 us (7%)
  matrix products  15.1 us (7%)
  other arithmetic  8.82 us (4%)
    psum x1, blocking collectives, local(): lax.psum((grad_fm, grad_proj, grad_lcb, grad_gain), ('grp', 'emb'))  60.4 us
    all_to_all x1, waiting for transfers between devices, local(): lax.all_to_all(grad_in, 'emb', split_axis=1, concat_axis=0, tiled=True)  45.8 us
    gather x1, local copies, waits for them, and re-layouts, local(): fetched = tables[feature_pos, next_seen]  30.6 us
    dot_general x13, matrix products, product(): return jnp.einsum(form, left, right, preferred_element_type=jnp.float32)  15.1 us
    unnamed x26, local copies, waits for them, and re-layouts  10.8 us
    all_to_all x1, starting transfers between devices, local(): lax.all_to_all(ids_now, 'emb', split_axis=1, concat_axis=0, tiled=True)  6.33 us
    all_to_all x1, starting transfers between devices, local(): lax.all_to_all(grad_in, 'emb', split_axis=1, concat_axis=0, tiled=True)  5.09 us
    convert_element_type x1, local copies, waits for them, and re-layouts, layer_backward(): grad_in.astype(jnp.bfloat16)  4.4 us
  transfers between devices with their start and end apart: 6, of which 2 were waited for; matrix products, arithmetic and copies ran while one was open for 31% of the time, Pallas kernels for 0%

commit v1 on v0

v1 whole, which is shorter than its diff:
```python
import jax
import jax.numpy as jnp
from jax import lax
from jax.sharding import PartitionSpec as P

BOTH = ("grp", "emb")


def product(form, left, right):
    return jnp.einsum(form, left, right, preferred_element_type=jnp.float32)


def layer_backward(embeds, cotangent, w_fm, w_proj, w_lcb, gain):
    fm_proj = product("bfc,fj->bcj", embeds, w_fm).astype(jnp.bfloat16)
    fm_rows = product("bfc,bcj->bfj", embeds, fm_proj).astype(jnp.bfloat16)
    projected = product("bfj,jc->bfc", fm_rows, w_proj)
    compressed = product("fi,bfc->bic", w_lcb, embeds)
    summed = embeds.astype(jnp.float32) + projected + compressed
    centre = jnp.mean(summed, axis=2, keepdims=True)
    spread = jnp.mean((summed - centre) ** 2, axis=2, keepdims=True)
    inverse = lax.rsqrt(spread + 1e-05)
    normed = (summed - centre) * inverse
    upper = cotangent.astype(jnp.float32)
    scaled = upper * gain
    grad_sum = inverse * (
        scaled
        - jnp.mean(scaled, axis=2, keepdims=True)
        - normed * jnp.mean(scaled * normed, axis=2, keepdims=True)
    )
    grad_sum = grad_sum.astype(jnp.bfloat16)
    grad_gain = jnp.sum(upper * normed, axis=(0, 1))
    grad_proj = product("bfj,bfc->jc", fm_rows, grad_sum)
    grad_rows = product("bfc,jc->bfj", grad_sum, w_proj).astype(jnp.bfloat16)
    grad_p = product("bfc,bfj->bcj", embeds, grad_rows).astype(jnp.bfloat16)
    grad_fm = product("bfc,bcj->fj", embeds, grad_p)
    grad_lcb = product("bfc,bic->fi", embeds, grad_sum)
    grad_in = (
        grad_sum.astype(jnp.float32)
        + product("bfj,bcj->bfc", grad_rows, fm_proj)
        + product("fj,bcj->bfc", w_fm, grad_p)
        + product("fi,bic->bfc", w_lcb, grad_sum)
    )
    return (grad_in.astype(jnp.bfloat16), (grad_fm, grad_proj, grad_lcb, grad_gain))


def exchange(blocks, axes):
    return lax.all_to_all(blocks, axes, split_axis=0, concat_axis=0, tiled=True)


def dense_sum(partials, factor):
    n = lax.axis_size("grp") * lax.axis_size("emb")
    shapes = [part.shape for part in partials]
    flat = jnp.concatenate([part.reshape(-1) for part in partials])
    unit = 128 * n
    padded = -(-flat.shape[0] // unit) * unit
    flat = jnp.pad(flat, (0, padded - flat.shape[0])).astype(jnp.bfloat16)
    seen = exchange(flat.reshape(n, padded // unit, 128), BOTH)
    share = (jnp.sum(seen.astype(jnp.float32), axis=0) * factor).astype(jnp.bfloat16)
    total = exchange(jnp.broadcast_to(share[None], (n,) + share.shape), BOTH).reshape(-1)
    total = total.astype(jnp.float32)
    outs, at = [], 0
    for shape in shapes:
        size = 1
        for extent in shape:
            size *= extent
        outs.append(total[at : at + size].reshape(shape))
        at += size
    return outs


def local(pooled, upstream, ids_now, ids_next, tables, w_fm, w_proj, w_lcb, gain):
    n_grp, n_emb = lax.axis_size("grp"), lax.axis_size("emb")
    count, features, width = pooled.shape
    owned, rows = tables.shape[:2]
    ids = jnp.stack([ids_now, ids_next]).reshape(2, count, n_emb, owned)
    ids = exchange(ids.transpose(2, 0, 1, 3), "emb")
    row_index = jnp.arange(rows)
    wanted = (ids[:, 1, :, :, None] == row_index).astype(jnp.bfloat16)
    fetched = product("esfr,frc->esfc", wanted, tables).astype(jnp.bfloat16)
    next_rows = exchange(fetched, "emb")
    next_rows = next_rows.transpose(1, 0, 2, 3).reshape(count, features, width)
    grad_in, partials = layer_backward(pooled, upstream, w_fm, w_proj, w_lcb, gain)
    grad_in = grad_in.reshape(count, n_emb, owned, width).transpose(1, 0, 2, 3)
    grads = exchange(grad_in, "emb")
    hit = (ids[:, 0, :, :, None] == row_index).astype(jnp.bfloat16)
    part = product("esfr,esfc->frc", hit, grads).astype(jnp.bfloat16)
    part = part.reshape(owned, n_grp, rows // n_grp, width).transpose(1, 0, 2, 3)
    table_grad = jnp.sum(exchange(part, "grp").astype(jnp.float32), axis=0)
    dense = dense_sum(partials, 1.0 / (count * n_grp * n_emb))
    return (next_rows, table_grad, *dense)


def solution(mesh):
    return jax.shard_map(
        local,
        mesh=mesh,
        in_specs=(
            P(BOTH, None, None),
            P(BOTH, None, None),
            P(BOTH, None),
            P(BOTH, None),
            P("emb", None, None),
            P(),
            P(),
            P(),
            P(),
        ),
        out_specs=(P(BOTH, None, None), P("emb", "grp", None), P(), P(), P(), P()),
        check_vma=False,
    )
```

time: 217 us -> 184 us (0.85)
  blocking collectives: 60.4 us -> 0 us
  waiting for transfers between devices: 48.1 us -> 80.3 us
  between operations: 15.8 us -> 0.94 us
  starting transfers between devices: 18.4 us -> 26.5 us
  local copies, waits for them, and re-layouts: 49.8 us -> 42.8 us
  matrix products: 15.1 us -> 19.4 us
  other arithmetic: 8.82 us -> 12.9 us
    psum x1 -> x0, blocking collectives: 60.4 us -> none  [local(): lax.psum((grad_fm, grad_proj, grad_lcb, grad_gain), ('grp', 'emb'))]
    all_to_all x4 -> x6, waiting for transfers between devices: 48 us -> 80.3 us  [exchange(): return lax.all_to_all(blocks, axes, split_axis=0, concat_axis=0, tiled=True)]
    gather x1 -> x0, local copies, waits for them, and re-layouts: 30.6 us -> none  [local(): fetched = tables[feature_pos, next_seen]]
    convert_element_type x0 -> x5, local copies, waits for them, and re-layouts: none -> 10.5 us  [the longest x3 4.62 us: dense_sum(): total = total.astype(jnp.float32)]
    all_to_all x4 -> x6, starting transfers between devices: 18.3 us -> 26.5 us  [exchange(): return lax.all_to_all(blocks, axes, split_axis=0, concat_axis=0, tiled=True)]
    transpose x1 -> x4, local copies, waits for them, and re-layouts: 0.06 us -> 6.54 us  [the longest x1 3.17 us: local(): part.reshape(owned, n_grp, rows // n_grp, width).transpose(1, 0, 2, 3)]
    dot_general x13 -> x14, matrix products: 15.1 us -> 19.4 us  [product(): return jnp.einsum(form, left, right, preferred_element_type=jnp.float32)]
    reduce_sum x0 -> x2, other arithmetic: none -> 4.09 us  [the longest x1 3.08 us: local(): table_grad = jnp.sum(exchange(part, 'grp').astype(jnp.float32), axis=0)]
  transfers between devices with their start and end apart: 6 -> 6, of which waited for: 2 -> 6; matrix products, arithmetic and copies ran while one was open for 31% -> 25% of each run, Pallas kernels for 0% -> 0%
where the time goes in v1:
time: 184 us; the launch traced here: 183 us
  waiting for transfers between devices  80.3 us (44%)
  local copies, waits for them, and re-layouts  42.8 us (23%)
  starting transfers between devices  26.5 us (14%)
  matrix products  19.4 us (11%)
  other arithmetic  12.9 us (7%)
    all_to_all x6, waiting for transfers between devices, exchange(): return lax.all_to_all(blocks, axes, split_axis=0, concat_axis=0, tiled=True)  80.3 us
    all_to_all x6, starting transfers between devices, exchange(): return lax.all_to_all(blocks, axes, split_axis=0, concat_axis=0, tiled=True)  26.5 us
    dot_general x14, matrix products, product(): return jnp.einsum(form, left, right, preferred_element_type=jnp.float32)  19.4 us
    unnamed x33, local copies, waits for them, and re-layouts  9.98 us
    convert_element_type x3, local copies, waits for them, and re-layouts, dense_sum(): total = total.astype(jnp.float32)  4.62 us
    convert_element_type x1, local copies, waits for them, and re-layouts, local(): part = product('esfr,esfc->frc', hit, grads).astype(jnp.bfloat16)  3.84 us
  transfers between devices with their start and end apart: 6, of which 6 were waited for; matrix products, arithmetic and copies ran while one was open for 25% of the time, Pallas kernels for 0%

profile of v1, /device:TPU:0, one launch (start us, length us, event | category | flops | bytes accessed | tf_op | source)
XLA Modules:
  0.0 182.8 jit_solution(7402024112785262678)
XLA Ops:
  0.7 1.9 %convolution_convert_fusion.3 = bf16[12,192,128]{2,1,0:T(8,128)(2,1)S(1)} fusion(bf16[12,256,192]{1,2,0:T(8,128)(2,1)} %param.9, bf16[256,128]{1,0:T(8,128)(2,1)} %param.14), kind=kOutput, calls=%fused_computation.28 | convolution fusion | flops 151289856 | bytes 1835008 | tf_op jit(solution)/shard_map/bfc,fj->bcj/dot_general | solution.py:10
  22.8 1.7 reshape.90
  24.5 7.4 %all-to-all-start.4 = ((bf16[32,31,128]{2,1,0:T(8,128)(2,1)}), bf16[32,31,128]{2,1,0:T(8,128)(2,1)}, u32[]{:S(2)}, u32[]{:S(2)}) async-start(bf16[32,31,128]{2,1,0:T(8,128)(2,1)} %reshape.90), calls=%async_computation.4 | async-start | bytes 524288 | tf_op jit(solution)/shard_map/all_to_all | solution.py:47
  37.3 2.8 %fusion.31 = f32[12,192,256]{2,1,0:T(8,128)} fusion(bf16[12,256,192]{1,2,0:T(8,128)(2,1)S(1)} %copy-done.3, bf16[256,256]{1,0:T(8,128)(2,1)} %param.16), kind=kOutput, calls=%fused_computation.51 | convolution fusion | flops 301989888 | bytes 3670016 | tf_op jit(solution)/shard_map/fi,bic->bfc/dot_general | solution.py:10
  40.1 2.2 %all-to-all-done.4 = bf16[32,31,128]{2,1,0:T(8,128)(2,1)} async-done(((bf16[32,31,128]{2,1,0:T(8,128)(2,1)}), bf16[32,31,128]{2,1,0:T(8,128)(2,1)}, u32[]{:S(2)}, u32[]{:S(2)}) %all-to-all-start.4) | async-done | bytes 253984 | tf_op jit(solution)/shard_map/all_to_all | solution.py:47
  42.3 4.0 %all-to-all-start = ((s32[8,1,768]{2,1,0:T(1,128)}), s32[8,1,768]{2,1,0:T(1,128)}, u32[]{:S(2)}, u32[]{:S(2)}) async-start(s32[8,1,768]{2,1,0:T(1,128)} %reshape.101), calls=%async_computation | async-start | bytes 49152 | tf_op jit(solution)/shard_map/all_to_all | solution.py:47
  47.3 4.7 %all-to-all-done = s32[8,1,768]{2,1,0:T(1,128)} async-done(((s32[8,1,768]{2,1,0:T(1,128)}), s32[8,1,768]{2,1,0:T(1,128)}, u32[]{:S(2)}, u32[]{:S(2)}) %all-to-all-start) | async-done | bytes 24608 | tf_op jit(solution)/shard_map/all_to_all | solution.py:47
  52.7 3.3 %all-to-all-start.5 = ((bf16[32,31,128]{2,1,0:T(8,128)(2,1)}), bf16[32,31,128]{2,1,0:T(8,128)(2,1)}, u32[]{:S(2)}, u32[]{:S(2)}) async-start(bf16[32,31,128]{2,1,0:T(8,128)(2,1)} %broadcast_in_dim.2), calls=%async_computation.5 | async-start | bytes 524288 | tf_op jit(solution)/shard_map/all_to_all | solution.py:47
  56.1 1.7 fusion.35
  62.6 3.8 %all-to-all-done.5 = bf16[32,31,128]{2,1,0:T(8,128)(2,1)} async-done(((bf16[32,31,128]{2,1,0:T(8,128)(2,1)}), bf16[32,31,128]{2,1,0:T(8,128)(2,1)}, u32[]{:S(2)}, u32[]{:S(2)}) %all-to-all-start.5) | async-done | bytes 253984 | tf_op jit(solution)/shard_map/all_to_all | solution.py:47
  66.4 3.6 %all-to-all-start.2 = ((bf16[8,12,32,192]{3,2,1,0:T(8,128)(2,1)}), bf16[8,12,32,192]{3,2,1,0:T(8,128)(2,1)S(1)}, u32[]{:S(2)}, u32[]{:S(2)}) async-start(bf16[8,12,32,192]{3,2,1,0:T(8,128)(2,1)} %copy.92), calls=%async_computation.2 | async-start | bytes 3145728 | tf_op jit(solution)/shard_map/all_to_all | solution.py:47
  74.0 2.1 %copy.86 = bf16[8,12,32,192]{3,2,1,0:T(8,128)(2,1)} copy(bf16[8,12,32,192]{3,1,0,2:T(8,128)(2,1)S(1)} %convert_bitcast_fusion) | data formatting | bytes 2359296 | tf_op jit(solution)/shard_map/convert_element_type | solution.py:79
  76.0 31.7 %all-to-all-done.2 = bf16[8,12,32,192]{3,2,1,0:T(8,128)(2,1)S(1)} async-done(((bf16[8,12,32,192]{3,2,1,0:T(8,128)(2,1)}), bf16[8,12,32,192]{3,2,1,0:T(8,128)(2,1)S(1)}, u32[]{:S(2)}, u32[]{:S(2)}) %all-to-all-start.2) | async-done | bytes 1179680 | tf_op jit(solution)/shard_map/all_to_all | solution.py:47
  108.9 3.8 %all-to-all-start.1 = ((bf16[8,12,32,192]{3,2,1,0:T(8,128)(2,1)}), bf16[8,12,32,192]{3,2,1,0:T(8,128)(2,1)S(1)}, u32[]{:S(2)}, u32[]{:S(2)}) async-start(bf16[8,12,32,192]{3,2,1,0:T(8,128)(2,1)} %copy.86), calls=%async_computation.1 | async-start | bytes 3145728 | tf_op jit(solution)/shard_map/all_to_all | solution.py:47
  112.8 3.9 %bitcast_convert_fusion = bf16[32,128,192]{1,2,0:T(8,128)(2,1)} fusion(bf16[8,12,32,192]{3,2,1,0:T(8,128)(2,1)} %copy-done.9, s32[8,12,32]{1,0,2:T(8,128)S(1)} %bitcast.110), kind=kOutput, calls=%fused_computation.1 | convolution fusion | flops 152174592 | bytes 2764800 | tf_op jit(solution)/shard_map/esfr,esfc->frc/dot_general | solution.py:10
  116.7 3.8 %copy.94 = bf16[32,128,192]{2,1,0:T(8,128)(2,1)} copy(bf16[32,128,192]{1,2,0:T(8,128)(2,1)} %bitcast_convert_fusion) | data formatting | bytes 3145728 | tf_op jit(solution)/shard_map/convert_element_type | solution.py:86
  120.6 3.2 %copy.95 = bf16[4,32,32,192]{3,2,1,0:T(8,128)(2,1)} copy(bf16[4,32,32,192]{3,2,0,1:T(8,128)(2,1)} %bitcast.100) | data formatting | bytes 3145728 | tf_op jit(solution)/shard_map/transpose | solution.py:87
  123.7 26.5 %all-to-all-done.1 = bf16[8,12,32,192]{3,2,1,0:T(8,128)(2,1)S(1)} async-done(((bf16[8,12,32,192]{3,2,1,0:T(8,128)(2,1)}), bf16[8,12,32,192]{3,2,1,0:T(8,128)(2,1)S(1)}, u32[]{:S(2)}, u32[]{:S(2)}) %all-to-all-start.1) | async-done | bytes 1179680 | tf_op jit(solution)/shard_map/all_to_all | solution.py:47
  150.2 4.5 %all-to-all-start.3 = ((bf16[4,32,32,192]{3,2,1,0:T(8,128)(2,1)}), bf16[4,32,32,192]{3,2,1,0:T(8,128)(2,1)}, u32[]{:S(2)}, u32[]{:S(2)}) async-start(bf16[4,32,32,192]{3,2,1,0:T(8,128)(2,1)} %copy.95), calls=%async_computation.3 | async-start | bytes 4194304 | tf_op jit(solution)/shard_map/all_to_all | solution.py:47
  154.7 1.8 reshape.92
  160.6 1.7 convert_element_type.91
  165.9 2.5 %copy.100 = bf16[12,256,192]{1,2,0:T(8,128)(2,1)} copy(bf16[12,256,192]{2,1,0:T(8,128)(2,1)} %bitcast.103) | data formatting | bytes 2359296
  168.4 11.3 %all-to-all-done.3 = bf16[4,32,32,192]{3,2,1,0:T(8,128)(2,1)} async-done(((bf16[4,32,32,192]{3,2,1,0:T(8,128)(2,1)}), bf16[4,32,32,192]{3,2,1,0:T(8,128)(2,1)}, u32[]{:S(2)}, u32[]{:S(2)}) %all-to-all-start.3) | async-done | bytes 1572896 | tf_op jit(solution)/shard_map/all_to_all | solution.py:47
  179.7 3.1 %convert_reduce_fusion = f32[32,32,192]{2,1,0:T(8,128)} fusion(bf16[4,32,32,192]{3,2,1,0:T(8,128)(2,1)} %all-to-all-done.3), kind=kLoop, calls=%fused_computation | loop fusion | flops 1376256 | bytes 2359296 | tf_op jit(solution)/shard_map/reduce_sum | solution.py:88
  (74 shorter events, 44.8 us)
Async XLA Ops:
  0.6 71.7 %copy-start = (bf16[32,128,192]{1,2,0:T(8,128)(2,1)S(1)}, bf16[32,128,192]{1,2,0:T(8,128)(2,1)}, u32[]{:S(2)}) copy-start(bf16[32,128,192]{1,2,0:T(8,128)(2,1)} %param.13) | copy-start | bytes 4718596
  0.6 1.9 %copy-start.1 = (bf16[12,256,192]{1,2,0:T(8,128)(2,1)S(1)}, bf16[12,256,192]{1,2,0:T(8,128)(2,1)}, u32[]{:S(2)}) copy-start(bf16[12,256,192]{1,2,0:T(8,128)(2,1)} %param.9) | copy-start | bytes 3538948
  0.7 2.7 %copy-start.10 = (bf16[256,256]{1,0:T(8,128)(2,1)S(1)}, bf16[256,256]{1,0:T(8,128)(2,1)}, u32[]{:S(2)}) copy-start(bf16[256,256]{1,0:T(8,128)(2,1)} %param.16) | copy-start | bytes 393220
  2.6 0.8 copy-start.5
  3.4 0.8 copy-start.11
  4.8 1.3 copy-start.8
  4.8 1.3 copy-start.13
  8.5 1.7 copy-start.2
  15.0 0.8 copy-start.7
  15.8 16.1 %copy-start.12 = (s32[12,256]{1,0:T(8,128)S(1)}, s32[12,256]{1,0:T(8,128)}, u32[]{:S(2)}) copy-start(s32[12,256]{1,0:T(8,128)} %param.12) | copy-start | bytes 36868
  16.8 20.4 %copy-start.3 = (bf16[12,256,192]{1,2,0:T(8,128)(2,1)S(1)}, bf16[12,256,192]{1,2,0:T(8,128)(2,1)}, u32[]{:S(2)}) copy-start(bf16[12,256,192]{1,2,0:T(8,128)(2,1)} %copy-done.2) | copy-start | bytes 3538948
  24.5 17.8 %all-to-all-start.4 = ((bf16[32,31,128]{2,1,0:T(8,128)(2,1)}), bf16[32,31,128]{2,1,0:T(8,128)(2,1)}, u32[]{:S(2)}, u32[]{:S(2)}) async-start(bf16[32,31,128]{2,1,0:T(8,128)(2,1)} %reshape.90), calls=%async_computation.4 | async-start | bytes 524288 | tf_op jit(solution)/shard_map/all_to_all | solution.py:47
  42.3 9.7 %all-to-all-start = ((s32[8,1,768]{2,1,0:T(1,128)}), s32[8,1,768]{2,1,0:T(1,128)}, u32[]{:S(2)}, u32[]{:S(2)}) async-start(s32[8,1,768]{2,1,0:T(1,128)} %reshape.101), calls=%async_computation | async-start | bytes 49152 | tf_op jit(solution)/shard_map/all_to_all | solution.py:47
  52.7 13.7 %all-to-all-start.5 = ((bf16[32,31,128]{2,1,0:T(8,128)(2,1)}), bf16[32,31,128]{2,1,0:T(8,128)(2,1)}, u32[]{:S(2)}, u32[]{:S(2)}) async-start(bf16[32,31,128]{2,1,0:T(8,128)(2,1)} %broadcast_in_dim.2), calls=%async_computation.5 | async-start | bytes 524288 | tf_op jit(solution)/shard_map/all_to_all | solution.py:47
  56.0 1.9 %copy-start.4 = (f32[12,192,256]{2,1,0:T(8,128)S(1)}, f32[12,192,256]{2,1,0:T(8,128)}, u32[]{:S(2)}) copy-start(f32[12,192,256]{2,1,0:T(8,128)} %fusion.31) | copy-start | bytes 7077892
  56.1 2.0 %copy-start.6 = (bf16[12,192,128]{2,1,0:T(8,128)(2,1)S(1)}, bf16[12,192,128]{2,1,0:T(8,128)(2,1)}, u32[]{:S(2)}) copy-start(bf16[12,192,128]{2,1,0:T(8,128)(2,1)} %copy-done.5) | copy-start | bytes 1769476
  66.4 41.3 %all-to-all-start.2 = ((bf16[8,12,32,192]{3,2,1,0:T(8,128)(2,1)}), bf16[8,12,32,192]{3,2,1,0:T(8,128)(2,1)S(1)}, u32[]{:S(2)}, u32[]{:S(2)}) async-start(bf16[8,12,32,192]{3,2,1,0:T(8,128)(2,1)} %copy.92), calls=%async_computation.2 | async-start | bytes 3145728 | tf_op jit(solution)/shard_map/all_to_all | solution.py:47
  107.7 1.2 copy-start.9
  108.9 41.3 %all-to-all-start.1 = ((bf16[8,12,32,192]{3,2,1,0:T(8,128)(2,1)}), bf16[8,12,32,192]{3,2,1,0:T(8,128)(2,1)S(1)}, u32[]{:S(2)}, u32[]{:S(2)}) async-start(bf16[8,12,32,192]{3,2,1,0:T(8,128)(2,1)} %copy.86), calls=%async_computation.1 | async-start | bytes 3145728 | tf_op jit(solution)/shard_map/all_to_all | solution.py:47
  150.2 29.5 %all-to-all-start.3 = ((bf16[4,32,32,192]{3,2,1,0:T(8,128)(2,1)}), bf16[4,32,32,192]{3,2,1,0:T(8,128)(2,1)}, u32[]{:S(2)}, u32[]{:S(2)}) async-start(bf16[4,32,32,192]{3,2,1,0:T(8,128)(2,1)} %copy.95), calls=%async_computation.3 | async-start | bytes 4194304 | tf_op jit(solution)/shard_map/all_to_all | solution.py:47

commit v2 on v1

--- a/solution.py
+++ b/solution.py
@@ -1,7 +1,20 @@
+import functools
+
 import jax
 import jax.numpy as jnp
 from jax import lax
-from jax.sharding import PartitionSpec as P
+from jax.experimental import pallas as pl
+from jax.experimental.pallas import tpu as pltpu
+from jax.sharding import Mesh, PartitionSpec as P
+
+F32, BF16 = jnp.float32, jnp.bfloat16
+VMEM = pl.BlockSpec(memory_space=pltpu.VMEM)
+LANES = 128
+TILE = 8
+STEP = 4
+LIMIT = 40 * 1024 * 1024
+PEER = ("grp", "lane")
+
 
 BOTH = ("grp", "emb")
 
@@ -90,21 +103,464 @@
     return (next_rows, table_grad, *dense)
 
 
+def mm(left, right, dims=((1,), (0,))):
+    return lax.dot_general(left, right, (dims, ((), ())), preferred_element_type=F32)
+
+
+def low_lanes(shape):
+    return lax.broadcasted_iota(jnp.int32, shape, 1) < LANES // 2
+
+
+def turn(tile):
+    return pltpu.roll(tile, LANES // 2, 1)
+
+
+def pair_up(first, second):
+    return jnp.where(low_lanes(first.shape), first, turn(second))
+
+
+class Wire:
+    def __init__(self, count, peers):
+        self.left = count * TILE
+        self.half = self.left + self.left // 2
+        self.dense = 2 * self.half
+        self.dense_rows = 1024 // peers
+        self.ids = self.dense + self.dense_rows
+        self.out_rows = self.ids + 16
+
+
+def pack_tables_kernel(place, tables, out):
+    for f in range(TILE):
+        whole = tables[f].astype(F32)
+        out[f, 0:128] = whole[:, 0:128].astype(BF16)
+        right = jnp.concatenate([whole[:, 128:192], whole[:, 128:192]], axis=1)
+        out[f, 128:192] = jnp.where(low_lanes((64, LANES)), right[0:64], right[64:128]).astype(BF16)
+
+
+def pack_tables(tables, place):
+    rows, width = tables.shape[1:]
+    return pl.pallas_call(
+        pack_tables_kernel,
+        grid_spec=pltpu.PrefetchScalarGridSpec(
+            num_scalar_prefetch=1,
+            grid=(1,),
+            in_specs=[pl.BlockSpec((TILE, rows, width), lambda i, place: (place[0], 0, 0))],
+            out_specs=pl.BlockSpec((TILE, 192, LANES), lambda i, place: (0, 0, 0)),
+        ),
+        out_shape=jax.ShapeDtypeStruct((TILE, 192, LANES), BF16),
+        compiler_params=pltpu.CompilerParams(vmem_limit_bytes=LIMIT),
+        name="pack_tables",
+    )(place, tables)
+
+
+def backward_kernel(
+    n_grp, n_lane, wire,
+    x_ref, u_ref, now_ref, next_ref, fm_ref, proj_ref, lcb_ref, gain_ref,
+    out_ref,
+    fm_t, lcb_t, grad, sum_fm, sum_proj, sum_lcb, sum_gain, ids,
+):
+    step = pl.program_id(0)
+    width = x_ref.shape[2]
+    scale = 1.0 / width
+
+    @pl.when(step == 0)
+    def _():
+        fm_t[...] = fm_ref[...].astype(F32).T.astype(BF16)
+        lcb_t[...] = lcb_ref[...].astype(F32).T.astype(BF16)
+        sum_fm[...] = jnp.zeros_like(sum_fm)
+        sum_proj[...] = jnp.zeros_like(sum_proj)
+        sum_lcb[...] = jnp.zeros_like(sum_lcb)
+        sum_gain[...] = jnp.zeros_like(sum_gain)
+
+    fm, proj, lcb = fm_ref[...], proj_ref[...], lcb_ref[...]
+    gain = gain_ref[...]
+    for s in range(STEP):
+        x = x_ref[s]
+        p_t = mm(fm_t[...], x).astype(BF16)
+        g = mm(x, p_t, ((1,), (1,))).astype(BF16)
+        summed = x.astype(F32) + mm(g, proj) + mm(lcb_t[...], x)
+        centre = jnp.sum(summed, axis=1, keepdims=True) * scale
+        summed = summed - centre
+        spread = jnp.sum(summed * summed, axis=1, keepdims=True) * scale
+        inverse = lax.rsqrt(spread + 1e-05)
+        normed = summed * inverse
+        upper = u_ref[s].astype(F32)
+        scaled = upper * gain
+        first = jnp.sum(scaled, axis=1, keepdims=True) * scale
+        second = jnp.sum(scaled * normed, axis=1, keepdims=True) * scale
+        d_sum = (inverse * (scaled - first - normed * second)).astype(BF16)
+        sum_gain[...] += jnp.sum((upper * normed).reshape(-1, 8, width), axis=0)
+        d_g = mm(d_sum, proj, ((1,), (1,))).astype(BF16)
+        d_p_t = mm(d_g, x, ((0,), (0,))).astype(BF16)
+        grad[s, :, 0:width] = (
+            d_sum.astype(F32) + mm(d_g, p_t) + mm(fm, d_p_t) + mm(lcb, d_sum)
+        )
+        sum_fm[...] += mm(x, d_p_t, ((1,), (1,)))
+        sum_proj[:, 0:width] += mm(g, d_sum, ((0,), (0,)))
+        sum_lcb[...] += mm(x, d_sum, ((1,), (1,)))
+
+    for half in range(2):
+        for peer in range(n_grp * n_lane):
+            at = half * (n_grp * n_lane * TILE) + (peer % n_lane) * n_grp * TILE + (peer // n_lane) * TILE
+            rows = [grad[s, at : at + TILE, 0:128] for s in range(STEP)]
+            row = pl.multiple_of(half * wire.half + step * (STEP * TILE), 16)
+            out_ref[peer, pl.ds(row, STEP * TILE)] = jnp.concatenate(rows, axis=0).astype(BF16)
+            rest = [grad[s, at : at + TILE, 128:256] for s in range(STEP)]
+            packed = pair_up(jnp.concatenate(rest[:2], axis=0), jnp.concatenate(rest[2:], axis=0))
+            row = pl.multiple_of(half * wire.half + wire.left + step * (STEP * TILE // 2), 16)
+            out_ref[peer, pl.ds(row, STEP * TILE // 2)] = packed.astype(BF16)
+
+    @pl.when(step == pl.num_programs(0) - 1)
+    def _():
+        peers = n_grp * n_lane
+        part = 256 // peers
+        total = jnp.sum(sum_gain[...], axis=0, keepdims=True)
+        high = total.astype(BF16).astype(F32)
+        low = total - high
+        both = [piece[:, 64 * c : 64 * c + 64] for piece in (high, low) for c in range(3)]
+        column = jnp.concatenate(both + [jnp.zeros((2, 64), F32)], axis=0)
+        column = jnp.concatenate([column, column], axis=1)
+        for peer in range(peers):
+            at = wire.dense
+            here = slice(peer * part, (peer + 1) * part)
+            out_ref[peer, at : at + part] = sum_fm[here].astype(BF16)
+            out_ref[peer, at + part : at + 2 * part] = sum_lcb[here, 0:128].astype(BF16)
+            out_ref[peer, at + 2 * part : at + 3 * part] = sum_lcb[here, 128:256].astype(BF16)
+            here = slice(peer * part // 2, (peer + 1) * part // 2)
+            right = jnp.where(low_lanes((part // 2, LANES)), sum_proj[here, 128:256], column)
+            both = jnp.concatenate([sum_proj[here, 0:128], right], axis=0)
+            out_ref[peer, at + 3 * part : at + 4 * part] = both.astype(BF16)
+
+        count = now_ref.shape[0]
+        lane = lax.broadcasted_iota(jnp.int32, (16, LANES), 1)
+        sample = lax.broadcasted_iota(jnp.int32, (16, LANES), 0)
+        mine = (lane // TILE == sample) & (sample < count)
+        for which, ref in enumerate((now_ref, next_ref)):
+            ids[which] = jnp.zeros_like(ids[which])
+            ids[which, 0:count] = ref[...].astype(F32)
+        for peer in range(peers):
+            at = (peer % n_lane) * n_grp * TILE + (peer // n_lane) * TILE
+            rows = []
+            for which in range(2):
+                for half in range(2):
+                    line = ids[which, :, half * 128 : half * 128 + 128]
+                    if at:
+                        line = pltpu.roll(line, LANES - at, 1)
+                    line = pltpu.roll(line, 0, 1, stride=TILE, stride_axis=0)
+                    rows.append(jnp.sum(jnp.where(mine, line, 0.0), axis=0, keepdims=True))
+            rows.append(jnp.zeros((12, LANES), F32))
+            out_ref[peer, wire.ids : wire.ids + 16] = jnp.concatenate(rows, axis=0).astype(BF16)
+
+
+def backward(n_grp, n_lane, wire, pooled, upstream, ids_now, ids_next, w_fm, w_proj, w_lcb, gain):
+    count, features, width = pooled.shape
+    rank = w_fm.shape[1]
+    peers = n_grp * n_lane
+    block = pl.BlockSpec((STEP, features, width), lambda i: (i, 0, 0))
+
+    def whole(array):
+        return pl.BlockSpec(array.shape, lambda i: (0,) * array.ndim)
+
+    gain = gain.reshape(1, width)
+    rest = (ids_now, ids_next, w_fm, w_proj, w_lcb, gain)
+    return pl.pallas_call(
+        functools.partial(backward_kernel, n_grp, n_lane, wire),
+        grid=(count // STEP,),
+        in_specs=[block, block] + [whole(array) for array in rest],
+        out_specs=pl.BlockSpec((peers, wire.out_rows, LANES), lambda i: (0, 0, 0)),
+        out_shape=jax.ShapeDtypeStruct((peers, wire.out_rows, LANES), BF16),
+        scratch_shapes=[
+            pltpu.VMEM((rank, features), BF16),
+            pltpu.VMEM((features, features), BF16),
+            pltpu.VMEM((STEP, features, 256), F32),
+            pltpu.VMEM((features, rank), F32),
+            pltpu.VMEM((rank, 256), F32),
+            pltpu.VMEM((features, features), F32),
+            pltpu.VMEM((8, width), F32),
+            pltpu.VMEM((2, 16, features), F32),
+        ],
+        compiler_params=pltpu.CompilerParams(vmem_limit_bytes=LIMIT),
+        cost_estimate=pl.CostEstimate(flops=6 * 10**9, bytes_accessed=4 * 10**6, transcendentals=0),
+        name="layer_backward",
+    )(pooled, upstream, *rest)
+
+
+def part_kernel(n_grp, wire, other, half_ref, seen, *refs):
+    out, held = refs[0], refs[-1]
+    peers = seen.shape[0]
+    half = 1 - half_ref[0] if other else half_ref[0]
+    if other:
+        dense = refs[1]
+        total = seen[0, wire.dense : wire.ids].astype(F32)
+        for peer in range(1, peers):
+            total = total + seen[peer, wire.dense : wire.ids].astype(F32)
+        dense[...] = total
+    lane = lax.broadcasted_iota(jnp.int32, (1, LANES), 1)
+    start = ((lane % TILE) * LANES).astype(F32)
+    keys = []
+    for peer in range(peers):
+        at = peer * LANES
+        base = pl.multiple_of(half * wire.half, 16)
+        held[at : at + wire.left, 0:128] = seen[peer, pl.ds(base, wire.left)]
+        base = pl.multiple_of(half * wire.half + wire.left, 16)
+        right = seen[peer, pl.ds(base, wire.left // 2)]
+        turned = turn(right.astype(F32)).astype(BF16)
+        for i in range(wire.left // 32):
+            held[at + 32 * i : at + 32 * i + 16, 128:256] = right[16 * i : 16 * i + 16]
+            held[at + 32 * i + 16 : at + 32 * i + 32, 128:256] = turned[16 * i : 16 * i + 16]
+        if wire.left < LANES:
+            held[at + wire.left : at + LANES] = jnp.zeros((LANES - wire.left, 256), BF16)
+        ids = seen[peer, wire.ids : wire.ids + 16].astype(F32)
+        key = jnp.where(half == 0, ids[0:1], ids[1:2]) + start
+        keys.append(jnp.where(lane < wire.left, key, -1.0))
+    keys = jnp.concatenate(keys, axis=1)
+    piece = LANES // n_grp
+    for pair in range(TILE // 2):
+        row = lax.broadcasted_iota(jnp.int32, (256, 1), 0).astype(F32) + 256.0 * pair
+        hit = jnp.where(keys == row, 1.0, 0.0).astype(BF16)
+        part = mm(hit, held[...])
+        for f in range(2):
+            for g in range(n_grp):
+                at = f * LANES + g * piece
+                rows = part[at : at + piece]
+                out[g, 2 * pair + f, 0:piece] = rows[:, 0:128].astype(out.dtype)
+                packed = pair_up(rows[: piece // 2, 128:256], rows[piece // 2 :, 128:256])
+                out[g, 2 * pair + f, piece : piece + piece // 2] = packed.astype(out.dtype)
+
+
+def part_sums(n_grp, wire, other, half, seen):
+    peers = seen.shape[0]
+    piece = LANES // n_grp
+    shape = (n_grp, TILE, piece + piece // 2, LANES)
+    out_shape = [jax.ShapeDtypeStruct(shape, BF16 if other else F32)]
+    if other:
+        out_shape.append(jax.ShapeDtypeStruct((wire.dense_rows, LANES), F32))
+    return pl.pallas_call(
+        functools.partial(part_kernel, n_grp, wire, other),
+        in_specs=[pl.BlockSpec(memory_space=pltpu.SMEM), VMEM],
+        out_specs=[VMEM] * len(out_shape),
+        out_shape=out_shape,
+        scratch_shapes=[pltpu.VMEM((peers * LANES, 256), BF16)],
+        compiler_params=pltpu.CompilerParams(vmem_limit_bytes=LIMIT),
+        cost_estimate=pl.CostEstimate(flops=2 * 10**9, bytes_accessed=2 * 10**6, transcendentals=0),
+        name="part_other" if other else "part_own",
+    )(half, seen)
+
+
+def lookup_kernel(wire, factor, place, tables, crossed, ids_ref, dense_own, dense_seen, out, held):
+    peers = ids_ref.shape[0]
+    half = place[1]
+    rows = tables.shape[1]
+    for f in range(TILE):
+        at = f * rows
+        held[half, at : at + rows, 0:192] = tables[f]
+        held[1 - half, at : at + rows, 0:128] = crossed[f, 0:128]
+        right = crossed[f, 128:192]
+        held[1 - half, at : at + 64, 128:256] = right
+        held[1 - half, at + 64 : at + 128, 128:256] = turn(right.astype(F32)).astype(BF16)
+    ids = ids_ref[...].astype(F32).reshape(peers * 16, LANES)
+    lane = lax.broadcasted_iota(jnp.int32, (1, LANES), 1)
+    keys = (ids + ((lane % TILE) * LANES).astype(F32)).T
+    column = lax.broadcasted_iota(jnp.int32, (1, TILE * rows), 1).astype(F32)
+    total = ((dense_own[...] + dense_seen[...]) * factor).astype(BF16)
+    for which in range(2):
+        for pair in range(peers // 2):
+            mine = []
+            for peer in (2 * pair, 2 * pair + 1):
+                at = peer * 16 + 2 + which
+                mine.append(keys[0 : wire.left, at : at + 1])
+            hit = jnp.where(jnp.concatenate(mine, axis=0) == column, 1.0, 0.0).astype(BF16)
+            both = mm(hit, held[which])
+            for k in range(2):
+                got = both[k * wire.left : (k + 1) * wire.left]
+                peer, base = 2 * pair + k, which * wire.half
+                out[peer, base : base + wire.left] = got[:, 0:128].astype(BF16)
+                for i in range(wire.left // 32):
+                    packed = pair_up(got[32 * i : 32 * i + 16, 128:256], got[32 * i + 16 : 32 * i + 32, 128:256])
+                    at = base + wire.left + 16 * i
+                    out[peer, at : at + 16] = packed.astype(BF16)
+    for peer in range(peers):
+        out[peer, wire.dense : wire.ids] = total
+
+
+def lookup(wire, factor, place, tables, crossed, seen, dense_own, dense_seen):
+    peers = seen.shape[0]
+    rows, width = tables.shape[1:]
+
+    def whole(array):
+        return pl.BlockSpec(array.shape, lambda i, place: (0,) * array.ndim)
+
+    at = wire.ids // 16
+    return pl.pallas_call(
+        functools.partial(lookup_kernel, wire, factor),
+        grid_spec=pltpu.PrefetchScalarGridSpec(
+            num_scalar_prefetch=1,
+            grid=(1,),
+            in_specs=[
+                pl.BlockSpec((TILE, rows, width), lambda i, place: (place[0], 0, 0)),
+                whole(crossed),
+                pl.BlockSpec((peers, 16, LANES), lambda i, place: (0, at, 0)),
+                whole(dense_own),
+                whole(dense_seen),
+            ],
+            out_specs=pl.BlockSpec((peers, wire.ids, LANES), lambda i, place: (0, 0, 0)),
+            scratch_shapes=[pltpu.VMEM((2, TILE * rows, 256), BF16)],
+        ),
+        out_shape=jax.ShapeDtypeStruct((peers, wire.ids, LANES), BF16),
+        compiler_params=pltpu.CompilerParams(vmem_limit_bytes=LIMIT),
+        cost_estimate=pl.CostEstimate(flops=2 * 10**9, bytes_accessed=4 * 10**6, transcendentals=0),
+        name="lookup",
+    )(place, tables, crossed, seen, dense_own, dense_seen)
+
+
+def unpack_kernel(n_grp, n_lane, wire, seen, rows_out, fm, proj, lcb, gain):
+    step = pl.program_id(0)
+    peers = n_grp * n_lane
+    for half in range(2):
+        for q in range(n_lane):
+            for gg in range(n_grp // 2):
+                left, right = [], []
+                for g in (2 * gg, 2 * gg + 1):
+                    peer = g * n_lane + q
+                    row = pl.multiple_of(half * wire.half + step * 32, 16)
+                    left.append(seen[peer, pl.ds(row, 32)].astype(F32))
+                    row = pl.multiple_of(half * wire.half + wire.left + step * 16, 16)
+                    packed = seen[peer, pl.ds(row, 16)].astype(F32)
+                    right.append(jnp.concatenate([packed, turn(packed)], axis=0))
+                at = half * 128 + q * n_grp * TILE + gg * 16
+                for s in range(STEP):
+                    here = slice(s * TILE, s * TILE + TILE)
+                    rows_out[s, at : at + 16, 0:128] = jnp.concatenate(
+                        [left[0][here], left[1][here]], axis=0
+                    ).astype(BF16)
+                    rows_out[s, at : at + 16, 128:192] = jnp.concatenate(
+                        [right[0][here], right[1][here]], axis=0
+                    )[:, 0:64].astype(BF16)
+
+    @pl.when(step == 0)
+    def _():
+        part = 256 // peers
+        for peer in range(peers):
+            dense = seen[peer, wire.dense : wire.ids].astype(F32)
+            here = slice(peer * part, (peer + 1) * part)
+            fm[here] = dense[0:part]
+            lcb[here, 0:128] = dense[part : 2 * part]
+            lcb[here, 128:256] = dense[2 * part : 3 * part]
+            here = slice(peer * part // 2, (peer + 1) * part // 2)
+            proj[here, 0:128] = dense[3 * part : 3 * part + part // 2]
+            last = dense[3 * part + part // 2 :]
+            proj[here, 128:192] = last[:, 0:64]
+            if peer == 0:
+                total = turn(last)
+                total = total[0:3] + total[3:6]
+                gain[:, 0:128] = jnp.where(low_lanes((1, LANES)), total[0:1], turn(total)[1:2])
+                gain[:, 128:192] = total[2:3, 0:64]
+
+
+def unpack(n_grp, n_lane, wire, count, seen):
+    def whole(*shape):
+        return pl.BlockSpec(shape, lambda i: (0,) * len(shape))
+
+    shapes = [(256, 128), (128, 192), (256, 256), (1, 192)]
+    return pl.pallas_call(
+        functools.partial(unpack_kernel, n_grp, n_lane, wire),
+        grid=(count // STEP,),
+        in_specs=[whole(*seen.shape)],
+        out_specs=[pl.BlockSpec((STEP, 256, 192), lambda i: (i, 0, 0))] + [whole(*shape) for shape in shapes],
+        out_shape=[jax.ShapeDtypeStruct((count, 256, 192), BF16)]
+        + [jax.ShapeDtypeStruct(shape, F32) for shape in shapes],
+        compiler_params=pltpu.CompilerParams(vmem_limit_bytes=LIMIT),
+        cost_estimate=pl.CostEstimate(flops=0, bytes_accessed=4 * 10**6, transcendentals=0),
+        name="unpack_rows",
+    )(seen)
+
+
+def finish_kernel(seen, out):
+    piece = out.shape[1]
+    for f in range(TILE):
+        out[f, :, 0:128] = seen[0, f, 0:piece].astype(F32)
+        packed = seen[0, f, piece : piece + piece // 2].astype(F32)
+        out[f, 0 : piece // 2, 128:192] = packed[:, 0:64]
+        out[f, piece // 2 : piece, 128:192] = turn(packed)[:, 0:64]
+
+
+def finish(seen):
+    n_grp, _, packed, _ = seen.shape
+    piece = packed * 2 // 3
+    return pl.pallas_call(
+        finish_kernel,
+        grid=(n_grp,),
+        in_specs=[pl.BlockSpec((1, TILE, packed, LANES), lambda i: (i, 0, 0, 0))],
+        out_specs=pl.BlockSpec((TILE, piece, 192), lambda i: (i, 0, 0)),
+        out_shape=jax.ShapeDtypeStruct((n_grp * TILE, piece, 192), F32),
+        compiler_params=pltpu.CompilerParams(vmem_limit_bytes=LIMIT),
+        name="finish_tables",
+    )(seen)
+
+
+def cross(array):
+    return lax.ppermute(array, "half", [(0, 1), (1, 0)])
+
+
+def halves(pooled, upstream, ids_now, ids_next, tables, w_fm, w_proj, w_lcb, gain):
+    n_grp, n_lane = lax.axis_size("grp"), lax.axis_size("lane")
+    count = pooled.shape[0]
+    wire = Wire(count, n_grp * n_lane)
+    factor = 1.0 / (count * n_grp * 2 * n_lane)
+    half = lax.axis_index("half").astype(jnp.int32)
+    place = jnp.stack([lax.axis_index("grp").astype(jnp.int32), half])
+    crossed = cross(pack_tables(tables, place))
+    sent = backward(n_grp, n_lane, wire, pooled, upstream, ids_now, ids_next, w_fm, w_proj, w_lcb, gain)
+    seen = exchange(sent, PEER)
+    part, dense = part_sums(n_grp, wire, True, half[None], seen)
+    dense_seen = cross(dense)
+    part_seen = cross(part)
+    (own,) = part_sums(n_grp, wire, False, half[None], seen)
+    rows = exchange(lookup(wire, factor, place, tables, crossed, seen, dense, dense_seen), PEER)
+    next_rows, grad_fm, grad_proj, grad_lcb, grad_gain = unpack(n_grp, n_lane, wire, count, rows)
+    both = (own + part_seen.astype(F32)).astype(BF16)
+    table_grad = finish(exchange(both, "grp"))
+    return next_rows, table_grad, grad_fm, grad_proj, grad_lcb, grad_gain.reshape(-1)
+
+
 def solution(mesh):
-    return jax.shard_map(
-        local,
-        mesh=mesh,
-        in_specs=(
-            P(BOTH, None, None),
-            P(BOTH, None, None),
-            P(BOTH, None),
-            P(BOTH, None),
-            P("emb", None, None),
-            P(),
-            P(),
-            P(),
-            P(),
-        ),
-        out_specs=(P(BOTH, None, None), P("emb", "grp", None), P(), P(), P(), P()),
-        check_vma=False,
-    )
+    n_grp, n_emb = mesh.shape["grp"], mesh.shape["emb"]
+    split = n_emb % 2 == 0 and n_grp * (n_emb // 2) == 16 and n_grp % 2 == 0
+
+    def run(*args):
+        pooled, _, _, _, tables, w_fm = args[:6]
+        count = pooled.shape[0] // (n_grp * n_emb)
+        fits = (
+            split
+            and pooled.shape[1:] == (256, 192)
+            and tables.shape[1] == 128
+            and w_fm.shape[1] == 128
+            and pooled.shape[1] == n_grp * n_emb * TILE
+            and count % STEP == 0
+            and count <= 16
+        )
+        if fits:
+            devices = mesh.devices.reshape(n_grp, 2, n_emb // 2)
+            where, emb, body = Mesh(devices, ("grp", "half", "lane")), ("half", "lane"), halves
+        else:
+            where, emb, body = mesh, ("emb",), local
+        both = ("grp",) + emb
+        return jax.shard_map(
+            body,
+            mesh=where,
+            in_specs=(
+                P(both, None, None),
+                P(both, None, None),
+                P(both, None),
+                P(both, None),
+                P(emb, None, None),
+                P(),
+                P(),
+                P(),
+                P(),
+            ),
+            out_specs=(P(both, None, None), P(emb, "grp", None), P(), P(), P(), P()),
+            check_vma=False,
+        )(*args)
+
+    return run

time: 184 us -> 126 us (0.68)
  local copies, waits for them, and re-layouts: 42.8 us -> 12.7 us
  Pallas kernels: 0 us -> 27.5 us
  matrix products: 19.4 us -> 0 us
  waiting for transfers between devices: 80.3 us -> 65.4 us
  other arithmetic: 12.9 us -> 1.9 us
  starting transfers between devices: 26.5 us -> 17.4 us
    all_to_all x6 -> x3, waiting for transfers between devices: 80.3 us -> 40.2 us  [exchange(): return lax.all_to_all(blocks, axes, split_axis=0, concat_axis=0, tiled=True)]
    pallas_call x0 -> x7, Pallas kernels: none -> 27.5 us  [the longest x1 18.4 us: backward(): pl.pallas_call(functools.partial(backward_kernel, n_grp, n_lane, wire), g...]
    ppermute x0 -> x3, waiting for transfers between devices: none -> 25.2 us  [cross(): return lax.ppermute(array, 'half', [(0, 1), (1, 0)])]
    dot_general x14 -> x0, matrix products: 19.4 us -> none  [product(): return jnp.einsum(form, left, right, preferred_element_type=jnp.float32)]
    all_to_all x6 -> x3, starting transfers between devices: 26.5 us -> 14.3 us  [exchange(): return lax.all_to_all(blocks, axes, split_axis=0, concat_axis=0, tiled=True)]
    convert_element_type x6 -> x0, local copies, waits for them, and re-layouts: 12.1 us -> none  [the longest x3 4.62 us: dense_sum(): total = total.astype(jnp.float32)]
    transpose x4 -> x0, local copies, waits for them, and re-layouts: 6.54 us -> none  [the longest x1 3.17 us: local(): part.reshape(owned, n_grp, rows // n_grp, width).transpose(1, 0, 2, 3)]
    reduce_sum x4 -> x0, other arithmetic: 5.97 us -> none  [the longest x1 3.08 us: local(): table_grad = jnp.sum(exchange(part, 'grp').astype(jnp.float32), axis=0)]
  transfers between devices with their start and end apart: 6 -> 6, of which waited for: 6 -> 5; matrix products, arithmetic and copies ran while one was open for 25% -> 4% of each run, Pallas kernels for 0% -> 5%
where the time goes in v2:
time: 126 us
  waiting for transfers between devices  65.4 us (52%)
  Pallas kernels  27.5 us (22%)
  starting transfers between devices  17.4 us (14%)
  local copies, waits for them, and re-layouts  12.7 us (10%)
  other arithmetic  1.9 us (2%)
    all_to_all x3, waiting for transfers between devices, exchange(): return lax.all_to_all(blocks, axes, split_axis=0, concat_axis=0, tiled=True)  40.2 us
    ppermute x3, waiting for transfers between devices, cross(): return lax.ppermute(array, 'half', [(0, 1), (1, 0)])  25.2 us
    pallas_call x1, Pallas kernels, backward(): pl.pallas_call(functools.partial(backward_kernel, n_grp, n_lane, wire), g...  18.4 us
    all_to_all x3, starting transfers between devices, exchange(): return lax.all_to_all(blocks, axes, split_axis=0, concat_axis=0, tiled=True)  14.3 us
    unnamed x28, local copies, waits for them, and re-layouts  12.7 us
    ppermute x3, starting transfers between devices, cross(): return lax.ppermute(array, 'half', [(0, 1), (1, 0)])  3.13 us
    pallas_call x2, Pallas kernels, part_sums(): pl.pallas_call(functools.partial(part_kernel, n_grp, wire, other), in_spe...  2.78 us
    pallas_call x1, Pallas kernels, lookup(): pl.pallas_call(functools.partial(lookup_kernel, wire, factor), grid_spec=...  2.69 us
  transfers between devices with their start and end apart: 6, of which 5 were waited for; matrix products, arithmetic and copies ran while one was open for 4% of the time, Pallas kernels for 5%

profile of v2, /device:TPU:0, one launch (start us, length us, event | category | flops | bytes accessed | tf_op | source)
XLA Modules:
  0.0 125.8 jit_solution(15138717167905279870)
XLA Ops:
  0.6 1.6 %copy.16.x_ref = bf16[12,256,192]{2,1,0:T(8,128)(2,1)S(1)} copy(bf16[12,256,192]{1,2,0:T(8,128)(2,1)} %param.9) | data formatting | bytes 2359296 | tf_op args[0]
  2.3 1.7 %copy.17.u_ref = bf16[12,256,192]{2,1,0:T(8,128)(2,1)S(1)} copy(bf16[12,256,192]{1,2,0:T(8,128)(2,1)} %param.10) | data formatting | bytes 2359296 | tf_op args[1]
  4.3 18.4 %layer_backward.1 = bf16[16,368,128]{2,1,0:T(8,128)(2,1)S(1)} custom-call(bf16[12,256,192]{2,1,0:T(8,128)(2,1)S(1)} %copy.16.x_ref, bf16[12,256,192]{2,1,0:T(8,128)(2,1)S(1)} %copy.17.u_ref, s32[12,256]{1,0:T(8,128)S(1)} %copy-done.7, s32[12,256]{1,0:T(8,128)S(1)} %copy-done.8, bf16[256,128]{1,0:T(8,128)(2,1)S(1)} %copy-done.6, ...), custom_call_target="tpu_custom_call" | custom-call | flops 6000000000 | bytes 4000000 | tf_op jit(solution)/shard_map/layer_backward/pallas_call | solution.py:266
  22.7 1.1 copy-done.3
  23.8 6.3 %all-to-all-start = ((bf16[16,368,128]{2,1,0:T(8,128)(2,1)}), bf16[16,368,128]{2,1,0:T(8,128)(2,1)S(1)}, u32[]{:S(2)}, u32[]{:S(2)}) async-start(bf16[16,368,128]{2,1,0:T(8,128)(2,1)} %copy-done.3), calls=%async_computation | async-start | bytes 3014656 | tf_op jit(solution)/shard_map/all_to_all | solution.py:60
  30.1 21.3 %all-to-all-done.seen.ids_ref = bf16[16,368,128]{2,1,0:T(8,128)(2,1)S(1)} async-done(((bf16[16,368,128]{2,1,0:T(8,128)(2,1)}), bf16[16,368,128]{2,1,0:T(8,128)(2,1)S(1)}, u32[]{:S(2)}, u32[]{:S(2)}) %all-to-all-start) | async-done | bytes 1507360 | tf_op jit(solution)/shard_map/all_to_all | solution.py:60
  51.4 1.4 %part_other.1 = (bf16[4,8,48,128]{3,2,1,0:T(8,128)(2,1)S(1)}, f32[64,128]{1,0:T(8,128)S(1)}) custom-call(s32[1]{0:T(128)} %bitcast.1.half_ref, bf16[16,368,128]{2,1,0:T(8,128)(2,1)S(1)} %all-to-all-done.seen.ids_ref), custom_call_target="tpu_custom_call" | custom-call | flops 2000000000 | bytes 2000000 | tf_op jit(solution)/shard_map/part_other/pallas_call | solution.py:338
  52.8 2.7 %collective-permute-start.2 = (bf16[4,8,48,128]{3,2,1,0:T(8,128)(2,1)S(1)}, bf16[4,8,48,128]{3,2,1,0:T(8,128)(2,1)}, u32[]{:S(2)}, u32[]{:S(2)}) collective-permute-start(bf16[4,8,48,128]{3,2,1,0:T(8,128)(2,1)S(1)} %get-tuple-element.15), channel_id=1, source_target_pairs={{0,4},{4,0},{1,5},{5,1},{2,6},{6,2},{3,7},{7,3},{8,12},{12,8},{9,1... | collective-permute-start | bytes 1179656 | tf_op jit(solution)/shard_map/ppermute | solution.py:502
  55.5 3.1 %copy.19.tables = bf16[32,128,192]{2,1,0:T(8,128)(2,1)S(1)} copy(bf16[32,128,192]{1,2,0:T(8,128)(2,1)} %param.13) | data formatting | bytes 3145728 | tf_op args[4]
  60.0 1.4 %part_own.1 = f32[4,8,48,128]{3,2,1,0:T(8,128)S(1)} custom-call(s32[1]{0:T(128)} %bitcast.1.half_ref, bf16[16,368,128]{2,1,0:T(8,128)(2,1)S(1)} %copy-done.1), custom_call_target="tpu_custom_call" | custom-call | flops 2000000000 | bytes 2000000 | tf_op jit(solution)/shard_map/part_own/pallas_call | solution.py:338
  61.4 20.4 %collective-permute-done.2 = bf16[4,8,48,128]{3,2,1,0:T(8,128)(2,1)} collective-permute-done((bf16[4,8,48,128]{3,2,1,0:T(8,128)(2,1)S(1)}, bf16[4,8,48,128]{3,2,1,0:T(8,128)(2,1)}, u32[]{:S(2)}, u32[]{:S(2)}) %collective-permute-start.2) | collective-permute-done | bytes 393248 | tf_op jit(solution)/shard_map/ppermute | solution.py:502
  81.8 1.8 %add_convert_fusion = bf16[4,8,48,128]{3,2,1,0:T(8,128)(2,1)} fusion(f32[4,8,48,128]{3,2,1,0:T(8,128)S(1)} %part_own.1, bf16[4,8,48,128]{3,2,1,0:T(8,128)(2,1)} %collective-permute-done.2), kind=kLoop, calls=%fused_computation | loop fusion | flops 589824 | bytes 1572864 | tf_op jit(solution)/shard_map/convert_element_type | solution.py:521
  83.6 3.5 %all-to-all-start.2 = ((bf16[4,8,48,128]{3,2,1,0:T(8,128)(2,1)}), bf16[4,8,48,128]{3,2,1,0:T(8,128)(2,1)S(1)}, u32[]{:S(2)}, u32[]{:S(2)}) async-start(bf16[4,8,48,128]{3,2,1,0:T(8,128)(2,1)} %add_convert_fusion), calls=%async_computation.2 | async-start | bytes 786432 | tf_op jit(solution)/shard_map/all_to_all | solution.py:60
  87.2 2.6 %collective-permute-done.crossed = bf16[8,192,128]{2,1,0:T(8,128)(2,1)S(1)} collective-permute-done((bf16[8,192,128]{2,1,0:T(8,128)(2,1)S(1)}, bf16[8,192,128]{2,1,0:T(8,128)(2,1)S(1)}, u32[]{:S(2)}, u32[]{:S(2)}) %collective-permute-start) | collective-permute-done | bytes 393248 | tf_op jit(solution)/shard_map/ppermute | solution.py:502
  89.7 2.2 %collective-permute-done.1.dense_seen = f32[64,128]{1,0:T(8,128)S(1)} collective-permute-done((f32[64,128]{1,0:T(8,128)S(1)}, f32[64,128]{1,0:T(8,128)S(1)}, u32[]{:S(2)}, u32[]{:S(2)}) %collective-permute-start.1) | collective-permute-done | bytes 32800 | tf_op jit(solution)/shard_map/ppermute | solution.py:502
  92.0 1.4 %copy-done.2 = bf16[16,368,128]{2,1,0:T(8,128)(2,1)S(1)} copy-done((bf16[16,368,128]{2,1,0:T(8,128)(2,1)S(1)}, bf16[16,368,128]{2,1,0:T(8,128)(2,1)}, u32[]{:S(2)}) %copy-start.2) | copy-done | bytes 1507352
  93.4 2.7 %lookup.1 = bf16[16,352,128]{2,1,0:T(8,128)(2,1)S(1)} custom-call(s32[2]{0:T(128)S(1)} %pad_add_fusion.place, bf16[32,128,192]{2,1,0:T(8,128)(2,1)S(1)} %copy.19.tables, bf16[8,192,128]{2,1,0:T(8,128)(2,1)S(1)} %collective-permute-done.crossed, bf16[16,368,128]{2,1,0:T(8,128)(2,1)S(1)} %copy-done.2, f32[64,128]{1,0:T(8,128)S(1)} %get-tuple-element.13.dense_own, ...), custom_call_target="tpu_custom_call" | custom-call | flops 2000000000 | bytes 4000000 | tf_op jit(solution)/shard_map/lookup/pallas_call | solution.py:394
  96.1 1.1 copy-done.4
  97.2 4.5 %all-to-all-start.1 = ((bf16[16,352,128]{2,1,0:T(8,128)(2,1)}), bf16[16,352,128]{2,1,0:T(8,128)(2,1)S(1)}, u32[]{:S(2)}, u32[]{:S(2)}) async-start(bf16[16,352,128]{2,1,0:T(8,128)(2,1)} %copy-done.4), calls=%async_computation.1 | async-start | bytes 2883584 | tf_op jit(solution)/shard_map/all_to_all | solution.py:60
  101.7 1.7 %finish_tables.1 = f32[32,32,192]{2,1,0:T(8,128)} custom-call(bf16[4,8,48,128]{3,2,1,0:T(8,128)(2,1)S(1)} %all-to-all-done.2.seen), custom_call_target="tpu_custom_call" | custom-call | tf_op jit(solution)/shard_map/finish_tables/pallas_call | solution.py:490
  103.4 18.9 %all-to-all-done.1.seen = bf16[16,352,128]{2,1,0:T(8,128)(2,1)S(1)} async-done(((bf16[16,352,128]{2,1,0:T(8,128)(2,1)}), bf16[16,352,128]{2,1,0:T(8,128)(2,1)S(1)}, u32[]{:S(2)}, u32[]{:S(2)}) %all-to-all-start.1) | async-done | bytes 1441824 | tf_op jit(solution)/shard_map/all_to_all | solution.py:60
  122.3 1.2 unpack_rows.1
  123.5 1.5 %copy.20 = bf16[12,256,192]{1,2,0:T(8,128)(2,1)} copy(bf16[12,256,192]{2,1,0:T(8,128)(2,1)S(1)} %get-tuple-element.20) | data formatting | bytes 2359296
  125.0 0.7 copy.21
  (25 shorter events, 1.6 us)
Async XLA Ops:
  2.3 1.8 %copy-start.10 = (bf16[128,192]{0,1:T(8,128)(2,1)S(1)}, bf16[128,192]{0,1:T(8,128)(2,1)}, u32[]{:S(2)}) copy-start(bf16[128,192]{0,1:T(8,128)(2,1)} %param.15) | copy-start | bytes 147460
  2.3 1.9 %copy-start.5 = (bf16[256,256]{1,0:T(8,128)(2,1)S(1)}, bf16[256,256]{1,0:T(8,128)(2,1)}, u32[]{:S(2)}) copy-start(bf16[256,256]{1,0:T(8,128)(2,1)} %lcb_ref.1) | copy-start | bytes 393220
  2.3 1.9 %copy-start.6 = (bf16[256,128]{1,0:T(8,128)(2,1)S(1)}, bf16[256,128]{1,0:T(8,128)(2,1)}, u32[]{:S(2)}) copy-start(bf16[256,128]{1,0:T(8,128)(2,1)} %fm_ref.1) | copy-start | bytes 196612
  2.3 1.9 %copy-start.7 = (s32[12,256]{1,0:T(8,128)S(1)}, s32[12,256]{1,0:T(8,128)}, u32[]{:S(2)}) copy-start(s32[12,256]{1,0:T(8,128)} %now_ref.1) | copy-start | bytes 36868
  2.3 1.9 %copy-start.8 = (s32[12,256]{1,0:T(8,128)S(1)}, s32[12,256]{1,0:T(8,128)}, u32[]{:S(2)}) copy-start(s32[12,256]{1,0:T(8,128)} %next_ref.1) | copy-start | bytes 36868
  2.3 1.9 %copy-start.9 = (f32[192]{0:T(256)S(1)}, f32[192]{0:T(256)}, u32[]{:S(2)}) copy-start(f32[192]{0:T(256)} %param.17) | copy-start | bytes 2308
  22.7 1.2 copy-start.3
  23.8 27.6 %all-to-all-start = ((bf16[16,368,128]{2,1,0:T(8,128)(2,1)}), bf16[16,368,128]{2,1,0:T(8,128)(2,1)S(1)}, u32[]{:S(2)}, u32[]{:S(2)}) async-start(bf16[16,368,128]{2,1,0:T(8,128)(2,1)} %copy-done.3), calls=%async_computation | async-start | bytes 3014656 | tf_op jit(solution)/shard_map/all_to_all | solution.py:60
  51.4 1.4 %copy-start = (bf16[16,368,128]{2,1,0:T(8,128)(2,1)}, bf16[16,368,128]{2,1,0:T(8,128)(2,1)S(1)}, u32[]{:S(2)}) copy-start(bf16[16,368,128]{2,1,0:T(8,128)(2,1)S(1)} %all-to-all-done.seen.ids_ref) | copy-start | bytes 4521988
  52.8 29.0 %collective-permute-start.2 = (bf16[4,8,48,128]{3,2,1,0:T(8,128)(2,1)S(1)}, bf16[4,8,48,128]{3,2,1,0:T(8,128)(2,1)}, u32[]{:S(2)}, u32[]{:S(2)}) collective-permute-start(bf16[4,8,48,128]{3,2,1,0:T(8,128)(2,1)S(1)} %get-tuple-element.15), channel_id=1, source_target_pairs={{0,4},{4,0},{1,5},{5,1},{2,6},{6,2},{3,7},{7,3},{8,12},{12,8},{9,1... | collective-permute-start | bytes 1179656 | tf_op jit(solution)/shard_map/ppermute | solution.py:502
  58.7 1.4 %copy-start.1 = (bf16[16,368,128]{2,1,0:T(8,128)(2,1)S(1)}, bf16[16,368,128]{2,1,0:T(8,128)(2,1)}, u32[]{:S(2)}) copy-start(bf16[16,368,128]{2,1,0:T(8,128)(2,1)} %copy-done) | copy-start | bytes 4521988
  59.5 30.3 %collective-permute-start = (bf16[8,192,128]{2,1,0:T(8,128)(2,1)S(1)}, bf16[8,192,128]{2,1,0:T(8,128)(2,1)S(1)}, u32[]{:S(2)}, u32[]{:S(2)}) collective-permute-start(bf16[8,192,128]{2,1,0:T(8,128)(2,1)S(1)} %pack_tables.1), channel_id=1, source_target_pairs={{0,4},{4,0},{1,5},{5,1},{2,6},{6,2},{3,7},{7,3},{8,12},{12,8},{9,1... | collective-permute-start | bytes 1179656 | tf_op jit(solution)/shard_map/ppermute | solution.py:502
  83.6 13.6 %all-to-all-start.2 = ((bf16[4,8,48,128]{3,2,1,0:T(8,128)(2,1)}), bf16[4,8,48,128]{3,2,1,0:T(8,128)(2,1)S(1)}, u32[]{:S(2)}, u32[]{:S(2)}) async-start(bf16[4,8,48,128]{3,2,1,0:T(8,128)(2,1)} %add_convert_fusion), calls=%async_computation.2 | async-start | bytes 786432 | tf_op jit(solution)/shard_map/all_to_all | solution.py:60
  87.1 4.9 %collective-permute-start.1 = (f32[64,128]{1,0:T(8,128)S(1)}, f32[64,128]{1,0:T(8,128)S(1)}, u32[]{:S(2)}, u32[]{:S(2)}) collective-permute-start(f32[64,128]{1,0:T(8,128)S(1)} %get-tuple-element.13.dense_own), channel_id=1, source_target_pairs={{0,4},{4,0},{1,5},{5,1},{2,6},{6,2},{3,7},{7,3},{8,12},{12,8},{9,1... | collective-permute-start | bytes 98312 | tf_op jit(solution)/shard_map/ppermute | solution.py:502
  92.0 1.4 %copy-start.2 = (bf16[16,368,128]{2,1,0:T(8,128)(2,1)S(1)}, bf16[16,368,128]{2,1,0:T(8,128)(2,1)}, u32[]{:S(2)}) copy-start(bf16[16,368,128]{2,1,0:T(8,128)(2,1)} %copy-done) | copy-start | bytes 4521988
  96.1 1.1 copy-start.4
  97.2 25.2 %all-to-all-start.1 = ((bf16[16,352,128]{2,1,0:T(8,128)(2,1)}), bf16[16,352,128]{2,1,0:T(8,128)(2,1)S(1)}, u32[]{:S(2)}, u32[]{:S(2)}) async-start(bf16[16,352,128]{2,1,0:T(8,128)(2,1)} %copy-done.4), calls=%async_computation.1 | async-start | bytes 2883584 | tf_op jit(solution)/shard_map/all_to_all | solution.py:60

commit v3 on v2

v3 whole, which is shorter than its diff:
```python
import functools

import jax
import jax.numpy as jnp
from jax import lax
from jax.experimental import pallas as pl
from jax.experimental.pallas import tpu as pltpu
from jax.sharding import Mesh, PartitionSpec as P

F32, BF16 = jnp.float32, jnp.bfloat16
SMEM = pl.BlockSpec(memory_space=pltpu.SMEM)
VMEM = pl.BlockSpec(memory_space=pltpu.VMEM)
LANES = 128
TILE = 8
STEP = 4
LIMIT = 40 * 1024 * 1024
PEER = ("grp", "lane")


BOTH = ("grp", "emb")


def product(form, left, right):
    return jnp.einsum(form, left, right, preferred_element_type=jnp.float32)


def layer_backward(embeds, cotangent, w_fm, w_proj, w_lcb, gain):
    fm_proj = product("bfc,fj->bcj", embeds, w_fm).astype(jnp.bfloat16)
    fm_rows = product("bfc,bcj->bfj", embeds, fm_proj).astype(jnp.bfloat16)
    projected = product("bfj,jc->bfc", fm_rows, w_proj)
    compressed = product("fi,bfc->bic", w_lcb, embeds)
    summed = embeds.astype(jnp.float32) + projected + compressed
    centre = jnp.mean(summed, axis=2, keepdims=True)
    spread = jnp.mean((summed - centre) ** 2, axis=2, keepdims=True)
    inverse = lax.rsqrt(spread + 1e-05)
    normed = (summed - centre) * inverse
    upper = cotangent.astype(jnp.float32)
    scaled = upper * gain
    grad_sum = inverse * (
        scaled
        - jnp.mean(scaled, axis=2, keepdims=True)
        - normed * jnp.mean(scaled * normed, axis=2, keepdims=True)
    )
    grad_sum = grad_sum.astype(jnp.bfloat16)
    grad_gain = jnp.sum(upper * normed, axis=(0, 1))
    grad_proj = product("bfj,bfc->jc", fm_rows, grad_sum)
    grad_rows = product("bfc,jc->bfj", grad_sum, w_proj).astype(jnp.bfloat16)
    grad_p = product("bfc,bfj->bcj", embeds, grad_rows).astype(jnp.bfloat16)
    grad_fm = product("bfc,bcj->fj", embeds, grad_p)
    grad_lcb = product("bfc,bic->fi", embeds, grad_sum)
    grad_in = (
        grad_sum.astype(jnp.float32)
        + product("bfj,bcj->bfc", grad_rows, fm_proj)
        + product("fj,bcj->bfc", w_fm, grad_p)
        + product("fi,bic->bfc", w_lcb, grad_sum)
    )
    return (grad_in.astype(jnp.bfloat16), (grad_fm, grad_proj, grad_lcb, grad_gain))


def exchange(blocks, axes):
    return lax.all_to_all(blocks, axes, split_axis=0, concat_axis=0, tiled=True)


def dense_sum(partials, factor):
    n = lax.axis_size("grp") * lax.axis_size("emb")
    shapes = [part.shape for part in partials]
    flat = jnp.concatenate([part.reshape(-1) for part in partials])
    unit = 128 * n
    padded = -(-flat.shape[0] // unit) * unit
    flat = jnp.pad(flat, (0, padded - flat.shape[0])).astype(jnp.bfloat16)
    seen = exchange(flat.reshape(n, padded // unit, 128), BOTH)
    share = (jnp.sum(seen.astype(jnp.float32), axis=0) * factor).astype(jnp.bfloat16)
    total = exchange(jnp.broadcast_to(share[None], (n,) + share.shape), BOTH).reshape(-1)
    total = total.astype(jnp.float32)
    outs, at = [], 0
    for shape in shapes:
        size = 1
        for extent in shape:
            size *= extent
        outs.append(total[at : at + size].reshape(shape))
        at += size
    return outs


def local(pooled, upstream, ids_now, ids_next, tables, w_fm, w_proj, w_lcb, gain):
    n_grp, n_emb = lax.axis_size("grp"), lax.axis_size("emb")
    count, features, width = pooled.shape
    owned, rows = tables.shape[:2]
    ids = jnp.stack([ids_now, ids_next]).reshape(2, count, n_emb, owned)
    ids = exchange(ids.transpose(2, 0, 1, 3), "emb")
    row_index = jnp.arange(rows)
    wanted = (ids[:, 1, :, :, None] == row_index).astype(jnp.bfloat16)
    fetched = product("esfr,frc->esfc", wanted, tables).astype(jnp.bfloat16)
    next_rows = exchange(fetched, "emb")
    next_rows = next_rows.transpose(1, 0, 2, 3).reshape(count, features, width)
    grad_in, partials = layer_backward(pooled, upstream, w_fm, w_proj, w_lcb, gain)
    grad_in = grad_in.reshape(count, n_emb, owned, width).transpose(1, 0, 2, 3)
    grads = exchange(grad_in, "emb")
    hit = (ids[:, 0, :, :, None] == row_index).astype(jnp.bfloat16)
    part = product("esfr,esfc->frc", hit, grads).astype(jnp.bfloat16)
    part = part.reshape(owned, n_grp, rows // n_grp, width).transpose(1, 0, 2, 3)
    table_grad = jnp.sum(exchange(part, "grp").astype(jnp.float32), axis=0)
    dense = dense_sum(partials, 1.0 / (count * n_grp * n_emb))
    return (next_rows, table_grad, *dense)


def params(**more):
    return pltpu.CompilerParams(vmem_limit_bytes=LIMIT, **more)


def mm(left, right, dims=((1,), (0,))):
    return lax.dot_general(left, right, (dims, ((), ())), preferred_element_type=F32)


def mm_nt(left, right):
    return mm(left, right, ((1,), (1,)))


def low_lanes(shape):
    return lax.broadcasted_iota(jnp.int32, shape, 1) < LANES // 2


def turn(tile):
    return pltpu.roll(tile, LANES // 2, 1)


def identity(rows, lanes):
    row = lax.broadcasted_iota(jnp.int32, (rows, lanes), 0)
    return jnp.where(row == lax.broadcasted_iota(jnp.int32, (rows, lanes), 1), 1.0, 0.0).astype(BF16)


class Wire:
    def __init__(self, count, peers):
        self.left = count * TILE
        self.half = self.left + self.left // 2
        self.ids = 16
        self.dense = 1024 // peers


def place_of(n_grp, n_lane, peer):
    return (peer % n_lane) * n_grp * TILE + (peer // n_lane) * TILE


def backward_kernel(
    n_grp, n_lane, wire,
    half_ref, x_ref, u_ref, now_ref, next_ref, fm_ref, proj_t_ref, lcb_ref, gain_ref,
    other_ref, own_ref,
    fm_t, proj, lcb_t, gains, eye, left_in, right_in, grads, turned, sum_fm_t, sum_proj_t, sum_lcb, sum_gain, ids,
):
    step = pl.program_id(0)
    width, features = x_ref.shape[1:]
    rank = fm_ref.shape[1]
    peers = n_grp * n_lane
    scale = 1.0 / width

    @pl.when(step == 0)
    def _():
        turned_fm = fm_ref[...].astype(F32).T.astype(BF16)
        fm_t[...] = turned_fm
        for s in range(STEP):
            right_in[s, rank : 2 * rank] = turned_fm
        proj[...] = proj_t_ref[...].astype(F32).T.astype(BF16)
        lcb_t[...] = lcb_ref[...].astype(F32).T.astype(BF16)
        column = jnp.broadcast_to(gain_ref[...], (LANES, width)).T
        gains[:, 0:128] = column
        gains[:, 128:256] = column
        eye[...] = identity(features, features)
        sum_fm_t[...] = jnp.zeros_like(sum_fm_t)
        sum_proj_t[...] = jnp.zeros_like(sum_proj_t)
        sum_lcb[...] = jnp.zeros_like(sum_lcb)
        sum_gain[...] = jnp.zeros_like(sum_gain)

    x_all = x_ref[...].reshape(STEP * width, features)
    p_all = mm(x_all, fm_ref[...]).astype(BF16)
    mixed = mm(x_all, lcb_ref[...])
    d_sums = []
    add_fm, add_proj, add_gain = 0.0, 0.0, 0.0
    for s in range(STEP):
        here = slice(s * width, (s + 1) * width)
        x = x_ref[s]
        left_in[s, :, 0:rank] = p_all[here]
        p_t = mm_nt(fm_t[...], x).astype(BF16)
        g_t = mm(p_t, x).astype(BF16)
        summed = x.astype(F32) + mm(proj_t_ref[...], g_t) + mixed[here]
        centre = jnp.sum(summed, axis=0, keepdims=True) * scale
        summed = summed - centre
        spread = jnp.sum(summed * summed, axis=0, keepdims=True) * scale
        inverse = lax.rsqrt(spread + 1e-05)
        normed = summed * inverse
        upper = u_ref[s].astype(F32)
        scaled = upper * gains[...]
        first = jnp.sum(scaled, axis=0, keepdims=True) * scale
        second = jnp.sum(scaled * normed, axis=0, keepdims=True) * scale
        d_sum = (inverse * (scaled - first - normed * second)).astype(BF16)
        add_gain += upper * normed
        d_g_t = mm(proj[...], d_sum).astype(BF16)
        right_in[s, 0:rank] = d_g_t
        left_in[s, :, rank : 2 * rank] = mm_nt(x, d_g_t).astype(BF16)
        d_p_t = mm_nt(d_g_t, x).astype(BF16)
        add_fm += mm(d_p_t, x)
        add_proj += mm_nt(d_sum, g_t)
        d_sums.append(d_sum)
    d_all = jnp.concatenate(d_sums, axis=0)
    back = mm(d_all, lcb_t[...])
    sum_lcb[...] += mm(x_all, d_all, ((0,), (0,)))
    sum_fm_t[...] += add_fm
    sum_proj_t[...] += add_proj
    sum_gain[...] += add_gain
    for s in range(STEP):
        here = slice(s * width, (s + 1) * width)
        grad = d_sums[s].astype(F32) + mm(left_in[s], right_in[s]) + back[here]
        grad = grad.astype(BF16)
        grads[s * 128 : s * 128 + 128] = grad[0:128]
        at = 512 + 64 * (2 * (s % 2) + s // 2)
        grads[at : at + 64] = grad[128:192]
    rows = mm_nt(eye[...], grads[...])
    turned[0] = rows[0:128]
    turned[1] = rows[128:256]

    half = half_ref[0]
    for out_ref, which in ((other_ref, 1 - half), (own_ref, half)):
        for peer in range(peers):
            at = place_of(n_grp, n_lane, peer)
            line = turned[which, at : at + TILE]
            left = jnp.concatenate([line[:, s * 128 : s * 128 + 128] for s in range(STEP)], axis=0)
            row = pl.multiple_of(step * 32, 16)
            out_ref[peer, pl.ds(row, 32)] = left.astype(BF16)
            right = jnp.concatenate([line[:, 512:640], line[:, 640:768]], axis=0)
            row = pl.multiple_of(wire.left + step * 16, 16)
            out_ref[peer, pl.ds(row, 16)] = right.astype(BF16)

    @pl.when(step == pl.num_programs(0) - 1)
    def _():
        part = features // peers
        third = width // peers
        total = jnp.sum((sum_gain[:, 0:128] + sum_gain[:, 128:256]).T, axis=0, keepdims=True)
        high = total.astype(BF16).astype(F32)
        low = total - high
        middle = jnp.concatenate([high[:, 128:192], low[:, 128:192]], axis=1)
        gain_rows = [high[:, 0:128], middle, low[:, 0:128], jnp.zeros((1, LANES), F32)]
        total_fm = sum_fm_t[...].T
        for peer in range(peers):
            at = wire.half
            here = slice(peer * part, (peer + 1) * part)
            own_ref[peer, at : at + part] = total_fm[here].astype(BF16)
            own_ref[peer, at + part : at + 2 * part] = sum_lcb[here, 0:128].astype(BF16)
            own_ref[peer, at + 2 * part : at + 3 * part] = sum_lcb[here, 128:256].astype(BF16)
            last = [sum_proj_t[peer * third : (peer + 1) * third]] + gain_rows
            own_ref[peer, at + 3 * part : at + 4 * part] = jnp.concatenate(last, axis=0).astype(BF16)

        count = now_ref.shape[0]
        lane = lax.broadcasted_iota(jnp.int32, (16, LANES), 1)
        sample = lax.broadcasted_iota(jnp.int32, (16, LANES), 0)
        mine = (lane // TILE == sample) & (sample < count)
        for which, ref in enumerate((now_ref, next_ref)):
            ids[which] = jnp.zeros_like(ids[which])
            ids[which, 0:count] = ref[...].astype(F32)
        for peer in range(peers):
            at = place_of(n_grp, n_lane, peer)
            lines = []
            for which in range(2):
                for side in range(2):
                    line = ids[which, :, side * 128 : side * 128 + 128]
                    if at:
                        line = pltpu.roll(line, LANES - at, 1)
                    line = pltpu.roll(line, 0, 1, stride=TILE, stride_axis=0)
                    lines.append(jnp.sum(jnp.where(mine, line, 0.0), axis=0, keepdims=True))
            lines.append(jnp.zeros((12, LANES), F32))
            other_ref[peer, wire.half : wire.half + 16] = jnp.concatenate(lines, axis=0).astype(BF16)


def backward(n_grp, n_lane, wire, half, pooled_t, upstream_t, ids_now, ids_next, w_fm, w_proj_t, w_lcb, gain):
    count, width, features = pooled_t.shape
    rank = w_fm.shape[1]
    peers = n_grp * n_lane
    block = pl.BlockSpec((STEP, width, features), lambda i: (i, 0, 0))

    def whole(shape):
        return pl.BlockSpec(shape, lambda i: (0,) * len(shape))

    rest = (ids_now, ids_next, w_fm, w_proj_t, w_lcb, gain.reshape(1, width))
    shapes = [(peers, wire.half + wire.ids, LANES), (peers, wire.half + wire.dense, LANES)]
    return pl.pallas_call(
        functools.partial(backward_kernel, n_grp, n_lane, wire),
        grid=(count // STEP,),
        in_specs=[SMEM, block, block] + [whole(array.shape) for array in rest],
        out_specs=[whole(shape) for shape in shapes],
        out_shape=[jax.ShapeDtypeStruct(shape, BF16) for shape in shapes],
        scratch_shapes=[
            pltpu.VMEM((rank, features), BF16),
            pltpu.VMEM((rank, width), BF16),
            pltpu.VMEM((features, features), BF16),
            pltpu.VMEM((width, features), F32),
            pltpu.VMEM((features, features), BF16),
            pltpu.VMEM((STEP, width, 2 * rank), BF16),
            pltpu.VMEM((STEP, 2 * rank, features), BF16),
            pltpu.VMEM((STEP * width, features), BF16),
            pltpu.VMEM((2, features // 2, STEP * width), F32),
            pltpu.VMEM((rank, features), F32),
            pltpu.VMEM((width, rank), F32),
            pltpu.VMEM((features, features), F32),
            pltpu.VMEM((width, features), F32),
            pltpu.VMEM((2, 16, features), F32),
        ],
        compiler_params=params(),
        cost_estimate=pl.CostEstimate(flops=10**9, bytes_accessed=4 * 10**6, transcendentals=0),
        name="layer_backward",
    )(half, pooled_t, upstream_t, *rest)


def part_kernel(n_grp, wire, other, half_ref, seen, ids_ref, *refs):
    out, held = refs[0], refs[-1]
    peers = seen.shape[0]
    half = 1 - half_ref[0] if other else half_ref[0]
    if not other:
        dense = refs[1]
        total = seen[0, wire.half : wire.half + wire.dense].astype(F32)
        for peer in range(1, peers):
            total = total + seen[peer, wire.half : wire.half + wire.dense].astype(F32)
        dense[...] = total
    lane = lax.broadcasted_iota(jnp.int32, (1, LANES), 1)
    start = ((lane % TILE) * LANES).astype(F32)
    keys = []
    for peer in range(peers):
        at = peer * LANES
        held[at : at + wire.left, 0:128] = seen[peer, 0 : wire.left]
        right = seen[peer, wire.left : wire.half]
        turned = turn(right.astype(F32)).astype(BF16)
        for i in range(wire.left // 32):
            held[at + 32 * i : at + 32 * i + 16, 128:256] = right[16 * i : 16 * i + 16]
            held[at + 32 * i + 16 : at + 32 * i + 32, 128:256] = turned[16 * i : 16 * i + 16]
        if wire.left < LANES:
            held[at + wire.left : at + LANES] = jnp.zeros((LANES - wire.left, 256), BF16)
        ids = ids_ref[peer].astype(F32)
        key = jnp.where(half == 0, ids[0:1], ids[1:2]) + start
        keys.append(jnp.where(lane < wire.left, key, -1.0))
    keys = jnp.concatenate(keys, axis=1)
    piece = LANES // n_grp
    for pair in range(TILE // 2):
        row = lax.broadcasted_iota(jnp.int32, (256, 1), 0).astype(F32) + 256.0 * pair
        hit = jnp.where(keys == row, 1.0, 0.0).astype(BF16)
        part = mm(hit, held[...])
        for f in range(2):
            for g in range(n_grp):
                at = f * LANES + g * piece
                rows = part[at : at + piece]
                out[g, 2 * pair + f, 0:piece] = rows[:, 0:128].astype(out.dtype)
                second = turn(rows[piece // 2 :, 128:256])
                packed = jnp.where(low_lanes(second.shape), rows[: piece // 2, 128:256], second)
                out[g, 2 * pair + f, piece : piece + piece // 2] = packed.astype(out.dtype)


def part_sums(n_grp, wire, other, half, seen, ids):
    peers = seen.shape[0]
    piece = LANES // n_grp
    shapes = [jax.ShapeDtypeStruct((n_grp, TILE, piece + piece // 2, LANES), BF16 if other else F32)]
    if not other:
        shapes.append(jax.ShapeDtypeStruct((wire.dense, LANES), F32))

    def whole(shape):
        return pl.BlockSpec(shape, lambda i: (0,) * len(shape))

    at = wire.half // 16
    return pl.pallas_call(
        functools.partial(part_kernel, n_grp, wire, other),
        grid=(1,),
        in_specs=[SMEM, whole(seen.shape), pl.BlockSpec((peers, 16, LANES), lambda i: (0, at, 0))],
        out_specs=[whole(shape.shape) for shape in shapes],
        out_shape=shapes,
        scratch_shapes=[pltpu.VMEM((peers * LANES, 256), BF16)],
        compiler_params=params(),
        cost_estimate=pl.CostEstimate(flops=10**9, bytes_accessed=10**6, transcendentals=0),
        name="part_other" if other else "part_own",
    )(half, seen, ids)


def lookup_kernel(wire, factor, half_ref, mine_t, crossed_t, ids_ref, dense_own, dense_seen, out, held):
    peers = ids_ref.shape[0]
    half = half_ref[0]
    for f in range(TILE):
        at = f * LANES
        for side, ref in ((half, mine_t), (1 - half, crossed_t)):
            held[side, 0:192, at : at + LANES] = ref[f]
            held[side, 192:256, at : at + LANES] = ref[f, 128:192]
    ids = ids_ref[...].astype(F32).reshape(peers * 16, LANES)
    lane = lax.broadcasted_iota(jnp.int32, (1, LANES), 1)
    keys = (ids + ((lane % TILE) * LANES).astype(F32)).T
    column = lax.broadcasted_iota(jnp.int32, (1, TILE * LANES), 1).astype(F32)
    total = ((dense_own[...] + dense_seen[...]) * factor).astype(BF16)
    for which in range(2):
        for pair in range(peers // 2):
            mine = []
            for peer in (2 * pair, 2 * pair + 1):
                at = peer * 16 + 2 + which
                mine.append(keys[0 : wire.left, at : at + 1])
            hit = jnp.where(jnp.concatenate(mine, axis=0) == column, 1.0, 0.0).astype(BF16)
            both = mm_nt(hit, held[which])
            for k in range(2):
                got = both[k * wire.left : (k + 1) * wire.left]
                peer, base = 2 * pair + k, which * wire.half
                out[peer, base : base + wire.left] = got[:, 0:128].astype(BF16)
                for i in range(wire.left // 32):
                    first, second = got[32 * i : 32 * i + 16, 128:256], got[32 * i + 16 : 32 * i + 32, 128:256]
                    at = base + wire.left + 16 * i
                    out[peer, at : at + 16] = jnp.where(low_lanes(first.shape), first, second).astype(BF16)
    for peer in range(peers):
        out[peer, 2 * wire.half :] = total


def lookup(wire, factor, half, mine_t, crossed_t, ids, dense_own, dense_seen):
    peers = ids.shape[0]
    rows = 2 * wire.half + wire.dense

    def whole(shape):
        return pl.BlockSpec(shape, lambda i: (0,) * len(shape))

    at = wire.half // 16
    return pl.pallas_call(
        functools.partial(lookup_kernel, wire, factor),
        grid=(1,),
        in_specs=[
            SMEM,
            whole(mine_t.shape),
            whole(crossed_t.shape),
            pl.BlockSpec((peers, 16, LANES), lambda i: (0, at, 0)),
            whole(dense_own.shape),
            whole(dense_seen.shape),
        ],
        out_specs=whole((peers, rows, LANES)),
        out_shape=jax.ShapeDtypeStruct((peers, rows, LANES), BF16),
        scratch_shapes=[pltpu.VMEM((2, 256, TILE * LANES), BF16)],
        compiler_params=params(),
        cost_estimate=pl.CostEstimate(flops=10**9, bytes_accessed=10**6, transcendentals=0),
        name="lookup",
    )(half, mine_t, crossed_t, ids, dense_own, dense_seen)


def unpack_kernel(n_grp, n_lane, wire, seen, rows_out, fm, proj_t, lcb, gain, held):
    step = pl.program_id(0)
    peers = n_grp * n_lane
    for side in range(2):
        for q in range(n_lane):
            for gg in range(n_grp // 2):
                left, right = [], []
                for g in (2 * gg, 2 * gg + 1):
                    peer = g * n_lane + q
                    row = pl.multiple_of(side * wire.half + step * 32, 16)
                    left.append(seen[peer, pl.ds(row, 32)].astype(F32))
                    row = pl.multiple_of(side * wire.half + wire.left + step * 16, 16)
                    packed = seen[peer, pl.ds(row, 16)].astype(F32)
                    right.append(jnp.concatenate([packed, turn(packed)], axis=0))
                at = side * 128 + q * n_grp * TILE + gg * 16
                for s in range(STEP):
                    here = slice(s * TILE, s * TILE + TILE)
                    both = jnp.concatenate([left[0][here], left[1][here]], axis=0)
                    held[s, at : at + 16, 0:128] = both.astype(BF16)
                    both = jnp.concatenate([right[0][here], right[1][here]], axis=0)
                    held[s, at : at + 16, 128:256] = both.astype(BF16)
    eye = identity(192, 256)
    for s in range(STEP):
        rows_out[s] = mm_nt(eye, held[s]).astype(BF16)

    @pl.when(step == 0)
    def _():
        part, third = 256 // peers, 192 // peers
        for peer in range(peers):
            dense = seen[peer, 2 * wire.half :].astype(F32)
            here = slice(peer * part, (peer + 1) * part)
            fm[here] = dense[0:part]
            lcb[here, 0:128] = dense[part : 2 * part]
            lcb[here, 128:256] = dense[2 * part : 3 * part]
            last = dense[3 * part : 4 * part]
            proj_t[peer * third : (peer + 1) * third] = last[0:third]
            if peer == 0:
                last = last[third : third + 3]
                gain[:, 0:128] = last[0:1] + last[2:3]
                gain[:, 128:192] = (last + turn(last))[1:2, 0:64]


def unpack(n_grp, n_lane, wire, count, seen):
    def whole(*shape):
        return pl.BlockSpec(shape, lambda i: (0,) * len(shape))

    shapes = [(256, 128), (192, 128), (256, 256), (1, 192)]
    return pl.pallas_call(
        functools.partial(unpack_kernel, n_grp, n_lane, wire),
        grid=(count // STEP,),
        in_specs=[whole(*seen.shape)],
        out_specs=[pl.BlockSpec((STEP, 192, 256), lambda i: (i, 0, 0))] + [whole(*shape) for shape in shapes],
        out_shape=[jax.ShapeDtypeStruct((count, 192, 256), BF16)]
        + [jax.ShapeDtypeStruct(shape, F32) for shape in shapes],
        scratch_shapes=[pltpu.VMEM((STEP, 256, 256), BF16)],
        compiler_params=params(),
        cost_estimate=pl.CostEstimate(flops=0, bytes_accessed=10**6, transcendentals=0),
        name="unpack_rows",
    )(seen)


def combine_kernel(place, own, seen, *outs):
    for k, out in enumerate(outs):
        g = jnp.bitwise_xor(place[0], k)
        out[...] = (own[g] + seen[g].astype(F32)).astype(BF16)


def combine(place, own, seen):
    n_grp = own.shape[0]
    shape = jax.ShapeDtypeStruct(own.shape[1:], BF16)
    return pl.pallas_call(
        combine_kernel,
        in_specs=[SMEM, VMEM, VMEM],
        out_specs=[VMEM] * n_grp,
        out_shape=[shape] * n_grp,
        compiler_params=params(),
        cost_estimate=pl.CostEstimate(flops=0, bytes_accessed=10**6, transcendentals=0),
        name="combine",
    )(place, own, seen)


def finish_kernel(place, *refs):
    out = refs[-1]
    piece = out.shape[1]
    for k, seen in enumerate(refs[:-1]):
        base = jnp.bitwise_xor(place[0], k) * TILE
        for f in range(TILE):
            out[base + f, :, 0:128] = seen[f, 0:piece].astype(F32)
            packed = seen[f, piece : piece + piece // 2].astype(F32)
            out[base + f, 0 : piece // 2, 128:192] = packed[:, 0:64]
            out[base + f, piece // 2 : piece, 128:192] = turn(packed)[:, 0:64]


def finish(place, pieces):
    n_grp = len(pieces)
    piece = pieces[0].shape[1] * 2 // 3
    return pl.pallas_call(
        finish_kernel,
        in_specs=[SMEM] + [VMEM] * n_grp,
        out_specs=VMEM,
        out_shape=jax.ShapeDtypeStruct((n_grp * TILE, piece, 192), F32),
        compiler_params=params(),
        cost_estimate=pl.CostEstimate(flops=0, bytes_accessed=10**6, transcendentals=0),
        name="finish_tables",
    )(place, *pieces)


def cross(array):
    return lax.ppermute(array, "half", [(0, 1), (1, 0)])


def halves(pooled, upstream, ids_now, ids_next, tables, w_fm, w_proj, w_lcb, gain):
    n_grp, n_lane = lax.axis_size("grp"), lax.axis_size("lane")
    count = pooled.shape[0]
    wire = Wire(count, n_grp * n_lane)
    factor = 1.0 / (count * n_grp * 2 * n_lane)
    half = lax.axis_index("half").astype(jnp.int32)[None]
    grp = lax.axis_index("grp").astype(jnp.int32)
    mine_t = lax.dynamic_slice_in_dim(tables.transpose(0, 2, 1), grp * TILE, TILE, 0)
    mine_t, pooled = lax.optimization_barrier((mine_t, pooled))
    crossed_t = cross(mine_t)
    other_wire, own_wire = backward(
        n_grp, n_lane, wire, half,
        pooled.transpose(0, 2, 1), upstream.transpose(0, 2, 1), ids_now, ids_next, w_fm, w_proj.T, w_lcb, gain,
    )
    seen_other = exchange(other_wire, PEER)
    crossed_t, seen_other = lax.optimization_barrier((crossed_t, seen_other))
    seen_own = exchange(own_wire, PEER)
    (part,) = part_sums(n_grp, wire, True, half, seen_other, seen_other)
    part_seen = cross(part)
    own, dense = part_sums(n_grp, wire, False, half, seen_own, seen_other)
    dense_seen = cross(dense)
    rows_wire = lookup(wire, factor, half, mine_t, crossed_t, seen_other, dense, dense_seen)
    rows = exchange(rows_wire, PEER)
    next_rows, grad_fm, grad_proj_t, grad_lcb, grad_gain = unpack(n_grp, n_lane, wire, count, rows)
    own, _ = lax.optimization_barrier((own, rows_wire))
    pieces = combine(grp[None], own, part_seen)
    pieces = [pieces[0]] + [
        lax.ppermute(pieces[k], "grp", [(g, g ^ k) for g in range(n_grp)]) for k in range(1, n_grp)
    ]
    table_grad = finish(grp[None], pieces)
    return next_rows.transpose(0, 2, 1), table_grad, grad_fm, grad_proj_t.T, grad_lcb, grad_gain.reshape(-1)


def solution(mesh):
    n_grp, n_emb = mesh.shape["grp"], mesh.shape["emb"]
    split = n_emb % 2 == 0 and n_grp * (n_emb // 2) == 16 and n_grp % 2 == 0

    def run(*args):
        pooled, _, _, _, tables, w_fm = args[:6]
        count = pooled.shape[0] // (n_grp * n_emb)
        fits = (
            split
            and pooled.shape[1:] == (256, 192)
            and tables.shape[1] == 128
            and w_fm.shape[1] == 128
            and pooled.shape[1] == n_grp * n_emb * TILE
            and count % STEP == 0
            and count <= 16
        )
        if fits:
            devices = mesh.devices.reshape(n_grp, 2, n_emb // 2)
            where, emb, body = Mesh(devices, ("grp", "half", "lane")), ("half", "lane"), halves
        else:
            where, emb, body = mesh, ("emb",), local
        both = ("grp",) + emb
        return jax.shard_map(
            body,
            mesh=where,
            in_specs=(
                P(both, None, None),
                P(both, None, None),
                P(both, None),
                P(both, None),
                P(emb, None, None),
                P(),
                P(),
                P(),
                P(),
            ),
            out_specs=(P(both, None, None), P(emb, "grp", None), P(), P(), P(), P()),
            check_vma=False,
        )(*args)

    return run
```

time: 126 us -> 126 us (level)
  blocking collectives: 0 us -> 18 us
  waiting for transfers between devices: 65.4 us -> 49.5 us
  other arithmetic: 1.9 us -> 0 us
    all_to_all x3 -> x2, waiting for transfers between devices: 40.2 us -> 3.21 us  [exchange(): return lax.all_to_all(blocks, axes, split_axis=0, concat_axis=0, tiled=True)]
    all_to_all x0 -> x1, blocking collectives: none -> 18 us  [exchange(): return lax.all_to_all(blocks, axes, split_axis=0, concat_axis=0, tiled=True)]
    ppermute x3, waiting for transfers between devices: 25.2 us -> 42.4 us  [cross(): return lax.ppermute(array, 'half', [(0, 1), (1, 0)])]
    all_to_all x3 -> x2, starting transfers between devices: 14.3 us -> 8.34 us  [exchange(): return lax.all_to_all(blocks, axes, split_axis=0, concat_axis=0, tiled=True)]
    ppermute x0 -> x3, waiting for transfers between devices: none -> 3.85 us  [halves(): lax.ppermute(pieces[k], 'grp', [(g, g ^ k) for g in range(n_grp)])]
    ppermute x0 -> x3, starting transfers between devices: none -> 3.55 us  [halves(): lax.ppermute(pieces[k], 'grp', [(g, g ^ k) for g in range(n_grp)])]
    convert_element_type x1 -> x0, other arithmetic: 1.82 us -> none  [halves(): both = (own + part_seen.astype(F32)).astype(BF16)]
    ppermute x3, starting transfers between devices: 3.13 us -> 4.75 us  [cross(): return lax.ppermute(array, 'half', [(0, 1), (1, 0)])]
  transfers between devices with their start and end apart: 6 -> 8, of which waited for: 5 -> 7; matrix products, arithmetic and copies ran while one was open for 4% -> 0% of each run, Pallas kernels for 5% -> 2%
where the time goes in v3:
time: 126 us; the launch traced here: 125 us
  waiting for transfers between devices  49.5 us (39%)
  Pallas kernels  27.2 us (22%)
  blocking collectives  18 us (14%)
  starting transfers between devices  16.6 us (13%)
  local copies, waits for them, and re-layouts  12.4 us (10%)
    ppermute x3, waiting for transfers between devices, cross(): return lax.ppermute(array, 'half', [(0, 1), (1, 0)])  42.4 us
    all_to_all x1, blocking collectives, exchange(): return lax.all_to_all(blocks, axes, split_axis=0, concat_axis=0, tiled=True)  18 us
    pallas_call x1, Pallas kernels, backward(): pl.pallas_call(functools.partial(backward_kernel, n_grp, n_lane, wire), g...  17.6 us
    unnamed x32, local copies, waits for them, and re-layouts  12.4 us
    all_to_all x2, starting transfers between devices, exchange(): return lax.all_to_all(blocks, axes, split_axis=0, concat_axis=0, tiled=True)  8.34 us
    ppermute x3, starting transfers between devices, cross(): return lax.ppermute(array, 'half', [(0, 1), (1, 0)])  4.75 us
    ppermute x3, waiting for transfers between devices, halves(): lax.ppermute(pieces[k], 'grp', [(g, g ^ k) for g in range(n_grp)])  3.85 us
    ppermute x3, starting transfers between devices, halves(): lax.ppermute(pieces[k], 'grp', [(g, g ^ k) for g in range(n_grp)])  3.55 us
  transfers between devices with their start and end apart: 8, of which 7 were waited for; matrix products, arithmetic and copies ran while one was open for 0% of the time, Pallas kernels for 2%

profile of v3, /device:TPU:0, one launch (start us, length us, event | category | flops | bytes accessed | tf_op | source)
XLA Modules:
  0.0 124.6 jit_solution(13842259561857104071)
XLA Ops:
  0.7 1.4 %copy-done = bf16[32,128,192]{1,2,0:T(8,128)(2,1)S(1)} copy-done((bf16[32,128,192]{1,2,0:T(8,128)(2,1)S(1)}, bf16[32,128,192]{1,2,0:T(8,128)(2,1)}, u32[]{:S(2)}) %copy-start) | copy-done | bytes 1572888
  2.1 1.3 %copy-done.6 = bf16[12,256,192]{1,2,0:T(8,128)(2,1)S(1)} copy-done((bf16[12,256,192]{1,2,0:T(8,128)(2,1)S(1)}, bf16[12,256,192]{1,2,0:T(8,128)(2,1)}, u32[]{:S(2)}) %copy-start.6) | copy-done | bytes 1179672
  3.4 1.3 %copy-done.7 = bf16[12,256,192]{1,2,0:T(8,128)(2,1)S(1)} copy-done((bf16[12,256,192]{1,2,0:T(8,128)(2,1)S(1)}, bf16[12,256,192]{1,2,0:T(8,128)(2,1)}, u32[]{:S(2)}) %copy-start.7) | copy-done | bytes 1179672
  9.3 17.6 %layer_backward.1 = (bf16[16,160,128]{2,1,0:T(8,128)(2,1)S(1)}, bf16[16,208,128]{2,1,0:T(8,128)(2,1)}) custom-call(s32[1]{0:T(128)} %bitcast.half_ref, bf16[12,192,256]{2,1,0:T(8,128)(2,1)S(1)} %bitcast.11, bf16[12,192,256]{2,1,0:T(8,128)(2,1)S(1)} %bitcast.12, s32[12,256]{1,0:T(8,128)S(1)} %copy-done.13, s32[12,256]{1,0:T(8,128)S(1)} %copy-done.14, ...), custom_call_target="tpu_custom_call" | custom-call | flops 1000000000 | bytes 4000000 | tf_op jit(solution)/shard_map/layer_backward/pallas_call | solution.py:283
  26.9 18.0 %all_to_all.15.ids_ref.seen = bf16[16,160,128]{2,1,0:T(8,128)(2,1)S(1)} all-to-all(bf16[16,160,128]{2,1,0:T(8,128)(2,1)S(1)} %get-tuple-element.26), channel_id=1, replica_groups=mesh['grp'=4,'half'=2,'lane'=4] {'grp','lane'}, dimensions={0} | all-to-all | bytes 1310720 | tf_op jit(solution)/shard_map/all_to_all | solution.py:61
  45.0 3.6 %all-to-all-start.1 = ((bf16[16,208,128]{2,1,0:T(8,128)(2,1)}), bf16[16,208,128]{2,1,0:T(8,128)(2,1)S(1)}, u32[]{:S(2)}, u32[]{:S(2)}) async-start(bf16[16,208,128]{2,1,0:T(8,128)(2,1)} %get-tuple-element.29), calls=%async_computation.1 | async-start | bytes 1703936 | tf_op jit(solution)/shard_map/all_to_all | solution.py:61
  48.6 2.6 %collective-permute-start = (bf16[8,192,128]{2,1,0:T(8,128)(2,1)S(1)}, bf16[8,192,128]{2,1,0:T(8,128)(2,1)S(1)}, u32[]{:S(2)}, u32[]{:S(2)}) collective-permute-start(bf16[8,192,128]{2,1,0:T(8,128)(2,1)S(1)} %dynamic-slice_bitcast_fusion.mine_t), channel_id=1, source_target_pairs={{0,4},{4,0},{1,5},{5,1},{2,6},{6,2},{3,7},{7,3},{8,12},{12,8},{9,1... | collective-permute-start | bytes 1179656 | tf_op jit(solution)/shard_map/ppermute | solution.py:546
  51.2 15.8 %collective-permute-done.crossed_t = bf16[8,192,128]{2,1,0:T(8,128)(2,1)S(1)} collective-permute-done((bf16[8,192,128]{2,1,0:T(8,128)(2,1)S(1)}, bf16[8,192,128]{2,1,0:T(8,128)(2,1)S(1)}, u32[]{:S(2)}, u32[]{:S(2)}) %collective-permute-start) | collective-permute-done | bytes 393248 | tf_op jit(solution)/shard_map/ppermute | solution.py:546
  67.8 3.2 %all-to-all-done.1.seen = bf16[16,208,128]{2,1,0:T(8,128)(2,1)S(1)} async-done(((bf16[16,208,128]{2,1,0:T(8,128)(2,1)}), bf16[16,208,128]{2,1,0:T(8,128)(2,1)S(1)}, u32[]{:S(2)}, u32[]{:S(2)}) %all-to-all-start.1) | async-done | bytes 852000 | tf_op jit(solution)/shard_map/all_to_all | solution.py:61
  71.0 1.4 %part_own.1 = (f32[4,8,48,128]{3,2,1,0:T(8,128)S(1)}, f32[64,128]{1,0:T(8,128)S(1)}) custom-call(s32[1]{0:T(128)} %bitcast.half_ref, bf16[16,208,128]{2,1,0:T(8,128)(2,1)S(1)} %all-to-all-done.1.seen, bf16[16,160,128]{2,1,0:T(8,128)(2,1)S(1)} %all_to_all.15.ids_ref.seen), custom_call_target="tpu_custom_call" | custom-call | flops 1000000000 | bytes 1000000 | tf_op jit(solution)/shard_map/part_own/pallas_call | solution.py:364
  73.5 4.6 %collective-permute-done.1.dense_seen = f32[64,128]{1,0:T(8,128)S(1)} collective-permute-done((f32[64,128]{1,0:T(8,128)S(1)}, f32[64,128]{1,0:T(8,128)S(1)}, u32[]{:S(2)}, u32[]{:S(2)}) %collective-permute-start.1) | collective-permute-done | bytes 32800 | tf_op jit(solution)/shard_map/ppermute | solution.py:546
  78.1 3.2 %lookup.1 = bf16[16,352,128]{2,1,0:T(8,128)(2,1)S(1)} custom-call(s32[1]{0:T(128)} %bitcast.half_ref, bf16[8,192,128]{2,1,0:T(8,128)(2,1)S(1)} %dynamic-slice_bitcast_fusion.mine_t, bf16[8,192,128]{2,1,0:T(8,128)(2,1)S(1)} %copy-done.9, bf16[16,160,128]{2,1,0:T(8,128)(2,1)S(1)} %all_to_all.15.ids_ref.seen, f32[64,128]{1,0:T(8,128)S(1)} %get-tuple-element.30.dense_own, ...), custom_call_target="tpu_custom_call" | custom-call | flops 1000000000 | bytes 1000000 | tf_op jit(solution)/shard_map/lookup/pallas_call | solution.py:418
  81.4 1.1 copy-done.1
  82.5 4.7 %all-to-all-start.2 = ((bf16[16,352,128]{2,1,0:T(8,128)(2,1)}), bf16[16,352,128]{2,1,0:T(8,128)(2,1)S(1)}, u32[]{:S(2)}, u32[]{:S(2)}) async-start(bf16[16,352,128]{2,1,0:T(8,128)(2,1)} %copy-done.1), calls=%async_computation.2 | async-start | bytes 2883584 | tf_op jit(solution)/shard_map/all_to_all | solution.py:61
  87.2 1.1 copy-done.5
  88.3 1.4 %part_other.1 = bf16[4,8,48,128]{3,2,1,0:T(8,128)(2,1)S(1)} custom-call(s32[1]{0:T(128)} %bitcast.half_ref, bf16[16,160,128]{2,1,0:T(8,128)(2,1)S(1)} %copy-done.5, bf16[16,160,128]{2,1,0:T(8,128)(2,1)S(1)} %copy-done.5), custom_call_target="tpu_custom_call" | custom-call | flops 1000000000 | bytes 1000000 | tf_op jit(solution)/shard_map/part_other/pallas_call | solution.py:364
  89.7 1.9 %collective-permute-start.2 = (bf16[4,8,48,128]{3,2,1,0:T(8,128)(2,1)S(1)}, bf16[4,8,48,128]{3,2,1,0:T(8,128)(2,1)S(1)}, u32[]{:S(2)}, u32[]{:S(2)}) collective-permute-start(bf16[4,8,48,128]{3,2,1,0:T(8,128)(2,1)S(1)} %part_other.1), channel_id=1, source_target_pairs={{0,4},{4,0},{1,5},{5,1},{2,6},{6,2},{3,7},{7,3},{8,12},{12,8},{9,1... | collective-permute-start | bytes 1179656 | tf_op jit(solution)/shard_map/ppermute | solution.py:546
  91.6 22.0 %collective-permute-done.2.seen = bf16[4,8,48,128]{3,2,1,0:T(8,128)(2,1)S(1)} collective-permute-done((bf16[4,8,48,128]{3,2,1,0:T(8,128)(2,1)S(1)}, bf16[4,8,48,128]{3,2,1,0:T(8,128)(2,1)S(1)}, u32[]{:S(2)}, u32[]{:S(2)}) %collective-permute-start.2) | collective-permute-done | bytes 393248 | tf_op jit(solution)/shard_map/ppermute | solution.py:546
  114.0 1.4 %collective-permute-start.4 = (bf16[8,48,128]{2,1,0:T(8,128)(2,1)S(1)}, bf16[8,48,128]{2,1,0:T(8,128)(2,1)S(1)}, u32[]{:S(2)}, u32[]{:S(2)}) collective-permute-start(bf16[8,48,128]{2,1,0:T(8,128)(2,1)S(1)} %get-tuple-element.36), channel_id=1, source_target_pairs={{0,16},{8,24},{16,0},{24,8},{1,17},{9,25},{17,1},{25,9},{2,18},{10... | collective-permute-start | bytes 294920 | tf_op jit(solution)/shard_map/ppermute | solution.py:576
  115.5 1.8 %collective-permute-start.5 = (bf16[8,48,128]{2,1,0:T(8,128)(2,1)S(1)}, bf16[8,48,128]{2,1,0:T(8,128)(2,1)S(1)}, u32[]{:S(2)}, u32[]{:S(2)}) collective-permute-start(bf16[8,48,128]{2,1,0:T(8,128)(2,1)S(1)} %get-tuple-element.37), channel_id=1, source_target_pairs={{0,24},{8,16},{16,8},{24,0},{1,25},{9,17},{17,9},{25,1},{2,26},{10... | collective-permute-start | bytes 294920 | tf_op jit(solution)/shard_map/ppermute | solution.py:576
  117.2 2.0 %collective-permute-done.3.refs_1_ = bf16[8,48,128]{2,1,0:T(8,128)(2,1)S(1)} collective-permute-done((bf16[8,48,128]{2,1,0:T(8,128)(2,1)S(1)}, bf16[8,48,128]{2,1,0:T(8,128)(2,1)S(1)}, u32[]{:S(2)}, u32[]{:S(2)}) %collective-permute-start.3) | collective-permute-done | bytes 98336 | tf_op jit(solution)/shard_map/ppermute | solution.py:576
  119.3 1.8 %collective-permute-done.5.refs_3_ = bf16[8,48,128]{2,1,0:T(8,128)(2,1)S(1)} collective-permute-done((bf16[8,48,128]{2,1,0:T(8,128)(2,1)S(1)}, bf16[8,48,128]{2,1,0:T(8,128)(2,1)S(1)}, u32[]{:S(2)}, u32[]{:S(2)}) %collective-permute-start.5) | collective-permute-done | bytes 98336 | tf_op jit(solution)/shard_map/ppermute | solution.py:576
  121.1 1.1 finish_tables.1
  122.2 2.4 %unpack_rows.1 = (bf16[12,192,256]{2,1,0:T(8,128)(2,1)}, f32[256,128]{1,0:T(8,128)}, f32[192,128]{1,0:T(8,128)}, f32[256,256]{1,0:T(8,128)}, f32[1,192]{1,0:T(1,128)}) custom-call(bf16[16,352,128]{2,1,0:T(8,128)(2,1)S(1)} %all-to-all-done.2.seen), custom_call_target="tpu_custom_call" | custom-call | bytes 1000000 | tf_op jit(solution)/shard_map/unpack_rows/pallas_call | solution.py:485
  (33 shorter events, 7.1 us)
Async XLA Ops:
  0.6 1.4 %copy-start = (bf16[32,128,192]{1,2,0:T(8,128)(2,1)S(1)}, bf16[32,128,192]{1,2,0:T(8,128)(2,1)}, u32[]{:S(2)}) copy-start(bf16[32,128,192]{1,2,0:T(8,128)(2,1)} %param.13) | copy-start | bytes 4718596
  2.1 1.3 %copy-start.6 = (bf16[12,256,192]{1,2,0:T(8,128)(2,1)S(1)}, bf16[12,256,192]{1,2,0:T(8,128)(2,1)}, u32[]{:S(2)}) copy-start(bf16[12,256,192]{1,2,0:T(8,128)(2,1)} %param.9) | copy-start | bytes 3538948
  3.4 1.3 %copy-start.7 = (bf16[12,256,192]{1,2,0:T(8,128)(2,1)S(1)}, bf16[12,256,192]{1,2,0:T(8,128)(2,1)}, u32[]{:S(2)}) copy-start(bf16[12,256,192]{1,2,0:T(8,128)(2,1)} %param.10) | copy-start | bytes 3538948
  4.6 0.9 copy-start.10
  5.5 0.8 copy-start.11
  6.4 0.8 copy-start.12
  7.2 0.7 copy-start.13
  7.9 0.7 copy-start.14
  8.6 0.7 copy-start.15
  44.9 33.2 %copy-start.4 = (bf16[16,160,128]{2,1,0:T(8,128)(2,1)}, bf16[16,160,128]{2,1,0:T(8,128)(2,1)S(1)}, u32[]{:S(2)}) copy-start(bf16[16,160,128]{2,1,0:T(8,128)(2,1)S(1)} %all_to_all.15.ids_ref.seen) | copy-start | bytes 1966084
  45.0 26.1 %all-to-all-start.1 = ((bf16[16,208,128]{2,1,0:T(8,128)(2,1)}), bf16[16,208,128]{2,1,0:T(8,128)(2,1)S(1)}, u32[]{:S(2)}, u32[]{:S(2)}) async-start(bf16[16,208,128]{2,1,0:T(8,128)(2,1)} %get-tuple-element.29), calls=%async_computation.1 | async-start | bytes 1703936 | tf_op jit(solution)/shard_map/all_to_all | solution.py:61
  48.6 18.5 %collective-permute-start = (bf16[8,192,128]{2,1,0:T(8,128)(2,1)S(1)}, bf16[8,192,128]{2,1,0:T(8,128)(2,1)S(1)}, u32[]{:S(2)}, u32[]{:S(2)}) collective-permute-start(bf16[8,192,128]{2,1,0:T(8,128)(2,1)S(1)} %dynamic-slice_bitcast_fusion.mine_t), channel_id=1, source_target_pairs={{0,4},{4,0},{1,5},{5,1},{2,6},{6,2},{3,7},{7,3},{8,12},{12,8},{9,1... | collective-permute-start | bytes 1179656 | tf_op jit(solution)/shard_map/ppermute | solution.py:546
  67.1 0.8 copy-start.8
  71.0 7.1 %copy-start.9 = (bf16[8,192,128]{2,1,0:T(8,128)(2,1)S(1)}, bf16[8,192,128]{2,1,0:T(8,128)(2,1)}, u32[]{:S(2)}) copy-start(bf16[8,192,128]{2,1,0:T(8,128)(2,1)} %copy-done.8) | copy-start | bytes 1179652
  72.4 0.9 copy-start.2
  73.3 4.8 %collective-permute-start.1 = (f32[64,128]{1,0:T(8,128)S(1)}, f32[64,128]{1,0:T(8,128)S(1)}, u32[]{:S(2)}, u32[]{:S(2)}) collective-permute-start(f32[64,128]{1,0:T(8,128)S(1)} %get-tuple-element.30.dense_own), channel_id=1, source_target_pairs={{0,4},{4,0},{1,5},{5,1},{2,6},{6,2},{3,7},{7,3},{8,12},{12,8},{9,1... | collective-permute-start | bytes 98312 | tf_op jit(solution)/shard_map/ppermute | solution.py:546
  81.4 1.1 copy-start.1
  82.5 39.7 %all-to-all-start.2 = ((bf16[16,352,128]{2,1,0:T(8,128)(2,1)}), bf16[16,352,128]{2,1,0:T(8,128)(2,1)S(1)}, u32[]{:S(2)}, u32[]{:S(2)}) async-start(bf16[16,352,128]{2,1,0:T(8,128)(2,1)} %copy-done.1), calls=%async_computation.2 | async-start | bytes 2883584 | tf_op jit(solution)/shard_map/all_to_all | solution.py:61
  87.2 1.1 copy-start.5
  88.3 25.3 %copy-start.3 = (f32[4,8,48,128]{3,2,1,0:T(8,128)S(1)}, f32[4,8,48,128]{3,2,1,0:T(8,128)}, u32[]{:S(2)}) copy-start(f32[4,8,48,128]{3,2,1,0:T(8,128)} %copy-done.2) | copy-start | bytes 2359300
  89.7 23.9 %collective-permute-start.2 = (bf16[4,8,48,128]{3,2,1,0:T(8,128)(2,1)S(1)}, bf16[4,8,48,128]{3,2,1,0:T(8,128)(2,1)S(1)}, u32[]{:S(2)}, u32[]{:S(2)}) collective-permute-start(bf16[4,8,48,128]{3,2,1,0:T(8,128)(2,1)S(1)} %part_other.1), channel_id=1, source_target_pairs={{0,4},{4,0},{1,5},{5,1},{2,6},{6,2},{3,7},{7,3},{8,12},{12,8},{9,1... | collective-permute-start | bytes 1179656 | tf_op jit(solution)/shard_map/ppermute | solution.py:546
  113.7 5.5 %collective-permute-start.3 = (bf16[8,48,128]{2,1,0:T(8,128)(2,1)S(1)}, bf16[8,48,128]{2,1,0:T(8,128)(2,1)S(1)}, u32[]{:S(2)}, u32[]{:S(2)}) collective-permute-start(bf16[8,48,128]{2,1,0:T(8,128)(2,1)S(1)} %get-tuple-element.35), channel_id=1, source_target_pairs={{0,8},{8,0},{16,24},{24,16},{1,9},{9,1},{17,25},{25,17},{2,10},{10... | collective-permute-start | bytes 294920 | tf_op jit(solution)/shard_map/ppermute | solution.py:576
  114.0 5.2 %collective-permute-start.4 = (bf16[8,48,128]{2,1,0:T(8,128)(2,1)S(1)}, bf16[8,48,128]{2,1,0:T(8,128)(2,1)S(1)}, u32[]{:S(2)}, u32[]{:S(2)}) collective-permute-start(bf16[8,48,128]{2,1,0:T(8,128)(2,1)S(1)} %get-tuple-element.36), channel_id=1, source_target_pairs={{0,16},{8,24},{16,0},{24,8},{1,17},{9,25},{17,1},{25,9},{2,18},{10... | collective-permute-start | bytes 294920 | tf_op jit(solution)/shard_map/ppermute | solution.py:576
  115.5 5.6 %collective-permute-start.5 = (bf16[8,48,128]{2,1,0:T(8,128)(2,1)S(1)}, bf16[8,48,128]{2,1,0:T(8,128)(2,1)S(1)}, u32[]{:S(2)}, u32[]{:S(2)}) collective-permute-start(bf16[8,48,128]{2,1,0:T(8,128)(2,1)S(1)} %get-tuple-element.37), channel_id=1, source_target_pairs={{0,24},{8,16},{16,8},{24,0},{1,25},{9,17},{17,9},{25,1},{2,26},{10... | collective-permute-start | bytes 294920 | tf_op jit(solution)/shard_map/ppermute | solution.py:576

commit v4 on v3

--- a/solution.py
+++ b/solution.py
@@ -133,8 +133,8 @@
     def __init__(self, count, peers):
         self.left = count * TILE
         self.half = self.left + self.left // 2
-        self.ids = 16
-        self.dense = 1024 // peers
+        self.dense = 2 * self.half
+        self.ids = self.dense + 1024 // peers
 
 
 def place_of(n_grp, n_lane, peer):
@@ -144,44 +144,37 @@
 def backward_kernel(
     n_grp, n_lane, wire,
     half_ref, x_ref, u_ref, now_ref, next_ref, fm_ref, proj_t_ref, lcb_ref, gain_ref,
-    other_ref, own_ref,
-    fm_t, proj, lcb_t, gains, eye, left_in, right_in, grads, turned, sum_fm_t, sum_proj_t, sum_lcb, sum_gain, ids,
+    out_ref,
+    fm_t, proj, lcb_t, gains, eye, mixed, p_t, g_t, d_sum, d_p_t, left_in, right_in, grads, turned, ids,
 ):
-    step = pl.program_id(0)
-    width, features = x_ref.shape[1:]
+    count, width, features = x_ref.shape
     rank = fm_ref.shape[1]
     peers = n_grp * n_lane
     scale = 1.0 / width
-
-    @pl.when(step == 0)
-    def _():
-        turned_fm = fm_ref[...].astype(F32).T.astype(BF16)
-        fm_t[...] = turned_fm
-        for s in range(STEP):
-            right_in[s, rank : 2 * rank] = turned_fm
-        proj[...] = proj_t_ref[...].astype(F32).T.astype(BF16)
-        lcb_t[...] = lcb_ref[...].astype(F32).T.astype(BF16)
-        column = jnp.broadcast_to(gain_ref[...], (LANES, width)).T
-        gains[:, 0:128] = column
-        gains[:, 128:256] = column
-        eye[...] = identity(features, features)
-        sum_fm_t[...] = jnp.zeros_like(sum_fm_t)
-        sum_proj_t[...] = jnp.zeros_like(sum_proj_t)
-        sum_lcb[...] = jnp.zeros_like(sum_lcb)
-        sum_gain[...] = jnp.zeros_like(sum_gain)
-
-    x_all = x_ref[...].reshape(STEP * width, features)
-    p_all = mm(x_all, fm_ref[...]).astype(BF16)
-    mixed = mm(x_all, lcb_ref[...])
-    d_sums = []
-    add_fm, add_proj, add_gain = 0.0, 0.0, 0.0
-    for s in range(STEP):
-        here = slice(s * width, (s + 1) * width)
-        x = x_ref[s]
-        left_in[s, :, 0:rank] = p_all[here]
-        p_t = mm_nt(fm_t[...], x).astype(BF16)
-        g_t = mm(p_t, x).astype(BF16)
-        summed = x.astype(F32) + mm(proj_t_ref[...], g_t) + mixed[here]
+    samples = range(count)
+
+    turned_fm = fm_ref[...].astype(F32).T.astype(BF16)
+    fm_t[...] = turned_fm
+    proj[...] = proj_t_ref[...].astype(F32).T.astype(BF16)
+    lcb_t[...] = lcb_ref[...].astype(F32).T.astype(BF16)
+    column = jnp.broadcast_to(gain_ref[...], (LANES, width)).T
+    gains[:, 0:128] = column
+    gains[:, 128:256] = column
+    eye[...] = identity(features, features)
+
+    x_all = x_ref[...].reshape(count * width, features)
+    left_in[:, :, 0:rank] = mm(x_all, fm_ref[...]).astype(BF16).reshape(count, width, rank)
+    mixed[...] = mm(x_all, lcb_ref[...]).reshape(count, width, features)
+    for s in samples:
+        p_t[s] = mm_nt(fm_t[...], x_ref[s]).astype(BF16)
+        right_in[s, rank : 2 * rank] = turned_fm
+    for s in samples:
+        g_t[s] = mm(p_t[s], x_ref[s]).astype(BF16)
+    for s in samples:
+        mixed[s] = mixed[s] + mm(proj_t_ref[...], g_t[s])
+    sum_gain = 0.0
+    for s in samples:
+        summed = x_ref[s].astype(F32) + mixed[s]
         centre = jnp.sum(summed, axis=0, keepdims=True) * scale
         summed = summed - centre
         spread = jnp.sum(summed * summed, axis=0, keepdims=True) * scale
@@ -191,147 +184,148 @@
         scaled = upper * gains[...]
         first = jnp.sum(scaled, axis=0, keepdims=True) * scale
         second = jnp.sum(scaled * normed, axis=0, keepdims=True) * scale
-        d_sum = (inverse * (scaled - first - normed * second)).astype(BF16)
-        add_gain += upper * normed
-        d_g_t = mm(proj[...], d_sum).astype(BF16)
-        right_in[s, 0:rank] = d_g_t
-        left_in[s, :, rank : 2 * rank] = mm_nt(x, d_g_t).astype(BF16)
-        d_p_t = mm_nt(d_g_t, x).astype(BF16)
-        add_fm += mm(d_p_t, x)
-        add_proj += mm_nt(d_sum, g_t)
-        d_sums.append(d_sum)
-    d_all = jnp.concatenate(d_sums, axis=0)
-    back = mm(d_all, lcb_t[...])
-    sum_lcb[...] += mm(x_all, d_all, ((0,), (0,)))
-    sum_fm_t[...] += add_fm
-    sum_proj_t[...] += add_proj
-    sum_gain[...] += add_gain
-    for s in range(STEP):
-        here = slice(s * width, (s + 1) * width)
-        grad = d_sums[s].astype(F32) + mm(left_in[s], right_in[s]) + back[here]
+        d_sum[s] = (inverse * (scaled - first - normed * second)).astype(BF16)
+        product_gain = upper * normed
+        sum_gain += product_gain[:, 0:128] + product_gain[:, 128:256]
+    for s in samples:
+        right_in[s, 0:rank] = mm(proj[...], d_sum[s]).astype(BF16)
+    for s in samples:
+        left_in[s, :, rank : 2 * rank] = mm_nt(x_ref[s], right_in[s, 0:rank]).astype(BF16)
+        d_p_t[s] = mm_nt(right_in[s, 0:rank], x_ref[s]).astype(BF16)
+    d_all = d_sum[...].reshape(count * width, features)
+    mixed[...] = mm(d_all, lcb_t[...]).reshape(count, width, features)
+    for s in samples:
+        grad = d_sum[s].astype(F32) + mixed[s] + mm(left_in[s], right_in[s])
         grad = grad.astype(BF16)
-        grads[s * 128 : s * 128 + 128] = grad[0:128]
-        at = 512 + 64 * (2 * (s % 2) + s // 2)
-        grads[at : at + 64] = grad[128:192]
-    rows = mm_nt(eye[...], grads[...])
-    turned[0] = rows[0:128]
-    turned[1] = rows[128:256]
+        group, k = s // STEP, s % STEP
+        grads[group, k * 128 : k * 128 + 128] = grad[0:128]
+        at = 512 + 64 * (2 * (k % 2) + k // 2)
+        grads[group, at : at + 64] = grad[128:192]
+    sum_lcb = mm(x_all, d_all, ((0,), (0,)))
+    sum_fm_t, sum_proj_t = 0.0, 0.0
+    for s in samples:
+        sum_fm_t += mm(d_p_t[s], x_ref[s])
+        sum_proj_t += mm_nt(d_sum[s], g_t[s])
 
     half = half_ref[0]
-    for out_ref, which in ((other_ref, 1 - half), (own_ref, half)):
-        for peer in range(peers):
-            at = place_of(n_grp, n_lane, peer)
-            line = turned[which, at : at + TILE]
-            left = jnp.concatenate([line[:, s * 128 : s * 128 + 128] for s in range(STEP)], axis=0)
-            row = pl.multiple_of(step * 32, 16)
-            out_ref[peer, pl.ds(row, 32)] = left.astype(BF16)
-            right = jnp.concatenate([line[:, 512:640], line[:, 640:768]], axis=0)
-            row = pl.multiple_of(wire.left + step * 16, 16)
-            out_ref[peer, pl.ds(row, 16)] = right.astype(BF16)
-
-    @pl.when(step == pl.num_programs(0) - 1)
-    def _():
-        part = features // peers
-        third = width // peers
-        total = jnp.sum((sum_gain[:, 0:128] + sum_gain[:, 128:256]).T, axis=0, keepdims=True)
-        high = total.astype(BF16).astype(F32)
-        low = total - high
-        middle = jnp.concatenate([high[:, 128:192], low[:, 128:192]], axis=1)
-        gain_rows = [high[:, 0:128], middle, low[:, 0:128], jnp.zeros((1, LANES), F32)]
-        total_fm = sum_fm_t[...].T
-        for peer in range(peers):
-            at = wire.half
-            here = slice(peer * part, (peer + 1) * part)
-            own_ref[peer, at : at + part] = total_fm[here].astype(BF16)
-            own_ref[peer, at + part : at + 2 * part] = sum_lcb[here, 0:128].astype(BF16)
-            own_ref[peer, at + 2 * part : at + 3 * part] = sum_lcb[here, 128:256].astype(BF16)
-            last = [sum_proj_t[peer * third : (peer + 1) * third]] + gain_rows
-            own_ref[peer, at + 3 * part : at + 4 * part] = jnp.concatenate(last, axis=0).astype(BF16)
-
-        count = now_ref.shape[0]
-        lane = lax.broadcasted_iota(jnp.int32, (16, LANES), 1)
-        sample = lax.broadcasted_iota(jnp.int32, (16, LANES), 0)
-        mine = (lane // TILE == sample) & (sample < count)
-        for which, ref in enumerate((now_ref, next_ref)):
-            ids[which] = jnp.zeros_like(ids[which])
-            ids[which, 0:count] = ref[...].astype(F32)
-        for peer in range(peers):
-            at = place_of(n_grp, n_lane, peer)
-            lines = []
-            for which in range(2):
-                for side in range(2):
-                    line = ids[which, :, side * 128 : side * 128 + 128]
-                    if at:
-                        line = pltpu.roll(line, LANES - at, 1)
-                    line = pltpu.roll(line, 0, 1, stride=TILE, stride_axis=0)
-                    lines.append(jnp.sum(jnp.where(mine, line, 0.0), axis=0, keepdims=True))
-            lines.append(jnp.zeros((12, LANES), F32))
-            other_ref[peer, wire.half : wire.half + 16] = jnp.concatenate(lines, axis=0).astype(BF16)
+    for group in range(count // STEP):
+        rows = mm_nt(eye[...], grads[group])
+        turned[group, 0] = rows[0:128]
+        turned[group, 1] = rows[128:256]
+    for group in range(count // STEP):
+        for which in range(2):
+            side = half if which else 1 - half
+            for peer in range(peers):
+                at = place_of(n_grp, n_lane, peer)
+                line = turned[group, side, at : at + TILE]
+                left = jnp.concatenate([line[:, k * 128 : k * 128 + 128] for k in range(STEP)], axis=0)
+                row = which * wire.half + group * 32
+                out_ref[peer, row : row + 32] = left.astype(BF16)
+                right = jnp.concatenate([line[:, 512:640], line[:, 640:768]], axis=0)
+                row = which * wire.half + wire.left + group * 16
+                out_ref[peer, row : row + 16] = right.astype(BF16)
+
+    part = features // peers
+    third = width // peers
+    total = jnp.sum(sum_gain.T, axis=0, keepdims=True)
+    high = total.astype(BF16).astype(F32)
+    low = total - high
+    middle = jnp.concatenate([high[:, 128:192], low[:, 128:192]], axis=1)
+    gain_rows = [high[:, 0:128], middle, low[:, 0:128], jnp.zeros((1, LANES), F32)]
+    sum_fm = sum_fm_t.T
+    for peer in range(peers):
+        at = wire.dense
+        here = slice(peer * part, (peer + 1) * part)
+        out_ref[peer, at : at + part] = sum_fm[here].astype(BF16)
+        out_ref[peer, at + part : at + 2 * part] = sum_lcb[here, 0:128].astype(BF16)
+        out_ref[peer, at + 2 * part : at + 3 * part] = sum_lcb[here, 128:256].astype(BF16)
+        last = [sum_proj_t[peer * third : (peer + 1) * third]] + gain_rows
+        out_ref[peer, at + 3 * part : at + 4 * part] = jnp.concatenate(last, axis=0).astype(BF16)
+
+    lane = lax.broadcasted_iota(jnp.int32, (16, LANES), 1)
+    sample = lax.broadcasted_iota(jnp.int32, (16, LANES), 0)
+    mine = (lane // TILE == sample) & (sample < count)
+    spread_ids = []
+    for which, ref in enumerate((now_ref, next_ref)):
+        ids[which] = jnp.zeros_like(ids[which])
+        ids[which, 0:count] = ref[...].astype(F32)
+        for side in range(2):
+            line = ids[which, :, side * 128 : side * 128 + 128]
+            spread_ids.append(pltpu.roll(line, 0, 1, stride=TILE, stride_axis=0))
+    for peer in range(peers):
+        at = place_of(n_grp, n_lane, peer)
+        lines = []
+        for line in spread_ids:
+            line = pltpu.roll(line, LANES - at, 1) if at else line
+            lines.append(jnp.sum(jnp.where(mine, line, 0.0), axis=0, keepdims=True))
+        lines.append(jnp.zeros((12, LANES), F32))
+        out_ref[peer, wire.ids : wire.ids + 16] = jnp.concatenate(lines, axis=0).astype(BF16)
 
 
 def backward(n_grp, n_lane, wire, half, pooled_t, upstream_t, ids_now, ids_next, w_fm, w_proj_t, w_lcb, gain):
     count, width, features = pooled_t.shape
     rank = w_fm.shape[1]
     peers = n_grp * n_lane
-    block = pl.BlockSpec((STEP, width, features), lambda i: (i, 0, 0))
 
     def whole(shape):
         return pl.BlockSpec(shape, lambda i: (0,) * len(shape))
 
-    rest = (ids_now, ids_next, w_fm, w_proj_t, w_lcb, gain.reshape(1, width))
-    shapes = [(peers, wire.half + wire.ids, LANES), (peers, wire.half + wire.dense, LANES)]
+    operands = (pooled_t, upstream_t, ids_now, ids_next, w_fm, w_proj_t, w_lcb, gain.reshape(1, width))
+    shape = (peers, wire.ids + 16, LANES)
     return pl.pallas_call(
         functools.partial(backward_kernel, n_grp, n_lane, wire),
-        grid=(count // STEP,),
-        in_specs=[SMEM, block, block] + [whole(array.shape) for array in rest],
-        out_specs=[whole(shape) for shape in shapes],
-        out_shape=[jax.ShapeDtypeStruct(shape, BF16) for shape in shapes],
+        grid=(1,),
+        in_specs=[SMEM] + [whole(array.shape) for array in operands],
+        out_specs=whole(shape),
+        out_shape=jax.ShapeDtypeStruct(shape, BF16),
         scratch_shapes=[
             pltpu.VMEM((rank, features), BF16),
             pltpu.VMEM((rank, width), BF16),
             pltpu.VMEM((features, features), BF16),
             pltpu.VMEM((width, features), F32),
             pltpu.VMEM((features, features), BF16),
-            pltpu.VMEM((STEP, width, 2 * rank), BF16),
-            pltpu.VMEM((STEP, 2 * rank, features), BF16),
-            pltpu.VMEM((STEP * width, features), BF16),
-            pltpu.VMEM((2, features // 2, STEP * width), F32),
-            pltpu.VMEM((rank, features), F32),
-            pltpu.VMEM((width, rank), F32),
-            pltpu.VMEM((features, features), F32),
-            pltpu.VMEM((width, features), F32),
+            pltpu.VMEM((count, width, features), F32),
+            pltpu.VMEM((count, rank, width), BF16),
+            pltpu.VMEM((count, rank, features), BF16),
+            pltpu.VMEM((count, width, features), BF16),
+            pltpu.VMEM((count, rank, width), BF16),
+            pltpu.VMEM((count, width, 2 * rank), BF16),
+            pltpu.VMEM((count, 2 * rank, features), BF16),
+            pltpu.VMEM((count // STEP, STEP * width, features), BF16),
+            pltpu.VMEM((count // STEP, 2, features // 2, STEP * width), F32),
             pltpu.VMEM((2, 16, features), F32),
         ],
-        compiler_params=params(),
+        compiler_params=pltpu.CompilerParams(vmem_limit_bytes=60 * 1024 * 1024),
         cost_estimate=pl.CostEstimate(flops=10**9, bytes_accessed=4 * 10**6, transcendentals=0),
         name="layer_backward",
-    )(half, pooled_t, upstream_t, *rest)
-
-
-def part_kernel(n_grp, wire, other, half_ref, seen, ids_ref, *refs):
+    )(half, *operands)
+
+
+def part_kernel(n_grp, wire, other, half_ref, seen, *refs):
     out, held = refs[0], refs[-1]
     peers = seen.shape[0]
     half = 1 - half_ref[0] if other else half_ref[0]
-    if not other:
+    base = 0 if other else wire.half
+    if other:
         dense = refs[1]
-        total = seen[0, wire.half : wire.half + wire.dense].astype(F32)
+        total = seen[0, wire.dense : wire.ids].astype(F32)
         for peer in range(1, peers):
-            total = total + seen[peer, wire.half : wire.half + wire.dense].astype(F32)
+            total = total + seen[peer, wire.dense : wire.ids].astype(F32)
         dense[...] = total
     lane = lax.broadcasted_iota(jnp.int32, (1, LANES), 1)
     start = ((lane % TILE) * LANES).astype(F32)
     keys = []
     for peer in range(peers):
         at = peer * LANES
-        held[at : at + wire.left, 0:128] = seen[peer, 0 : wire.left]
-        right = seen[peer, wire.left : wire.half]
+        held[at : at + wire.left, 0:128] = seen[peer, base : base + wire.left]
+        right = seen[peer, base + wire.left : base + wire.half]
         turned = turn(right.astype(F32)).astype(BF16)
         for i in range(wire.left // 32):
             held[at + 32 * i : at + 32 * i + 16, 128:256] = right[16 * i : 16 * i + 16]
             held[at + 32 * i + 16 : at + 32 * i + 32, 128:256] = turned[16 * i : 16 * i + 16]
         if wire.left < LANES:
             held[at + wire.left : at + LANES] = jnp.zeros((LANES - wire.left, 256), BF16)
-        ids = ids_ref[peer].astype(F32)
+        ids = seen[peer, wire.ids : wire.ids + 16].astype(F32)
         key = jnp.where(half == 0, ids[0:1], ids[1:2]) + start
         keys.append(jnp.where(lane < wire.left, key, -1.0))
     keys = jnp.concatenate(keys, axis=1)
@@ -350,32 +344,26 @@
                 out[g, 2 * pair + f, piece : piece + piece // 2] = packed.astype(out.dtype)
 
 
-def part_sums(n_grp, wire, other, half, seen, ids):
+def part_sums(n_grp, wire, other, half, seen):
     peers = seen.shape[0]
     piece = LANES // n_grp
     shapes = [jax.ShapeDtypeStruct((n_grp, TILE, piece + piece // 2, LANES), BF16 if other else F32)]
-    if not other:
-        shapes.append(jax.ShapeDtypeStruct((wire.dense, LANES), F32))
-
-    def whole(shape):
-        return pl.BlockSpec(shape, lambda i: (0,) * len(shape))
-
-    at = wire.half // 16
+    if other:
+        shapes.append(jax.ShapeDtypeStruct((wire.ids - wire.dense, LANES), F32))
     return pl.pallas_call(
         functools.partial(part_kernel, n_grp, wire, other),
-        grid=(1,),
-        in_specs=[SMEM, whole(seen.shape), pl.BlockSpec((peers, 16, LANES), lambda i: (0, at, 0))],
-        out_specs=[whole(shape.shape) for shape in shapes],
+        in_specs=[SMEM, VMEM],
+        out_specs=[VMEM] * len(shapes),
         out_shape=shapes,
         scratch_shapes=[pltpu.VMEM((peers * LANES, 256), BF16)],
         compiler_params=params(),
         cost_estimate=pl.CostEstimate(flops=10**9, bytes_accessed=10**6, transcendentals=0),
         name="part_other" if other else "part_own",
-    )(half, seen, ids)
+    )(half, seen)
 
 
 def lookup_kernel(wire, factor, half_ref, mine_t, crossed_t, ids_ref, dense_own, dense_seen, out, held):
-    peers = ids_ref.shape[0]
+    peers = out.shape[0]
     half = half_ref[0]
     for f in range(TILE):
         at = f * LANES
@@ -404,17 +392,17 @@
                     at = base + wire.left + 16 * i
                     out[peer, at : at + 16] = jnp.where(low_lanes(first.shape), first, second).astype(BF16)
     for peer in range(peers):
-        out[peer, 2 * wire.half :] = total
+        out[peer, wire.dense : wire.ids] = total
 
 
 def lookup(wire, factor, half, mine_t, crossed_t, ids, dense_own, dense_seen):
     peers = ids.shape[0]
-    rows = 2 * wire.half + wire.dense
+    rows = wire.ids
 
     def whole(shape):
         return pl.BlockSpec(shape, lambda i: (0,) * len(shape))
 
-    at = wire.half // 16
+    at = wire.ids // 16
     return pl.pallas_call(
         functools.partial(lookup_kernel, wire, factor),
         grid=(1,),
@@ -464,7 +452,7 @@
     def _():
         part, third = 256 // peers, 192 // peers
         for peer in range(peers):
-            dense = seen[peer, 2 * wire.half :].astype(F32)
+            dense = seen[peer, wire.dense : wire.ids].astype(F32)
             here = slice(peer * part, (peer + 1) * part)
             fm[here] = dense[0:part]
             lcb[here, 0:128] = dense[part : 2 * part]
@@ -554,20 +542,18 @@
     half = lax.axis_index("half").astype(jnp.int32)[None]
     grp = lax.axis_index("grp").astype(jnp.int32)
     mine_t = lax.dynamic_slice_in_dim(tables.transpose(0, 2, 1), grp * TILE, TILE, 0)
-    mine_t, pooled = lax.optimization_barrier((mine_t, pooled))
     crossed_t = cross(mine_t)
-    other_wire, own_wire = backward(
+    sent = backward(
         n_grp, n_lane, wire, half,
         pooled.transpose(0, 2, 1), upstream.transpose(0, 2, 1), ids_now, ids_next, w_fm, w_proj.T, w_lcb, gain,
     )
-    seen_other = exchange(other_wire, PEER)
-    crossed_t, seen_other = lax.optimization_barrier((crossed_t, seen_other))
-    seen_own = exchange(own_wire, PEER)
-    (part,) = part_sums(n_grp, wire, True, half, seen_other, seen_other)
+    seen = exchange(sent, PEER)
+    crossed_t, seen = lax.optimization_barrier((crossed_t, seen))
+    part, dense = part_sums(n_grp, wire, True, half, seen)
+    dense_seen = cross(dense)
     part_seen = cross(part)
-    own, dense = part_sums(n_grp, wire, False, half, seen_own, seen_other)
-    dense_seen = cross(dense)
-    rows_wire = lookup(wire, factor, half, mine_t, crossed_t, seen_other, dense, dense_seen)
+    (own,) = part_sums(n_grp, wire, False, half, seen)
+    rows_wire = lookup(wire, factor, half, mine_t, crossed_t, seen, dense, dense_seen)
     rows = exchange(rows_wire, PEER)
     next_rows, grad_fm, grad_proj_t, grad_lcb, grad_gain = unpack(n_grp, n_lane, wire, count, rows)
     own, _ = lax.optimization_barrier((own, rows_wire))

time: 126 us -> 102 us (0.81)
  blocking collectives: 18 us -> 0 us
  local copies, waits for them, and re-layouts: 12.4 us -> 2.65 us
  waiting for transfers between devices: 49.5 us -> 57 us
  Pallas kernels: 27.2 us -> 20.3 us
  starting transfers between devices: 16.6 us -> 20.6 us
    all_to_all x1 -> x0, blocking collectives: 18 us -> none  [exchange(): return lax.all_to_all(blocks, axes, split_axis=0, concat_axis=0, tiled=True)]
    unnamed x32 -> x12, local copies, waits for them, and re-layouts: 12.4 us -> 2.62 us
    ppermute x3, waiting for transfers between devices: 42.4 us -> 51.5 us  [cross(): return lax.ppermute(array, 'half', [(0, 1), (1, 0)])]
    pallas_call x1, Pallas kernels: 17.6 us -> 9.29 us  [backward(): pl.pallas_call(functools.partial(backward_kernel, n_grp, n_lane, wire), g...]
    all_to_all x2, starting transfers between devices: 8.34 us -> 11.8 us  [exchange(): return lax.all_to_all(blocks, axes, split_axis=0, concat_axis=0, tiled=True)]
    all_to_all x2, waiting for transfers between devices: 3.21 us -> 1.67 us  [exchange(): return lax.all_to_all(blocks, axes, split_axis=0, concat_axis=0, tiled=True)]
    pallas_call x1, Pallas kernels: 2.42 us -> 3.8 us  [unpack(): pl.pallas_call(functools.partial(unpack_kernel, n_grp, n_lane, wire), gri...]
  transfers between devices with their start and end apart: 8 -> 8, of which waited for: 7 -> 7; matrix products, arithmetic and copies ran while one was open for 0% -> 0% of each run, Pallas kernels for 2% -> 3%
where the time goes in v4:
time: 102 us; the launch traced here: 101 us
  waiting for transfers between devices  57 us (56%)
  starting transfers between devices  20.6 us (20%)
  Pallas kernels  20.3 us (20%)
  local copies, waits for them, and re-layouts  2.65 us (3%)
    ppermute x3, waiting for transfers between devices, cross(): return lax.ppermute(array, 'half', [(0, 1), (1, 0)])  51.5 us
    all_to_all x2, starting transfers between devices, exchange(): return lax.all_to_all(blocks, axes, split_axis=0, concat_axis=0, tiled=True)  11.8 us
    pallas_call x1, Pallas kernels, backward(): pl.pallas_call(functools.partial(backward_kernel, n_grp, n_lane, wire), g...  9.29 us
    ppermute x3, starting transfers between devices, cross(): return lax.ppermute(array, 'half', [(0, 1), (1, 0)])  5.31 us
    ppermute x3, waiting for transfers between devices, halves(): lax.ppermute(pieces[k], 'grp', [(g, g ^ k) for g in range(n_grp)])  3.85 us
    pallas_call x1, Pallas kernels, unpack(): pl.pallas_call(functools.partial(unpack_kernel, n_grp, n_lane, wire), gri...  3.8 us
    ppermute x3, starting transfers between devices, halves(): lax.ppermute(pieces[k], 'grp', [(g, g ^ k) for g in range(n_grp)])  3.55 us
    pallas_call x1, Pallas kernels, lookup(): pl.pallas_call(functools.partial(lookup_kernel, wire, factor), grid=(1,),...  3.22 us
  transfers between devices with their start and end apart: 8, of which 7 were waited for; matrix products, arithmetic and copies ran while one was open for 0% of the time, Pallas kernels for 3%

profile of v4, /device:TPU:0, one launch (start us, length us, event | category | flops | bytes accessed | tf_op | source)
XLA Modules:
  0.0 101.3 jit_solution(14225135268685283820)
XLA Ops:
  0.7 9.3 %layer_backward.1 = bf16[16,368,128]{2,1,0:T(8,128)(2,1)} custom-call(s32[1]{0:T(128)} %bitcast.half_ref, bf16[12,192,256]{2,1,0:T(8,128)(2,1)} %bitcast.11, bf16[12,192,256]{2,1,0:T(8,128)(2,1)} %bitcast.12, s32[12,256]{1,0:T(8,128)} %now_ref.1, s32[12,256]{1,0:T(8,128)} %next_ref.1, bf16[256,128]{1,0:T(8,128)(2,1)} %fm_ref.1, bf16[192,128]{1,0:T(8,128)(2,1)} %bitcast.13, ...), custom_call_target="tpu_custom_call" | custom-call | flops 1000000000 | bytes 4000000 | tf_op jit(solution)/shard_map/layer_backward/pallas_call | solution.py:275
  9.9 6.3 %all-to-all-start = ((bf16[16,368,128]{2,1,0:T(8,128)(2,1)}), bf16[16,368,128]{2,1,0:T(8,128)(2,1)S(1)}, u32[]{:S(2)}, u32[]{:S(2)}) async-start(bf16[16,368,128]{2,1,0:T(8,128)(2,1)} %layer_backward.1), calls=%async_computation | async-start | bytes 3014656 | tf_op jit(solution)/shard_map/all_to_all | solution.py:61
  16.3 2.6 %collective-permute-start = (bf16[8,192,128]{2,1,0:T(8,128)(2,1)S(1)}, bf16[8,192,128]{2,1,0:T(8,128)(2,1)S(1)}, u32[]{:S(2)}, u32[]{:S(2)}) collective-permute-start(bf16[8,192,128]{2,1,0:T(8,128)(2,1)S(1)} %dynamic-slice_bitcast_fusion.mine_t), channel_id=1, source_target_pairs={{0,4},{4,0},{1,5},{5,1},{2,6},{6,2},{3,7},{7,3},{8,12},{12,8},{9,1... | collective-permute-start | bytes 1179656 | tf_op jit(solution)/shard_map/ppermute | solution.py:534
  19.0 24.4 %collective-permute-done.crossed_t = bf16[8,192,128]{2,1,0:T(8,128)(2,1)S(1)} collective-permute-done((bf16[8,192,128]{2,1,0:T(8,128)(2,1)S(1)}, bf16[8,192,128]{2,1,0:T(8,128)(2,1)S(1)}, u32[]{:S(2)}, u32[]{:S(2)}) %collective-permute-start) | collective-permute-done | bytes 393248 | tf_op jit(solution)/shard_map/ppermute | solution.py:534
  43.4 0.7 copy-done.2
  44.1 1.7 %all-to-all-done.seen.ids_ref = bf16[16,368,128]{2,1,0:T(8,128)(2,1)S(1)} async-done(((bf16[16,368,128]{2,1,0:T(8,128)(2,1)}), bf16[16,368,128]{2,1,0:T(8,128)(2,1)S(1)}, u32[]{:S(2)}, u32[]{:S(2)}) %all-to-all-start) | async-done | bytes 1507360 | tf_op jit(solution)/shard_map/all_to_all | solution.py:61
  45.8 1.4 %part_other.1 = (bf16[4,8,48,128]{3,2,1,0:T(8,128)(2,1)S(1)}, f32[64,128]{1,0:T(8,128)S(1)}) custom-call(s32[1]{0:T(128)} %bitcast.half_ref, bf16[16,368,128]{2,1,0:T(8,128)(2,1)S(1)} %all-to-all-done.seen.ids_ref), custom_call_target="tpu_custom_call" | custom-call | flops 1000000000 | bytes 1000000 | tf_op jit(solution)/shard_map/part_other/pallas_call | solution.py:353
  47.2 0.7 copy-done.4
  47.9 1.7 %collective-permute-start.1 = (f32[64,128]{1,0:T(8,128)S(1)}, f32[64,128]{1,0:T(8,128)S(1)}, u32[]{:S(2)}, u32[]{:S(2)}) collective-permute-start(f32[64,128]{1,0:T(8,128)S(1)} %get-tuple-element.22.dense_own), channel_id=1, source_target_pairs={{0,4},{4,0},{1,5},{5,1},{2,6},{6,2},{3,7},{7,3},{8,12},{12,8},{9,1... | collective-permute-start | bytes 98312 | tf_op jit(solution)/shard_map/ppermute | solution.py:534
  49.7 3.1 %collective-permute-done.1.dense_seen = f32[64,128]{1,0:T(8,128)S(1)} collective-permute-done((f32[64,128]{1,0:T(8,128)S(1)}, f32[64,128]{1,0:T(8,128)S(1)}, u32[]{:S(2)}, u32[]{:S(2)}) %collective-permute-start.1) | collective-permute-done | bytes 32800 | tf_op jit(solution)/shard_map/ppermute | solution.py:534
  52.8 3.2 %lookup.1 = bf16[16,352,128]{2,1,0:T(8,128)(2,1)S(1)} custom-call(s32[1]{0:T(128)} %bitcast.half_ref, bf16[8,192,128]{2,1,0:T(8,128)(2,1)S(1)} %dynamic-slice_bitcast_fusion.mine_t, bf16[8,192,128]{2,1,0:T(8,128)(2,1)S(1)} %copy-done.3, bf16[16,368,128]{2,1,0:T(8,128)(2,1)S(1)} %all-to-all-done.seen.ids_ref, f32[64,128]{1,0:T(8,128)S(1)} %get-tuple-element.22.dense_own, ...), custom_call_target="tpu_custom_call" | custom-call | flops 1000000000 | bytes 1000000 | tf_op jit(solution)/shard_map/lookup/pallas_call | solution.py:406
  56.0 1.1 %copy-done.1 = bf16[16,352,128]{2,1,0:T(8,128)(2,1)} copy-done((bf16[16,352,128]{2,1,0:T(8,128)(2,1)}, bf16[16,352,128]{2,1,0:T(8,128)(2,1)S(1)}, u32[]{:S(2)}) %copy-start.1) | copy-done | bytes 1441816
  57.1 5.5 %all-to-all-start.1 = ((bf16[16,352,128]{2,1,0:T(8,128)(2,1)}), bf16[16,352,128]{2,1,0:T(8,128)(2,1)}, u32[]{:S(2)}, u32[]{:S(2)}) async-start(bf16[16,352,128]{2,1,0:T(8,128)(2,1)} %copy-done.1), calls=%async_computation.1 | async-start | bytes 2883584 | tf_op jit(solution)/shard_map/all_to_all | solution.py:61
  62.6 0.9 collective-permute-start.2
  63.6 1.4 %part_own.1.own = f32[4,8,48,128]{3,2,1,0:T(8,128)S(1)} custom-call(s32[1]{0:T(128)} %bitcast.half_ref, bf16[16,368,128]{2,1,0:T(8,128)(2,1)S(1)} %all-to-all-done.seen.ids_ref), custom_call_target="tpu_custom_call" | custom-call | flops 1000000000 | bytes 1000000 | tf_op jit(solution)/shard_map/part_own/pallas_call | solution.py:353
  64.9 24.0 %collective-permute-done.2.seen = bf16[4,8,48,128]{3,2,1,0:T(8,128)(2,1)S(1)} collective-permute-done((bf16[4,8,48,128]{3,2,1,0:T(8,128)(2,1)S(1)}, bf16[4,8,48,128]{3,2,1,0:T(8,128)(2,1)S(1)}, u32[]{:S(2)}, u32[]{:S(2)}) %collective-permute-start.2) | collective-permute-done | bytes 393248 | tf_op jit(solution)/shard_map/ppermute | solution.py:534
  89.0 0.4 collective-permute-start.3
  89.4 1.4 %collective-permute-start.4 = (bf16[8,48,128]{2,1,0:T(8,128)(2,1)S(1)}, bf16[8,48,128]{2,1,0:T(8,128)(2,1)S(1)}, u32[]{:S(2)}, u32[]{:S(2)}) collective-permute-start(bf16[8,48,128]{2,1,0:T(8,128)(2,1)S(1)} %get-tuple-element.28), channel_id=1, source_target_pairs={{0,16},{8,24},{16,0},{24,8},{1,17},{9,25},{17,1},{25,9},{2,18},{10... | collective-permute-start | bytes 294920 | tf_op jit(solution)/shard_map/ppermute | solution.py:562
  90.8 1.8 %collective-permute-start.5 = (bf16[8,48,128]{2,1,0:T(8,128)(2,1)S(1)}, bf16[8,48,128]{2,1,0:T(8,128)(2,1)S(1)}, u32[]{:S(2)}, u32[]{:S(2)}) collective-permute-start(bf16[8,48,128]{2,1,0:T(8,128)(2,1)S(1)} %get-tuple-element.29), channel_id=1, source_target_pairs={{0,24},{8,16},{16,8},{24,0},{1,25},{9,17},{17,9},{25,1},{2,26},{10... | collective-permute-start | bytes 294920 | tf_op jit(solution)/shard_map/ppermute | solution.py:562
  92.6 2.0 %collective-permute-done.3.refs_1_ = bf16[8,48,128]{2,1,0:T(8,128)(2,1)S(1)} collective-permute-done((bf16[8,48,128]{2,1,0:T(8,128)(2,1)S(1)}, bf16[8,48,128]{2,1,0:T(8,128)(2,1)S(1)}, u32[]{:S(2)}, u32[]{:S(2)}) %collective-permute-start.3) | collective-permute-done | bytes 98336 | tf_op jit(solution)/shard_map/ppermute | solution.py:562
  94.5 0.1 collective-permute-done.4.refs_2_
  94.6 1.8 %collective-permute-done.5.refs_3_ = bf16[8,48,128]{2,1,0:T(8,128)(2,1)S(1)} collective-permute-done((bf16[8,48,128]{2,1,0:T(8,128)(2,1)S(1)}, bf16[8,48,128]{2,1,0:T(8,128)(2,1)S(1)}, u32[]{:S(2)}, u32[]{:S(2)}) %collective-permute-start.5) | collective-permute-done | bytes 98336 | tf_op jit(solution)/shard_map/ppermute | solution.py:562
  96.4 1.1 %finish_tables.1 = f32[32,32,192]{2,1,0:T(8,128)} custom-call(s32[1]{0:T(128)} %bitcast.7.place, bf16[8,48,128]{2,1,0:T(8,128)(2,1)S(1)} %get-tuple-element.26.refs_0_, bf16[8,48,128]{2,1,0:T(8,128)(2,1)S(1)} %collective-permute-done.3.refs_1_, bf16[8,48,128]{2,1,0:T(8,128)(2,1)S(1)} %collective-permute-done.4.refs_2_, ...), custom_call_target="tpu_custom_call" | custom-call | bytes 1000000 | tf_op jit(solution)/shard_map/finish_tables/pallas_call | solution.py:522
  97.5 3.8 %unpack_rows.1 = (bf16[12,192,256]{2,1,0:T(8,128)(2,1)}, f32[256,128]{1,0:T(8,128)}, f32[192,128]{1,0:T(8,128)}, f32[256,256]{1,0:T(8,128)}, f32[1,192]{1,0:T(1,128)}) custom-call(bf16[16,352,128]{2,1,0:T(8,128)(2,1)} %all-to-all-done.1.seen), custom_call_target="tpu_custom_call" | custom-call | bytes 1000000 | tf_op jit(solution)/shard_map/unpack_rows/pallas_call | solution.py:473
  (12 shorter events, 0.1 us)
Async XLA Ops:
  0.6 15.6 %copy-start = (bf16[32,128,192]{1,2,0:T(8,128)(2,1)S(1)}, bf16[32,128,192]{1,2,0:T(8,128)(2,1)}, u32[]{:S(2)}) copy-start(bf16[32,128,192]{1,2,0:T(8,128)(2,1)} %param.13) | copy-start | bytes 4718596
  9.9 35.9 %all-to-all-start = ((bf16[16,368,128]{2,1,0:T(8,128)(2,1)}), bf16[16,368,128]{2,1,0:T(8,128)(2,1)S(1)}, u32[]{:S(2)}, u32[]{:S(2)}) async-start(bf16[16,368,128]{2,1,0:T(8,128)(2,1)} %layer_backward.1), calls=%async_computation | async-start | bytes 3014656 | tf_op jit(solution)/shard_map/all_to_all | solution.py:61
  16.3 27.1 %collective-permute-start = (bf16[8,192,128]{2,1,0:T(8,128)(2,1)S(1)}, bf16[8,192,128]{2,1,0:T(8,128)(2,1)S(1)}, u32[]{:S(2)}, u32[]{:S(2)}) collective-permute-start(bf16[8,192,128]{2,1,0:T(8,128)(2,1)S(1)} %dynamic-slice_bitcast_fusion.mine_t), channel_id=1, source_target_pairs={{0,4},{4,0},{1,5},{5,1},{2,6},{6,2},{3,7},{7,3},{8,12},{12,8},{9,1... | collective-permute-start | bytes 1179656 | tf_op jit(solution)/shard_map/ppermute | solution.py:534
  43.4 0.7 copy-start.2
  45.8 7.0 %copy-start.3 = (bf16[8,192,128]{2,1,0:T(8,128)(2,1)S(1)}, bf16[8,192,128]{2,1,0:T(8,128)(2,1)}, u32[]{:S(2)}) copy-start(bf16[8,192,128]{2,1,0:T(8,128)(2,1)} %copy-done.2) | copy-start | bytes 1179652
  47.2 0.8 copy-start.4
  47.9 4.8 %collective-permute-start.1 = (f32[64,128]{1,0:T(8,128)S(1)}, f32[64,128]{1,0:T(8,128)S(1)}, u32[]{:S(2)}, u32[]{:S(2)}) collective-permute-start(f32[64,128]{1,0:T(8,128)S(1)} %get-tuple-element.22.dense_own), channel_id=1, source_target_pairs={{0,4},{4,0},{1,5},{5,1},{2,6},{6,2},{3,7},{7,3},{8,12},{12,8},{9,1... | collective-permute-start | bytes 98312 | tf_op jit(solution)/shard_map/ppermute | solution.py:534
  56.0 1.1 %copy-start.1 = (bf16[16,352,128]{2,1,0:T(8,128)(2,1)}, bf16[16,352,128]{2,1,0:T(8,128)(2,1)S(1)}, u32[]{:S(2)}) copy-start(bf16[16,352,128]{2,1,0:T(8,128)(2,1)S(1)} %lookup.1) | copy-start | bytes 4325380
  57.1 5.5 %copy-start.5 = (bf16[4,8,48,128]{3,2,1,0:T(8,128)(2,1)S(1)}, bf16[4,8,48,128]{3,2,1,0:T(8,128)(2,1)}, u32[]{:S(2)}) copy-start(bf16[4,8,48,128]{3,2,1,0:T(8,128)(2,1)} %copy-done.4) | copy-start | bytes 1179652
  57.1 40.4 %all-to-all-start.1 = ((bf16[16,352,128]{2,1,0:T(8,128)(2,1)}), bf16[16,352,128]{2,1,0:T(8,128)(2,1)}, u32[]{:S(2)}, u32[]{:S(2)}) async-start(bf16[16,352,128]{2,1,0:T(8,128)(2,1)} %copy-done.1), calls=%async_computation.1 | async-start | bytes 2883584 | tf_op jit(solution)/shard_map/all_to_all | solution.py:61
  62.6 26.3 %collective-permute-start.2 = (bf16[4,8,48,128]{3,2,1,0:T(8,128)(2,1)S(1)}, bf16[4,8,48,128]{3,2,1,0:T(8,128)(2,1)S(1)}, u32[]{:S(2)}, u32[]{:S(2)}) collective-permute-start(bf16[4,8,48,128]{3,2,1,0:T(8,128)(2,1)S(1)} %copy-done.5), channel_id=1, source_target_pairs={{0,4},{4,0},{1,5},{5,1},{2,6},{6,2},{3,7},{7,3},{8,12},{12,8},{9,1... | collective-permute-start | bytes 1179656 | tf_op jit(solution)/shard_map/ppermute | solution.py:534
  89.0 5.5 %collective-permute-start.3 = (bf16[8,48,128]{2,1,0:T(8,128)(2,1)S(1)}, bf16[8,48,128]{2,1,0:T(8,128)(2,1)S(1)}, u32[]{:S(2)}, u32[]{:S(2)}) collective-permute-start(bf16[8,48,128]{2,1,0:T(8,128)(2,1)S(1)} %get-tuple-element.27), channel_id=1, source_target_pairs={{0,8},{8,0},{16,24},{24,16},{1,9},{9,1},{17,25},{25,17},{2,10},{10... | collective-permute-start | bytes 294920 | tf_op jit(solution)/shard_map/ppermute | solution.py:562
  89.4 5.2 %collective-permute-start.4 = (bf16[8,48,128]{2,1,0:T(8,128)(2,1)S(1)}, bf16[8,48,128]{2,1,0:T(8,128)(2,1)S(1)}, u32[]{:S(2)}, u32[]{:S(2)}) collective-permute-start(bf16[8,48,128]{2,1,0:T(8,128)(2,1)S(1)} %get-tuple-element.28), channel_id=1, source_target_pairs={{0,16},{8,24},{16,0},{24,8},{1,17},{9,25},{17,1},{25,9},{2,18},{10... | collective-permute-start | bytes 294920 | tf_op jit(solution)/shard_map/ppermute | solution.py:562
  90.8 5.6 %collective-permute-start.5 = (bf16[8,48,128]{2,1,0:T(8,128)(2,1)S(1)}, bf16[8,48,128]{2,1,0:T(8,128)(2,1)S(1)}, u32[]{:S(2)}, u32[]{:S(2)}) collective-permute-start(bf16[8,48,128]{2,1,0:T(8,128)(2,1)S(1)} %get-tuple-element.29), channel_id=1, source_target_pairs={{0,24},{8,16},{16,8},{24,0},{1,25},{9,17},{17,9},{25,1},{2,26},{10... | collective-permute-start | bytes 294920 | tf_op jit(solution)/shard_map/ppermute | solution.py:562

commit v5 on v4

--- a/solution.py
+++ b/solution.py
@@ -13,7 +13,7 @@
 LANES = 128
 TILE = 8
 STEP = 4
-LIMIT = 40 * 1024 * 1024
+LIMIT = 30 * 1024 * 1024
 PEER = ("grp", "lane")
 
 
@@ -104,8 +104,12 @@
     return (next_rows, table_grad, *dense)
 
 
-def params(**more):
-    return pltpu.CompilerParams(vmem_limit_bytes=LIMIT, **more)
+def params(share=1):
+    return pltpu.CompilerParams(vmem_limit_bytes=share * LIMIT)
+
+
+def cost(weight):
+    return pl.CostEstimate(flops=weight * 10**9, bytes_accessed=10**5, transcendentals=0)
 
 
 def mm(left, right, dims=((1,), (0,))):
@@ -134,7 +138,10 @@
         self.left = count * TILE
         self.half = self.left + self.left // 2
         self.dense = 2 * self.half
-        self.ids = self.dense + 1024 // peers
+        self.share = 1024 // peers
+        self.ids = self.dense + self.share
+        self.back_left = (self.share, self.share + self.left)
+        self.back_right = (self.share + 2 * self.left, self.share + 2 * self.left + self.left // 2)
 
 
 def place_of(n_grp, n_lane, peer):
@@ -295,13 +302,14 @@
             pltpu.VMEM((count // STEP, 2, features // 2, STEP * width), F32),
             pltpu.VMEM((2, 16, features), F32),
         ],
-        compiler_params=pltpu.CompilerParams(vmem_limit_bytes=60 * 1024 * 1024),
-        cost_estimate=pl.CostEstimate(flops=10**9, bytes_accessed=4 * 10**6, transcendentals=0),
+        compiler_params=params(2),
+        cost_estimate=cost(1),
         name="layer_backward",
     )(half, *operands)
 
 
 def part_kernel(n_grp, wire, other, half_ref, seen, *refs):
+    refs = refs if other else refs[1:]
     out, held = refs[0], refs[-1]
     peers = seen.shape[0]
     half = 1 - half_ref[0] if other else half_ref[0]
@@ -344,25 +352,25 @@
                 out[g, 2 * pair + f, piece : piece + piece // 2] = packed.astype(out.dtype)
 
 
-def part_sums(n_grp, wire, other, half, seen):
+def part_sums(n_grp, wire, other, half, seen, *after):
     peers = seen.shape[0]
     piece = LANES // n_grp
     shapes = [jax.ShapeDtypeStruct((n_grp, TILE, piece + piece // 2, LANES), BF16 if other else F32)]
     if other:
-        shapes.append(jax.ShapeDtypeStruct((wire.ids - wire.dense, LANES), F32))
+        shapes.append(jax.ShapeDtypeStruct((wire.share, LANES), F32))
     return pl.pallas_call(
         functools.partial(part_kernel, n_grp, wire, other),
-        in_specs=[SMEM, VMEM],
+        in_specs=[SMEM, VMEM] + [pl.BlockSpec(memory_space=pl.ANY)] * len(after),
         out_specs=[VMEM] * len(shapes),
         out_shape=shapes,
         scratch_shapes=[pltpu.VMEM((peers * LANES, 256), BF16)],
         compiler_params=params(),
-        cost_estimate=pl.CostEstimate(flops=10**9, bytes_accessed=10**6, transcendentals=0),
+        cost_estimate=cost(1),
         name="part_other" if other else "part_own",
-    )(half, seen)
-
-
-def lookup_kernel(wire, factor, half_ref, mine_t, crossed_t, ids_ref, dense_own, dense_seen, out, held):
+    )(half, seen, *after)
+
+
+def lookup_kernel(wire, half_ref, mine_t, crossed_t, ids_ref, out, held, hit):
     peers = out.shape[0]
     half = half_ref[0]
     for f in range(TILE):
@@ -374,68 +382,90 @@
     lane = lax.broadcasted_iota(jnp.int32, (1, LANES), 1)
     keys = (ids + ((lane % TILE) * LANES).astype(F32)).T
     column = lax.broadcasted_iota(jnp.int32, (1, TILE * LANES), 1).astype(F32)
-    total = ((dense_own[...] + dense_seen[...]) * factor).astype(BF16)
     for which in range(2):
-        for pair in range(peers // 2):
-            mine = []
-            for peer in (2 * pair, 2 * pair + 1):
-                at = peer * 16 + 2 + which
-                mine.append(keys[0 : wire.left, at : at + 1])
-            hit = jnp.where(jnp.concatenate(mine, axis=0) == column, 1.0, 0.0).astype(BF16)
-            both = mm_nt(hit, held[which])
-            for k in range(2):
-                got = both[k * wire.left : (k + 1) * wire.left]
-                peer, base = 2 * pair + k, which * wire.half
-                out[peer, base : base + wire.left] = got[:, 0:128].astype(BF16)
-                for i in range(wire.left // 32):
-                    first, second = got[32 * i : 32 * i + 16, 128:256], got[32 * i + 16 : 32 * i + 32, 128:256]
-                    at = base + wire.left + 16 * i
-                    out[peer, at : at + 16] = jnp.where(low_lanes(first.shape), first, second).astype(BF16)
-    for peer in range(peers):
-        out[peer, wire.dense : wire.ids] = total
-
-
-def lookup(wire, factor, half, mine_t, crossed_t, ids, dense_own, dense_seen):
+        for peer in range(peers):
+            at = peer * 16 + 2 + which
+            mine = jnp.where(keys[0 : wire.left, at : at + 1] == column, 1.0, 0.0)
+            hit[which, peer * wire.left : (peer + 1) * wire.left] = mine.astype(BF16)
+    for which in range(2):
+        rows = mm_nt(hit[which], held[which])
+        for peer in range(peers):
+            got = rows[peer * wire.left : (peer + 1) * wire.left]
+            base = wire.back_left[which]
+            out[peer, base : base + wire.left] = got[:, 0:128].astype(BF16)
+            packed = []
+            for i in range(wire.left // 32):
+                first, second = got[32 * i : 32 * i + 16, 128:256], got[32 * i + 16 : 32 * i + 32, 128:256]
+                packed.append(jnp.where(low_lanes(first.shape), first, second))
+            base = wire.back_right[which]
+            out[peer, base : base + wire.left // 2] = jnp.concatenate(packed, axis=0).astype(BF16)
+
+
+def lookup(wire, half, mine_t, crossed_t, ids):
     peers = ids.shape[0]
-    rows = wire.ids
 
     def whole(shape):
         return pl.BlockSpec(shape, lambda i: (0,) * len(shape))
 
     at = wire.ids // 16
     return pl.pallas_call(
-        functools.partial(lookup_kernel, wire, factor),
+        functools.partial(lookup_kernel, wire),
         grid=(1,),
         in_specs=[
             SMEM,
             whole(mine_t.shape),
             whole(crossed_t.shape),
             pl.BlockSpec((peers, 16, LANES), lambda i: (0, at, 0)),
-            whole(dense_own.shape),
-            whole(dense_seen.shape),
         ],
-        out_specs=whole((peers, rows, LANES)),
-        out_shape=jax.ShapeDtypeStruct((peers, rows, LANES), BF16),
-        scratch_shapes=[pltpu.VMEM((2, 256, TILE * LANES), BF16)],
-        compiler_params=params(),
-        cost_estimate=pl.CostEstimate(flops=10**9, bytes_accessed=10**6, transcendentals=0),
+        out_specs=whole((peers, wire.ids, LANES)),
+        out_shape=jax.ShapeDtypeStruct((peers, wire.ids, LANES), BF16),
+        scratch_shapes=[
+            pltpu.VMEM((2, 256, TILE * LANES), BF16),
+            pltpu.VMEM((2, peers * wire.left, TILE * LANES), BF16),
+        ],
+        compiler_params=params(2),
+        cost_estimate=cost(100),
         name="lookup",
-    )(half, mine_t, crossed_t, ids, dense_own, dense_seen)
-
-
-def unpack_kernel(n_grp, n_lane, wire, seen, rows_out, fm, proj_t, lcb, gain, held):
+    )(half, mine_t, crossed_t, ids)
+
+
+def fill_kernel(factor, rows, own, seen, out, token):
+    token[...] = jnp.zeros_like(token)
+    total = ((own[...] + seen[...]) * factor).astype(BF16)
+    for peer in range(out.shape[0]):
+        out[peer] = total
+
+
+def fill(wire, factor, rows, own, seen):
+    peers = rows.shape[0]
+
+    def whole(shape):
+        return pl.BlockSpec(shape, lambda i: (0,) * len(shape))
+
+    return pl.pallas_call(
+        functools.partial(fill_kernel, factor),
+        grid=(1,),
+        in_specs=[pl.BlockSpec(memory_space=pl.ANY), whole(own.shape), whole(seen.shape)],
+        out_specs=[whole((peers, wire.share, LANES)), whole((8, LANES))],
+        out_shape=[jax.ShapeDtypeStruct(rows.shape, BF16), jax.ShapeDtypeStruct((8, LANES), F32)],
+        input_output_aliases={0: 0},
+        compiler_params=params(2),
+        cost_estimate=cost(1),
+        name="fill_dense",
+    )(rows, own, seen)
+
+
+def unpack_kernel(n_grp, n_lane, dense_ref, left0, left1, right0, right1, rows_out, fm, proj_t, lcb, gain, held):
     step = pl.program_id(0)
     peers = n_grp * n_lane
-    for side in range(2):
+    for side, (left_ref, right_ref) in enumerate(((left0, right0), (left1, right1))):
         for q in range(n_lane):
             for gg in range(n_grp // 2):
                 left, right = [], []
                 for g in (2 * gg, 2 * gg + 1):
                     peer = g * n_lane + q
-                    row = pl.multiple_of(side * wire.half + step * 32, 16)
-                    left.append(seen[peer, pl.ds(row, 32)].astype(F32))
-                    row = pl.multiple_of(side * wire.half + wire.left + step * 16, 16)
-                    packed = seen[peer, pl.ds(row, 16)].astype(F32)
+                    left.append(left_ref[peer].astype(F32))
+                    packed = right_ref[peer].astype(F32)
                     right.append(jnp.concatenate([packed, turn(packed)], axis=0))
                 at = side * 128 + q * n_grp * TILE + gg * 16
                 for s in range(STEP):
@@ -452,7 +482,7 @@
     def _():
         part, third = 256 // peers, 192 // peers
         for peer in range(peers):
-            dense = seen[peer, wire.dense : wire.ids].astype(F32)
+            dense = dense_ref[peer].astype(F32)
             here = slice(peer * part, (peer + 1) * part)
             fm[here] = dense[0:part]
             lcb[here, 0:128] = dense[part : 2 * part]
@@ -469,39 +499,45 @@
     def whole(*shape):
         return pl.BlockSpec(shape, lambda i: (0,) * len(shape))
 
+    def part(rows, start):
+        return pl.BlockSpec((peers, rows, LANES), lambda i: (0, start // rows + i, 0))
+
+    peers = n_grp * n_lane
     shapes = [(256, 128), (192, 128), (256, 256), (1, 192)]
     return pl.pallas_call(
-        functools.partial(unpack_kernel, n_grp, n_lane, wire),
+        functools.partial(unpack_kernel, n_grp, n_lane),
         grid=(count // STEP,),
-        in_specs=[whole(*seen.shape)],
+        in_specs=[pl.BlockSpec((peers, wire.share, LANES), lambda i: (0, 0, 0))]
+        + [part(32, start) for start in wire.back_left]
+        + [part(16, start) for start in wire.back_right],
         out_specs=[pl.BlockSpec((STEP, 192, 256), lambda i: (i, 0, 0))] + [whole(*shape) for shape in shapes],
         out_shape=[jax.ShapeDtypeStruct((count, 192, 256), BF16)]
         + [jax.ShapeDtypeStruct(shape, F32) for shape in shapes],
         scratch_shapes=[pltpu.VMEM((STEP, 256, 256), BF16)],
         compiler_params=params(),
-        cost_estimate=pl.CostEstimate(flops=0, bytes_accessed=10**6, transcendentals=0),
+        cost_estimate=cost(1),
         name="unpack_rows",
-    )(seen)
-
-
-def combine_kernel(place, own, seen, *outs):
+    )(seen, seen, seen, seen, seen)
+
+
+def combine_kernel(place, own, seen, after, *outs):
     for k, out in enumerate(outs):
         g = jnp.bitwise_xor(place[0], k)
         out[...] = (own[g] + seen[g].astype(F32)).astype(BF16)
 
 
-def combine(place, own, seen):
+def combine(place, own, seen, after):
     n_grp = own.shape[0]
     shape = jax.ShapeDtypeStruct(own.shape[1:], BF16)
     return pl.pallas_call(
         combine_kernel,
-        in_specs=[SMEM, VMEM, VMEM],
+        in_specs=[SMEM, VMEM, VMEM, pl.BlockSpec(memory_space=pl.ANY)],
         out_specs=[VMEM] * n_grp,
         out_shape=[shape] * n_grp,
         compiler_params=params(),
-        cost_estimate=pl.CostEstimate(flops=0, bytes_accessed=10**6, transcendentals=0),
+        cost_estimate=cost(100),
         name="combine",
-    )(place, own, seen)
+    )(place, own, seen, after)
 
 
 def finish_kernel(place, *refs):
@@ -525,7 +561,7 @@
         out_specs=VMEM,
         out_shape=jax.ShapeDtypeStruct((n_grp * TILE, piece, 192), F32),
         compiler_params=params(),
-        cost_estimate=pl.CostEstimate(flops=0, bytes_accessed=10**6, transcendentals=0),
+        cost_estimate=cost(0),
         name="finish_tables",
     )(place, *pieces)
 
@@ -548,16 +584,15 @@
         pooled.transpose(0, 2, 1), upstream.transpose(0, 2, 1), ids_now, ids_next, w_fm, w_proj.T, w_lcb, gain,
     )
     seen = exchange(sent, PEER)
-    crossed_t, seen = lax.optimization_barrier((crossed_t, seen))
     part, dense = part_sums(n_grp, wire, True, half, seen)
     dense_seen = cross(dense)
     part_seen = cross(part)
-    (own,) = part_sums(n_grp, wire, False, half, seen)
-    rows_wire = lookup(wire, factor, half, mine_t, crossed_t, seen, dense, dense_seen)
+    rows_wire = lookup(wire, half, mine_t, crossed_t, seen)
+    rows_wire, token = fill(wire, factor, rows_wire, dense, dense_seen)
     rows = exchange(rows_wire, PEER)
+    (own,) = part_sums(n_grp, wire, False, half, seen, token)
     next_rows, grad_fm, grad_proj_t, grad_lcb, grad_gain = unpack(n_grp, n_lane, wire, count, rows)
-    own, _ = lax.optimization_barrier((own, rows_wire))
-    pieces = combine(grp[None], own, part_seen)
+    pieces = combine(grp[None], own, part_seen, token)
     pieces = [pieces[0]] + [
         lax.ppermute(pieces[k], "grp", [(g, g ^ k) for g in range(n_grp)]) for k in range(1, n_grp)
     ]

time: 102 us -> 95.5 us (0.936)
  waiting for transfers between devices: 57 us -> 49.3 us
  Pallas kernels: 20.3 us -> 23 us
  starting transfers between devices: 20.6 us -> 19.3 us
    ppermute x3, waiting for transfers between devices: 51.5 us -> 6.06 us  [cross(): return lax.ppermute(array, 'half', [(0, 1), (1, 0)])]
    all_to_all x2, waiting for transfers between devices: 1.67 us -> 26.2 us  [exchange(): return lax.all_to_all(blocks, axes, split_axis=0, concat_axis=0, tiled=True)]
    ppermute x3, waiting for transfers between devices: 3.85 us -> 17.1 us  [halves(): lax.ppermute(pieces[k], 'grp', [(g, g ^ k) for g in range(n_grp)])]
    pallas_call x3 -> x4, Pallas kernels: 7.09 us -> 9.79 us  [the longest x1 4.64 us: lookup(): pl.pallas_call(functools.partial(lookup_kernel, wire), grid=(1,), in_spec...]
    all_to_all x2, starting transfers between devices: 11.8 us -> 10.1 us  [exchange(): return lax.all_to_all(blocks, axes, split_axis=0, concat_axis=0, tiled=True)]
  transfers between devices with their start and end apart: 8 -> 8, of which waited for: 7 -> 4; matrix products, arithmetic and copies ran while one was open for 0% -> 1% of each run, Pallas kernels for 3% -> 12%
where the time goes in v5:
time: 95.5 us; the launch traced here: 95.1 us
  waiting for transfers between devices  49.3 us (52%)
  Pallas kernels  23 us (24%)
  starting transfers between devices  19.3 us (20%)
  local copies, waits for them, and re-layouts  2.79 us (3%)
    all_to_all x2, waiting for transfers between devices, exchange(): return lax.all_to_all(blocks, axes, split_axis=0, concat_axis=0, tiled=True)  26.2 us
    ppermute x3, waiting for transfers between devices, halves(): lax.ppermute(pieces[k], 'grp', [(g, g ^ k) for g in range(n_grp)])  17.1 us
    all_to_all x2, starting transfers between devices, exchange(): return lax.all_to_all(blocks, axes, split_axis=0, concat_axis=0, tiled=True)  10.1 us
    pallas_call x1, Pallas kernels, backward(): pl.pallas_call(functools.partial(backward_kernel, n_grp, n_lane, wire), g...  9.28 us
    ppermute x3, waiting for transfers between devices, cross(): return lax.ppermute(array, 'half', [(0, 1), (1, 0)])  6.06 us
    ppermute x3, starting transfers between devices, cross(): return lax.ppermute(array, 'half', [(0, 1), (1, 0)])  5.57 us
    pallas_call x1, Pallas kernels, lookup(): pl.pallas_call(functools.partial(lookup_kernel, wire), grid=(1,), in_spec...  4.64 us
    ppermute x3, starting transfers between devices, halves(): lax.ppermute(pieces[k], 'grp', [(g, g ^ k) for g in range(n_grp)])  3.55 us
  transfers between devices with their start and end apart: 8, of which 4 were waited for; matrix products, arithmetic and copies ran while one was open for 1% of the time, Pallas kernels for 12%

profile of v5, /device:TPU:0, one launch (start us, length us, event | category | flops | bytes accessed | tf_op | source)
XLA Modules:
  0.0 95.1 jit_solution(5932093721856978486)
XLA Ops:
  0.6 0.0 copy-start
  0.7 9.3 %layer_backward.1 = bf16[16,368,128]{2,1,0:T(8,128)(2,1)} custom-call(s32[1]{0:T(128)} %bitcast.half_ref, bf16[12,192,256]{2,1,0:T(8,128)(2,1)} %bitcast.11, bf16[12,192,256]{2,1,0:T(8,128)(2,1)} %bitcast.12, s32[12,256]{1,0:T(8,128)} %now_ref.1, s32[12,256]{1,0:T(8,128)} %next_ref.1, bf16[256,128]{1,0:T(8,128)(2,1)} %fm_ref.1, bf16[192,128]{1,0:T(8,128)(2,1)} %bitcast.13, ...), custom_call_target="tpu_custom_call" | custom-call | flops 1000000000 | bytes 100000 | tf_op jit(solution)/shard_map/layer_backward/pallas_call | solution.py:282
  9.9 6.3 %all-to-all-start = ((bf16[16,368,128]{2,1,0:T(8,128)(2,1)}), bf16[16,368,128]{2,1,0:T(8,128)(2,1)S(1)}, u32[]{:S(2)}, u32[]{:S(2)}) async-start(bf16[16,368,128]{2,1,0:T(8,128)(2,1)} %layer_backward.1), calls=%async_computation | async-start | bytes 3014656 | tf_op jit(solution)/shard_map/all_to_all | solution.py:61
  16.3 0.8 dynamic-slice_bitcast_fusion.mine_t
  17.0 2.6 %collective-permute-start = (bf16[8,192,128]{2,1,0:T(8,128)(2,1)}, bf16[8,192,128]{2,1,0:T(8,128)(2,1)}, u32[]{:S(2)}, u32[]{:S(2)}) collective-permute-start(bf16[8,192,128]{2,1,0:T(8,128)(2,1)} %dynamic-slice_bitcast_fusion.mine_t), channel_id=1, source_target_pairs={{0,4},{4,0},{1,5},{5,1},{2,6},{6,2},{3,7},{7,3},{8,12},{12,8},{9,1... | collective-permute-start | bytes 1179656 | tf_op jit(solution)/shard_map/ppermute | solution.py:570
  19.6 26.2 %all-to-all-done.ids_ref.seen = bf16[16,368,128]{2,1,0:T(8,128)(2,1)S(1)} async-done(((bf16[16,368,128]{2,1,0:T(8,128)(2,1)}), bf16[16,368,128]{2,1,0:T(8,128)(2,1)S(1)}, u32[]{:S(2)}, u32[]{:S(2)}) %all-to-all-start) | async-done | bytes 1507360 | tf_op jit(solution)/shard_map/all_to_all | solution.py:61
  45.8 1.4 %part_other.1 = (bf16[4,8,48,128]{3,2,1,0:T(8,128)(2,1)S(1)}, f32[64,128]{1,0:T(8,128)S(1)}) custom-call(s32[1]{0:T(128)} %bitcast.half_ref, bf16[16,368,128]{2,1,0:T(8,128)(2,1)S(1)} %all-to-all-done.ids_ref.seen), custom_call_target="tpu_custom_call" | custom-call | flops 1000000000 | bytes 100000 | tf_op jit(solution)/shard_map/part_other/pallas_call | solution.py:361
  47.2 0.1 collective-permute-start.1
  47.3 2.9 %collective-permute-start.2 = (bf16[4,8,48,128]{3,2,1,0:T(8,128)(2,1)S(1)}, bf16[4,8,48,128]{3,2,1,0:T(8,128)(2,1)}, u32[]{:S(2)}, u32[]{:S(2)}) collective-permute-start(bf16[4,8,48,128]{3,2,1,0:T(8,128)(2,1)S(1)} %get-tuple-element.23), channel_id=1, source_target_pairs={{0,4},{4,0},{1,5},{5,1},{2,6},{6,2},{3,7},{7,3},{8,12},{12,8},{9,1... | collective-permute-start | bytes 1179656 | tf_op jit(solution)/shard_map/ppermute | solution.py:570
  50.2 4.6 %lookup.1.rows = bf16[16,352,128]{2,1,0:T(8,128)(2,1)} custom-call(s32[1]{0:T(128)} %bitcast.half_ref, bf16[8,192,128]{2,1,0:T(8,128)(2,1)} %dynamic-slice_bitcast_fusion.mine_t, bf16[8,192,128]{2,1,0:T(8,128)(2,1)} %collective-permute-done.crossed_t, bf16[16,368,128]{2,1,0:T(8,128)(2,1)} %copy-done.1), custom_call_target="tpu_custom_call" | custom-call | flops 99999997952 | bytes 100000 | tf_op jit(solution)/shard_map/lookup/pallas_call | solution.py:411
  54.9 6.1 %collective-permute-done.1.seen = f32[64,128]{1,0:T(8,128)S(1)} collective-permute-done((f32[64,128]{1,0:T(8,128)S(1)}, f32[64,128]{1,0:T(8,128)S(1)}, u32[]{:S(2)}, u32[]{:S(2)}) %collective-permute-start.1) | collective-permute-done | bytes 32800 | tf_op jit(solution)/shard_map/ppermute | solution.py:570
  60.9 0.6 copy-done.5
  61.5 1.5 %fill_dense.1 = (bf16[16,352,128]{2,1,0:T(8,128)(2,1)}, f32[8,128]{1,0:T(8,128)}) custom-call(bf16[16,352,128]{2,1,0:T(8,128)(2,1)} %lookup.1.rows, f32[64,128]{1,0:T(8,128)} %copy-done.3, f32[64,128]{1,0:T(8,128)} %copy-done.5), custom_call_target="tpu_custom_call", output_to_operand_aliasing={{0}: (0, {})} | custom-call | flops 1000000000 | bytes 100000 | tf_op jit(solution)/shard_map/fill_dense/pallas_call | solution.py:445
  63.1 3.8 %all-to-all-start.1 = ((bf16[16,352,128]{2,1,0:T(8,128)(2,1)}), bf16[16,352,128]{2,1,0:T(8,128)(2,1)S(1)}, u32[]{:S(2)}, u32[]{:S(2)}) async-start(bf16[16,352,128]{2,1,0:T(8,128)(2,1)} %get-tuple-element.20), calls=%async_computation.1 | async-start | bytes 2883584 | tf_op jit(solution)/shard_map/all_to_all | solution.py:61
  66.9 1.4 %copy-done.2 = bf16[16,368,128]{2,1,0:T(8,128)(2,1)S(1)} copy-done((bf16[16,368,128]{2,1,0:T(8,128)(2,1)S(1)}, bf16[16,368,128]{2,1,0:T(8,128)(2,1)}, u32[]{:S(2)}) %copy-start.2) | copy-done | bytes 1507352
  68.3 1.4 %part_own.1.own = f32[4,8,48,128]{3,2,1,0:T(8,128)S(1)} custom-call(s32[1]{0:T(128)} %bitcast.half_ref, bf16[16,368,128]{2,1,0:T(8,128)(2,1)S(1)} %copy-done.2, f32[8,128]{1,0:T(8,128)S(1)} %copy-done.4), custom_call_target="tpu_custom_call" | custom-call | flops 1000000000 | bytes 100000 | tf_op jit(solution)/shard_map/part_own/pallas_call | solution.py:361
  69.7 1.1 %combine.1 = (bf16[8,48,128]{2,1,0:T(8,128)(2,1)S(1)}, bf16[8,48,128]{2,1,0:T(8,128)(2,1)S(1)}, bf16[8,48,128]{2,1,0:T(8,128)(2,1)S(1)}, bf16[8,48,128]{2,1,0:T(8,128)(2,1)S(1)}) custom-call(s32[1]{0:T(128)} %bitcast.7.place, f32[4,8,48,128]{3,2,1,0:T(8,128)S(1)} %part_own.1.own, bf16[4,8,48,128]{3,2,1,0:T(8,128)(2,1)} %collective-permute-done.2.seen, ...), custom_call_target="tpu_custom_call" | custom-call | flops 99999997952 | bytes 100000 | tf_op jit(solution)/shard_map/combine/pallas_call | solution.py:532
  70.8 1.9 %collective-permute-start.3 = (bf16[8,48,128]{2,1,0:T(8,128)(2,1)S(1)}, bf16[8,48,128]{2,1,0:T(8,128)(2,1)S(1)}, u32[]{:S(2)}, u32[]{:S(2)}) collective-permute-start(bf16[8,48,128]{2,1,0:T(8,128)(2,1)S(1)} %get-tuple-element.25), channel_id=1, source_target_pairs={{0,8},{8,0},{16,24},{24,16},{1,9},{9,1},{17,25},{25,17},{2,10},{10... | collective-permute-start | bytes 294920 | tf_op jit(solution)/shard_map/ppermute | solution.py:597
  72.7 1.5 %collective-permute-start.4 = (bf16[8,48,128]{2,1,0:T(8,128)(2,1)S(1)}, bf16[8,48,128]{2,1,0:T(8,128)(2,1)S(1)}, u32[]{:S(2)}, u32[]{:S(2)}) collective-permute-start(bf16[8,48,128]{2,1,0:T(8,128)(2,1)S(1)} %get-tuple-element.26), channel_id=1, source_target_pairs={{0,16},{8,24},{16,0},{24,8},{1,17},{9,25},{17,1},{25,9},{2,18},{10... | collective-permute-start | bytes 294920 | tf_op jit(solution)/shard_map/ppermute | solution.py:597
  74.2 0.2 collective-permute-start.5
  74.4 14.5 %collective-permute-done.3.refs_1_ = bf16[8,48,128]{2,1,0:T(8,128)(2,1)S(1)} collective-permute-done((bf16[8,48,128]{2,1,0:T(8,128)(2,1)S(1)}, bf16[8,48,128]{2,1,0:T(8,128)(2,1)S(1)}, u32[]{:S(2)}, u32[]{:S(2)}) %collective-permute-start.3) | collective-permute-done | bytes 98336 | tf_op jit(solution)/shard_map/ppermute | solution.py:597
  88.9 2.6 %collective-permute-done.5.refs_3_ = bf16[8,48,128]{2,1,0:T(8,128)(2,1)S(1)} collective-permute-done((bf16[8,48,128]{2,1,0:T(8,128)(2,1)S(1)}, bf16[8,48,128]{2,1,0:T(8,128)(2,1)S(1)}, u32[]{:S(2)}, u32[]{:S(2)}) %collective-permute-start.5) | collective-permute-done | bytes 98336 | tf_op jit(solution)/shard_map/ppermute | solution.py:597
  91.4 1.1 %finish_tables.1 = f32[32,32,192]{2,1,0:T(8,128)} custom-call(s32[1]{0:T(128)} %bitcast.7.place, bf16[8,48,128]{2,1,0:T(8,128)(2,1)S(1)} %get-tuple-element.24.refs_0_, bf16[8,48,128]{2,1,0:T(8,128)(2,1)S(1)} %collective-permute-done.3.refs_1_, bf16[8,48,128]{2,1,0:T(8,128)(2,1)S(1)} %collective-permute-done.4.refs_2_, ...), custom_call_target="tpu_custom_call" | custom-call | bytes 100000 | tf_op jit(solution)/shard_map/finish_tables/pallas_call | solution.py:558
  92.5 2.5 %unpack_rows.1 = (bf16[12,192,256]{2,1,0:T(8,128)(2,1)}, f32[256,128]{1,0:T(8,128)}, f32[192,128]{1,0:T(8,128)}, f32[256,256]{1,0:T(8,128)}, f32[1,192]{1,0:T(1,128)}) custom-call(bf16[16,352,128]{2,1,0:T(8,128)(2,1)S(1)} %all-to-all-done.1.dense_ref.left0.left1.right0.right1, bf16[16,352,128]{2,1,0:T(8,128)(2,1)S(1)} %all-to-all-done.1.dense_ref.left0.left1.right0.right1, ...), custom_call_target="tpu_custom_call" | custom-call | flops 1000000000 | bytes 100000 | tf_op jit(solution)/shard_map/unpack_rows/pallas_call | solution.py:507
  (13 shorter events, 0.0 us)
Async XLA Ops:
  0.6 15.6 %copy-start = (bf16[32,128,192]{1,2,0:T(8,128)(2,1)S(1)}, bf16[32,128,192]{1,2,0:T(8,128)(2,1)}, u32[]{:S(2)}) copy-start(bf16[32,128,192]{1,2,0:T(8,128)(2,1)} %param.13) | copy-start | bytes 4718596
  9.9 35.9 %all-to-all-start = ((bf16[16,368,128]{2,1,0:T(8,128)(2,1)}), bf16[16,368,128]{2,1,0:T(8,128)(2,1)S(1)}, u32[]{:S(2)}, u32[]{:S(2)}) async-start(bf16[16,368,128]{2,1,0:T(8,128)(2,1)} %layer_backward.1), calls=%async_computation | async-start | bytes 3014656 | tf_op jit(solution)/shard_map/all_to_all | solution.py:61
  17.0 33.2 %collective-permute-start = (bf16[8,192,128]{2,1,0:T(8,128)(2,1)}, bf16[8,192,128]{2,1,0:T(8,128)(2,1)}, u32[]{:S(2)}, u32[]{:S(2)}) collective-permute-start(bf16[8,192,128]{2,1,0:T(8,128)(2,1)} %dynamic-slice_bitcast_fusion.mine_t), channel_id=1, source_target_pairs={{0,4},{4,0},{1,5},{5,1},{2,6},{6,2},{3,7},{7,3},{8,12},{12,8},{9,1... | collective-permute-start | bytes 1179656 | tf_op jit(solution)/shard_map/ppermute | solution.py:570
  45.8 1.4 %copy-start.1 = (bf16[16,368,128]{2,1,0:T(8,128)(2,1)}, bf16[16,368,128]{2,1,0:T(8,128)(2,1)S(1)}, u32[]{:S(2)}) copy-start(bf16[16,368,128]{2,1,0:T(8,128)(2,1)S(1)} %all-to-all-done.ids_ref.seen) | copy-start | bytes 4521988
  47.2 7.6 %copy-start.3 = (f32[64,128]{1,0:T(8,128)}, f32[64,128]{1,0:T(8,128)S(1)}, u32[]{:S(2)}) copy-start(f32[64,128]{1,0:T(8,128)S(1)} %get-tuple-element.19.own) | copy-start | bytes 98308
  47.2 13.7 %collective-permute-start.1 = (f32[64,128]{1,0:T(8,128)S(1)}, f32[64,128]{1,0:T(8,128)S(1)}, u32[]{:S(2)}, u32[]{:S(2)}) collective-permute-start(f32[64,128]{1,0:T(8,128)S(1)} %get-tuple-element.19.own), channel_id=1, source_target_pairs={{0,4},{4,0},{1,5},{5,1},{2,6},{6,2},{3,7},{7,3},{8,12},{12,8},{9,1... | collective-permute-start | bytes 98312 | tf_op jit(solution)/shard_map/ppermute | solution.py:570
  47.3 22.4 %collective-permute-start.2 = (bf16[4,8,48,128]{3,2,1,0:T(8,128)(2,1)S(1)}, bf16[4,8,48,128]{3,2,1,0:T(8,128)(2,1)}, u32[]{:S(2)}, u32[]{:S(2)}) collective-permute-start(bf16[4,8,48,128]{3,2,1,0:T(8,128)(2,1)S(1)} %get-tuple-element.23), channel_id=1, source_target_pairs={{0,4},{4,0},{1,5},{5,1},{2,6},{6,2},{3,7},{7,3},{8,12},{12,8},{9,1... | collective-permute-start | bytes 1179656 | tf_op jit(solution)/shard_map/ppermute | solution.py:570
  60.9 0.6 copy-start.5
  63.1 3.8 %copy-start.4 = (f32[8,128]{1,0:T(8,128)S(1)}, f32[8,128]{1,0:T(8,128)}, u32[]{:S(2)}) copy-start(f32[8,128]{1,0:T(8,128)} %get-tuple-element.22.refs_0_.after) | copy-start | bytes 12292
  63.1 29.5 %all-to-all-start.1 = ((bf16[16,352,128]{2,1,0:T(8,128)(2,1)}), bf16[16,352,128]{2,1,0:T(8,128)(2,1)S(1)}, u32[]{:S(2)}, u32[]{:S(2)}) async-start(bf16[16,352,128]{2,1,0:T(8,128)(2,1)} %get-tuple-element.20), calls=%async_computation.1 | async-start | bytes 2883584 | tf_op jit(solution)/shard_map/all_to_all | solution.py:61
  66.9 1.4 %copy-start.2 = (bf16[16,368,128]{2,1,0:T(8,128)(2,1)S(1)}, bf16[16,368,128]{2,1,0:T(8,128)(2,1)}, u32[]{:S(2)}) copy-start(bf16[16,368,128]{2,1,0:T(8,128)(2,1)} %copy-done.1) | copy-start | bytes 4521988
  70.8 18.1 %collective-permute-start.3 = (bf16[8,48,128]{2,1,0:T(8,128)(2,1)S(1)}, bf16[8,48,128]{2,1,0:T(8,128)(2,1)S(1)}, u32[]{:S(2)}, u32[]{:S(2)}) collective-permute-start(bf16[8,48,128]{2,1,0:T(8,128)(2,1)S(1)} %get-tuple-element.25), channel_id=1, source_target_pairs={{0,8},{8,0},{16,24},{24,16},{1,9},{9,1},{17,25},{25,17},{2,10},{10... | collective-permute-start | bytes 294920 | tf_op jit(solution)/shard_map/ppermute | solution.py:597
  72.7 16.2 %collective-permute-start.4 = (bf16[8,48,128]{2,1,0:T(8,128)(2,1)S(1)}, bf16[8,48,128]{2,1,0:T(8,128)(2,1)S(1)}, u32[]{:S(2)}, u32[]{:S(2)}) collective-permute-start(bf16[8,48,128]{2,1,0:T(8,128)(2,1)S(1)} %get-tuple-element.26), channel_id=1, source_target_pairs={{0,16},{8,24},{16,0},{24,8},{1,17},{9,25},{17,1},{25,9},{2,18},{10... | collective-permute-start | bytes 294920 | tf_op jit(solution)/shard_map/ppermute | solution.py:597
  74.2 17.2 %collective-permute-start.5 = (bf16[8,48,128]{2,1,0:T(8,128)(2,1)S(1)}, bf16[8,48,128]{2,1,0:T(8,128)(2,1)S(1)}, u32[]{:S(2)}, u32[]{:S(2)}) collective-permute-start(bf16[8,48,128]{2,1,0:T(8,128)(2,1)S(1)} %get-tuple-element.27), channel_id=1, source_target_pairs={{0,24},{8,16},{16,8},{24,0},{1,25},{9,17},{17,9},{25,1},{2,26},{10... | collective-permute-start | bytes 294920 | tf_op jit(solution)/shard_map/ppermute | solution.py:597

commit v6 on v5

--- a/solution.py
+++ b/solution.py
@@ -137,9 +137,10 @@
     def __init__(self, count, peers):
         self.left = count * TILE
         self.half = self.left + self.left // 2
-        self.dense = 2 * self.half
+        self.dense = self.half
         self.share = 1024 // peers
         self.ids = self.dense + self.share
+        self.back = 2 * self.half + self.share
         self.back_left = (self.share, self.share + self.left)
         self.back_right = (self.share + 2 * self.left, self.share + 2 * self.left + self.left // 2)
 
@@ -151,7 +152,7 @@
 def backward_kernel(
     n_grp, n_lane, wire,
     half_ref, x_ref, u_ref, now_ref, next_ref, fm_ref, proj_t_ref, lcb_ref, gain_ref,
-    out_ref,
+    out_ref, own_ref,
     fm_t, proj, lcb_t, gains, eye, mixed, p_t, g_t, d_sum, d_p_t, left_in, right_in, grads, turned, ids,
 ):
     count, width, features = x_ref.shape
@@ -220,17 +221,15 @@
         turned[group, 0] = rows[0:128]
         turned[group, 1] = rows[128:256]
     for group in range(count // STEP):
-        for which in range(2):
-            side = half if which else 1 - half
+        for side, ref in ((1 - half, out_ref), (half, own_ref)):
             for peer in range(peers):
                 at = place_of(n_grp, n_lane, peer)
                 line = turned[group, side, at : at + TILE]
                 left = jnp.concatenate([line[:, k * 128 : k * 128 + 128] for k in range(STEP)], axis=0)
-                row = which * wire.half + group * 32
-                out_ref[peer, row : row + 32] = left.astype(BF16)
+                ref[peer, group * 32 : group * 32 + 32] = left.astype(BF16)
                 right = jnp.concatenate([line[:, 512:640], line[:, 640:768]], axis=0)
-                row = which * wire.half + wire.left + group * 16
-                out_ref[peer, row : row + 16] = right.astype(BF16)
+                row = wire.left + group * 16
+                ref[peer, row : row + 16] = right.astype(BF16)
 
     part = features // peers
     third = width // peers
@@ -278,13 +277,13 @@
         return pl.BlockSpec(shape, lambda i: (0,) * len(shape))
 
     operands = (pooled_t, upstream_t, ids_now, ids_next, w_fm, w_proj_t, w_lcb, gain.reshape(1, width))
-    shape = (peers, wire.ids + 16, LANES)
+    shapes = [(peers, wire.ids + 16, LANES), (peers, wire.half, LANES)]
     return pl.pallas_call(
         functools.partial(backward_kernel, n_grp, n_lane, wire),
         grid=(1,),
         in_specs=[SMEM] + [whole(array.shape) for array in operands],
-        out_specs=whole(shape),
-        out_shape=jax.ShapeDtypeStruct(shape, BF16),
+        out_specs=[whole(shape) for shape in shapes],
+        out_shape=[jax.ShapeDtypeStruct(shape, BF16) for shape in shapes],
         scratch_shapes=[
             pltpu.VMEM((rank, features), BF16),
             pltpu.VMEM((rank, width), BF16),
@@ -309,31 +308,33 @@
 
 
 def part_kernel(n_grp, wire, other, half_ref, seen, *refs):
-    refs = refs if other else refs[1:]
-    out, held = refs[0], refs[-1]
+    held = refs[-1]
     peers = seen.shape[0]
-    half = 1 - half_ref[0] if other else half_ref[0]
-    base = 0 if other else wire.half
     if other:
-        dense = refs[1]
+        half = 1 - half_ref[0]
+        out, dense, all_ids = refs[:3]
         total = seen[0, wire.dense : wire.ids].astype(F32)
         for peer in range(1, peers):
             total = total + seen[peer, wire.dense : wire.ids].astype(F32)
         dense[...] = total
+        all_ids[...] = seen[:, wire.ids : wire.ids + 16].astype(F32)
+    else:
+        half = half_ref[0]
+        all_ids, out = refs[0], refs[2]
     lane = lax.broadcasted_iota(jnp.int32, (1, LANES), 1)
     start = ((lane % TILE) * LANES).astype(F32)
     keys = []
     for peer in range(peers):
         at = peer * LANES
-        held[at : at + wire.left, 0:128] = seen[peer, base : base + wire.left]
-        right = seen[peer, base + wire.left : base + wire.half]
+        held[at : at + wire.left, 0:128] = seen[peer, 0 : wire.left]
+        right = seen[peer, wire.left : wire.half]
         turned = turn(right.astype(F32)).astype(BF16)
         for i in range(wire.left // 32):
             held[at + 32 * i : at + 32 * i + 16, 128:256] = right[16 * i : 16 * i + 16]
             held[at + 32 * i + 16 : at + 32 * i + 32, 128:256] = turned[16 * i : 16 * i + 16]
         if wire.left < LANES:
             held[at + wire.left : at + LANES] = jnp.zeros((LANES - wire.left, 256), BF16)
-        ids = seen[peer, wire.ids : wire.ids + 16].astype(F32)
+        ids = all_ids[peer]
         key = jnp.where(half == 0, ids[0:1], ids[1:2]) + start
         keys.append(jnp.where(lane < wire.left, key, -1.0))
     keys = jnp.concatenate(keys, axis=1)
@@ -352,25 +353,26 @@
                 out[g, 2 * pair + f, piece : piece + piece // 2] = packed.astype(out.dtype)
 
 
-def part_sums(n_grp, wire, other, half, seen, *after):
+def part_sums(n_grp, wire, other, half, seen, *more):
     peers = seen.shape[0]
     piece = LANES // n_grp
     shapes = [jax.ShapeDtypeStruct((n_grp, TILE, piece + piece // 2, LANES), BF16 if other else F32)]
     if other:
         shapes.append(jax.ShapeDtypeStruct((wire.share, LANES), F32))
+        shapes.append(jax.ShapeDtypeStruct((peers, 16, LANES), F32))
     return pl.pallas_call(
         functools.partial(part_kernel, n_grp, wire, other),
-        in_specs=[SMEM, VMEM] + [pl.BlockSpec(memory_space=pl.ANY)] * len(after),
+        in_specs=[SMEM, VMEM] + [VMEM] * len(more),
         out_specs=[VMEM] * len(shapes),
         out_shape=shapes,
         scratch_shapes=[pltpu.VMEM((peers * LANES, 256), BF16)],
         compiler_params=params(),
         cost_estimate=cost(1),
         name="part_other" if other else "part_own",
-    )(half, seen, *after)
-
-
-def lookup_kernel(wire, half_ref, mine_t, crossed_t, ids_ref, out, held, hit):
+    )(half, seen, *more)
+
+
+def lookup_kernel(wire, half_ref, mine_t, crossed_t, ids_ref, out, held):
     peers = out.shape[0]
     half = half_ref[0]
     for f in range(TILE):
@@ -378,51 +380,38 @@
         for side, ref in ((half, mine_t), (1 - half, crossed_t)):
             held[side, 0:192, at : at + LANES] = ref[f]
             held[side, 192:256, at : at + LANES] = ref[f, 128:192]
-    ids = ids_ref[...].astype(F32).reshape(peers * 16, LANES)
+    ids = ids_ref[...].reshape(peers * 16, LANES)
     lane = lax.broadcasted_iota(jnp.int32, (1, LANES), 1)
     keys = (ids + ((lane % TILE) * LANES).astype(F32)).T
     column = lax.broadcasted_iota(jnp.int32, (1, TILE * LANES), 1).astype(F32)
     for which in range(2):
-        for peer in range(peers):
-            at = peer * 16 + 2 + which
-            mine = jnp.where(keys[0 : wire.left, at : at + 1] == column, 1.0, 0.0)
-            hit[which, peer * wire.left : (peer + 1) * wire.left] = mine.astype(BF16)
-    for which in range(2):
-        rows = mm_nt(hit[which], held[which])
-        for peer in range(peers):
-            got = rows[peer * wire.left : (peer + 1) * wire.left]
-            base = wire.back_left[which]
-            out[peer, base : base + wire.left] = got[:, 0:128].astype(BF16)
-            packed = []
-            for i in range(wire.left // 32):
-                first, second = got[32 * i : 32 * i + 16, 128:256], got[32 * i + 16 : 32 * i + 32, 128:256]
-                packed.append(jnp.where(low_lanes(first.shape), first, second))
-            base = wire.back_right[which]
-            out[peer, base : base + wire.left // 2] = jnp.concatenate(packed, axis=0).astype(BF16)
+        for pair in range(peers // 2):
+            mine = []
+            for peer in (2 * pair, 2 * pair + 1):
+                at = peer * 16 + 2 + which
+                mine.append(keys[0 : wire.left, at : at + 1])
+            hit = jnp.where(jnp.concatenate(mine, axis=0) == column, 1.0, 0.0).astype(BF16)
+            rows = mm_nt(hit, held[which])
+            for k in range(2):
+                got, peer = rows[k * wire.left : (k + 1) * wire.left], 2 * pair + k
+                base = wire.back_left[which]
+                out[peer, base : base + wire.left] = got[:, 0:128].astype(BF16)
+                packed = []
+                for i in range(wire.left // 32):
+                    first, second = got[32 * i : 32 * i + 16, 128:256], got[32 * i + 16 : 32 * i + 32, 128:256]
+                    packed.append(jnp.where(low_lanes(first.shape), first, second))
+                base = wire.back_right[which]
+                out[peer, base : base + wire.left // 2] = jnp.concatenate(packed, axis=0).astype(BF16)
 
 
 def lookup(wire, half, mine_t, crossed_t, ids):
-    peers = ids.shape[0]
-
-    def whole(shape):
-        return pl.BlockSpec(shape, lambda i: (0,) * len(shape))
-
-    at = wire.ids // 16
+    shape = (ids.shape[0], wire.back, LANES)
     return pl.pallas_call(
         functools.partial(lookup_kernel, wire),
-        grid=(1,),
-        in_specs=[
-            SMEM,
-            whole(mine_t.shape),
-            whole(crossed_t.shape),
-            pl.BlockSpec((peers, 16, LANES), lambda i: (0, at, 0)),
-        ],
-        out_specs=whole((peers, wire.ids, LANES)),
-        out_shape=jax.ShapeDtypeStruct((peers, wire.ids, LANES), BF16),
-        scratch_shapes=[
-            pltpu.VMEM((2, 256, TILE * LANES), BF16),
-            pltpu.VMEM((2, peers * wire.left, TILE * LANES), BF16),
-        ],
+        in_specs=[SMEM, VMEM, VMEM, VMEM],
+        out_specs=VMEM,
+        out_shape=jax.ShapeDtypeStruct(shape, BF16),
+        scratch_shapes=[pltpu.VMEM((2, 256, TILE * LANES), BF16)],
         compiler_params=params(2),
         cost_estimate=cost(100),
         name="lookup",
@@ -579,18 +568,19 @@
     grp = lax.axis_index("grp").astype(jnp.int32)
     mine_t = lax.dynamic_slice_in_dim(tables.transpose(0, 2, 1), grp * TILE, TILE, 0)
     crossed_t = cross(mine_t)
-    sent = backward(
+    sent, sent_own = backward(
         n_grp, n_lane, wire, half,
         pooled.transpose(0, 2, 1), upstream.transpose(0, 2, 1), ids_now, ids_next, w_fm, w_proj.T, w_lcb, gain,
     )
     seen = exchange(sent, PEER)
-    part, dense = part_sums(n_grp, wire, True, half, seen)
+    seen_own = exchange(sent_own, PEER)
+    part, dense, ids = part_sums(n_grp, wire, True, half, seen)
     dense_seen = cross(dense)
     part_seen = cross(part)
-    rows_wire = lookup(wire, half, mine_t, crossed_t, seen)
+    rows_wire = lookup(wire, half, mine_t, crossed_t, ids)
     rows_wire, token = fill(wire, factor, rows_wire, dense, dense_seen)
     rows = exchange(rows_wire, PEER)
-    (own,) = part_sums(n_grp, wire, False, half, seen, token)
+    (own,) = part_sums(n_grp, wire, False, half, seen_own, ids, token)
     next_rows, grad_fm, grad_proj_t, grad_lcb, grad_gain = unpack(n_grp, n_lane, wire, count, rows)
     pieces = combine(grp[None], own, part_seen, token)
     pieces = [pieces[0]] + [

time: 95.5 us -> 90 us (0.942)
  waiting for transfers between devices: 49.3 us -> 36.7 us
  starting transfers between devices: 19.3 us -> 23.4 us
  local copies, waits for them, and re-layouts: 2.79 us -> 4.85 us
    all_to_all x2 -> x3, waiting for transfers between devices: 26.2 us -> 20.5 us  [exchange(): return lax.all_to_all(blocks, axes, split_axis=0, concat_axis=0, tiled=True)]
    all_to_all x2 -> x3, starting transfers between devices: 10.1 us -> 14.4 us  [exchange(): return lax.all_to_all(blocks, axes, split_axis=0, concat_axis=0, tiled=True)]
    ppermute x3, waiting for transfers between devices: 6.06 us -> 2.31 us  [cross(): return lax.ppermute(array, 'half', [(0, 1), (1, 0)])]
    ppermute x3, waiting for transfers between devices: 17.1 us -> 13.9 us  [halves(): lax.ppermute(pieces[k], 'grp', [(g, g ^ k) for g in range(n_grp)])]
    unnamed x12 -> x16, local copies, waits for them, and re-layouts: 2.02 us -> 4.06 us
  transfers between devices with their start and end apart: 8 -> 9, of which waited for: 4 -> 5; matrix products, arithmetic and copies ran while one was open for 1% -> 1% of each run, Pallas kernels for 12% -> 13%
where the time goes in v6:
time: 90 us; the launch traced here: 89.4 us
  waiting for transfers between devices  36.7 us (41%)
  Pallas kernels  23.7 us (26%)
  starting transfers between devices  23.4 us (26%)
  local copies, waits for them, and re-layouts  4.85 us (5%)
    all_to_all x3, waiting for transfers between devices, exchange(): return lax.all_to_all(blocks, axes, split_axis=0, concat_axis=0, tiled=True)  20.5 us
    all_to_all x3, starting transfers between devices, exchange(): return lax.all_to_all(blocks, axes, split_axis=0, concat_axis=0, tiled=True)  14.4 us
    ppermute x3, waiting for transfers between devices, halves(): lax.ppermute(pieces[k], 'grp', [(g, g ^ k) for g in range(n_grp)])  13.9 us
    pallas_call x1, Pallas kernels, backward(): pl.pallas_call(functools.partial(backward_kernel, n_grp, n_lane, wire), g...  9.2 us
    ppermute x3, starting transfers between devices, cross(): return lax.ppermute(array, 'half', [(0, 1), (1, 0)])  5.51 us
    pallas_call x1, Pallas kernels, lookup(): pl.pallas_call(functools.partial(lookup_kernel, wire), in_specs=[SMEM, VM...  5.48 us
    unnamed x16, local copies, waits for them, and re-layouts  4.06 us
    ppermute x3, starting transfers between devices, halves(): lax.ppermute(pieces[k], 'grp', [(g, g ^ k) for g in range(n_grp)])  3.55 us
  transfers between devices with their start and end apart: 9, of which 5 were waited for; matrix products, arithmetic and copies ran while one was open for 1% of the time, Pallas kernels for 13%

profile of v6, /device:TPU:0, one launch (start us, length us, event | category | flops | bytes accessed | tf_op | source)
XLA Modules:
  0.0 89.4 jit_solution(1383013040620691369)
XLA Ops:
  0.7 9.2 %layer_backward.1 = (bf16[16,224,128]{2,1,0:T(8,128)(2,1)}, bf16[16,144,128]{2,1,0:T(8,128)(2,1)}) custom-call(s32[1]{0:T(128)} %bitcast.half_ref, bf16[12,192,256]{2,1,0:T(8,128)(2,1)} %bitcast.11, bf16[12,192,256]{2,1,0:T(8,128)(2,1)} %bitcast.12, s32[12,256]{1,0:T(8,128)} %now_ref.1, s32[12,256]{1,0:T(8,128)} %next_ref.1, bf16[256,128]{1,0:T(8,128)(2,1)} %fm_ref.1, ...), custom_call_target="tpu_custom_call" | custom-call | flops 1000000000 | bytes 100000 | tf_op jit(solution)/shard_map/layer_backward/pallas_call | solution.py:281
  9.9 6.3 %all-to-all-start = ((bf16[16,224,128]{2,1,0:T(8,128)(2,1)}), bf16[16,224,128]{2,1,0:T(8,128)(2,1)S(1)}, u32[]{:S(2)}, u32[]{:S(2)}) async-start(bf16[16,224,128]{2,1,0:T(8,128)(2,1)} %get-tuple-element.22), calls=%async_computation | async-start | bytes 1835008 | tf_op jit(solution)/shard_map/all_to_all | solution.py:61
  16.2 0.8 dynamic-slice_bitcast_fusion.mine_t
  17.0 2.6 %collective-permute-start = (bf16[8,192,128]{2,1,0:T(8,128)(2,1)}, bf16[8,192,128]{2,1,0:T(8,128)(2,1)}, u32[]{:S(2)}, u32[]{:S(2)}) collective-permute-start(bf16[8,192,128]{2,1,0:T(8,128)(2,1)} %dynamic-slice_bitcast_fusion.mine_t), channel_id=1, source_target_pairs={{0,4},{4,0},{1,5},{5,1},{2,6},{6,2},{3,7},{7,3},{8,12},{12,8},{9,1... | collective-permute-start | bytes 1179656 | tf_op jit(solution)/shard_map/ppermute | solution.py:559
  19.5 19.8 %all-to-all-done.seen = bf16[16,224,128]{2,1,0:T(8,128)(2,1)S(1)} async-done(((bf16[16,224,128]{2,1,0:T(8,128)(2,1)}), bf16[16,224,128]{2,1,0:T(8,128)(2,1)S(1)}, u32[]{:S(2)}, u32[]{:S(2)}) %all-to-all-start) | async-done | bytes 917536 | tf_op jit(solution)/shard_map/all_to_all | solution.py:61
  39.3 3.6 %all-to-all-start.2 = ((bf16[16,144,128]{2,1,0:T(8,128)(2,1)}), bf16[16,144,128]{2,1,0:T(8,128)(2,1)S(1)}, u32[]{:S(2)}, u32[]{:S(2)}) async-start(bf16[16,144,128]{2,1,0:T(8,128)(2,1)} %get-tuple-element.27), calls=%async_computation.2 | async-start | bytes 1179648 | tf_op jit(solution)/shard_map/all_to_all | solution.py:61
  42.9 1.4 %part_other.1 = (bf16[4,8,48,128]{3,2,1,0:T(8,128)(2,1)S(1)}, f32[64,128]{1,0:T(8,128)S(1)}, f32[16,16,128]{2,1,0:T(8,128)S(1)}) custom-call(s32[1]{0:T(128)} %bitcast.half_ref, bf16[16,224,128]{2,1,0:T(8,128)(2,1)S(1)} %all-to-all-done.seen), custom_call_target="tpu_custom_call" | custom-call | flops 1000000000 | bytes 100000 | tf_op jit(solution)/shard_map/part_other/pallas_call | solution.py:363
  45.0 2.9 %collective-permute-start.2 = (bf16[4,8,48,128]{3,2,1,0:T(8,128)(2,1)S(1)}, bf16[4,8,48,128]{3,2,1,0:T(8,128)(2,1)}, u32[]{:S(2)}, u32[]{:S(2)}) collective-permute-start(bf16[4,8,48,128]{3,2,1,0:T(8,128)(2,1)S(1)} %get-tuple-element.29), channel_id=1, source_target_pairs={{0,4},{4,0},{1,5},{5,1},{2,6},{6,2},{3,7},{7,3},{8,12},{12,8},{9,1... | collective-permute-start | bytes 1179656 | tf_op jit(solution)/shard_map/ppermute | solution.py:559
  47.9 5.5 %lookup.1.rows = bf16[16,352,128]{2,1,0:T(8,128)(2,1)} custom-call(s32[1]{0:T(128)} %bitcast.half_ref, bf16[8,192,128]{2,1,0:T(8,128)(2,1)} %dynamic-slice_bitcast_fusion.mine_t, bf16[8,192,128]{2,1,0:T(8,128)(2,1)} %collective-permute-done.crossed_t, f32[16,16,128]{2,1,0:T(8,128)} %copy-done.4), custom_call_target="tpu_custom_call" | custom-call | flops 99999997952 | bytes 100000 | tf_op jit(solution)/shard_map/lookup/pallas_call | solution.py:409
  54.0 1.5 %fill_dense.1 = (bf16[16,352,128]{2,1,0:T(8,128)(2,1)}, f32[8,128]{1,0:T(8,128)}) custom-call(bf16[16,352,128]{2,1,0:T(8,128)(2,1)} %lookup.1.rows, f32[64,128]{1,0:T(8,128)} %copy-done.3, f32[64,128]{1,0:T(8,128)} %copy-done.7), custom_call_target="tpu_custom_call", output_to_operand_aliasing={{0}: (0, {})} | custom-call | flops 1000000000 | bytes 100000 | tf_op jit(solution)/shard_map/fill_dense/pallas_call | solution.py:434
  55.6 0.7 all-to-all-done.2.seen
  56.3 0.8 copy-done.1
  57.1 4.5 %all-to-all-start.1 = ((bf16[16,352,128]{2,1,0:T(8,128)(2,1)}), bf16[16,352,128]{2,1,0:T(8,128)(2,1)S(1)}, u32[]{:S(2)}, u32[]{:S(2)}) async-start(bf16[16,352,128]{2,1,0:T(8,128)(2,1)} %get-tuple-element.25), calls=%async_computation.1 | async-start | bytes 2883584 | tf_op jit(solution)/shard_map/all_to_all | solution.py:61
  61.6 1.1 %copy-done.2 = bf16[16,144,128]{2,1,0:T(8,128)(2,1)S(1)} copy-done((bf16[16,144,128]{2,1,0:T(8,128)(2,1)S(1)}, bf16[16,144,128]{2,1,0:T(8,128)(2,1)}, u32[]{:S(2)}) %copy-start.2) | copy-done | bytes 589848
  62.7 0.9 %copy-done.5 = f32[16,16,128]{2,1,0:T(8,128)S(1)} copy-done((f32[16,16,128]{2,1,0:T(8,128)S(1)}, f32[16,16,128]{2,1,0:T(8,128)}, u32[]{:S(2)}) %copy-start.5) | copy-done | bytes 131096
  63.6 1.4 %part_own.1.own = f32[4,8,48,128]{3,2,1,0:T(8,128)S(1)} custom-call(s32[1]{0:T(128)} %bitcast.half_ref, bf16[16,144,128]{2,1,0:T(8,128)(2,1)S(1)} %copy-done.2, f32[16,16,128]{2,1,0:T(8,128)S(1)} %copy-done.5, f32[8,128]{1,0:T(8,128)S(1)} %copy-done.6), custom_call_target="tpu_custom_call" | custom-call | flops 1000000000 | bytes 100000 | tf_op jit(solution)/shard_map/part_own/pallas_call | solution.py:363
  65.0 2.3 %collective-permute-done.2.seen = bf16[4,8,48,128]{3,2,1,0:T(8,128)(2,1)} collective-permute-done((bf16[4,8,48,128]{3,2,1,0:T(8,128)(2,1)S(1)}, bf16[4,8,48,128]{3,2,1,0:T(8,128)(2,1)}, u32[]{:S(2)}, u32[]{:S(2)}) %collective-permute-start.2) | collective-permute-done | bytes 393248 | tf_op jit(solution)/shard_map/ppermute | solution.py:559
  67.3 1.1 %combine.1 = (bf16[8,48,128]{2,1,0:T(8,128)(2,1)S(1)}, bf16[8,48,128]{2,1,0:T(8,128)(2,1)S(1)}, bf16[8,48,128]{2,1,0:T(8,128)(2,1)S(1)}, bf16[8,48,128]{2,1,0:T(8,128)(2,1)S(1)}) custom-call(s32[1]{0:T(128)} %bitcast.7.place, f32[4,8,48,128]{3,2,1,0:T(8,128)S(1)} %part_own.1.own, bf16[4,8,48,128]{3,2,1,0:T(8,128)(2,1)} %collective-permute-done.2.seen, ...), custom_call_target="tpu_custom_call" | custom-call | flops 99999997952 | bytes 100000 | tf_op jit(solution)/shard_map/combine/pallas_call | solution.py:521
  68.4 1.8 %collective-permute-start.3 = (bf16[8,48,128]{2,1,0:T(8,128)(2,1)S(1)}, bf16[8,48,128]{2,1,0:T(8,128)(2,1)S(1)}, u32[]{:S(2)}, u32[]{:S(2)}) collective-permute-start(bf16[8,48,128]{2,1,0:T(8,128)(2,1)S(1)} %get-tuple-element.31), channel_id=1, source_target_pairs={{0,8},{8,0},{16,24},{24,16},{1,9},{9,1},{17,25},{25,17},{2,10},{10... | collective-permute-start | bytes 294920 | tf_op jit(solution)/shard_map/ppermute | solution.py:587
  70.1 1.5 %collective-permute-start.4 = (bf16[8,48,128]{2,1,0:T(8,128)(2,1)S(1)}, bf16[8,48,128]{2,1,0:T(8,128)(2,1)S(1)}, u32[]{:S(2)}, u32[]{:S(2)}) collective-permute-start(bf16[8,48,128]{2,1,0:T(8,128)(2,1)S(1)} %get-tuple-element.32), channel_id=1, source_target_pairs={{0,16},{8,24},{16,0},{24,8},{1,17},{9,25},{17,1},{25,9},{2,18},{10... | collective-permute-start | bytes 294920 | tf_op jit(solution)/shard_map/ppermute | solution.py:587
  71.9 9.2 %collective-permute-done.3.refs_1_ = bf16[8,48,128]{2,1,0:T(8,128)(2,1)S(1)} collective-permute-done((bf16[8,48,128]{2,1,0:T(8,128)(2,1)S(1)}, bf16[8,48,128]{2,1,0:T(8,128)(2,1)S(1)}, u32[]{:S(2)}, u32[]{:S(2)}) %collective-permute-start.3) | collective-permute-done | bytes 98336 | tf_op jit(solution)/shard_map/ppermute | solution.py:587
  81.1 4.6 %collective-permute-done.5.refs_3_ = bf16[8,48,128]{2,1,0:T(8,128)(2,1)S(1)} collective-permute-done((bf16[8,48,128]{2,1,0:T(8,128)(2,1)S(1)}, bf16[8,48,128]{2,1,0:T(8,128)(2,1)S(1)}, u32[]{:S(2)}, u32[]{:S(2)}) %collective-permute-start.5) | collective-permute-done | bytes 98336 | tf_op jit(solution)/shard_map/ppermute | solution.py:587
  85.8 1.1 %finish_tables.1 = f32[32,32,192]{2,1,0:T(8,128)} custom-call(s32[1]{0:T(128)} %bitcast.7.place, bf16[8,48,128]{2,1,0:T(8,128)(2,1)S(1)} %get-tuple-element.30.refs_0_, bf16[8,48,128]{2,1,0:T(8,128)(2,1)S(1)} %collective-permute-done.3.refs_1_, bf16[8,48,128]{2,1,0:T(8,128)(2,1)S(1)} %collective-permute-done.4.refs_2_, ...), custom_call_target="tpu_custom_call" | custom-call | bytes 100000 | tf_op jit(solution)/shard_map/finish_tables/pallas_call | solution.py:547
  86.9 2.5 %unpack_rows.1 = (bf16[12,192,256]{2,1,0:T(8,128)(2,1)}, f32[256,128]{1,0:T(8,128)}, f32[192,128]{1,0:T(8,128)}, f32[256,256]{1,0:T(8,128)}, f32[1,192]{1,0:T(1,128)}) custom-call(bf16[16,352,128]{2,1,0:T(8,128)(2,1)S(1)} %all-to-all-done.1.dense_ref.left0.left1.right0.right1, bf16[16,352,128]{2,1,0:T(8,128)(2,1)S(1)} %all-to-all-done.1.dense_ref.left0.left1.right0.right1, ...), custom_call_target="tpu_custom_call" | custom-call | flops 1000000000 | bytes 100000 | tf_op jit(solution)/shard_map/unpack_rows/pallas_call | solution.py:496
  (19 shorter events, 1.6 us)
Async XLA Ops:
  0.6 15.5 %copy-start = (bf16[32,128,192]{1,2,0:T(8,128)(2,1)S(1)}, bf16[32,128,192]{1,2,0:T(8,128)(2,1)}, u32[]{:S(2)}) copy-start(bf16[32,128,192]{1,2,0:T(8,128)(2,1)} %param.13) | copy-start | bytes 4718596
  9.9 29.5 %all-to-all-start = ((bf16[16,224,128]{2,1,0:T(8,128)(2,1)}), bf16[16,224,128]{2,1,0:T(8,128)(2,1)S(1)}, u32[]{:S(2)}, u32[]{:S(2)}) async-start(bf16[16,224,128]{2,1,0:T(8,128)(2,1)} %get-tuple-element.22), calls=%async_computation | async-start | bytes 1835008 | tf_op jit(solution)/shard_map/all_to_all | solution.py:61
  17.0 31.0 %collective-permute-start = (bf16[8,192,128]{2,1,0:T(8,128)(2,1)}, bf16[8,192,128]{2,1,0:T(8,128)(2,1)}, u32[]{:S(2)}, u32[]{:S(2)}) collective-permute-start(bf16[8,192,128]{2,1,0:T(8,128)(2,1)} %dynamic-slice_bitcast_fusion.mine_t), channel_id=1, source_target_pairs={{0,4},{4,0},{1,5},{5,1},{2,6},{6,2},{3,7},{7,3},{8,12},{12,8},{9,1... | collective-permute-start | bytes 1179656 | tf_op jit(solution)/shard_map/ppermute | solution.py:559
  39.3 16.9 %all-to-all-start.2 = ((bf16[16,144,128]{2,1,0:T(8,128)(2,1)}), bf16[16,144,128]{2,1,0:T(8,128)(2,1)S(1)}, u32[]{:S(2)}, u32[]{:S(2)}) async-start(bf16[16,144,128]{2,1,0:T(8,128)(2,1)} %get-tuple-element.27), calls=%async_computation.2 | async-start | bytes 1179648 | tf_op jit(solution)/shard_map/all_to_all | solution.py:61
  44.3 0.7 copy-start.4
  45.0 8.4 %copy-start.3 = (f32[64,128]{1,0:T(8,128)}, f32[64,128]{1,0:T(8,128)S(1)}, u32[]{:S(2)}) copy-start(f32[64,128]{1,0:T(8,128)S(1)} %get-tuple-element.24.own) | copy-start | bytes 98308
  45.0 8.4 %collective-permute-start.1 = (f32[64,128]{1,0:T(8,128)S(1)}, f32[64,128]{1,0:T(8,128)S(1)}, u32[]{:S(2)}, u32[]{:S(2)}) collective-permute-start(f32[64,128]{1,0:T(8,128)S(1)} %get-tuple-element.24.own), channel_id=1, source_target_pairs={{0,4},{4,0},{1,5},{5,1},{2,6},{6,2},{3,7},{7,3},{8,12},{12,8},{9,1... | collective-permute-start | bytes 98312 | tf_op jit(solution)/shard_map/ppermute | solution.py:559
  45.0 22.3 %collective-permute-start.2 = (bf16[4,8,48,128]{3,2,1,0:T(8,128)(2,1)S(1)}, bf16[4,8,48,128]{3,2,1,0:T(8,128)(2,1)}, u32[]{:S(2)}, u32[]{:S(2)}) collective-permute-start(bf16[4,8,48,128]{3,2,1,0:T(8,128)(2,1)S(1)} %get-tuple-element.29), channel_id=1, source_target_pairs={{0,4},{4,0},{1,5},{5,1},{2,6},{6,2},{3,7},{7,3},{8,12},{12,8},{9,1... | collective-permute-start | bytes 1179656 | tf_op jit(solution)/shard_map/ppermute | solution.py:559
  53.4 0.6 copy-start.7
  56.3 0.8 copy-start.1
  57.1 4.5 %copy-start.6 = (f32[8,128]{1,0:T(8,128)S(1)}, f32[8,128]{1,0:T(8,128)}, u32[]{:S(2)}) copy-start(f32[8,128]{1,0:T(8,128)} %get-tuple-element.28.refs_1_.after) | copy-start | bytes 12292
  57.1 29.8 %all-to-all-start.1 = ((bf16[16,352,128]{2,1,0:T(8,128)(2,1)}), bf16[16,352,128]{2,1,0:T(8,128)(2,1)S(1)}, u32[]{:S(2)}, u32[]{:S(2)}) async-start(bf16[16,352,128]{2,1,0:T(8,128)(2,1)} %get-tuple-element.25), calls=%async_computation.1 | async-start | bytes 2883584 | tf_op jit(solution)/shard_map/all_to_all | solution.py:61
  61.6 1.1 %copy-start.2 = (bf16[16,144,128]{2,1,0:T(8,128)(2,1)S(1)}, bf16[16,144,128]{2,1,0:T(8,128)(2,1)}, u32[]{:S(2)}) copy-start(bf16[16,144,128]{2,1,0:T(8,128)(2,1)} %copy-done.1) | copy-start | bytes 1769476
  62.7 0.9 %copy-start.5 = (f32[16,16,128]{2,1,0:T(8,128)S(1)}, f32[16,16,128]{2,1,0:T(8,128)}, u32[]{:S(2)}) copy-start(f32[16,16,128]{2,1,0:T(8,128)} %copy-done.4) | copy-start | bytes 393220
  68.4 12.8 %collective-permute-start.3 = (bf16[8,48,128]{2,1,0:T(8,128)(2,1)S(1)}, bf16[8,48,128]{2,1,0:T(8,128)(2,1)S(1)}, u32[]{:S(2)}, u32[]{:S(2)}) collective-permute-start(bf16[8,48,128]{2,1,0:T(8,128)(2,1)S(1)} %get-tuple-element.31), channel_id=1, source_target_pairs={{0,8},{8,0},{16,24},{24,16},{1,9},{9,1},{17,25},{25,17},{2,10},{10... | collective-permute-start | bytes 294920 | tf_op jit(solution)/shard_map/ppermute | solution.py:587
  70.1 11.0 %collective-permute-start.4 = (bf16[8,48,128]{2,1,0:T(8,128)(2,1)S(1)}, bf16[8,48,128]{2,1,0:T(8,128)(2,1)S(1)}, u32[]{:S(2)}, u32[]{:S(2)}) collective-permute-start(bf16[8,48,128]{2,1,0:T(8,128)(2,1)S(1)} %get-tuple-element.32), channel_id=1, source_target_pairs={{0,16},{8,24},{16,0},{24,8},{1,17},{9,25},{17,1},{25,9},{2,18},{10... | collective-permute-start | bytes 294920 | tf_op jit(solution)/shard_map/ppermute | solution.py:587
  71.6 14.1 %collective-permute-start.5 = (bf16[8,48,128]{2,1,0:T(8,128)(2,1)S(1)}, bf16[8,48,128]{2,1,0:T(8,128)(2,1)S(1)}, u32[]{:S(2)}, u32[]{:S(2)}) collective-permute-start(bf16[8,48,128]{2,1,0:T(8,128)(2,1)S(1)} %get-tuple-element.33), channel_id=1, source_target_pairs={{0,24},{8,16},{16,8},{24,0},{1,25},{9,17},{17,9},{25,1},{2,26},{10... | collective-permute-start | bytes 294920 | tf_op jit(solution)/shard_map/ppermute | solution.py:587

commit v7 on v6

--- a/solution.py
+++ b/solution.py
@@ -283,7 +283,7 @@
         grid=(1,),
         in_specs=[SMEM] + [whole(array.shape) for array in operands],
         out_specs=[whole(shape) for shape in shapes],
-        out_shape=[jax.ShapeDtypeStruct(shape, BF16) for shape in shapes],
+        out_shape=[pltpu.HBM(shape, BF16) for shape in shapes],
         scratch_shapes=[
             pltpu.VMEM((rank, features), BF16),
             pltpu.VMEM((rank, width), BF16),
@@ -366,20 +366,35 @@
         out_specs=[VMEM] * len(shapes),
         out_shape=shapes,
         scratch_shapes=[pltpu.VMEM((peers * LANES, 256), BF16)],
-        compiler_params=params(),
+        compiler_params=params(1 if other else 2),
         cost_estimate=cost(1),
         name="part_other" if other else "part_own",
     )(half, seen, *more)
 
 
-def lookup_kernel(wire, half_ref, mine_t, crossed_t, ids_ref, out, held):
-    peers = out.shape[0]
+def stack_kernel(half_ref, mine_t, crossed_t, out):
     half = half_ref[0]
     for f in range(TILE):
         at = f * LANES
         for side, ref in ((half, mine_t), (1 - half, crossed_t)):
-            held[side, 0:192, at : at + LANES] = ref[f]
-            held[side, 192:256, at : at + LANES] = ref[f, 128:192]
+            out[side, 0:192, at : at + LANES] = ref[f]
+            out[side, 192:256, at : at + LANES] = ref[f, 128:192]
+
+
+def stack_tables(half, mine_t, crossed_t):
+    return pl.pallas_call(
+        stack_kernel,
+        in_specs=[SMEM, VMEM, VMEM],
+        out_specs=VMEM,
+        out_shape=jax.ShapeDtypeStruct((2, 256, TILE * LANES), BF16),
+        compiler_params=params(),
+        cost_estimate=cost(100),
+        name="stack_tables",
+    )(half, mine_t, crossed_t)
+
+
+def lookup_kernel(wire, stacked, ids_ref, out):
+    peers = out.shape[0]
     ids = ids_ref[...].reshape(peers * 16, LANES)
     lane = lax.broadcasted_iota(jnp.int32, (1, LANES), 1)
     keys = (ids + ((lane % TILE) * LANES).astype(F32)).T
@@ -391,7 +406,7 @@
                 at = peer * 16 + 2 + which
                 mine.append(keys[0 : wire.left, at : at + 1])
             hit = jnp.where(jnp.concatenate(mine, axis=0) == column, 1.0, 0.0).astype(BF16)
-            rows = mm_nt(hit, held[which])
+            rows = mm_nt(hit, stacked[which])
             for k in range(2):
                 got, peer = rows[k * wire.left : (k + 1) * wire.left], 2 * pair + k
                 base = wire.back_left[which]
@@ -404,18 +419,22 @@
                 out[peer, base : base + wire.left // 2] = jnp.concatenate(packed, axis=0).astype(BF16)
 
 
-def lookup(wire, half, mine_t, crossed_t, ids):
-    shape = (ids.shape[0], wire.back, LANES)
+def lookup(wire, stacked, ids):
+    peers = ids.shape[0]
+    some = peers // 4
     return pl.pallas_call(
         functools.partial(lookup_kernel, wire),
-        in_specs=[SMEM, VMEM, VMEM, VMEM],
-        out_specs=VMEM,
-        out_shape=jax.ShapeDtypeStruct(shape, BF16),
-        scratch_shapes=[pltpu.VMEM((2, 256, TILE * LANES), BF16)],
-        compiler_params=params(2),
+        grid=(4,),
+        in_specs=[
+            pl.BlockSpec(stacked.shape, lambda i: (0, 0, 0)),
+            pl.BlockSpec((some, 16, LANES), lambda i: (i, 0, 0)),
+        ],
+        out_specs=pl.BlockSpec((some, wire.back, LANES), lambda i: (i, 0, 0)),
+        out_shape=pltpu.HBM((peers, wire.back, LANES), BF16),
+        compiler_params=params(),
         cost_estimate=cost(100),
         name="lookup",
-    )(half, mine_t, crossed_t, ids)
+    )(stacked, ids)
 
 
 def fill_kernel(factor, rows, own, seen, out, token):
@@ -436,16 +455,17 @@
         grid=(1,),
         in_specs=[pl.BlockSpec(memory_space=pl.ANY), whole(own.shape), whole(seen.shape)],
         out_specs=[whole((peers, wire.share, LANES)), whole((8, LANES))],
-        out_shape=[jax.ShapeDtypeStruct(rows.shape, BF16), jax.ShapeDtypeStruct((8, LANES), F32)],
+        out_shape=[pltpu.HBM(rows.shape, BF16), jax.ShapeDtypeStruct((8, LANES), F32)],
         input_output_aliases={0: 0},
-        compiler_params=params(2),
+        compiler_params=params(),
         cost_estimate=cost(1),
         name="fill_dense",
     )(rows, own, seen)
 
 
-def unpack_kernel(n_grp, n_lane, dense_ref, left0, left1, right0, right1, rows_out, fm, proj_t, lcb, gain, held):
+def unpack_kernel(n_grp, n_lane, dense_ref, left0, left1, right0, right1, rows_out, fm, proj_t, lcb, gain, token, held):
     step = pl.program_id(0)
+    token[...] = jnp.zeros_like(token)
     peers = n_grp * n_lane
     for side, (left_ref, right_ref) in enumerate(((left0, right0), (left1, right1))):
         for q in range(n_lane):
@@ -492,7 +512,7 @@
         return pl.BlockSpec((peers, rows, LANES), lambda i: (0, start // rows + i, 0))
 
     peers = n_grp * n_lane
-    shapes = [(256, 128), (192, 128), (256, 256), (1, 192)]
+    shapes = [(256, 128), (192, 128), (256, 256), (1, 192), (8, 128)]
     return pl.pallas_call(
         functools.partial(unpack_kernel, n_grp, n_lane),
         grid=(count // STEP,),
@@ -532,7 +552,7 @@
 def finish_kernel(place, *refs):
     out = refs[-1]
     piece = out.shape[1]
-    for k, seen in enumerate(refs[:-1]):
+    for k, seen in enumerate(refs[:-2]):
         base = jnp.bitwise_xor(place[0], k) * TILE
         for f in range(TILE):
             out[base + f, :, 0:128] = seen[f, 0:piece].astype(F32)
@@ -541,18 +561,18 @@
             out[base + f, piece // 2 : piece, 128:192] = turn(packed)[:, 0:64]
 
 
-def finish(place, pieces):
+def finish(place, pieces, after):
     n_grp = len(pieces)
     piece = pieces[0].shape[1] * 2 // 3
     return pl.pallas_call(
         finish_kernel,
-        in_specs=[SMEM] + [VMEM] * n_grp,
+        in_specs=[SMEM] + [VMEM] * n_grp + [pl.BlockSpec(memory_space=pl.ANY)],
         out_specs=VMEM,
         out_shape=jax.ShapeDtypeStruct((n_grp * TILE, piece, 192), F32),
         compiler_params=params(),
         cost_estimate=cost(0),
         name="finish_tables",
-    )(place, *pieces)
+    )(place, *pieces, after)
 
 
 def cross(array):
@@ -577,16 +597,16 @@
     part, dense, ids = part_sums(n_grp, wire, True, half, seen)
     dense_seen = cross(dense)
     part_seen = cross(part)
-    rows_wire = lookup(wire, half, mine_t, crossed_t, ids)
+    rows_wire = lookup(wire, stack_tables(half, mine_t, crossed_t), ids)
     rows_wire, token = fill(wire, factor, rows_wire, dense, dense_seen)
     rows = exchange(rows_wire, PEER)
     (own,) = part_sums(n_grp, wire, False, half, seen_own, ids, token)
-    next_rows, grad_fm, grad_proj_t, grad_lcb, grad_gain = unpack(n_grp, n_lane, wire, count, rows)
+    next_rows, grad_fm, grad_proj_t, grad_lcb, grad_gain, token_out = unpack(n_grp, n_lane, wire, count, rows)
     pieces = combine(grp[None], own, part_seen, token)
     pieces = [pieces[0]] + [
         lax.ppermute(pieces[k], "grp", [(g, g ^ k) for g in range(n_grp)]) for k in range(1, n_grp)
     ]
-    table_grad = finish(grp[None], pieces)
+    table_grad = finish(grp[None], pieces, token_out)
     return next_rows.transpose(0, 2, 1), table_grad, grad_fm, grad_proj_t.T, grad_lcb, grad_gain.reshape(-1)
 
 

time: 90 us -> 87 us (0.967)
  waiting for transfers between devices: 36.7 us -> 33.3 us
  Pallas kernels: 23.7 us -> 24.9 us
    ppermute x3, waiting for transfers between devices: 13.9 us -> 0.01 us  [halves(): lax.ppermute(pieces[k], 'grp', [(g, g ^ k) for g in range(n_grp)])]
    all_to_all x3, waiting for transfers between devices: 20.5 us -> 28.1 us  [exchange(): return lax.all_to_all(blocks, axes, split_axis=0, concat_axis=0, tiled=True)]
    ppermute x3, waiting for transfers between devices: 2.31 us -> 5.18 us  [cross(): return lax.ppermute(array, 'half', [(0, 1), (1, 0)])]
    pallas_call x2, Pallas kernels: 2.78 us -> 4.81 us  [part_sums(): pl.pallas_call(functools.partial(part_kernel, n_grp, wire, other), in_spe...]
    ppermute x3, starting transfers between devices: 5.51 us -> 7.09 us  [cross(): return lax.ppermute(array, 'half', [(0, 1), (1, 0)])]
    all_to_all x3, starting transfers between devices: 14.4 us -> 12.8 us  [exchange(): return lax.all_to_all(blocks, axes, split_axis=0, concat_axis=0, tiled=True)]
    pallas_call x2 -> x3, Pallas kernels: 6.58 us -> 6 us  [the longest x1 4.62 us: lookup(): pl.pallas_call(functools.partial(lookup_kernel, wire), grid=(4,), in_spec...]
    unnamed x16 -> x14, local copies, waits for them, and re-layouts: 4.06 us -> 4.11 us
  transfers between devices with their start and end apart: 9 -> 9, of which waited for: 5 -> 5; matrix products, arithmetic and copies ran while one was open for 1% -> 0% of each run, Pallas kernels for 13% -> 28%
where the time goes in v7:
time: 87 us; the launch traced here: 86.4 us
  waiting for transfers between devices  33.3 us (38%)
  Pallas kernels  24.9 us (29%)
  starting transfers between devices  23.4 us (27%)
  local copies, waits for them, and re-layouts  4.14 us (5%)
    all_to_all x3, waiting for transfers between devices, exchange(): return lax.all_to_all(blocks, axes, split_axis=0, concat_axis=0, tiled=True)  28.1 us
    all_to_all x3, starting transfers between devices, exchange(): return lax.all_to_all(blocks, axes, split_axis=0, concat_axis=0, tiled=True)  12.8 us
    pallas_call x1, Pallas kernels, backward(): pl.pallas_call(functools.partial(backward_kernel, n_grp, n_lane, wire), g...  9.07 us
    ppermute x3, starting transfers between devices, cross(): return lax.ppermute(array, 'half', [(0, 1), (1, 0)])  7.09 us
    ppermute x3, waiting for transfers between devices, cross(): return lax.ppermute(array, 'half', [(0, 1), (1, 0)])  5.18 us
    pallas_call x2, Pallas kernels, part_sums(): pl.pallas_call(functools.partial(part_kernel, n_grp, wire, other), in_spe...  4.81 us
    pallas_call x1, Pallas kernels, lookup(): pl.pallas_call(functools.partial(lookup_kernel, wire), grid=(4,), in_spec...  4.62 us
    unnamed x14, local copies, waits for them, and re-layouts  4.11 us
  transfers between devices with their start and end apart: 9, of which 5 were waited for; matrix products, arithmetic and copies ran while one was open for 0% of the time, Pallas kernels for 28%

profile of v7, /device:TPU:0, one launch (start us, length us, event | category | flops | bytes accessed | tf_op | source)
XLA Modules:
  0.0 86.4 jit_solution(12279866213572699808)
XLA Ops:
  0.7 1.4 %copy-done = bf16[32,128,192]{1,2,0:T(8,128)(2,1)S(1)} copy-done((bf16[32,128,192]{1,2,0:T(8,128)(2,1)S(1)}, bf16[32,128,192]{1,2,0:T(8,128)(2,1)}, u32[]{:S(2)}) %copy-start) | copy-done | bytes 1572888
  2.1 4.1 %collective-permute-start = (bf16[8,192,128]{2,1,0:T(8,128)(2,1)S(1)}, bf16[8,192,128]{2,1,0:T(8,128)(2,1)S(1)}, u32[]{:S(2)}, u32[]{:S(2)}) collective-permute-start(bf16[8,192,128]{2,1,0:T(8,128)(2,1)S(1)} %dynamic-slice_bitcast_fusion.mine_t), channel_id=1, source_target_pairs={{0,4},{4,0},{1,5},{5,1},{2,6},{6,2},{3,7},{7,3},{8,12},{12,8},{9,1... | collective-permute-start | bytes 1179656 | tf_op jit(solution)/shard_map/ppermute | solution.py:579
  6.2 9.1 %layer_backward.1 = (bf16[16,224,128]{2,1,0:T(8,128)(2,1)}, bf16[16,144,128]{2,1,0:T(8,128)(2,1)}) custom-call(s32[1]{0:T(128)} %bitcast.half_ref, bf16[12,192,256]{2,1,0:T(8,128)(2,1)} %bitcast.11, bf16[12,192,256]{2,1,0:T(8,128)(2,1)} %bitcast.12, s32[12,256]{1,0:T(8,128)} %now_ref.1, s32[12,256]{1,0:T(8,128)} %next_ref.1, bf16[256,128]{1,0:T(8,128)(2,1)} %fm_ref.1, ...), custom_call_target="tpu_custom_call" | custom-call | flops 1000000000 | bytes 100000 | tf_op jit(solution)/shard_map/layer_backward/pallas_call | solution.py:281
  15.2 4.8 %all-to-all-start = ((bf16[16,224,128]{2,1,0:T(8,128)(2,1)}), bf16[16,224,128]{2,1,0:T(8,128)(2,1)S(1)}, u32[]{:S(2)}, u32[]{:S(2)}) async-start(bf16[16,224,128]{2,1,0:T(8,128)(2,1)} %get-tuple-element.23), calls=%async_computation | async-start | bytes 1835008 | tf_op jit(solution)/shard_map/all_to_all | solution.py:61
  20.1 3.7 %collective-permute-done.crossed_t = bf16[8,192,128]{2,1,0:T(8,128)(2,1)S(1)} collective-permute-done((bf16[8,192,128]{2,1,0:T(8,128)(2,1)S(1)}, bf16[8,192,128]{2,1,0:T(8,128)(2,1)S(1)}, u32[]{:S(2)}, u32[]{:S(2)}) %collective-permute-start) | collective-permute-done | bytes 393248 | tf_op jit(solution)/shard_map/ppermute | solution.py:579
  24.1 1.0 %copy-done.5 = bf16[2,256,1024]{2,1,0:T(8,128)(2,1)} copy-done((bf16[2,256,1024]{2,1,0:T(8,128)(2,1)}, bf16[2,256,1024]{2,1,0:T(8,128)(2,1)S(1)}, u32[]{:S(2)}) %copy-start.5) | copy-done | bytes 1048600
  25.0 10.6 %all-to-all-done.seen = bf16[16,224,128]{2,1,0:T(8,128)(2,1)S(1)} async-done(((bf16[16,224,128]{2,1,0:T(8,128)(2,1)}), bf16[16,224,128]{2,1,0:T(8,128)(2,1)S(1)}, u32[]{:S(2)}, u32[]{:S(2)}) %all-to-all-start) | async-done | bytes 917536 | tf_op jit(solution)/shard_map/all_to_all | solution.py:61
  35.6 4.3 %all-to-all-start.2 = ((bf16[16,144,128]{2,1,0:T(8,128)(2,1)}), bf16[16,144,128]{2,1,0:T(8,128)(2,1)}, u32[]{:S(2)}, u32[]{:S(2)}) async-start(bf16[16,144,128]{2,1,0:T(8,128)(2,1)} %get-tuple-element.28), calls=%async_computation.2 | async-start | bytes 1179648 | tf_op jit(solution)/shard_map/all_to_all | solution.py:61
  39.9 1.4 %part_other.1 = (bf16[4,8,48,128]{3,2,1,0:T(8,128)(2,1)S(1)}, f32[64,128]{1,0:T(8,128)S(1)}, f32[16,16,128]{2,1,0:T(8,128)S(1)}) custom-call(s32[1]{0:T(128)} %bitcast.half_ref, bf16[16,224,128]{2,1,0:T(8,128)(2,1)S(1)} %all-to-all-done.seen), custom_call_target="tpu_custom_call" | custom-call | flops 1000000000 | bytes 100000 | tf_op jit(solution)/shard_map/part_other/pallas_call | solution.py:363
  41.3 1.2 %collective-permute-start.1 = (f32[64,128]{1,0:T(8,128)S(1)}, f32[64,128]{1,0:T(8,128)S(1)}, u32[]{:S(2)}, u32[]{:S(2)}) collective-permute-start(f32[64,128]{1,0:T(8,128)S(1)} %get-tuple-element.25.own), channel_id=1, source_target_pairs={{0,4},{4,0},{1,5},{5,1},{2,6},{6,2},{3,7},{7,3},{8,12},{12,8},{9,1... | collective-permute-start | bytes 98312 | tf_op jit(solution)/shard_map/ppermute | solution.py:579
  42.6 1.8 %collective-permute-start.2 = (bf16[4,8,48,128]{3,2,1,0:T(8,128)(2,1)S(1)}, bf16[4,8,48,128]{3,2,1,0:T(8,128)(2,1)}, u32[]{:S(2)}, u32[]{:S(2)}) collective-permute-start(bf16[4,8,48,128]{3,2,1,0:T(8,128)(2,1)S(1)} %get-tuple-element.30), channel_id=1, source_target_pairs={{0,4},{4,0},{1,5},{5,1},{2,6},{6,2},{3,7},{7,3},{8,12},{12,8},{9,1... | collective-permute-start | bytes 1179656 | tf_op jit(solution)/shard_map/ppermute | solution.py:579
  44.3 4.6 %lookup.1.rows = bf16[16,352,128]{2,1,0:T(8,128)(2,1)} custom-call(bf16[2,256,1024]{2,1,0:T(8,128)(2,1)S(1)} %copy-done.6, f32[16,16,128]{2,1,0:T(8,128)S(1)} %get-tuple-element.24.ids_ref.refs_0_), custom_call_target="tpu_custom_call" | custom-call | flops 99999997952 | bytes 100000 | tf_op jit(solution)/shard_map/lookup/pallas_call | solution.py:425
  48.9 0.8 fill_dense.1
  50.3 5.0 %all-to-all-done.2.seen = bf16[16,144,128]{2,1,0:T(8,128)(2,1)} async-done(((bf16[16,144,128]{2,1,0:T(8,128)(2,1)}), bf16[16,144,128]{2,1,0:T(8,128)(2,1)}, u32[]{:S(2)}, u32[]{:S(2)}) %all-to-all-start.2) | async-done | bytes 589856 | tf_op jit(solution)/shard_map/all_to_all | solution.py:61
  55.3 3.7 %all-to-all-start.1 = ((bf16[16,352,128]{2,1,0:T(8,128)(2,1)}), bf16[16,352,128]{2,1,0:T(8,128)(2,1)S(1)}, u32[]{:S(2)}, u32[]{:S(2)}) async-start(bf16[16,352,128]{2,1,0:T(8,128)(2,1)} %get-tuple-element.26), calls=%async_computation.1 | async-start | bytes 2883584 | tf_op jit(solution)/shard_map/all_to_all | solution.py:61
  59.0 3.4 %part_own.1.own = f32[4,8,48,128]{3,2,1,0:T(8,128)} custom-call(s32[1]{0:T(128)} %bitcast.half_ref, bf16[16,144,128]{2,1,0:T(8,128)(2,1)} %all-to-all-done.2.seen, f32[16,16,128]{2,1,0:T(8,128)} %copy-done.2, f32[8,128]{1,0:T(8,128)} %copy-done.3), custom_call_target="tpu_custom_call" | custom-call | flops 1000000000 | bytes 100000 | tf_op jit(solution)/shard_map/part_own/pallas_call | solution.py:363
  62.4 1.5 %collective-permute-done.2.seen = bf16[4,8,48,128]{3,2,1,0:T(8,128)(2,1)} collective-permute-done((bf16[4,8,48,128]{3,2,1,0:T(8,128)(2,1)S(1)}, bf16[4,8,48,128]{3,2,1,0:T(8,128)(2,1)}, u32[]{:S(2)}, u32[]{:S(2)}) %collective-permute-start.2) | collective-permute-done | bytes 393248 | tf_op jit(solution)/shard_map/ppermute | solution.py:579
  64.0 1.1 %copy-done.1 = f32[4,8,48,128]{3,2,1,0:T(8,128)S(1)} copy-done((f32[4,8,48,128]{3,2,1,0:T(8,128)S(1)}, f32[4,8,48,128]{3,2,1,0:T(8,128)}, u32[]{:S(2)}) %copy-start.1) | copy-done | bytes 786456
  65.1 1.7 %combine.1 = (bf16[8,48,128]{2,1,0:T(8,128)(2,1)S(1)}, bf16[8,48,128]{2,1,0:T(8,128)(2,1)}, bf16[8,48,128]{2,1,0:T(8,128)(2,1)}, bf16[8,48,128]{2,1,0:T(8,128)(2,1)S(1)}) custom-call(s32[1]{0:T(128)} %bitcast.7.place, f32[4,8,48,128]{3,2,1,0:T(8,128)S(1)} %copy-done.1, bf16[4,8,48,128]{3,2,1,0:T(8,128)(2,1)} %collective-permute-done.2.seen, ...), custom_call_target="tpu_custom_call" | custom-call | flops 99999997952 | bytes 100000 | tf_op jit(solution)/shard_map/combine/pallas_call | solution.py:541
  66.8 1.8 %collective-permute-start.3 = (bf16[8,48,128]{2,1,0:T(8,128)(2,1)}, bf16[8,48,128]{2,1,0:T(8,128)(2,1)S(1)}, u32[]{:S(2)}, u32[]{:S(2)}) collective-permute-start(bf16[8,48,128]{2,1,0:T(8,128)(2,1)} %get-tuple-element.32), channel_id=1, source_target_pairs={{0,8},{8,0},{16,24},{24,16},{1,9},{9,1},{17,25},{25,17},{2,10},{10... | collective-permute-start | bytes 294920 | tf_op jit(solution)/shard_map/ppermute | solution.py:607
  68.6 1.5 %collective-permute-start.4 = (bf16[8,48,128]{2,1,0:T(8,128)(2,1)}, bf16[8,48,128]{2,1,0:T(8,128)(2,1)S(1)}, u32[]{:S(2)}, u32[]{:S(2)}) collective-permute-start(bf16[8,48,128]{2,1,0:T(8,128)(2,1)} %get-tuple-element.33), channel_id=1, source_target_pairs={{0,16},{8,24},{16,0},{24,8},{1,17},{9,25},{17,1},{25,9},{2,18},{10... | collective-permute-start | bytes 294920 | tf_op jit(solution)/shard_map/ppermute | solution.py:607
  70.3 12.5 %all-to-all-done.1.dense_ref.left0.left1.right0.right1 = bf16[16,352,128]{2,1,0:T(8,128)(2,1)S(1)} async-done(((bf16[16,352,128]{2,1,0:T(8,128)(2,1)}), bf16[16,352,128]{2,1,0:T(8,128)(2,1)S(1)}, u32[]{:S(2)}, u32[]{:S(2)}) %all-to-all-start.1) | async-done | bytes 1441824 | tf_op jit(solution)/shard_map/all_to_all | solution.py:61
  82.8 2.6 %unpack_rows.1 = (bf16[12,192,256]{2,1,0:T(8,128)(2,1)}, f32[256,128]{1,0:T(8,128)}, f32[192,128]{1,0:T(8,128)}, f32[256,256]{1,0:T(8,128)}, f32[1,192]{1,0:T(1,128)}, /*index=5*/f32[8,128]{1,0:T(8,128)S(1)}) custom-call(bf16[16,352,128]{2,1,0:T(8,128)(2,1)S(1)} %all-to-all-done.1.dense_ref.left0.left1.right0.right1, ...), custom_call_target="tpu_custom_call" | custom-call | flops 1000000000 | bytes 100000 | tf_op jit(solution)/shard_map/unpack_rows/pallas_call | solution.py:516
  85.3 1.1 %finish_tables.1 = f32[32,32,192]{2,1,0:T(8,128)} custom-call(s32[1]{0:T(128)} %bitcast.7.place, bf16[8,48,128]{2,1,0:T(8,128)(2,1)S(1)} %get-tuple-element.31.refs_0_, bf16[8,48,128]{2,1,0:T(8,128)(2,1)S(1)} %collective-permute-done.3.refs_1_, bf16[8,48,128]{2,1,0:T(8,128)(2,1)S(1)} %collective-permute-done.4.refs_2_, ...), custom_call_target="tpu_custom_call" | custom-call | bytes 100000 | tf_op jit(solution)/shard_map/finish_tables/pallas_call | solution.py:567
  (18 shorter events, 1.1 us)
Async XLA Ops:
  0.6 1.4 %copy-start = (bf16[32,128,192]{1,2,0:T(8,128)(2,1)S(1)}, bf16[32,128,192]{1,2,0:T(8,128)(2,1)}, u32[]{:S(2)}) copy-start(bf16[32,128,192]{1,2,0:T(8,128)(2,1)} %param.13) | copy-start | bytes 4718596
  2.1 21.7 %collective-permute-start = (bf16[8,192,128]{2,1,0:T(8,128)(2,1)S(1)}, bf16[8,192,128]{2,1,0:T(8,128)(2,1)S(1)}, u32[]{:S(2)}, u32[]{:S(2)}) collective-permute-start(bf16[8,192,128]{2,1,0:T(8,128)(2,1)S(1)} %dynamic-slice_bitcast_fusion.mine_t), channel_id=1, source_target_pairs={{0,4},{4,0},{1,5},{5,1},{2,6},{6,2},{3,7},{7,3},{8,12},{12,8},{9,1... | collective-permute-start | bytes 1179656 | tf_op jit(solution)/shard_map/ppermute | solution.py:579
  15.2 20.4 %all-to-all-start = ((bf16[16,224,128]{2,1,0:T(8,128)(2,1)}), bf16[16,224,128]{2,1,0:T(8,128)(2,1)S(1)}, u32[]{:S(2)}, u32[]{:S(2)}) async-start(bf16[16,224,128]{2,1,0:T(8,128)(2,1)} %get-tuple-element.23), calls=%async_computation | async-start | bytes 1835008 | tf_op jit(solution)/shard_map/all_to_all | solution.py:61
  24.1 1.0 %copy-start.5 = (bf16[2,256,1024]{2,1,0:T(8,128)(2,1)}, bf16[2,256,1024]{2,1,0:T(8,128)(2,1)S(1)}, u32[]{:S(2)}) copy-start(bf16[2,256,1024]{2,1,0:T(8,128)(2,1)S(1)} %stack_tables.1.stacked) | copy-start | bytes 3145732
  35.6 19.7 %all-to-all-start.2 = ((bf16[16,144,128]{2,1,0:T(8,128)(2,1)}), bf16[16,144,128]{2,1,0:T(8,128)(2,1)}, u32[]{:S(2)}, u32[]{:S(2)}) async-start(bf16[16,144,128]{2,1,0:T(8,128)(2,1)} %get-tuple-element.28), calls=%async_computation.2 | async-start | bytes 1179648 | tf_op jit(solution)/shard_map/all_to_all | solution.py:61
  39.9 4.4 %copy-start.6 = (bf16[2,256,1024]{2,1,0:T(8,128)(2,1)S(1)}, bf16[2,256,1024]{2,1,0:T(8,128)(2,1)}, u32[]{:S(2)}) copy-start(bf16[2,256,1024]{2,1,0:T(8,128)(2,1)} %copy-done.5) | copy-start | bytes 3145732
  41.3 7.6 %copy-start.2 = (f32[16,16,128]{2,1,0:T(8,128)}, f32[16,16,128]{2,1,0:T(8,128)S(1)}, u32[]{:S(2)}) copy-start(f32[16,16,128]{2,1,0:T(8,128)S(1)} %get-tuple-element.24.ids_ref.refs_0_) | copy-start | bytes 393220
  41.3 7.6 %collective-permute-start.1 = (f32[64,128]{1,0:T(8,128)S(1)}, f32[64,128]{1,0:T(8,128)S(1)}, u32[]{:S(2)}, u32[]{:S(2)}) collective-permute-start(f32[64,128]{1,0:T(8,128)S(1)} %get-tuple-element.25.own), channel_id=1, source_target_pairs={{0,4},{4,0},{1,5},{5,1},{2,6},{6,2},{3,7},{7,3},{8,12},{12,8},{9,1... | collective-permute-start | bytes 98312 | tf_op jit(solution)/shard_map/ppermute | solution.py:579
  42.6 21.4 %collective-permute-start.2 = (bf16[4,8,48,128]{3,2,1,0:T(8,128)(2,1)S(1)}, bf16[4,8,48,128]{3,2,1,0:T(8,128)(2,1)}, u32[]{:S(2)}, u32[]{:S(2)}) collective-permute-start(bf16[4,8,48,128]{3,2,1,0:T(8,128)(2,1)S(1)} %get-tuple-element.30), channel_id=1, source_target_pairs={{0,4},{4,0},{1,5},{5,1},{2,6},{6,2},{3,7},{7,3},{8,12},{12,8},{9,1... | collective-permute-start | bytes 1179656 | tf_op jit(solution)/shard_map/ppermute | solution.py:579
  49.7 0.6 copy-start.3
  55.3 27.5 %all-to-all-start.1 = ((bf16[16,352,128]{2,1,0:T(8,128)(2,1)}), bf16[16,352,128]{2,1,0:T(8,128)(2,1)S(1)}, u32[]{:S(2)}, u32[]{:S(2)}) async-start(bf16[16,352,128]{2,1,0:T(8,128)(2,1)} %get-tuple-element.26), calls=%async_computation.1 | async-start | bytes 2883584 | tf_op jit(solution)/shard_map/all_to_all | solution.py:61
  59.0 4.9 %copy-start.4 = (f32[8,128]{1,0:T(8,128)S(1)}, f32[8,128]{1,0:T(8,128)}, u32[]{:S(2)}) copy-start(f32[8,128]{1,0:T(8,128)} %copy-done.3) | copy-start | bytes 12292
  64.0 1.1 %copy-start.1 = (f32[4,8,48,128]{3,2,1,0:T(8,128)S(1)}, f32[4,8,48,128]{3,2,1,0:T(8,128)}, u32[]{:S(2)}) copy-start(f32[4,8,48,128]{3,2,1,0:T(8,128)} %part_own.1.own) | copy-start | bytes 2359300
  66.8 18.5 %collective-permute-start.3 = (bf16[8,48,128]{2,1,0:T(8,128)(2,1)}, bf16[8,48,128]{2,1,0:T(8,128)(2,1)S(1)}, u32[]{:S(2)}, u32[]{:S(2)}) collective-permute-start(bf16[8,48,128]{2,1,0:T(8,128)(2,1)} %get-tuple-element.32), channel_id=1, source_target_pairs={{0,8},{8,0},{16,24},{24,16},{1,9},{9,1},{17,25},{25,17},{2,10},{10... | collective-permute-start | bytes 294920 | tf_op jit(solution)/shard_map/ppermute | solution.py:607
  68.6 16.8 %collective-permute-start.4 = (bf16[8,48,128]{2,1,0:T(8,128)(2,1)}, bf16[8,48,128]{2,1,0:T(8,128)(2,1)S(1)}, u32[]{:S(2)}, u32[]{:S(2)}) collective-permute-start(bf16[8,48,128]{2,1,0:T(8,128)(2,1)} %get-tuple-element.33), channel_id=1, source_target_pairs={{0,16},{8,24},{16,0},{24,8},{1,17},{9,25},{17,1},{25,9},{2,18},{10... | collective-permute-start | bytes 294920 | tf_op jit(solution)/shard_map/ppermute | solution.py:607
  70.1 15.3 %collective-permute-start.5 = (bf16[8,48,128]{2,1,0:T(8,128)(2,1)S(1)}, bf16[8,48,128]{2,1,0:T(8,128)(2,1)S(1)}, u32[]{:S(2)}, u32[]{:S(2)}) collective-permute-start(bf16[8,48,128]{2,1,0:T(8,128)(2,1)S(1)} %get-tuple-element.34), channel_id=1, source_target_pairs={{0,24},{8,16},{16,8},{24,0},{1,25},{9,17},{17,9},{25,1},{2,26},{10... | collective-permute-start | bytes 294920 | tf_op jit(solution)/shard_map/ppermute | solution.py:607

commit v8 on v7

--- a/solution.py
+++ b/solution.py
@@ -137,7 +137,7 @@
     def __init__(self, count, peers):
         self.left = count * TILE
         self.half = self.left + self.left // 2
-        self.dense = self.half
+        self.dense = 2 * self.half
         self.share = 1024 // peers
         self.ids = self.dense + self.share
         self.back = 2 * self.half + self.share
@@ -152,7 +152,7 @@
 def backward_kernel(
     n_grp, n_lane, wire,
     half_ref, x_ref, u_ref, now_ref, next_ref, fm_ref, proj_t_ref, lcb_ref, gain_ref,
-    out_ref, own_ref,
+    out_ref,
     fm_t, proj, lcb_t, gains, eye, mixed, p_t, g_t, d_sum, d_p_t, left_in, right_in, grads, turned, ids,
 ):
     count, width, features = x_ref.shape
@@ -221,15 +221,16 @@
         turned[group, 0] = rows[0:128]
         turned[group, 1] = rows[128:256]
     for group in range(count // STEP):
-        for side, ref in ((1 - half, out_ref), (half, own_ref)):
+        for side, base in ((1 - half, 0), (half, wire.half)):
             for peer in range(peers):
                 at = place_of(n_grp, n_lane, peer)
                 line = turned[group, side, at : at + TILE]
                 left = jnp.concatenate([line[:, k * 128 : k * 128 + 128] for k in range(STEP)], axis=0)
-                ref[peer, group * 32 : group * 32 + 32] = left.astype(BF16)
+                row = base + group * 32
+                out_ref[peer, row : row + 32] = left.astype(BF16)
                 right = jnp.concatenate([line[:, 512:640], line[:, 640:768]], axis=0)
-                row = wire.left + group * 16
-                ref[peer, row : row + 16] = right.astype(BF16)
+                row = base + wire.left + group * 16
+                out_ref[peer, row : row + 16] = right.astype(BF16)
 
     part = features // peers
     third = width // peers
@@ -277,13 +278,13 @@
         return pl.BlockSpec(shape, lambda i: (0,) * len(shape))
 
     operands = (pooled_t, upstream_t, ids_now, ids_next, w_fm, w_proj_t, w_lcb, gain.reshape(1, width))
-    shapes = [(peers, wire.ids + 16, LANES), (peers, wire.half, LANES)]
+    shape = (peers, wire.ids + 16, LANES)
     return pl.pallas_call(
         functools.partial(backward_kernel, n_grp, n_lane, wire),
         grid=(1,),
         in_specs=[SMEM] + [whole(array.shape) for array in operands],
-        out_specs=[whole(shape) for shape in shapes],
-        out_shape=[pltpu.HBM(shape, BF16) for shape in shapes],
+        out_specs=whole(shape),
+        out_shape=pltpu.HBM(shape, BF16),
         scratch_shapes=[
             pltpu.VMEM((rank, features), BF16),
             pltpu.VMEM((rank, width), BF16),
@@ -310,6 +311,7 @@
 def part_kernel(n_grp, wire, other, half_ref, seen, *refs):
     held = refs[-1]
     peers = seen.shape[0]
+    base = 0 if other else wire.half
     if other:
         half = 1 - half_ref[0]
         out, dense, all_ids = refs[:3]
@@ -322,12 +324,11 @@
         half = half_ref[0]
         all_ids, out = refs[0], refs[2]
     lane = lax.broadcasted_iota(jnp.int32, (1, LANES), 1)
-    start = ((lane % TILE) * LANES).astype(F32)
     keys = []
     for peer in range(peers):
         at = peer * LANES
-        held[at : at + wire.left, 0:128] = seen[peer, 0 : wire.left]
-        right = seen[peer, wire.left : wire.half]
+        held[at : at + wire.left, 0:128] = seen[peer, base : base + wire.left]
+        right = seen[peer, base + wire.left : base + wire.half]
         turned = turn(right.astype(F32)).astype(BF16)
         for i in range(wire.left // 32):
             held[at + 32 * i : at + 32 * i + 16, 128:256] = right[16 * i : 16 * i + 16]
@@ -335,13 +336,17 @@
         if wire.left < LANES:
             held[at + wire.left : at + LANES] = jnp.zeros((LANES - wire.left, 256), BF16)
         ids = all_ids[peer]
-        key = jnp.where(half == 0, ids[0:1], ids[1:2]) + start
+        key = jnp.where(half == 0, ids[0:1], ids[1:2])
         keys.append(jnp.where(lane < wire.left, key, -1.0))
     keys = jnp.concatenate(keys, axis=1)
     piece = LANES // n_grp
+    row = lax.broadcasted_iota(jnp.int32, (LANES, 1), 0).astype(F32)
+    same = jnp.where(keys == row, 1.0, 0.0).astype(BF16)
+    feature = lax.broadcasted_iota(jnp.int32, (16, peers * LANES), 1) % TILE
+    feature = jnp.concatenate([feature] * (LANES // 16), axis=0)
     for pair in range(TILE // 2):
-        row = lax.broadcasted_iota(jnp.int32, (256, 1), 0).astype(F32) + 256.0 * pair
-        hit = jnp.where(keys == row, 1.0, 0.0).astype(BF16)
+        hit = [same * jnp.where(feature == 2 * pair + f, 1.0, 0.0).astype(BF16) for f in range(2)]
+        hit = jnp.concatenate(hit, axis=0)
         part = mm(hit, held[...])
         for f in range(2):
             for g in range(n_grp):
@@ -396,27 +401,29 @@
 def lookup_kernel(wire, stacked, ids_ref, out):
     peers = out.shape[0]
     ids = ids_ref[...].reshape(peers * 16, LANES)
-    lane = lax.broadcasted_iota(jnp.int32, (1, LANES), 1)
-    keys = (ids + ((lane % TILE) * LANES).astype(F32)).T
-    column = lax.broadcasted_iota(jnp.int32, (1, TILE * LANES), 1).astype(F32)
+    keys = ids.T
+    rows = peers * wire.left
+    lane = lax.broadcasted_iota(jnp.int32, (1, LANES), 1).astype(F32)
+    feature = lax.broadcasted_iota(jnp.int32, (rows, LANES), 0) % TILE
+    masks = [jnp.where(feature == f, 1.0, 0.0).astype(BF16) for f in range(TILE)]
     for which in range(2):
-        for pair in range(peers // 2):
-            mine = []
-            for peer in (2 * pair, 2 * pair + 1):
-                at = peer * 16 + 2 + which
-                mine.append(keys[0 : wire.left, at : at + 1])
-            hit = jnp.where(jnp.concatenate(mine, axis=0) == column, 1.0, 0.0).astype(BF16)
-            rows = mm_nt(hit, stacked[which])
-            for k in range(2):
-                got, peer = rows[k * wire.left : (k + 1) * wire.left], 2 * pair + k
-                base = wire.back_left[which]
-                out[peer, base : base + wire.left] = got[:, 0:128].astype(BF16)
-                packed = []
-                for i in range(wire.left // 32):
-                    first, second = got[32 * i : 32 * i + 16, 128:256], got[32 * i + 16 : 32 * i + 32, 128:256]
-                    packed.append(jnp.where(low_lanes(first.shape), first, second))
-                base = wire.back_right[which]
-                out[peer, base : base + wire.left // 2] = jnp.concatenate(packed, axis=0).astype(BF16)
+        same = []
+        for peer in range(peers):
+            at = peer * 16 + 2 + which
+            same.append(jnp.where(keys[0 : wire.left, at : at + 1] == lane, 1.0, 0.0))
+        same = jnp.concatenate(same, axis=0).astype(BF16)
+        hit = jnp.concatenate([same * mask for mask in masks], axis=1)
+        both = mm_nt(hit, stacked[which])
+        for peer in range(peers):
+            got = both[peer * wire.left : (peer + 1) * wire.left]
+            base = wire.back_left[which]
+            out[peer, base : base + wire.left] = got[:, 0:128].astype(BF16)
+            packed = []
+            for i in range(wire.left // 32):
+                first, second = got[32 * i : 32 * i + 16, 128:256], got[32 * i + 16 : 32 * i + 32, 128:256]
+                packed.append(jnp.where(low_lanes(first.shape), first, second))
+            base = wire.back_right[which]
+            out[peer, base : base + wire.left // 2] = jnp.concatenate(packed, axis=0).astype(BF16)
 
 
 def lookup(wire, stacked, ids):
@@ -455,7 +462,7 @@
         grid=(1,),
         in_specs=[pl.BlockSpec(memory_space=pl.ANY), whole(own.shape), whole(seen.shape)],
         out_specs=[whole((peers, wire.share, LANES)), whole((8, LANES))],
-        out_shape=[pltpu.HBM(rows.shape, BF16), jax.ShapeDtypeStruct((8, LANES), F32)],
+        out_shape=[pltpu.HBM(rows.shape, BF16), pltpu.HBM((8, LANES), F32)],
         input_output_aliases={0: 0},
         compiler_params=params(),
         cost_estimate=cost(1),
@@ -588,19 +595,18 @@
     grp = lax.axis_index("grp").astype(jnp.int32)
     mine_t = lax.dynamic_slice_in_dim(tables.transpose(0, 2, 1), grp * TILE, TILE, 0)
     crossed_t = cross(mine_t)
-    sent, sent_own = backward(
+    sent = backward(
         n_grp, n_lane, wire, half,
         pooled.transpose(0, 2, 1), upstream.transpose(0, 2, 1), ids_now, ids_next, w_fm, w_proj.T, w_lcb, gain,
     )
     seen = exchange(sent, PEER)
-    seen_own = exchange(sent_own, PEER)
     part, dense, ids = part_sums(n_grp, wire, True, half, seen)
     dense_seen = cross(dense)
     part_seen = cross(part)
     rows_wire = lookup(wire, stack_tables(half, mine_t, crossed_t), ids)
     rows_wire, token = fill(wire, factor, rows_wire, dense, dense_seen)
     rows = exchange(rows_wire, PEER)
-    (own,) = part_sums(n_grp, wire, False, half, seen_own, ids, token)
+    (own,) = part_sums(n_grp, wire, False, half, seen, ids, token)
     next_rows, grad_fm, grad_proj_t, grad_lcb, grad_gain, token_out = unpack(n_grp, n_lane, wire, count, rows)
     pieces = combine(grp[None], own, part_seen, token)
     pieces = [pieces[0]] + [

time: 87 us -> 88.3 us (1.015)
  waiting for transfers between devices: 33.3 us -> 34.7 us
    pallas_call x2, Pallas kernels: 4.81 us -> 5.92 us  [part_sums(): pl.pallas_call(functools.partial(part_kernel, n_grp, wire, other), in_spe...]
    pallas_call x1, Pallas kernels: 0.28 us -> 1.27 us  [stack_tables(): pl.pallas_call(stack_kernel, in_specs=[SMEM, VMEM, VMEM], out_specs=VMEM,...]
    pallas_call x1, Pallas kernels: 1.7 us -> 0.73 us  [combine(): pl.pallas_call(combine_kernel, in_specs=[SMEM, VMEM, VMEM, pl.BlockSpec(m...]
    all_to_all x3 -> x2, waiting for transfers between devices: 28.1 us -> 28.9 us  [exchange(): return lax.all_to_all(blocks, axes, split_axis=0, concat_axis=0, tiled=True)]
    all_to_all x3 -> x2, starting transfers between devices: 12.8 us -> 13 us  [exchange(): return lax.all_to_all(blocks, axes, split_axis=0, concat_axis=0, tiled=True)]
  transfers between devices with their start and end apart: 9 -> 8, of which waited for: 5 -> 4; matrix products, arithmetic and copies ran while one was open for 0% -> 0% of each run, Pallas kernels for 28% -> 25%
where the time goes in v8:
time: 88.3 us; the launch traced here: 87.8 us
  waiting for transfers between devices  34.7 us (39%)
  Pallas kernels  25.3 us (29%)
  starting transfers between devices  23.5 us (27%)
  local copies, waits for them, and re-layouts  3.54 us (4%)
    all_to_all x2, waiting for transfers between devices, exchange(): return lax.all_to_all(blocks, axes, split_axis=0, concat_axis=0, tiled=True)  28.9 us
    all_to_all x2, starting transfers between devices, exchange(): return lax.all_to_all(blocks, axes, split_axis=0, concat_axis=0, tiled=True)  13 us
    pallas_call x1, Pallas kernels, backward(): pl.pallas_call(functools.partial(backward_kernel, n_grp, n_lane, wire), g...  9.17 us
    ppermute x3, starting transfers between devices, cross(): return lax.ppermute(array, 'half', [(0, 1), (1, 0)])  7.03 us
    pallas_call x2, Pallas kernels, part_sums(): pl.pallas_call(functools.partial(part_kernel, n_grp, wire, other), in_spe...  5.92 us
    ppermute x3, waiting for transfers between devices, cross(): return lax.ppermute(array, 'half', [(0, 1), (1, 0)])  5.84 us
    pallas_call x1, Pallas kernels, lookup(): pl.pallas_call(functools.partial(lookup_kernel, wire), grid=(4,), in_spec...  3.77 us
    unnamed x14, local copies, waits for them, and re-layouts  3.52 us
  transfers between devices with their start and end apart: 8, of which 4 were waited for; matrix products, arithmetic and copies ran while one was open for 0% of the time, Pallas kernels for 25%

profile of v8, /device:TPU:0, one launch (start us, length us, event | category | flops | bytes accessed | tf_op | source)
XLA Modules:
  0.0 87.8 jit_solution(5348380931583027438)
XLA Ops:
  0.7 1.4 %copy-done = bf16[32,128,192]{1,2,0:T(8,128)(2,1)S(1)} copy-done((bf16[32,128,192]{1,2,0:T(8,128)(2,1)S(1)}, bf16[32,128,192]{1,2,0:T(8,128)(2,1)}, u32[]{:S(2)}) %copy-start) | copy-done | bytes 1572888
  2.1 4.1 %collective-permute-start = (bf16[8,192,128]{2,1,0:T(8,128)(2,1)S(1)}, bf16[8,192,128]{2,1,0:T(8,128)(2,1)}, u32[]{:S(2)}, u32[]{:S(2)}) collective-permute-start(bf16[8,192,128]{2,1,0:T(8,128)(2,1)S(1)} %dynamic-slice_bitcast_fusion.mine_t), channel_id=1, source_target_pairs={{0,4},{4,0},{1,5},{5,1},{2,6},{6,2},{3,7},{7,3},{8,12},{12,8},{9,1... | collective-permute-start | bytes 1179656 | tf_op jit(solution)/shard_map/ppermute | solution.py:586
  6.2 9.2 %layer_backward.1 = bf16[16,368,128]{2,1,0:T(8,128)(2,1)} custom-call(s32[1]{0:T(128)} %bitcast.half_ref, bf16[12,192,256]{2,1,0:T(8,128)(2,1)} %bitcast.11, bf16[12,192,256]{2,1,0:T(8,128)(2,1)} %bitcast.12, s32[12,256]{1,0:T(8,128)} %now_ref.1, s32[12,256]{1,0:T(8,128)} %next_ref.1, bf16[256,128]{1,0:T(8,128)(2,1)} %fm_ref.1, bf16[192,128]{1,0:T(8,128)(2,1)} %bitcast.13, ...), custom_call_target="tpu_custom_call" | custom-call | flops 1000000000 | bytes 100000 | tf_op jit(solution)/shard_map/layer_backward/pallas_call | solution.py:282
  15.3 4.8 %all-to-all-start = ((bf16[16,368,128]{2,1,0:T(8,128)(2,1)}), bf16[16,368,128]{2,1,0:T(8,128)(2,1)S(1)}, u32[]{:S(2)}, u32[]{:S(2)}) async-start(bf16[16,368,128]{2,1,0:T(8,128)(2,1)} %layer_backward.1), calls=%async_computation | async-start | bytes 3014656 | tf_op jit(solution)/shard_map/all_to_all | solution.py:61
  20.2 3.7 %collective-permute-done.crossed_t = bf16[8,192,128]{2,1,0:T(8,128)(2,1)} collective-permute-done((bf16[8,192,128]{2,1,0:T(8,128)(2,1)S(1)}, bf16[8,192,128]{2,1,0:T(8,128)(2,1)}, u32[]{:S(2)}, u32[]{:S(2)}) %collective-permute-start) | collective-permute-done | bytes 393248 | tf_op jit(solution)/shard_map/ppermute | solution.py:586
  23.9 1.3 %stack_tables.1.stacked = bf16[2,256,1024]{2,1,0:T(8,128)(2,1)S(1)} custom-call(s32[1]{0:T(128)} %bitcast.half_ref, bf16[8,192,128]{2,1,0:T(8,128)(2,1)S(1)} %dynamic-slice_bitcast_fusion.mine_t, bf16[8,192,128]{2,1,0:T(8,128)(2,1)} %collective-permute-done.crossed_t), custom_call_target="tpu_custom_call" | custom-call | flops 99999997952 | bytes 100000 | tf_op jit(solution)/shard_map/stack_tables/pallas_call | solution.py:390
  25.2 1.0 %copy-done.5 = bf16[2,256,1024]{2,1,0:T(8,128)(2,1)} copy-done((bf16[2,256,1024]{2,1,0:T(8,128)(2,1)}, bf16[2,256,1024]{2,1,0:T(8,128)(2,1)S(1)}, u32[]{:S(2)}) %copy-start.5) | copy-done | bytes 1048600
  26.1 16.4 %all-to-all-done.seen = bf16[16,368,128]{2,1,0:T(8,128)(2,1)S(1)} async-done(((bf16[16,368,128]{2,1,0:T(8,128)(2,1)}), bf16[16,368,128]{2,1,0:T(8,128)(2,1)S(1)}, u32[]{:S(2)}, u32[]{:S(2)}) %all-to-all-start) | async-done | bytes 1507360 | tf_op jit(solution)/shard_map/all_to_all | solution.py:61
  42.5 2.2 %part_other.1 = (bf16[4,8,48,128]{3,2,1,0:T(8,128)(2,1)}, f32[64,128]{1,0:T(8,128)S(1)}, f32[16,16,128]{2,1,0:T(8,128)S(1)}) custom-call(s32[1]{0:T(128)} %bitcast.half_ref, bf16[16,368,128]{2,1,0:T(8,128)(2,1)S(1)} %all-to-all-done.seen), custom_call_target="tpu_custom_call" | custom-call | flops 1000000000 | bytes 100000 | tf_op jit(solution)/shard_map/part_other/pallas_call | solution.py:368
  44.7 0.5 collective-permute-start.1
  45.2 2.4 %collective-permute-start.2 = (bf16[4,8,48,128]{3,2,1,0:T(8,128)(2,1)}, bf16[4,8,48,128]{3,2,1,0:T(8,128)(2,1)S(1)}, u32[]{:S(2)}, u32[]{:S(2)}) collective-permute-start(bf16[4,8,48,128]{3,2,1,0:T(8,128)(2,1)} %get-tuple-element.26), channel_id=1, source_target_pairs={{0,4},{4,0},{1,5},{5,1},{2,6},{6,2},{3,7},{7,3},{8,12},{12,8},{9,1... | collective-permute-start | bytes 1179656 | tf_op jit(solution)/shard_map/ppermute | solution.py:586
  47.6 3.8 %lookup.1.rows = bf16[16,352,128]{2,1,0:T(8,128)(2,1)} custom-call(bf16[2,256,1024]{2,1,0:T(8,128)(2,1)S(1)} %copy-done.6, f32[16,16,128]{2,1,0:T(8,128)S(1)} %get-tuple-element.21.ids_ref.refs_0_), custom_call_target="tpu_custom_call" | custom-call | flops 99999997952 | bytes 100000 | tf_op jit(solution)/shard_map/lookup/pallas_call | solution.py:432
  51.4 0.8 fill_dense.1
  52.2 8.2 %all-to-all-start.1 = ((bf16[16,352,128]{2,1,0:T(8,128)(2,1)}), bf16[16,352,128]{2,1,0:T(8,128)(2,1)S(1)}, u32[]{:S(2)}, u32[]{:S(2)}) async-start(bf16[16,352,128]{2,1,0:T(8,128)(2,1)} %get-tuple-element.23), calls=%async_computation.1 | async-start | bytes 2883584 | tf_op jit(solution)/shard_map/all_to_all | solution.py:61
  60.3 3.8 %part_own.1.own = f32[4,8,48,128]{3,2,1,0:T(8,128)} custom-call(s32[1]{0:T(128)} %bitcast.half_ref, bf16[16,368,128]{2,1,0:T(8,128)(2,1)} %copy-done.1, f32[16,16,128]{2,1,0:T(8,128)} %copy-done.3, f32[8,128]{1,0:T(8,128)} %get-tuple-element.25.refs_1_.after), custom_call_target="tpu_custom_call" | custom-call | flops 1000000000 | bytes 100000 | tf_op jit(solution)/shard_map/part_own/pallas_call | solution.py:368
  64.1 2.2 %collective-permute-done.2.seen = bf16[4,8,48,128]{3,2,1,0:T(8,128)(2,1)S(1)} collective-permute-done((bf16[4,8,48,128]{3,2,1,0:T(8,128)(2,1)}, bf16[4,8,48,128]{3,2,1,0:T(8,128)(2,1)S(1)}, u32[]{:S(2)}, u32[]{:S(2)}) %collective-permute-start.2) | collective-permute-done | bytes 393248 | tf_op jit(solution)/shard_map/ppermute | solution.py:586
  66.3 1.1 %copy-done.2 = f32[4,8,48,128]{3,2,1,0:T(8,128)S(1)} copy-done((f32[4,8,48,128]{3,2,1,0:T(8,128)S(1)}, f32[4,8,48,128]{3,2,1,0:T(8,128)}, u32[]{:S(2)}) %copy-start.2) | copy-done | bytes 786456
  67.4 0.7 combine.1
  68.1 0.8 collective-permute-start.3
  69.0 1.5 %collective-permute-start.4 = (bf16[8,48,128]{2,1,0:T(8,128)(2,1)}, bf16[8,48,128]{2,1,0:T(8,128)(2,1)S(1)}, u32[]{:S(2)}, u32[]{:S(2)}) collective-permute-start(bf16[8,48,128]{2,1,0:T(8,128)(2,1)} %get-tuple-element.29), channel_id=1, source_target_pairs={{0,16},{8,24},{16,0},{24,8},{1,17},{9,25},{17,1},{25,9},{2,18},{10... | collective-permute-start | bytes 294920 | tf_op jit(solution)/shard_map/ppermute | solution.py:613
  70.5 1.2 %collective-permute-start.5 = (bf16[8,48,128]{2,1,0:T(8,128)(2,1)}, bf16[8,48,128]{2,1,0:T(8,128)(2,1)S(1)}, u32[]{:S(2)}, u32[]{:S(2)}) collective-permute-start(bf16[8,48,128]{2,1,0:T(8,128)(2,1)} %get-tuple-element.30), channel_id=1, source_target_pairs={{0,24},{8,16},{16,8},{24,0},{1,25},{9,17},{17,9},{25,1},{2,26},{10... | collective-permute-start | bytes 294920 | tf_op jit(solution)/shard_map/ppermute | solution.py:613
  71.6 12.5 %all-to-all-done.1.dense_ref.left0.left1.right0.right1 = bf16[16,352,128]{2,1,0:T(8,128)(2,1)S(1)} async-done(((bf16[16,352,128]{2,1,0:T(8,128)(2,1)}), bf16[16,352,128]{2,1,0:T(8,128)(2,1)S(1)}, u32[]{:S(2)}, u32[]{:S(2)}) %all-to-all-start.1) | async-done | bytes 1441824 | tf_op jit(solution)/shard_map/all_to_all | solution.py:61
  84.1 2.6 %unpack_rows.1 = (bf16[12,192,256]{2,1,0:T(8,128)(2,1)}, f32[256,128]{1,0:T(8,128)}, f32[192,128]{1,0:T(8,128)}, f32[256,256]{1,0:T(8,128)}, f32[1,192]{1,0:T(1,128)}, /*index=5*/f32[8,128]{1,0:T(8,128)S(1)}) custom-call(bf16[16,352,128]{2,1,0:T(8,128)(2,1)S(1)} %all-to-all-done.1.dense_ref.left0.left1.right0.right1, ...), custom_call_target="tpu_custom_call" | custom-call | flops 1000000000 | bytes 100000 | tf_op jit(solution)/shard_map/unpack_rows/pallas_call | solution.py:523
  86.7 1.1 %finish_tables.1 = f32[32,32,192]{2,1,0:T(8,128)} custom-call(s32[1]{0:T(128)} %bitcast.7.place, bf16[8,48,128]{2,1,0:T(8,128)(2,1)S(1)} %get-tuple-element.27.refs_0_, bf16[8,48,128]{2,1,0:T(8,128)(2,1)S(1)} %collective-permute-done.3.refs_1_, bf16[8,48,128]{2,1,0:T(8,128)(2,1)S(1)} %collective-permute-done.4.refs_2_, ...), custom_call_target="tpu_custom_call" | custom-call | bytes 100000 | tf_op jit(solution)/shard_map/finish_tables/pallas_call | solution.py:574
  (16 shorter events, 0.1 us)
Async XLA Ops:
  0.6 1.4 %copy-start = (bf16[32,128,192]{1,2,0:T(8,128)(2,1)S(1)}, bf16[32,128,192]{1,2,0:T(8,128)(2,1)}, u32[]{:S(2)}) copy-start(bf16[32,128,192]{1,2,0:T(8,128)(2,1)} %param.13) | copy-start | bytes 4718596
  2.1 21.8 %collective-permute-start = (bf16[8,192,128]{2,1,0:T(8,128)(2,1)S(1)}, bf16[8,192,128]{2,1,0:T(8,128)(2,1)}, u32[]{:S(2)}, u32[]{:S(2)}) collective-permute-start(bf16[8,192,128]{2,1,0:T(8,128)(2,1)S(1)} %dynamic-slice_bitcast_fusion.mine_t), channel_id=1, source_target_pairs={{0,4},{4,0},{1,5},{5,1},{2,6},{6,2},{3,7},{7,3},{8,12},{12,8},{9,1... | collective-permute-start | bytes 1179656 | tf_op jit(solution)/shard_map/ppermute | solution.py:586
  15.3 27.2 %all-to-all-start = ((bf16[16,368,128]{2,1,0:T(8,128)(2,1)}), bf16[16,368,128]{2,1,0:T(8,128)(2,1)S(1)}, u32[]{:S(2)}, u32[]{:S(2)}) async-start(bf16[16,368,128]{2,1,0:T(8,128)(2,1)} %layer_backward.1), calls=%async_computation | async-start | bytes 3014656 | tf_op jit(solution)/shard_map/all_to_all | solution.py:61
  25.1 1.0 %copy-start.5 = (bf16[2,256,1024]{2,1,0:T(8,128)(2,1)}, bf16[2,256,1024]{2,1,0:T(8,128)(2,1)S(1)}, u32[]{:S(2)}) copy-start(bf16[2,256,1024]{2,1,0:T(8,128)(2,1)S(1)} %stack_tables.1.stacked) | copy-start | bytes 3145732
  42.5 2.2 %copy-start.1 = (bf16[16,368,128]{2,1,0:T(8,128)(2,1)}, bf16[16,368,128]{2,1,0:T(8,128)(2,1)S(1)}, u32[]{:S(2)}) copy-start(bf16[16,368,128]{2,1,0:T(8,128)(2,1)S(1)} %all-to-all-done.seen) | copy-start | bytes 4521988
  42.5 5.1 %copy-start.6 = (bf16[2,256,1024]{2,1,0:T(8,128)(2,1)S(1)}, bf16[2,256,1024]{2,1,0:T(8,128)(2,1)}, u32[]{:S(2)}) copy-start(bf16[2,256,1024]{2,1,0:T(8,128)(2,1)} %copy-done.5) | copy-start | bytes 3145732
  44.7 6.7 %copy-start.3 = (f32[16,16,128]{2,1,0:T(8,128)}, f32[16,16,128]{2,1,0:T(8,128)S(1)}, u32[]{:S(2)}) copy-start(f32[16,16,128]{2,1,0:T(8,128)S(1)} %get-tuple-element.21.ids_ref.refs_0_) | copy-start | bytes 393220
  44.7 6.7 %collective-permute-start.1 = (f32[64,128]{1,0:T(8,128)S(1)}, f32[64,128]{1,0:T(8,128)S(1)}, u32[]{:S(2)}, u32[]{:S(2)}) collective-permute-start(f32[64,128]{1,0:T(8,128)S(1)} %get-tuple-element.22.own), channel_id=1, source_target_pairs={{0,4},{4,0},{1,5},{5,1},{2,6},{6,2},{3,7},{7,3},{8,12},{12,8},{9,1... | collective-permute-start | bytes 98312 | tf_op jit(solution)/shard_map/ppermute | solution.py:586
  45.2 21.1 %collective-permute-start.2 = (bf16[4,8,48,128]{3,2,1,0:T(8,128)(2,1)}, bf16[4,8,48,128]{3,2,1,0:T(8,128)(2,1)S(1)}, u32[]{:S(2)}, u32[]{:S(2)}) collective-permute-start(bf16[4,8,48,128]{3,2,1,0:T(8,128)(2,1)} %get-tuple-element.26), channel_id=1, source_target_pairs={{0,4},{4,0},{1,5},{5,1},{2,6},{6,2},{3,7},{7,3},{8,12},{12,8},{9,1... | collective-permute-start | bytes 1179656 | tf_op jit(solution)/shard_map/ppermute | solution.py:586
  52.2 32.0 %all-to-all-start.1 = ((bf16[16,352,128]{2,1,0:T(8,128)(2,1)}), bf16[16,352,128]{2,1,0:T(8,128)(2,1)S(1)}, u32[]{:S(2)}, u32[]{:S(2)}) async-start(bf16[16,352,128]{2,1,0:T(8,128)(2,1)} %get-tuple-element.23), calls=%async_computation.1 | async-start | bytes 2883584 | tf_op jit(solution)/shard_map/all_to_all | solution.py:61
  60.3 6.0 %copy-start.4 = (f32[8,128]{1,0:T(8,128)S(1)}, f32[8,128]{1,0:T(8,128)}, u32[]{:S(2)}) copy-start(f32[8,128]{1,0:T(8,128)} %get-tuple-element.25.refs_1_.after) | copy-start | bytes 12292
  66.3 1.1 %copy-start.2 = (f32[4,8,48,128]{3,2,1,0:T(8,128)S(1)}, f32[4,8,48,128]{3,2,1,0:T(8,128)}, u32[]{:S(2)}) copy-start(f32[4,8,48,128]{3,2,1,0:T(8,128)} %part_own.1.own) | copy-start | bytes 2359300
  68.1 18.6 %collective-permute-start.3 = (bf16[8,48,128]{2,1,0:T(8,128)(2,1)}, bf16[8,48,128]{2,1,0:T(8,128)(2,1)S(1)}, u32[]{:S(2)}, u32[]{:S(2)}) collective-permute-start(bf16[8,48,128]{2,1,0:T(8,128)(2,1)} %get-tuple-element.28), channel_id=1, source_target_pairs={{0,8},{8,0},{16,24},{24,16},{1,9},{9,1},{17,25},{25,17},{2,10},{10... | collective-permute-start | bytes 294920 | tf_op jit(solution)/shard_map/ppermute | solution.py:613
  69.0 17.8 %collective-permute-start.4 = (bf16[8,48,128]{2,1,0:T(8,128)(2,1)}, bf16[8,48,128]{2,1,0:T(8,128)(2,1)S(1)}, u32[]{:S(2)}, u32[]{:S(2)}) collective-permute-start(bf16[8,48,128]{2,1,0:T(8,128)(2,1)} %get-tuple-element.29), channel_id=1, source_target_pairs={{0,16},{8,24},{16,0},{24,8},{1,17},{9,25},{17,1},{25,9},{2,18},{10... | collective-permute-start | bytes 294920 | tf_op jit(solution)/shard_map/ppermute | solution.py:613
  70.5 16.3 %collective-permute-start.5 = (bf16[8,48,128]{2,1,0:T(8,128)(2,1)}, bf16[8,48,128]{2,1,0:T(8,128)(2,1)S(1)}, u32[]{:S(2)}, u32[]{:S(2)}) collective-permute-start(bf16[8,48,128]{2,1,0:T(8,128)(2,1)} %get-tuple-element.30), channel_id=1, source_target_pairs={{0,24},{8,16},{16,8},{24,0},{1,25},{9,17},{17,9},{25,1},{2,26},{10... | collective-permute-start | bytes 294920 | tf_op jit(solution)/shard_map/ppermute | solution.py:613

commit v9 on v8

--- a/solution.py
+++ b/solution.py
@@ -308,22 +308,46 @@
     )(half, *operands)
 
 
-def part_kernel(n_grp, wire, other, half_ref, seen, *refs):
-    held = refs[-1]
+def dense_kernel(dense_ref, ids_ref, dense, all_ids):
+    total = dense_ref[0].astype(F32)
+    for peer in range(1, dense_ref.shape[0]):
+        total = total + dense_ref[peer].astype(F32)
+    dense[...] = total
+    all_ids[...] = ids_ref[...].astype(F32)
+
+
+def half_dense(wire, seen):
+    peers = seen.shape[0]
+    rows = wire.share // 2
+    at_ids = wire.ids // 16
+    return pl.pallas_call(
+        dense_kernel,
+        grid=(2,),
+        in_specs=[
+            pl.BlockSpec((peers, rows, LANES), lambda i: (0, wire.dense // rows + i, 0)),
+            pl.BlockSpec((peers, 16, LANES), lambda i: (0, at_ids, 0)),
+        ],
+        out_specs=[
+            pl.BlockSpec((rows, LANES), lambda i: (i, 0)),
+            pl.BlockSpec((peers, 16, LANES), lambda i: (0, 0, 0)),
+        ],
+        out_shape=[
+            jax.ShapeDtypeStruct((wire.share, LANES), F32),
+            jax.ShapeDtypeStruct((peers, 16, LANES), F32),
+        ],
+        compiler_params=params(),
+        cost_estimate=cost(1),
+        name="half_dense",
+    )(seen, seen)
+
+
+def part_kernel(n_grp, wire, other, half_ref, seen, all_ids, *refs):
+    out, held = refs[-2:]
     peers = seen.shape[0]
     base = 0 if other else wire.half
-    if other:
-        half = 1 - half_ref[0]
-        out, dense, all_ids = refs[:3]
-        total = seen[0, wire.dense : wire.ids].astype(F32)
-        for peer in range(1, peers):
-            total = total + seen[peer, wire.dense : wire.ids].astype(F32)
-        dense[...] = total
-        all_ids[...] = seen[:, wire.ids : wire.ids + 16].astype(F32)
-    else:
-        half = half_ref[0]
-        all_ids, out = refs[0], refs[2]
+    half = 1 - half_ref[0] if other else half_ref[0]
     lane = lax.broadcasted_iota(jnp.int32, (1, LANES), 1)
+    start = ((lane % TILE) * LANES).astype(F32)
     keys = []
     for peer in range(peers):
         at = peer * LANES
@@ -336,17 +360,13 @@
         if wire.left < LANES:
             held[at + wire.left : at + LANES] = jnp.zeros((LANES - wire.left, 256), BF16)
         ids = all_ids[peer]
-        key = jnp.where(half == 0, ids[0:1], ids[1:2])
+        key = jnp.where(half == 0, ids[0:1], ids[1:2]) + start
         keys.append(jnp.where(lane < wire.left, key, -1.0))
     keys = jnp.concatenate(keys, axis=1)
     piece = LANES // n_grp
-    row = lax.broadcasted_iota(jnp.int32, (LANES, 1), 0).astype(F32)
-    same = jnp.where(keys == row, 1.0, 0.0).astype(BF16)
-    feature = lax.broadcasted_iota(jnp.int32, (16, peers * LANES), 1) % TILE
-    feature = jnp.concatenate([feature] * (LANES // 16), axis=0)
     for pair in range(TILE // 2):
-        hit = [same * jnp.where(feature == 2 * pair + f, 1.0, 0.0).astype(BF16) for f in range(2)]
-        hit = jnp.concatenate(hit, axis=0)
+        row = lax.broadcasted_iota(jnp.int32, (256, 1), 0).astype(F32) + 256.0 * pair
+        hit = jnp.where(keys == row, 1.0, 0.0).astype(BF16)
         part = mm(hit, held[...])
         for f in range(2):
             for g in range(n_grp):
@@ -358,23 +378,20 @@
                 out[g, 2 * pair + f, piece : piece + piece // 2] = packed.astype(out.dtype)
 
 
-def part_sums(n_grp, wire, other, half, seen, *more):
+def part_sums(n_grp, wire, other, half, seen, ids, *after):
     peers = seen.shape[0]
     piece = LANES // n_grp
-    shapes = [jax.ShapeDtypeStruct((n_grp, TILE, piece + piece // 2, LANES), BF16 if other else F32)]
-    if other:
-        shapes.append(jax.ShapeDtypeStruct((wire.share, LANES), F32))
-        shapes.append(jax.ShapeDtypeStruct((peers, 16, LANES), F32))
+    shape = (n_grp, TILE, piece + piece // 2, LANES)
     return pl.pallas_call(
         functools.partial(part_kernel, n_grp, wire, other),
-        in_specs=[SMEM, VMEM] + [VMEM] * len(more),
-        out_specs=[VMEM] * len(shapes),
-        out_shape=shapes,
+        in_specs=[SMEM, VMEM, VMEM] + [pl.BlockSpec(memory_space=pl.ANY)] * len(after),
+        out_specs=VMEM,
+        out_shape=jax.ShapeDtypeStruct(shape, BF16 if other else F32),
         scratch_shapes=[pltpu.VMEM((peers * LANES, 256), BF16)],
         compiler_params=params(1 if other else 2),
         cost_estimate=cost(1),
         name="part_other" if other else "part_own",
-    )(half, seen, *more)
+    )(half, seen, ids, *after)
 
 
 def stack_kernel(half_ref, mine_t, crossed_t, out):
@@ -600,13 +617,13 @@
         pooled.transpose(0, 2, 1), upstream.transpose(0, 2, 1), ids_now, ids_next, w_fm, w_proj.T, w_lcb, gain,
     )
     seen = exchange(sent, PEER)
-    part, dense, ids = part_sums(n_grp, wire, True, half, seen)
+    dense, ids = half_dense(wire, seen)
     dense_seen = cross(dense)
-    part_seen = cross(part)
+    part_seen = cross(part_sums(n_grp, wire, True, half, seen, ids))
     rows_wire = lookup(wire, stack_tables(half, mine_t, crossed_t), ids)
     rows_wire, token = fill(wire, factor, rows_wire, dense, dense_seen)
     rows = exchange(rows_wire, PEER)
-    (own,) = part_sums(n_grp, wire, False, half, seen, ids, token)
+    own = part_sums(n_grp, wire, False, half, seen, ids, token)
     next_rows, grad_fm, grad_proj_t, grad_lcb, grad_gain, token_out = unpack(n_grp, n_lane, wire, count, rows)
     pieces = combine(grp[None], own, part_seen, token)
     pieces = [pieces[0]] + [

time: 88.3 us -> 87.8 us (level)
  starting transfers between devices: 23.5 us -> 18.7 us
  waiting for transfers between devices: 34.7 us -> 38.6 us
    ppermute x3, waiting for transfers between devices: 5.84 us -> 10.4 us  [cross(): return lax.ppermute(array, 'half', [(0, 1), (1, 0)])]
    all_to_all x2, starting transfers between devices: 13 us -> 8.55 us  [exchange(): return lax.all_to_all(blocks, axes, split_axis=0, concat_axis=0, tiled=True)]
  transfers between devices with their start and end apart: 8 -> 8, of which waited for: 4 -> 4; matrix products, arithmetic and copies ran while one was open for 0% -> 0% of each run, Pallas kernels for 25% -> 28%
where the time goes in v9:
time: 87.8 us; the launch traced here: 87.4 us
  waiting for transfers between devices  38.6 us (44%)
  Pallas kernels  25.4 us (29%)
  starting transfers between devices  18.7 us (21%)
  local copies, waits for them, and re-layouts  3.94 us (4%)
    all_to_all x2, waiting for transfers between devices, exchange(): return lax.all_to_all(blocks, axes, split_axis=0, concat_axis=0, tiled=True)  28.2 us
    ppermute x3, waiting for transfers between devices, cross(): return lax.ppermute(array, 'half', [(0, 1), (1, 0)])  10.4 us
    pallas_call x1, Pallas kernels, backward(): pl.pallas_call(functools.partial(backward_kernel, n_grp, n_lane, wire), g...  9.17 us
    all_to_all x2, starting transfers between devices, exchange(): return lax.all_to_all(blocks, axes, split_axis=0, concat_axis=0, tiled=True)  8.55 us
    ppermute x3, starting transfers between devices, cross(): return lax.ppermute(array, 'half', [(0, 1), (1, 0)])  6.68 us
    pallas_call x2, Pallas kernels, part_sums(): pl.pallas_call(functools.partial(part_kernel, n_grp, wire, other), in_spe...  5.83 us
    unnamed x14, local copies, waits for them, and re-layouts  3.92 us
    pallas_call x1, Pallas kernels, lookup(): pl.pallas_call(functools.partial(lookup_kernel, wire), grid=(4,), in_spec...  3.77 us
  transfers between devices with their start and end apart: 8, of which 4 were waited for; matrix products, arithmetic and copies ran while one was open for 0% of the time, Pallas kernels for 28%

profile of v9, /device:TPU:0, one launch (start us, length us, event | category | flops | bytes accessed | tf_op | source)
XLA Modules:
  0.0 87.4 jit_solution(6154952777903786582)
XLA Ops:
  0.7 1.4 %copy-done = bf16[32,128,192]{1,2,0:T(8,128)(2,1)S(1)} copy-done((bf16[32,128,192]{1,2,0:T(8,128)(2,1)S(1)}, bf16[32,128,192]{1,2,0:T(8,128)(2,1)}, u32[]{:S(2)}) %copy-start) | copy-done | bytes 1572888
  2.1 4.1 %collective-permute-start = (bf16[8,192,128]{2,1,0:T(8,128)(2,1)S(1)}, bf16[8,192,128]{2,1,0:T(8,128)(2,1)}, u32[]{:S(2)}, u32[]{:S(2)}) collective-permute-start(bf16[8,192,128]{2,1,0:T(8,128)(2,1)S(1)} %dynamic-slice_bitcast_fusion.mine_t), channel_id=1, source_target_pairs={{0,4},{4,0},{1,5},{5,1},{2,6},{6,2},{3,7},{7,3},{8,12},{12,8},{9,1... | collective-permute-start | bytes 1179656 | tf_op jit(solution)/shard_map/ppermute | solution.py:603
  6.2 9.2 %layer_backward.1 = bf16[16,368,128]{2,1,0:T(8,128)(2,1)} custom-call(s32[1]{0:T(128)} %bitcast.half_ref, bf16[12,192,256]{2,1,0:T(8,128)(2,1)} %bitcast.11, bf16[12,192,256]{2,1,0:T(8,128)(2,1)} %bitcast.12, s32[12,256]{1,0:T(8,128)} %now_ref.1, s32[12,256]{1,0:T(8,128)} %next_ref.1, bf16[256,128]{1,0:T(8,128)(2,1)} %fm_ref.1, bf16[192,128]{1,0:T(8,128)(2,1)} %bitcast.13, ...), custom_call_target="tpu_custom_call" | custom-call | flops 1000000000 | bytes 100000 | tf_op jit(solution)/shard_map/layer_backward/pallas_call | solution.py:282
  15.3 4.8 %all-to-all-start = ((bf16[16,368,128]{2,1,0:T(8,128)(2,1)}), bf16[16,368,128]{2,1,0:T(8,128)(2,1)S(1)}, u32[]{:S(2)}, u32[]{:S(2)}) async-start(bf16[16,368,128]{2,1,0:T(8,128)(2,1)} %layer_backward.1), calls=%async_computation | async-start | bytes 3014656 | tf_op jit(solution)/shard_map/all_to_all | solution.py:61
  20.2 3.7 %collective-permute-done.crossed_t = bf16[8,192,128]{2,1,0:T(8,128)(2,1)} collective-permute-done((bf16[8,192,128]{2,1,0:T(8,128)(2,1)S(1)}, bf16[8,192,128]{2,1,0:T(8,128)(2,1)}, u32[]{:S(2)}, u32[]{:S(2)}) %collective-permute-start) | collective-permute-done | bytes 393248 | tf_op jit(solution)/shard_map/ppermute | solution.py:603
  23.9 1.3 %stack_tables.1.stacked = bf16[2,256,1024]{2,1,0:T(8,128)(2,1)S(1)} custom-call(s32[1]{0:T(128)} %bitcast.half_ref, bf16[8,192,128]{2,1,0:T(8,128)(2,1)S(1)} %dynamic-slice_bitcast_fusion.mine_t, bf16[8,192,128]{2,1,0:T(8,128)(2,1)} %collective-permute-done.crossed_t), custom_call_target="tpu_custom_call" | custom-call | flops 99999997952 | bytes 100000 | tf_op jit(solution)/shard_map/stack_tables/pallas_call | solution.py:407
  25.2 1.0 %copy-done.5 = bf16[2,256,1024]{2,1,0:T(8,128)(2,1)} copy-done((bf16[2,256,1024]{2,1,0:T(8,128)(2,1)}, bf16[2,256,1024]{2,1,0:T(8,128)(2,1)S(1)}, u32[]{:S(2)}) %copy-start.5) | copy-done | bytes 1048600
  26.1 16.4 %all-to-all-done.dense_ref.ids_ref.seen = bf16[16,368,128]{2,1,0:T(8,128)(2,1)S(1)} async-done(((bf16[16,368,128]{2,1,0:T(8,128)(2,1)}), bf16[16,368,128]{2,1,0:T(8,128)(2,1)S(1)}, u32[]{:S(2)}, u32[]{:S(2)}) %all-to-all-start) | async-done | bytes 1507360 | tf_op jit(solution)/shard_map/all_to_all | solution.py:61
  42.7 0.5 collective-permute-start.1
  43.7 2.2 %part_other.1 = bf16[4,8,48,128]{3,2,1,0:T(8,128)(2,1)} custom-call(s32[1]{0:T(128)} %bitcast.half_ref, bf16[16,368,128]{2,1,0:T(8,128)(2,1)S(1)} %all-to-all-done.dense_ref.ids_ref.seen, f32[16,16,128]{2,1,0:T(8,128)S(1)} %get-tuple-element.20.ids_ref.all_ids), custom_call_target="tpu_custom_call" | custom-call | flops 1000000000 | bytes 100000 | tf_op jit(solution)/shard_map/part_other/pallas_call | solution.py:385
  45.8 2.0 %collective-permute-start.2 = (bf16[4,8,48,128]{3,2,1,0:T(8,128)(2,1)}, bf16[4,8,48,128]{3,2,1,0:T(8,128)(2,1)S(1)}, u32[]{:S(2)}, u32[]{:S(2)}) collective-permute-start(bf16[4,8,48,128]{3,2,1,0:T(8,128)(2,1)} %part_other.1), channel_id=1, source_target_pairs={{0,4},{4,0},{1,5},{5,1},{2,6},{6,2},{3,7},{7,3},{8,12},{12,8},{9,1... | collective-permute-start | bytes 1179656 | tf_op jit(solution)/shard_map/ppermute | solution.py:603
  47.9 3.8 %lookup.1.rows = bf16[16,352,128]{2,1,0:T(8,128)(2,1)} custom-call(bf16[2,256,1024]{2,1,0:T(8,128)(2,1)S(1)} %copy-done.6, f32[16,16,128]{2,1,0:T(8,128)S(1)} %get-tuple-element.20.ids_ref.all_ids), custom_call_target="tpu_custom_call" | custom-call | flops 99999997952 | bytes 100000 | tf_op jit(solution)/shard_map/lookup/pallas_call | solution.py:449
  51.6 0.8 fill_dense.1
  52.4 3.7 %all-to-all-start.1 = ((bf16[16,352,128]{2,1,0:T(8,128)(2,1)}), bf16[16,352,128]{2,1,0:T(8,128)(2,1)S(1)}, u32[]{:S(2)}, u32[]{:S(2)}) async-start(bf16[16,352,128]{2,1,0:T(8,128)(2,1)} %get-tuple-element.22), calls=%async_computation.1 | async-start | bytes 2883584 | tf_op jit(solution)/shard_map/all_to_all | solution.py:61
  56.1 3.7 %part_own.1.own = f32[4,8,48,128]{3,2,1,0:T(8,128)} custom-call(s32[1]{0:T(128)} %bitcast.half_ref, bf16[16,368,128]{2,1,0:T(8,128)(2,1)} %copy-done.1, f32[16,16,128]{2,1,0:T(8,128)} %copy-done.3, f32[8,128]{1,0:T(8,128)} %get-tuple-element.24.refs_0_.after), custom_call_target="tpu_custom_call" | custom-call | flops 1000000000 | bytes 100000 | tf_op jit(solution)/shard_map/part_own/pallas_call | solution.py:385
  59.8 6.7 %collective-permute-done.2.seen = bf16[4,8,48,128]{3,2,1,0:T(8,128)(2,1)S(1)} collective-permute-done((bf16[4,8,48,128]{3,2,1,0:T(8,128)(2,1)}, bf16[4,8,48,128]{3,2,1,0:T(8,128)(2,1)S(1)}, u32[]{:S(2)}, u32[]{:S(2)}) %collective-permute-start.2) | collective-permute-done | bytes 393248 | tf_op jit(solution)/shard_map/ppermute | solution.py:603
  66.5 1.1 %copy-done.2 = f32[4,8,48,128]{3,2,1,0:T(8,128)S(1)} copy-done((f32[4,8,48,128]{3,2,1,0:T(8,128)S(1)}, f32[4,8,48,128]{3,2,1,0:T(8,128)}, u32[]{:S(2)}) %copy-start.2) | copy-done | bytes 786456
  67.7 0.7 combine.1
  68.4 0.9 %collective-permute-start.3 = (bf16[8,48,128]{2,1,0:T(8,128)(2,1)}, bf16[8,48,128]{2,1,0:T(8,128)(2,1)S(1)}, u32[]{:S(2)}, u32[]{:S(2)}) collective-permute-start(bf16[8,48,128]{2,1,0:T(8,128)(2,1)} %get-tuple-element.26), channel_id=1, source_target_pairs={{0,8},{8,0},{16,24},{24,16},{1,9},{9,1},{17,25},{25,17},{2,10},{10... | collective-permute-start | bytes 294920 | tf_op jit(solution)/shard_map/ppermute | solution.py:630
  69.3 1.6 %collective-permute-start.4 = (bf16[8,48,128]{2,1,0:T(8,128)(2,1)}, bf16[8,48,128]{2,1,0:T(8,128)(2,1)S(1)}, u32[]{:S(2)}, u32[]{:S(2)}) collective-permute-start(bf16[8,48,128]{2,1,0:T(8,128)(2,1)} %get-tuple-element.27), channel_id=1, source_target_pairs={{0,16},{8,24},{16,0},{24,8},{1,17},{9,25},{17,1},{25,9},{2,18},{10... | collective-permute-start | bytes 294920 | tf_op jit(solution)/shard_map/ppermute | solution.py:630
  70.9 1.0 %collective-permute-start.5 = (bf16[8,48,128]{2,1,0:T(8,128)(2,1)}, bf16[8,48,128]{2,1,0:T(8,128)(2,1)S(1)}, u32[]{:S(2)}, u32[]{:S(2)}) collective-permute-start(bf16[8,48,128]{2,1,0:T(8,128)(2,1)} %get-tuple-element.28), channel_id=1, source_target_pairs={{0,24},{8,16},{16,8},{24,0},{1,25},{9,17},{17,9},{25,1},{2,26},{10... | collective-permute-start | bytes 294920 | tf_op jit(solution)/shard_map/ppermute | solution.py:630
  71.9 11.8 %all-to-all-done.1.dense_ref.left0.left1.right0.right1 = bf16[16,352,128]{2,1,0:T(8,128)(2,1)S(1)} async-done(((bf16[16,352,128]{2,1,0:T(8,128)(2,1)}), bf16[16,352,128]{2,1,0:T(8,128)(2,1)S(1)}, u32[]{:S(2)}, u32[]{:S(2)}) %all-to-all-start.1) | async-done | bytes 1441824 | tf_op jit(solution)/shard_map/all_to_all | solution.py:61
  83.7 2.6 %unpack_rows.1 = (bf16[12,192,256]{2,1,0:T(8,128)(2,1)}, f32[256,128]{1,0:T(8,128)}, f32[192,128]{1,0:T(8,128)}, f32[256,256]{1,0:T(8,128)}, f32[1,192]{1,0:T(1,128)}, /*index=5*/f32[8,128]{1,0:T(8,128)S(1)}) custom-call(bf16[16,352,128]{2,1,0:T(8,128)(2,1)S(1)} %all-to-all-done.1.dense_ref.left0.left1.right0.right1, ...), custom_call_target="tpu_custom_call" | custom-call | flops 1000000000 | bytes 100000 | tf_op jit(solution)/shard_map/unpack_rows/pallas_call | solution.py:540
  86.3 1.1 %finish_tables.1 = f32[32,32,192]{2,1,0:T(8,128)} custom-call(s32[1]{0:T(128)} %bitcast.7.place, bf16[8,48,128]{2,1,0:T(8,128)(2,1)S(1)} %get-tuple-element.25.refs_0_, bf16[8,48,128]{2,1,0:T(8,128)(2,1)S(1)} %collective-permute-done.3.refs_1_, bf16[8,48,128]{2,1,0:T(8,128)(2,1)S(1)} %collective-permute-done.4.refs_2_, ...), custom_call_target="tpu_custom_call" | custom-call | bytes 100000 | tf_op jit(solution)/shard_map/finish_tables/pallas_call | solution.py:591
  (17 shorter events, 0.6 us)
Async XLA Ops:
  0.6 1.4 %copy-start = (bf16[32,128,192]{1,2,0:T(8,128)(2,1)S(1)}, bf16[32,128,192]{1,2,0:T(8,128)(2,1)}, u32[]{:S(2)}) copy-start(bf16[32,128,192]{1,2,0:T(8,128)(2,1)} %param.13) | copy-start | bytes 4718596
  2.1 21.8 %collective-permute-start = (bf16[8,192,128]{2,1,0:T(8,128)(2,1)S(1)}, bf16[8,192,128]{2,1,0:T(8,128)(2,1)}, u32[]{:S(2)}, u32[]{:S(2)}) collective-permute-start(bf16[8,192,128]{2,1,0:T(8,128)(2,1)S(1)} %dynamic-slice_bitcast_fusion.mine_t), channel_id=1, source_target_pairs={{0,4},{4,0},{1,5},{5,1},{2,6},{6,2},{3,7},{7,3},{8,12},{12,8},{9,1... | collective-permute-start | bytes 1179656 | tf_op jit(solution)/shard_map/ppermute | solution.py:603
  15.3 27.2 %all-to-all-start = ((bf16[16,368,128]{2,1,0:T(8,128)(2,1)}), bf16[16,368,128]{2,1,0:T(8,128)(2,1)S(1)}, u32[]{:S(2)}, u32[]{:S(2)}) async-start(bf16[16,368,128]{2,1,0:T(8,128)(2,1)} %layer_backward.1), calls=%async_computation | async-start | bytes 3014656 | tf_op jit(solution)/shard_map/all_to_all | solution.py:61
  25.1 1.0 %copy-start.5 = (bf16[2,256,1024]{2,1,0:T(8,128)(2,1)}, bf16[2,256,1024]{2,1,0:T(8,128)(2,1)S(1)}, u32[]{:S(2)}) copy-start(bf16[2,256,1024]{2,1,0:T(8,128)(2,1)S(1)} %stack_tables.1.stacked) | copy-start | bytes 3145732
  42.5 1.2 %copy-start.1 = (bf16[16,368,128]{2,1,0:T(8,128)(2,1)}, bf16[16,368,128]{2,1,0:T(8,128)(2,1)S(1)}, u32[]{:S(2)}) copy-start(bf16[16,368,128]{2,1,0:T(8,128)(2,1)S(1)} %all-to-all-done.dense_ref.ids_ref.seen) | copy-start | bytes 4521988
  42.7 5.2 %copy-start.3 = (f32[16,16,128]{2,1,0:T(8,128)}, f32[16,16,128]{2,1,0:T(8,128)S(1)}, u32[]{:S(2)}) copy-start(f32[16,16,128]{2,1,0:T(8,128)S(1)} %get-tuple-element.20.ids_ref.all_ids) | copy-start | bytes 393220
  42.7 8.9 %collective-permute-start.1 = (f32[64,128]{1,0:T(8,128)S(1)}, f32[64,128]{1,0:T(8,128)S(1)}, u32[]{:S(2)}, u32[]{:S(2)}) collective-permute-start(f32[64,128]{1,0:T(8,128)S(1)} %get-tuple-element.21.own), channel_id=1, source_target_pairs={{0,4},{4,0},{1,5},{5,1},{2,6},{6,2},{3,7},{7,3},{8,12},{12,8},{9,1... | collective-permute-start | bytes 98312 | tf_op jit(solution)/shard_map/ppermute | solution.py:603
  43.7 4.2 %copy-start.6 = (bf16[2,256,1024]{2,1,0:T(8,128)(2,1)S(1)}, bf16[2,256,1024]{2,1,0:T(8,128)(2,1)}, u32[]{:S(2)}) copy-start(bf16[2,256,1024]{2,1,0:T(8,128)(2,1)} %copy-done.5) | copy-start | bytes 3145732
  45.8 20.7 %collective-permute-start.2 = (bf16[4,8,48,128]{3,2,1,0:T(8,128)(2,1)}, bf16[4,8,48,128]{3,2,1,0:T(8,128)(2,1)S(1)}, u32[]{:S(2)}, u32[]{:S(2)}) collective-permute-start(bf16[4,8,48,128]{3,2,1,0:T(8,128)(2,1)} %part_other.1), channel_id=1, source_target_pairs={{0,4},{4,0},{1,5},{5,1},{2,6},{6,2},{3,7},{7,3},{8,12},{12,8},{9,1... | collective-permute-start | bytes 1179656 | tf_op jit(solution)/shard_map/ppermute | solution.py:603
  52.4 31.3 %all-to-all-start.1 = ((bf16[16,352,128]{2,1,0:T(8,128)(2,1)}), bf16[16,352,128]{2,1,0:T(8,128)(2,1)S(1)}, u32[]{:S(2)}, u32[]{:S(2)}) async-start(bf16[16,352,128]{2,1,0:T(8,128)(2,1)} %get-tuple-element.22), calls=%async_computation.1 | async-start | bytes 2883584 | tf_op jit(solution)/shard_map/all_to_all | solution.py:61
  56.1 10.4 %copy-start.4 = (f32[8,128]{1,0:T(8,128)S(1)}, f32[8,128]{1,0:T(8,128)}, u32[]{:S(2)}) copy-start(f32[8,128]{1,0:T(8,128)} %get-tuple-element.24.refs_0_.after) | copy-start | bytes 12292
  66.5 1.1 %copy-start.2 = (f32[4,8,48,128]{3,2,1,0:T(8,128)S(1)}, f32[4,8,48,128]{3,2,1,0:T(8,128)}, u32[]{:S(2)}) copy-start(f32[4,8,48,128]{3,2,1,0:T(8,128)} %part_own.1.own) | copy-start | bytes 2359300
  68.4 17.9 %collective-permute-start.3 = (bf16[8,48,128]{2,1,0:T(8,128)(2,1)}, bf16[8,48,128]{2,1,0:T(8,128)(2,1)S(1)}, u32[]{:S(2)}, u32[]{:S(2)}) collective-permute-start(bf16[8,48,128]{2,1,0:T(8,128)(2,1)} %get-tuple-element.26), channel_id=1, source_target_pairs={{0,8},{8,0},{16,24},{24,16},{1,9},{9,1},{17,25},{25,17},{2,10},{10... | collective-permute-start | bytes 294920 | tf_op jit(solution)/shard_map/ppermute | solution.py:630
  69.3 16.9 %collective-permute-start.4 = (bf16[8,48,128]{2,1,0:T(8,128)(2,1)}, bf16[8,48,128]{2,1,0:T(8,128)(2,1)S(1)}, u32[]{:S(2)}, u32[]{:S(2)}) collective-permute-start(bf16[8,48,128]{2,1,0:T(8,128)(2,1)} %get-tuple-element.27), channel_id=1, source_target_pairs={{0,16},{8,24},{16,0},{24,8},{1,17},{9,25},{17,1},{25,9},{2,18},{10... | collective-permute-start | bytes 294920 | tf_op jit(solution)/shard_map/ppermute | solution.py:630
  70.9 15.4 %collective-permute-start.5 = (bf16[8,48,128]{2,1,0:T(8,128)(2,1)}, bf16[8,48,128]{2,1,0:T(8,128)(2,1)S(1)}, u32[]{:S(2)}, u32[]{:S(2)}) collective-permute-start(bf16[8,48,128]{2,1,0:T(8,128)(2,1)} %get-tuple-element.28), channel_id=1, source_target_pairs={{0,24},{8,16},{16,8},{24,0},{1,25},{9,17},{17,9},{25,1},{2,26},{10... | collective-permute-start | bytes 294920 | tf_op jit(solution)/shard_map/ppermute | solution.py:630

commit v10 on v9

--- a/solution.py
+++ b/solution.py
@@ -139,8 +139,7 @@
         self.half = self.left + self.left // 2
         self.dense = 2 * self.half
         self.share = 1024 // peers
-        self.ids = self.dense + self.share
-        self.back = 2 * self.half + self.share
+        self.rows = self.dense + self.share
         self.back_left = (self.share, self.share + self.left)
         self.back_right = (self.share + 2 * self.left, self.share + 2 * self.left + self.left // 2)
 
@@ -151,15 +150,17 @@
 
 def backward_kernel(
     n_grp, n_lane, wire,
-    half_ref, x_ref, u_ref, now_ref, next_ref, fm_ref, proj_t_ref, lcb_ref, gain_ref,
-    out_ref,
+    half_ref, x_ref, u_any, now_ref, next_ref, fm_ref, proj_t_ref, lcb_ref, gain_ref,
+    out_any,
     fm_t, proj, lcb_t, gains, eye, mixed, p_t, g_t, d_sum, d_p_t, left_in, right_in, grads, turned, ids,
+    u_ref, out_ref, sems,
 ):
     count, width, features = x_ref.shape
     rank = fm_ref.shape[1]
     peers = n_grp * n_lane
     scale = 1.0 / width
-    samples = range(count)
+    load = pltpu.make_async_copy(u_any, u_ref, sems.at[0])
+    load.start()
 
     turned_fm = fm_ref[...].astype(F32).T.astype(BF16)
     fm_t[...] = turned_fm
@@ -169,19 +170,19 @@
     gains[:, 0:128] = column
     gains[:, 128:256] = column
     eye[...] = identity(features, features)
-
-    x_all = x_ref[...].reshape(count * width, features)
-    left_in[:, :, 0:rank] = mm(x_all, fm_ref[...]).astype(BF16).reshape(count, width, rank)
-    mixed[...] = mm(x_all, lcb_ref[...]).reshape(count, width, features)
-    for s in samples:
+    sum_gain, sum_fm_t, sum_proj_t = [], [], []
+
+    def project(s):
         p_t[s] = mm_nt(fm_t[...], x_ref[s]).astype(BF16)
-        right_in[s, rank : 2 * rank] = turned_fm
-    for s in samples:
+        right_in[s, rank : 2 * rank] = fm_t[...]
+
+    def interact(s):
         g_t[s] = mm(p_t[s], x_ref[s]).astype(BF16)
-    for s in samples:
+
+    def add_up(s):
         mixed[s] = mixed[s] + mm(proj_t_ref[...], g_t[s])
-    sum_gain = 0.0
-    for s in samples:
+
+    def normalise(s):
         summed = x_ref[s].astype(F32) + mixed[s]
         centre = jnp.sum(summed, axis=0, keepdims=True) * scale
         summed = summed - centre
@@ -194,26 +195,49 @@
         second = jnp.sum(scaled * normed, axis=0, keepdims=True) * scale
         d_sum[s] = (inverse * (scaled - first - normed * second)).astype(BF16)
         product_gain = upper * normed
-        sum_gain += product_gain[:, 0:128] + product_gain[:, 128:256]
-    for s in samples:
+        sum_gain.append(product_gain[:, 0:128] + product_gain[:, 128:256])
+
+    def back_rows(s):
         right_in[s, 0:rank] = mm(proj[...], d_sum[s]).astype(BF16)
-    for s in samples:
+
+    def back_project(s):
         left_in[s, :, rank : 2 * rank] = mm_nt(x_ref[s], right_in[s, 0:rank]).astype(BF16)
         d_p_t[s] = mm_nt(right_in[s, 0:rank], x_ref[s]).astype(BF16)
-    d_all = d_sum[...].reshape(count * width, features)
-    mixed[...] = mm(d_all, lcb_t[...]).reshape(count, width, features)
-    for s in samples:
-        grad = d_sum[s].astype(F32) + mixed[s] + mm(left_in[s], right_in[s])
+
+    def gather(s):
+        grad = d_sum[s].astype(F32) + mm(d_sum[s], lcb_t[...]) + mm(left_in[s], right_in[s])
         grad = grad.astype(BF16)
         group, k = s // STEP, s % STEP
         grads[group, k * 128 : k * 128 + 128] = grad[0:128]
         at = 512 + 64 * (2 * (k % 2) + k // 2)
         grads[group, at : at + 64] = grad[128:192]
-    sum_lcb = mm(x_all, d_all, ((0,), (0,)))
-    sum_fm_t, sum_proj_t = 0.0, 0.0
-    for s in samples:
-        sum_fm_t += mm(d_p_t[s], x_ref[s])
-        sum_proj_t += mm_nt(d_sum[s], g_t[s])
+        sum_fm_t.append(mm(d_p_t[s], x_ref[s]))
+        sum_proj_t.append(mm_nt(d_sum[s], g_t[s]))
+
+    x_all = x_ref[...].reshape(count * width, features)
+    left_in[:, :, 0:rank] = mm(x_all, fm_ref[...]).astype(BF16).reshape(count, width, rank)
+    mixed[...] = mm(x_all, lcb_ref[...]).reshape(count, width, features)
+    ahead, behind = range(count // 2), range(count // 2, count)
+    for stage in (project, interact, add_up):
+        for s in ahead:
+            stage(s)
+    load.wait()
+    for one, other in zip(ahead, behind):
+        normalise(one)
+        project(other)
+    for one, other in zip(ahead, behind):
+        back_rows(one)
+        interact(other)
+    for one, other in zip(ahead, behind):
+        back_project(one)
+        add_up(other)
+    for one, other in zip(ahead, behind):
+        gather(one)
+        normalise(other)
+    for stage in (back_rows, back_project, gather):
+        for s in behind:
+            stage(s)
+    sum_gain, sum_fm_t, sum_proj_t = sum(sum_gain), sum(sum_fm_t), sum(sum_proj_t)
 
     half = half_ref[0]
     for group in range(count // STEP):
@@ -232,13 +256,30 @@
                 row = base + wire.left + group * 16
                 out_ref[peer, row : row + 16] = right.astype(BF16)
 
+    first_store = pltpu.make_async_copy(
+        out_ref.at[:, 0 : wire.dense], out_any.at[:, 0 : wire.dense], sems.at[1]
+    )
+    first_store.start()
+
+    sum_lcb = mm(x_all, d_sum[...].reshape(count * width, features), ((0,), (0,)))
     part = features // peers
     third = width // peers
     total = jnp.sum(sum_gain.T, axis=0, keepdims=True)
     high = total.astype(BF16).astype(F32)
-    low = total - high
-    middle = jnp.concatenate([high[:, 128:192], low[:, 128:192]], axis=1)
-    gain_rows = [high[:, 0:128], middle, low[:, 0:128], jnp.zeros((1, LANES), F32)]
+    shares = jnp.concatenate([high, total - high, jnp.zeros((2, width), F32)], axis=0)
+    shares = jnp.concatenate([shares, jnp.zeros((4, 256 - width), F32)], axis=1)
+
+    lane = lax.broadcasted_iota(jnp.int32, (16, LANES), 1)
+    sample = lax.broadcasted_iota(jnp.int32, (16, LANES), 0)
+    mine = (lane // TILE == sample) & (sample < count)
+    behind_ids = (lane[0:4] >= wire.left) & (lane[0:4] < wire.left + third)
+    spread_ids = []
+    for which, ref in enumerate((now_ref, next_ref)):
+        ids[which] = jnp.zeros_like(ids[which])
+        ids[which, 0:count] = ref[...].astype(F32)
+        for side in range(2):
+            line = ids[which, :, side * 128 : side * 128 + 128]
+            spread_ids.append(pltpu.roll(line, 0, 1, stride=TILE, stride_axis=0))
     sum_fm = sum_fm_t.T
     for peer in range(peers):
         at = wire.dense
@@ -246,27 +287,21 @@
         out_ref[peer, at : at + part] = sum_fm[here].astype(BF16)
         out_ref[peer, at + part : at + 2 * part] = sum_lcb[here, 0:128].astype(BF16)
         out_ref[peer, at + 2 * part : at + 3 * part] = sum_lcb[here, 128:256].astype(BF16)
-        last = [sum_proj_t[peer * third : (peer + 1) * third]] + gain_rows
-        out_ref[peer, at + 3 * part : at + 4 * part] = jnp.concatenate(last, axis=0).astype(BF16)
-
-    lane = lax.broadcasted_iota(jnp.int32, (16, LANES), 1)
-    sample = lax.broadcasted_iota(jnp.int32, (16, LANES), 0)
-    mine = (lane // TILE == sample) & (sample < count)
-    spread_ids = []
-    for which, ref in enumerate((now_ref, next_ref)):
-        ids[which] = jnp.zeros_like(ids[which])
-        ids[which, 0:count] = ref[...].astype(F32)
-        for side in range(2):
-            line = ids[which, :, side * 128 : side * 128 + 128]
-            spread_ids.append(pltpu.roll(line, 0, 1, stride=TILE, stride_axis=0))
-    for peer in range(peers):
-        at = place_of(n_grp, n_lane, peer)
+        place = place_of(n_grp, n_lane, peer)
         lines = []
         for line in spread_ids:
-            line = pltpu.roll(line, LANES - at, 1) if at else line
+            line = pltpu.roll(line, LANES - place, 1) if place else line
             lines.append(jnp.sum(jnp.where(mine, line, 0.0), axis=0, keepdims=True))
-        lines.append(jnp.zeros((12, LANES), F32))
-        out_ref[peer, wire.ids : wire.ids + 16] = jnp.concatenate(lines, axis=0).astype(BF16)
+        share = pltpu.roll(shares, (wire.left - peer * third) % 256, 1)[:, 0:128]
+        lines = jnp.where(behind_ids, share, jnp.concatenate(lines, axis=0))
+        last = jnp.concatenate([sum_proj_t[peer * third : (peer + 1) * third], lines], axis=0)
+        out_ref[peer, at + 3 * part : at + 4 * part] = last.astype(BF16)
+    second_store = pltpu.make_async_copy(
+        out_ref.at[:, wire.dense : wire.rows], out_any.at[:, wire.dense : wire.rows], sems.at[2]
+    )
+    second_store.start()
+    first_store.wait()
+    second_store.wait()
 
 
 def backward(n_grp, n_lane, wire, half, pooled_t, upstream_t, ids_now, ids_next, w_fm, w_proj_t, w_lcb, gain):
@@ -278,12 +313,13 @@
         return pl.BlockSpec(shape, lambda i: (0,) * len(shape))
 
     operands = (pooled_t, upstream_t, ids_now, ids_next, w_fm, w_proj_t, w_lcb, gain.reshape(1, width))
-    shape = (peers, wire.ids + 16, LANES)
+    shape = (peers, wire.rows, LANES)
+    free = pl.BlockSpec(memory_space=pl.ANY)
     return pl.pallas_call(
         functools.partial(backward_kernel, n_grp, n_lane, wire),
         grid=(1,),
-        in_specs=[SMEM] + [whole(array.shape) for array in operands],
-        out_specs=whole(shape),
+        in_specs=[SMEM, whole(pooled_t.shape), free] + [whole(array.shape) for array in operands[2:]],
+        out_specs=free,
         out_shape=pltpu.HBM(shape, BF16),
         scratch_shapes=[
             pltpu.VMEM((rank, features), BF16),
@@ -301,6 +337,9 @@
             pltpu.VMEM((count // STEP, STEP * width, features), BF16),
             pltpu.VMEM((count // STEP, 2, features // 2, STEP * width), F32),
             pltpu.VMEM((2, 16, features), F32),
+            pltpu.VMEM(upstream_t.shape, BF16),
+            pltpu.VMEM(shape, BF16),
+            pltpu.SemaphoreType.DMA((3,)),
         ],
         compiler_params=params(2),
         cost_estimate=cost(1),
@@ -319,7 +358,7 @@
 def half_dense(wire, seen):
     peers = seen.shape[0]
     rows = wire.share // 2
-    at_ids = wire.ids // 16
+    at_ids = wire.rows // 16 - 1
     return pl.pallas_call(
         dense_kernel,
         grid=(2,),
@@ -344,15 +383,14 @@
 def part_kernel(n_grp, wire, other, half_ref, seen, all_ids, *refs):
     out, held = refs[-2:]
     peers = seen.shape[0]
-    base = 0 if other else wire.half
     half = 1 - half_ref[0] if other else half_ref[0]
     lane = lax.broadcasted_iota(jnp.int32, (1, LANES), 1)
     start = ((lane % TILE) * LANES).astype(F32)
     keys = []
     for peer in range(peers):
         at = peer * LANES
-        held[at : at + wire.left, 0:128] = seen[peer, base : base + wire.left]
-        right = seen[peer, base + wire.left : base + wire.half]
+        held[at : at + wire.left, 0:128] = seen[peer, 0 : wire.left]
+        right = seen[peer, wire.left : wire.half]
         turned = turn(right.astype(F32)).astype(BF16)
         for i in range(wire.left // 32):
             held[at + 32 * i : at + 32 * i + 16, 128:256] = right[16 * i : 16 * i + 16]
@@ -360,7 +398,7 @@
         if wire.left < LANES:
             held[at + wire.left : at + LANES] = jnp.zeros((LANES - wire.left, 256), BF16)
         ids = all_ids[peer]
-        key = jnp.where(half == 0, ids[0:1], ids[1:2]) + start
+        key = jnp.where(half == 0, ids[12:13], ids[13:14]) + start
         keys.append(jnp.where(lane < wire.left, key, -1.0))
     keys = jnp.concatenate(keys, axis=1)
     piece = LANES // n_grp
@@ -382,16 +420,42 @@
     peers = seen.shape[0]
     piece = LANES // n_grp
     shape = (n_grp, TILE, piece + piece // 2, LANES)
+    which = 0 if other else 1
     return pl.pallas_call(
         functools.partial(part_kernel, n_grp, wire, other),
-        in_specs=[SMEM, VMEM, VMEM] + [pl.BlockSpec(memory_space=pl.ANY)] * len(after),
-        out_specs=VMEM,
+        grid=(1,),
+        in_specs=[
+            SMEM,
+            pl.BlockSpec((peers, wire.half, LANES), lambda i: (0, which, 0)),
+            pl.BlockSpec(ids.shape, lambda i: (0, 0, 0)),
+        ]
+        + [pl.BlockSpec(memory_space=pl.ANY)] * len(after),
+        out_specs=pl.BlockSpec(shape, lambda i: (0, 0, 0, 0)),
         out_shape=jax.ShapeDtypeStruct(shape, BF16 if other else F32),
         scratch_shapes=[pltpu.VMEM((peers * LANES, 256), BF16)],
         compiler_params=params(1 if other else 2),
         cost_estimate=cost(1),
         name="part_other" if other else "part_own",
     )(half, seen, ids, *after)
+
+
+def take_kernel(place, tables, out, sem):
+    copy = pltpu.make_async_copy(tables.at[pl.ds(place[0] * TILE, TILE)], out, sem)
+    copy.start()
+    copy.wait()
+
+
+def take_tables(place, tables_t):
+    return pl.pallas_call(
+        take_kernel,
+        in_specs=[SMEM, pl.BlockSpec(memory_space=pl.ANY)],
+        out_specs=pl.BlockSpec(memory_space=pl.ANY),
+        out_shape=pltpu.HBM((TILE,) + tables_t.shape[1:], BF16),
+        scratch_shapes=[pltpu.SemaphoreType.DMA],
+        compiler_params=params(2),
+        cost_estimate=cost(1),
+        name="take_tables",
+    )(place, tables_t)
 
 
 def stack_kernel(half_ref, mine_t, crossed_t, out):
@@ -426,7 +490,7 @@
     for which in range(2):
         same = []
         for peer in range(peers):
-            at = peer * 16 + 2 + which
+            at = peer * 16 + 14 + which
             same.append(jnp.where(keys[0 : wire.left, at : at + 1] == lane, 1.0, 0.0))
         same = jnp.concatenate(same, axis=0).astype(BF16)
         hit = jnp.concatenate([same * mask for mask in masks], axis=1)
@@ -453,8 +517,8 @@
             pl.BlockSpec(stacked.shape, lambda i: (0, 0, 0)),
             pl.BlockSpec((some, 16, LANES), lambda i: (i, 0, 0)),
         ],
-        out_specs=pl.BlockSpec((some, wire.back, LANES), lambda i: (i, 0, 0)),
-        out_shape=pltpu.HBM((peers, wire.back, LANES), BF16),
+        out_specs=pl.BlockSpec((some, wire.rows, LANES), lambda i: (i, 0, 0)),
+        out_shape=pltpu.HBM((peers, wire.rows, LANES), BF16),
         compiler_params=params(),
         cost_estimate=cost(100),
         name="lookup",
@@ -487,9 +551,21 @@
     )(rows, own, seen)
 
 
-def unpack_kernel(n_grp, n_lane, dense_ref, left0, left1, right0, right1, rows_out, fm, proj_t, lcb, gain, token, held):
+def finish_pieces(grp, pieces, out):
+    piece = out.shape[1]
+    for k, seen in enumerate(pieces):
+        base = jnp.bitwise_xor(grp, k) * TILE
+        for f in range(TILE):
+            out[base + f, :, 0:128] = seen[f, 0:piece].astype(F32)
+            packed = seen[f, piece : piece + piece // 2].astype(F32)
+            out[base + f, 0 : piece // 2, 128:192] = packed[:, 0:64]
+            out[base + f, piece // 2 : piece, 128:192] = turn(packed)[:, 0:64]
+
+
+def unpack_kernel(n_grp, n_lane, wire, place, dense_ref, left0, left1, right0, right1, *refs):
+    pieces, refs = refs[:n_grp], refs[n_grp:]
+    rows_out, table_grad, fm, proj_t, lcb, gain, held = refs
     step = pl.program_id(0)
-    token[...] = jnp.zeros_like(token)
     peers = n_grp * n_lane
     for side, (left_ref, right_ref) in enumerate(((left0, right0), (left1, right1))):
         for q in range(n_lane):
@@ -514,6 +590,9 @@
     @pl.when(step == 0)
     def _():
         part, third = 256 // peers, 192 // peers
+        lane = lax.broadcasted_iota(jnp.int32, (1, LANES), 1)
+        behind_ids = (lane >= wire.left) & (lane < wire.left + third)
+        total = jnp.zeros((1, 256), F32)
         for peer in range(peers):
             dense = dense_ref[peer].astype(F32)
             here = slice(peer * part, (peer + 1) * part)
@@ -522,13 +601,17 @@
             lcb[here, 128:256] = dense[2 * part : 3 * part]
             last = dense[3 * part : 4 * part]
             proj_t[peer * third : (peer + 1) * third] = last[0:third]
-            if peer == 0:
-                last = last[third : third + 3]
-                gain[:, 0:128] = last[0:1] + last[2:3]
-                gain[:, 128:192] = (last + turn(last))[1:2, 0:64]
-
-
-def unpack(n_grp, n_lane, wire, count, seen):
+            share = jnp.where(behind_ids, last[third : third + 1] + last[third + 1 : third + 2], 0.0)
+            share = jnp.concatenate([share, jnp.zeros((1, LANES), F32)], axis=1)
+            total += pltpu.roll(share, (peer * third - wire.left) % 256, 1)
+        gain[...] = total[:, 0:192]
+
+    @pl.when(step == pl.num_programs(0) - 1)
+    def _():
+        finish_pieces(place[0], pieces, table_grad)
+
+
+def unpack(n_grp, n_lane, wire, count, place, seen, pieces):
     def whole(*shape):
         return pl.BlockSpec(shape, lambda i: (0,) * len(shape))
 
@@ -536,21 +619,22 @@
         return pl.BlockSpec((peers, rows, LANES), lambda i: (0, start // rows + i, 0))
 
     peers = n_grp * n_lane
-    shapes = [(256, 128), (192, 128), (256, 256), (1, 192), (8, 128)]
-    return pl.pallas_call(
-        functools.partial(unpack_kernel, n_grp, n_lane),
+    shapes = [(n_grp * TILE, pieces[0].shape[1] * 2 // 3, 192), (256, 128), (192, 128), (256, 256), (1, 192)]
+    return pl.pallas_call(
+        functools.partial(unpack_kernel, n_grp, n_lane, wire),
         grid=(count // STEP,),
-        in_specs=[pl.BlockSpec((peers, wire.share, LANES), lambda i: (0, 0, 0))]
+        in_specs=[SMEM, pl.BlockSpec((peers, wire.share, LANES), lambda i: (0, 0, 0))]
         + [part(32, start) for start in wire.back_left]
-        + [part(16, start) for start in wire.back_right],
+        + [part(16, start) for start in wire.back_right]
+        + [whole(*piece.shape) for piece in pieces],
         out_specs=[pl.BlockSpec((STEP, 192, 256), lambda i: (i, 0, 0))] + [whole(*shape) for shape in shapes],
         out_shape=[jax.ShapeDtypeStruct((count, 192, 256), BF16)]
         + [jax.ShapeDtypeStruct(shape, F32) for shape in shapes],
         scratch_shapes=[pltpu.VMEM((STEP, 256, 256), BF16)],
         compiler_params=params(),
         cost_estimate=cost(1),
-        name="unpack_rows",
-    )(seen, seen, seen, seen, seen)
+        name="unpack",
+    )(place, seen, seen, seen, seen, seen, *pieces)
 
 
 def combine_kernel(place, own, seen, after, *outs):
@@ -573,32 +657,6 @@
     )(place, own, seen, after)
 
 
-def finish_kernel(place, *refs):
-    out = refs[-1]
-    piece = out.shape[1]
-    for k, seen in enumerate(refs[:-2]):
-        base = jnp.bitwise_xor(place[0], k) * TILE
-        for f in range(TILE):
-            out[base + f, :, 0:128] = seen[f, 0:piece].astype(F32)
-            packed = seen[f, piece : piece + piece // 2].astype(F32)
-            out[base + f, 0 : piece // 2, 128:192] = packed[:, 0:64]
-            out[base + f, piece // 2 : piece, 128:192] = turn(packed)[:, 0:64]
-
-
-def finish(place, pieces, after):
-    n_grp = len(pieces)
-    piece = pieces[0].shape[1] * 2 // 3
-    return pl.pallas_call(
-        finish_kernel,
-        in_specs=[SMEM] + [VMEM] * n_grp + [pl.BlockSpec(memory_space=pl.ANY)],
-        out_specs=VMEM,
-        out_shape=jax.ShapeDtypeStruct((n_grp * TILE, piece, 192), F32),
-        compiler_params=params(),
-        cost_estimate=cost(0),
-        name="finish_tables",
-    )(place, *pieces, after)
-
-
 def cross(array):
     return lax.ppermute(array, "half", [(0, 1), (1, 0)])
 
@@ -610,7 +668,7 @@
     factor = 1.0 / (count * n_grp * 2 * n_lane)
     half = lax.axis_index("half").astype(jnp.int32)[None]
     grp = lax.axis_index("grp").astype(jnp.int32)
-    mine_t = lax.dynamic_slice_in_dim(tables.transpose(0, 2, 1), grp * TILE, TILE, 0)
+    mine_t = take_tables(grp[None], tables.transpose(0, 2, 1))
     crossed_t = cross(mine_t)
     sent = backward(
         n_grp, n_lane, wire, half,
@@ -624,12 +682,13 @@
     rows_wire, token = fill(wire, factor, rows_wire, dense, dense_seen)
     rows = exchange(rows_wire, PEER)
     own = part_sums(n_grp, wire, False, half, seen, ids, token)
-    next_rows, grad_fm, grad_proj_t, grad_lcb, grad_gain, token_out = unpack(n_grp, n_lane, wire, count, rows)
     pieces = combine(grp[None], own, part_seen, token)
     pieces = [pieces[0]] + [
         lax.ppermute(pieces[k], "grp", [(g, g ^ k) for g in range(n_grp)]) for k in range(1, n_grp)
     ]
-    table_grad = finish(grp[None], pieces, token_out)
+    next_rows, table_grad, grad_fm, grad_proj_t, grad_lcb, grad_gain = unpack(
+        n_grp, n_lane, wire, count, grp[None], rows, pieces
+    )
     return next_rows.transpose(0, 2, 1), table_grad, grad_fm, grad_proj_t.T, grad_lcb, grad_gain.reshape(-1)
 
 
@@ -647,7 +706,7 @@
             and w_fm.shape[1] == 128
             and pooled.shape[1] == n_grp * n_emb * TILE
             and count % STEP == 0
-            and count <= 16
+            and count <= 12
         )
         if fits:
             devices = mesh.devices.reshape(n_grp, 2, n_emb // 2)

time: 87.8 us -> 98 us (1.12)
  Pallas kernels: 25.4 us -> 34.6 us
  waiting for transfers between devices: 38.6 us -> 41.8 us
  local copies, waits for them, and re-layouts: 3.94 us -> 1.88 us
    pallas_call x4, Pallas kernels: 9.48 us -> 20.9 us  [the longest x1 13 us: take_tables(): pl.pallas_call(take_kernel, in_specs=[SMEM, pl.BlockSpec(memory_space=pl....]
    ppermute x3, waiting for transfers between devices: 0.01 us -> 9.86 us  [halves(): lax.ppermute(pieces[k], 'grp', [(g, g ^ k) for g in range(n_grp)])]
    all_to_all x2, waiting for transfers between devices: 28.2 us -> 20.9 us  [exchange(): return lax.all_to_all(blocks, axes, split_axis=0, concat_axis=0, tiled=True)]
    unnamed x14 -> x10, local copies, waits for them, and re-layouts: 3.92 us -> 1.88 us
    pallas_call x1, Pallas kernels: 1.27 us -> 0.28 us  [stack_tables(): pl.pallas_call(stack_kernel, in_specs=[SMEM, VMEM, VMEM], out_specs=VMEM,...]
  transfers between devices with their start and end apart: 8 -> 8, of which waited for: 4 -> 7; matrix products, arithmetic and copies ran while one was open for 0% -> 0% of each run, Pallas kernels for 28% -> 19%
where the time goes in v10:
time: 98 us; the launch traced here: 97.7 us
  waiting for transfers between devices  41.8 us (43%)
  Pallas kernels  34.6 us (35%)
  starting transfers between devices  18.7 us (19%)
  local copies, waits for them, and re-layouts  1.88 us (2%)
    all_to_all x2, waiting for transfers between devices, exchange(): return lax.all_to_all(blocks, axes, split_axis=0, concat_axis=0, tiled=True)  20.9 us
    pallas_call x1, Pallas kernels, take_tables(): pl.pallas_call(take_kernel, in_specs=[SMEM, pl.BlockSpec(memory_space=pl....  13 us
    ppermute x3, waiting for transfers between devices, cross(): return lax.ppermute(array, 'half', [(0, 1), (1, 0)])  11 us
    ppermute x3, waiting for transfers between devices, halves(): lax.ppermute(pieces[k], 'grp', [(g, g ^ k) for g in range(n_grp)])  9.86 us
    all_to_all x2, starting transfers between devices, exchange(): return lax.all_to_all(blocks, axes, split_axis=0, concat_axis=0, tiled=True)  8.68 us
    pallas_call x1, Pallas kernels, backward(): pl.pallas_call(functools.partial(backward_kernel, n_grp, n_lane, wire), g...  8.63 us
    ppermute x3, starting transfers between devices, cross(): return lax.ppermute(array, 'half', [(0, 1), (1, 0)])  6.43 us
    pallas_call x2, Pallas kernels, part_sums(): pl.pallas_call(functools.partial(part_kernel, n_grp, wire, other), grid=(...  4.83 us
  transfers between devices with their start and end apart: 8, of which 7 were waited for; matrix products, arithmetic and copies ran while one was open for 0% of the time, Pallas kernels for 19%

profile of v10, /device:TPU:0, one launch (start us, length us, event | category | flops | bytes accessed | tf_op | source)
XLA Modules:
  0.0 97.7 jit_solution(7084245097167679972)
XLA Ops:
  0.6 13.0 %take_tables.1.mine_t = bf16[8,192,128]{2,1,0:T(8,128)(2,1)} custom-call(s32[1]{0:T(128)} %bitcast.place, bf16[32,192,128]{2,1,0:T(8,128)(2,1)} %bitcast.14), custom_call_target="tpu_custom_call" | custom-call | flops 1000000000 | bytes 100000 | tf_op jit(solution)/shard_map/take_tables/pallas_call | solution.py:449
  13.7 4.1 %collective-permute-start = (bf16[8,192,128]{2,1,0:T(8,128)(2,1)}, bf16[8,192,128]{2,1,0:T(8,128)(2,1)S(1)}, u32[]{:S(2)}, u32[]{:S(2)}) collective-permute-start(bf16[8,192,128]{2,1,0:T(8,128)(2,1)} %take_tables.1.mine_t), channel_id=1, source_target_pairs={{0,4},{4,0},{1,5},{5,1},{2,6},{6,2},{3,7},{7,3},{8,12},{12,8},{9,1... | collective-permute-start | bytes 1179656 | tf_op jit(solution)/shard_map/ppermute | solution.py:661
  17.8 8.6 %layer_backward.1 = bf16[16,352,128]{2,1,0:T(8,128)(2,1)} custom-call(s32[1]{0:T(128)} %bitcast.1.half_ref, bf16[12,192,256]{2,1,0:T(8,128)(2,1)} %bitcast.10, bf16[12,192,256]{2,1,0:T(8,128)(2,1)} %bitcast.11, s32[12,256]{1,0:T(8,128)} %now_ref.1, s32[12,256]{1,0:T(8,128)} %next_ref.1, bf16[256,128]{1,0:T(8,128)(2,1)} %fm_ref.1, bf16[192,128]{1,0:T(8,128)(2,1)} %bitcast.12, ...), custom_call_target="tpu_custom_call" | custom-call | flops 1000000000 | bytes 100000 | tf_op jit(solution)/shard_map/layer_backward/pallas_call | solution.py:318
  26.4 5.0 %all-to-all-start = ((bf16[16,352,128]{2,1,0:T(8,128)(2,1)}), bf16[16,352,128]{2,1,0:T(8,128)(2,1)S(1)}, u32[]{:S(2)}, u32[]{:S(2)}) async-start(bf16[16,352,128]{2,1,0:T(8,128)(2,1)} %layer_backward.1), calls=%async_computation | async-start | bytes 2883584 | tf_op jit(solution)/shard_map/all_to_all | solution.py:61
  31.4 4.2 %collective-permute-done.crossed_t = bf16[8,192,128]{2,1,0:T(8,128)(2,1)S(1)} collective-permute-done((bf16[8,192,128]{2,1,0:T(8,128)(2,1)}, bf16[8,192,128]{2,1,0:T(8,128)(2,1)S(1)}, u32[]{:S(2)}, u32[]{:S(2)}) %collective-permute-start) | collective-permute-done | bytes 393248 | tf_op jit(solution)/shard_map/ppermute | solution.py:661
  35.6 0.3 stack_tables.1.stacked
  35.9 17.9 %all-to-all-done.dense_ref.ids_ref.seen = bf16[16,352,128]{2,1,0:T(8,128)(2,1)S(1)} async-done(((bf16[16,352,128]{2,1,0:T(8,128)(2,1)}), bf16[16,352,128]{2,1,0:T(8,128)(2,1)S(1)}, u32[]{:S(2)}, u32[]{:S(2)}) %all-to-all-start) | async-done | bytes 1441824 | tf_op jit(solution)/shard_map/all_to_all | solution.py:61
  54.2 0.7 copy-done
  54.9 1.5 %part_other.1 = bf16[4,8,48,128]{3,2,1,0:T(8,128)(2,1)S(1)} custom-call(s32[1]{0:T(128)} %bitcast.1.half_ref, bf16[16,352,128]{2,1,0:T(8,128)(2,1)S(1)} %all-to-all-done.dense_ref.ids_ref.seen, f32[16,16,128]{2,1,0:T(8,128)S(1)} %get-tuple-element.20.ids_ref.all_ids), custom_call_target="tpu_custom_call" | custom-call | flops 1000000000 | bytes 100000 | tf_op jit(solution)/shard_map/part_other/pallas_call | solution.py:424
  56.4 2.1 %collective-permute-start.2 = (bf16[4,8,48,128]{3,2,1,0:T(8,128)(2,1)S(1)}, bf16[4,8,48,128]{3,2,1,0:T(8,128)(2,1)S(1)}, u32[]{:S(2)}, u32[]{:S(2)}) collective-permute-start(bf16[4,8,48,128]{3,2,1,0:T(8,128)(2,1)S(1)} %part_other.1), channel_id=1, source_target_pairs={{0,4},{4,0},{1,5},{5,1},{2,6},{6,2},{3,7},{7,3},{8,12},{12,8},{9,1... | collective-permute-start | bytes 1179656 | tf_op jit(solution)/shard_map/ppermute | solution.py:661
  58.5 3.8 %lookup.1.rows = bf16[16,352,128]{2,1,0:T(8,128)(2,1)} custom-call(bf16[2,256,1024]{2,1,0:T(8,128)(2,1)S(1)} %stack_tables.1.stacked, f32[16,16,128]{2,1,0:T(8,128)S(1)} %get-tuple-element.20.ids_ref.all_ids), custom_call_target="tpu_custom_call" | custom-call | flops 99999997952 | bytes 100000 | tf_op jit(solution)/shard_map/lookup/pallas_call | solution.py:513
  62.3 0.8 fill_dense.1
  63.1 3.7 %all-to-all-start.1 = ((bf16[16,352,128]{2,1,0:T(8,128)(2,1)}), bf16[16,352,128]{2,1,0:T(8,128)(2,1)S(1)}, u32[]{:S(2)}, u32[]{:S(2)}) async-start(bf16[16,352,128]{2,1,0:T(8,128)(2,1)} %get-tuple-element.22), calls=%async_computation.1 | async-start | bytes 2883584 | tf_op jit(solution)/shard_map/all_to_all | solution.py:61
  66.8 3.4 %part_own.1.own = f32[4,8,48,128]{3,2,1,0:T(8,128)} custom-call(s32[1]{0:T(128)} %bitcast.1.half_ref, bf16[16,352,128]{2,1,0:T(8,128)(2,1)} %copy-done, f32[16,16,128]{2,1,0:T(8,128)} %copy-done.3, f32[8,128]{1,0:T(8,128)} %get-tuple-element.23.refs_0_.after), custom_call_target="tpu_custom_call" | custom-call | flops 1000000000 | bytes 100000 | tf_op jit(solution)/shard_map/part_own/pallas_call | solution.py:424
  70.2 6.8 %collective-permute-done.2.seen = bf16[4,8,48,128]{3,2,1,0:T(8,128)(2,1)S(1)} collective-permute-done((bf16[4,8,48,128]{3,2,1,0:T(8,128)(2,1)S(1)}, bf16[4,8,48,128]{3,2,1,0:T(8,128)(2,1)S(1)}, u32[]{:S(2)}, u32[]{:S(2)}) %collective-permute-start.2) | collective-permute-done | bytes 393248 | tf_op jit(solution)/shard_map/ppermute | solution.py:661
  77.0 1.1 %copy-done.2 = f32[4,8,48,128]{3,2,1,0:T(8,128)S(1)} copy-done((f32[4,8,48,128]{3,2,1,0:T(8,128)S(1)}, f32[4,8,48,128]{3,2,1,0:T(8,128)}, u32[]{:S(2)}) %copy-start.2) | copy-done | bytes 786456
  78.2 0.5 collective-permute-start.3
  78.7 1.4 %collective-permute-start.4 = (bf16[8,48,128]{2,1,0:T(8,128)(2,1)S(1)}, bf16[8,48,128]{2,1,0:T(8,128)(2,1)S(1)}, u32[]{:S(2)}, u32[]{:S(2)}) collective-permute-start(bf16[8,48,128]{2,1,0:T(8,128)(2,1)S(1)} %get-tuple-element.26), channel_id=1, source_target_pairs={{0,16},{8,24},{16,0},{24,8},{1,17},{9,25},{17,1},{25,9},{2,18},{10... | collective-permute-start | bytes 294920 | tf_op jit(solution)/shard_map/ppermute | solution.py:687
  80.1 1.6 %collective-permute-start.5 = (bf16[8,48,128]{2,1,0:T(8,128)(2,1)S(1)}, bf16[8,48,128]{2,1,0:T(8,128)(2,1)S(1)}, u32[]{:S(2)}, u32[]{:S(2)}) collective-permute-start(bf16[8,48,128]{2,1,0:T(8,128)(2,1)S(1)} %get-tuple-element.27), channel_id=1, source_target_pairs={{0,24},{8,16},{16,8},{24,0},{1,25},{9,17},{17,9},{25,1},{2,26},{10... | collective-permute-start | bytes 294920 | tf_op jit(solution)/shard_map/ppermute | solution.py:687
  81.8 4.2 %collective-permute-done.3.refs_1_ = bf16[8,48,128]{2,1,0:T(8,128)(2,1)S(1)} collective-permute-done((bf16[8,48,128]{2,1,0:T(8,128)(2,1)S(1)}, bf16[8,48,128]{2,1,0:T(8,128)(2,1)S(1)}, u32[]{:S(2)}, u32[]{:S(2)}) %collective-permute-start.3) | collective-permute-done | bytes 98336 | tf_op jit(solution)/shard_map/ppermute | solution.py:687
  85.9 1.9 %collective-permute-done.4.refs_2_ = bf16[8,48,128]{2,1,0:T(8,128)(2,1)S(1)} collective-permute-done((bf16[8,48,128]{2,1,0:T(8,128)(2,1)S(1)}, bf16[8,48,128]{2,1,0:T(8,128)(2,1)S(1)}, u32[]{:S(2)}, u32[]{:S(2)}) %collective-permute-start.4) | collective-permute-done | bytes 98336 | tf_op jit(solution)/shard_map/ppermute | solution.py:687
  87.8 3.8 %collective-permute-done.5.refs_3_ = bf16[8,48,128]{2,1,0:T(8,128)(2,1)S(1)} collective-permute-done((bf16[8,48,128]{2,1,0:T(8,128)(2,1)S(1)}, bf16[8,48,128]{2,1,0:T(8,128)(2,1)S(1)}, u32[]{:S(2)}, u32[]{:S(2)}) %collective-permute-start.5) | collective-permute-done | bytes 98336 | tf_op jit(solution)/shard_map/ppermute | solution.py:687
  91.6 3.0 %all-to-all-done.1.dense_ref.left0.left1.right0.right1 = bf16[16,352,128]{2,1,0:T(8,128)(2,1)S(1)} async-done(((bf16[16,352,128]{2,1,0:T(8,128)(2,1)}), bf16[16,352,128]{2,1,0:T(8,128)(2,1)S(1)}, u32[]{:S(2)}, u32[]{:S(2)}) %all-to-all-start.1) | async-done | bytes 1441824 | tf_op jit(solution)/shard_map/all_to_all | solution.py:61
  94.6 3.1 %unpack.1 = (bf16[12,192,256]{2,1,0:T(8,128)(2,1)}, f32[32,32,192]{2,1,0:T(8,128)}, f32[256,128]{1,0:T(8,128)}, f32[192,128]{1,0:T(8,128)}, f32[256,256]{1,0:T(8,128)}, /*index=5*/f32[1,192]{1,0:T(1,128)}) custom-call(s32[1]{0:T(128)} %bitcast.place, bf16[16,352,128]{2,1,0:T(8,128)(2,1)S(1)} %all-to-all-done.1.dense_ref.left0.left1.right0.right1, ...), custom_call_target="tpu_custom_call" | custom-call | flops 1000000000 | bytes 100000 | tf_op jit(solution)/shard_map/unpack/pallas_call | solution.py:623
  (12 shorter events, 0.5 us)
Async XLA Ops:
  13.7 22.0 %collective-permute-start = (bf16[8,192,128]{2,1,0:T(8,128)(2,1)}, bf16[8,192,128]{2,1,0:T(8,128)(2,1)S(1)}, u32[]{:S(2)}, u32[]{:S(2)}) collective-permute-start(bf16[8,192,128]{2,1,0:T(8,128)(2,1)} %take_tables.1.mine_t), channel_id=1, source_target_pairs={{0,4},{4,0},{1,5},{5,1},{2,6},{6,2},{3,7},{7,3},{8,12},{12,8},{9,1... | collective-permute-start | bytes 1179656 | tf_op jit(solution)/shard_map/ppermute | solution.py:661
  26.4 9.2 %copy-start.1 = (bf16[8,192,128]{2,1,0:T(8,128)(2,1)S(1)}, bf16[8,192,128]{2,1,0:T(8,128)(2,1)}, u32[]{:S(2)}) copy-start(bf16[8,192,128]{2,1,0:T(8,128)(2,1)} %take_tables.1.mine_t) | copy-start | bytes 1179652
  26.4 27.4 %all-to-all-start = ((bf16[16,352,128]{2,1,0:T(8,128)(2,1)}), bf16[16,352,128]{2,1,0:T(8,128)(2,1)S(1)}, u32[]{:S(2)}, u32[]{:S(2)}) async-start(bf16[16,352,128]{2,1,0:T(8,128)(2,1)} %layer_backward.1), calls=%async_computation | async-start | bytes 2883584 | tf_op jit(solution)/shard_map/all_to_all | solution.py:61
  53.8 1.1 %copy-start = (bf16[16,352,128]{2,1,0:T(8,128)(2,1)}, bf16[16,352,128]{2,1,0:T(8,128)(2,1)S(1)}, u32[]{:S(2)}) copy-start(bf16[16,352,128]{2,1,0:T(8,128)(2,1)S(1)} %all-to-all-done.dense_ref.ids_ref.seen) | copy-start | bytes 4325380
  54.0 4.5 %copy-start.3 = (f32[16,16,128]{2,1,0:T(8,128)}, f32[16,16,128]{2,1,0:T(8,128)S(1)}, u32[]{:S(2)}) copy-start(f32[16,16,128]{2,1,0:T(8,128)S(1)} %get-tuple-element.20.ids_ref.all_ids) | copy-start | bytes 393220
  54.0 8.3 %collective-permute-start.1 = (f32[64,128]{1,0:T(8,128)S(1)}, f32[64,128]{1,0:T(8,128)S(1)}, u32[]{:S(2)}, u32[]{:S(2)}) collective-permute-start(f32[64,128]{1,0:T(8,128)S(1)} %get-tuple-element.21.own), channel_id=1, source_target_pairs={{0,4},{4,0},{1,5},{5,1},{2,6},{6,2},{3,7},{7,3},{8,12},{12,8},{9,1... | collective-permute-start | bytes 98312 | tf_op jit(solution)/shard_map/ppermute | solution.py:661
  56.4 20.6 %collective-permute-start.2 = (bf16[4,8,48,128]{3,2,1,0:T(8,128)(2,1)S(1)}, bf16[4,8,48,128]{3,2,1,0:T(8,128)(2,1)S(1)}, u32[]{:S(2)}, u32[]{:S(2)}) collective-permute-start(bf16[4,8,48,128]{3,2,1,0:T(8,128)(2,1)S(1)} %part_other.1), channel_id=1, source_target_pairs={{0,4},{4,0},{1,5},{5,1},{2,6},{6,2},{3,7},{7,3},{8,12},{12,8},{9,1... | collective-permute-start | bytes 1179656 | tf_op jit(solution)/shard_map/ppermute | solution.py:661
  63.1 31.5 %all-to-all-start.1 = ((bf16[16,352,128]{2,1,0:T(8,128)(2,1)}), bf16[16,352,128]{2,1,0:T(8,128)(2,1)S(1)}, u32[]{:S(2)}, u32[]{:S(2)}) async-start(bf16[16,352,128]{2,1,0:T(8,128)(2,1)} %get-tuple-element.22), calls=%async_computation.1 | async-start | bytes 2883584 | tf_op jit(solution)/shard_map/all_to_all | solution.py:61
  66.8 10.2 %copy-start.4 = (f32[8,128]{1,0:T(8,128)S(1)}, f32[8,128]{1,0:T(8,128)}, u32[]{:S(2)}) copy-start(f32[8,128]{1,0:T(8,128)} %get-tuple-element.23.refs_0_.after) | copy-start | bytes 12292
  77.0 1.1 %copy-start.2 = (f32[4,8,48,128]{3,2,1,0:T(8,128)S(1)}, f32[4,8,48,128]{3,2,1,0:T(8,128)}, u32[]{:S(2)}) copy-start(f32[4,8,48,128]{3,2,1,0:T(8,128)} %part_own.1.own) | copy-start | bytes 2359300
  78.2 7.7 %collective-permute-start.3 = (bf16[8,48,128]{2,1,0:T(8,128)(2,1)S(1)}, bf16[8,48,128]{2,1,0:T(8,128)(2,1)S(1)}, u32[]{:S(2)}, u32[]{:S(2)}) collective-permute-start(bf16[8,48,128]{2,1,0:T(8,128)(2,1)S(1)} %get-tuple-element.25), channel_id=1, source_target_pairs={{0,8},{8,0},{16,24},{24,16},{1,9},{9,1},{17,25},{25,17},{2,10},{10... | collective-permute-start | bytes 294920 | tf_op jit(solution)/shard_map/ppermute | solution.py:687
  78.7 9.1 %collective-permute-start.4 = (bf16[8,48,128]{2,1,0:T(8,128)(2,1)S(1)}, bf16[8,48,128]{2,1,0:T(8,128)(2,1)S(1)}, u32[]{:S(2)}, u32[]{:S(2)}) collective-permute-start(bf16[8,48,128]{2,1,0:T(8,128)(2,1)S(1)} %get-tuple-element.26), channel_id=1, source_target_pairs={{0,16},{8,24},{16,0},{24,8},{1,17},{9,25},{17,1},{25,9},{2,18},{10... | collective-permute-start | bytes 294920 | tf_op jit(solution)/shard_map/ppermute | solution.py:687
  80.1 11.5 %collective-permute-start.5 = (bf16[8,48,128]{2,1,0:T(8,128)(2,1)S(1)}, bf16[8,48,128]{2,1,0:T(8,128)(2,1)S(1)}, u32[]{:S(2)}, u32[]{:S(2)}) collective-permute-start(bf16[8,48,128]{2,1,0:T(8,128)(2,1)S(1)} %get-tuple-element.27), channel_id=1, source_target_pairs={{0,24},{8,16},{16,8},{24,0},{1,25},{9,17},{17,9},{25,1},{2,26},{10... | collective-permute-start | bytes 294920 | tf_op jit(solution)/shard_map/ppermute | solution.py:687

commit v11 on v10

--- a/solution.py
+++ b/solution.py
@@ -433,25 +433,27 @@
         out_specs=pl.BlockSpec(shape, lambda i: (0, 0, 0, 0)),
         out_shape=jax.ShapeDtypeStruct(shape, BF16 if other else F32),
         scratch_shapes=[pltpu.VMEM((peers * LANES, 256), BF16)],
-        compiler_params=params(1 if other else 2),
+        compiler_params=params(),
         cost_estimate=cost(1),
         name="part_other" if other else "part_own",
     )(half, seen, ids, *after)
 
 
-def take_kernel(place, tables, out, sem):
-    copy = pltpu.make_async_copy(tables.at[pl.ds(place[0] * TILE, TILE)], out, sem)
-    copy.start()
-    copy.wait()
+def take_kernel(place, tables, out):
+    out[...] = tables[...]
 
 
 def take_tables(place, tables_t):
+    rows, lanes = tables_t.shape[1:]
     return pl.pallas_call(
         take_kernel,
-        in_specs=[SMEM, pl.BlockSpec(memory_space=pl.ANY)],
-        out_specs=pl.BlockSpec(memory_space=pl.ANY),
-        out_shape=pltpu.HBM((TILE,) + tables_t.shape[1:], BF16),
-        scratch_shapes=[pltpu.SemaphoreType.DMA],
+        grid_spec=pltpu.PrefetchScalarGridSpec(
+            num_scalar_prefetch=1,
+            grid=(1,),
+            in_specs=[pl.BlockSpec((TILE, rows, lanes), lambda i, place: (place[0], 0, 0))],
+            out_specs=pl.BlockSpec((TILE, rows, lanes), lambda i, place: (0, 0, 0)),
+        ),
+        out_shape=jax.ShapeDtypeStruct((TILE, rows, lanes), BF16),
         compiler_params=params(2),
         cost_estimate=cost(1),
         name="take_tables",
@@ -509,10 +511,10 @@
 
 def lookup(wire, stacked, ids):
     peers = ids.shape[0]
-    some = peers // 4
+    some = peers // 2
     return pl.pallas_call(
         functools.partial(lookup_kernel, wire),
-        grid=(4,),
+        grid=(2,),
         in_specs=[
             pl.BlockSpec(stacked.shape, lambda i: (0, 0, 0)),
             pl.BlockSpec((some, 16, LANES), lambda i: (i, 0, 0)),

time: 98 us -> 86.8 us (0.89)
  Pallas kernels: 34.6 us -> 21.8 us
  waiting for transfers between devices: 41.8 us -> 43.6 us
    pallas_call x2, Pallas kernels: 16.8 us -> 5.1 us  [the longest x1 3.33 us: lookup(): pl.pallas_call(functools.partial(lookup_kernel, wire), grid=(2,), in_spec...]
    ppermute x3, waiting for transfers between devices: 11 us -> 12.6 us  [cross(): return lax.ppermute(array, 'half', [(0, 1), (1, 0)])]
    all_to_all x2, waiting for transfers between devices: 20.9 us -> 22.2 us  [exchange(): return lax.all_to_all(blocks, axes, split_axis=0, concat_axis=0, tiled=True)]
    pallas_call x2, Pallas kernels: 4.83 us -> 3.69 us  [part_sums(): pl.pallas_call(functools.partial(part_kernel, n_grp, wire, other), grid=(...]
    ppermute x3, waiting for transfers between devices: 9.86 us -> 8.76 us  [halves(): lax.ppermute(pieces[k], 'grp', [(g, g ^ k) for g in range(n_grp)])]
  transfers between devices with their start and end apart: 8 -> 8, of which waited for: 7 -> 6; matrix products, arithmetic and copies ran while one was open for 0% -> 0% of each run, Pallas kernels for 19% -> 19%
where the time goes in v11:
time: 86.8 us; the launch traced here: 86.4 us
  waiting for transfers between devices  43.6 us (50%)
  Pallas kernels  21.8 us (25%)
  starting transfers between devices  19.4 us (22%)
  local copies, waits for them, and re-layouts  0.98 us (1%)
    all_to_all x2, waiting for transfers between devices, exchange(): return lax.all_to_all(blocks, axes, split_axis=0, concat_axis=0, tiled=True)  22.2 us
    ppermute x3, waiting for transfers between devices, cross(): return lax.ppermute(array, 'half', [(0, 1), (1, 0)])  12.6 us
    all_to_all x2, starting transfers between devices, exchange(): return lax.all_to_all(blocks, axes, split_axis=0, concat_axis=0, tiled=True)  8.82 us
    ppermute x3, waiting for transfers between devices, halves(): lax.ppermute(pieces[k], 'grp', [(g, g ^ k) for g in range(n_grp)])  8.76 us
    pallas_call x1, Pallas kernels, backward(): pl.pallas_call(functools.partial(backward_kernel, n_grp, n_lane, wire), g...  8.65 us
    ppermute x3, starting transfers between devices, cross(): return lax.ppermute(array, 'half', [(0, 1), (1, 0)])  7.03 us
    pallas_call x2, Pallas kernels, part_sums(): pl.pallas_call(functools.partial(part_kernel, n_grp, wire, other), grid=(...  3.69 us
    ppermute x3, starting transfers between devices, halves(): lax.ppermute(pieces[k], 'grp', [(g, g ^ k) for g in range(n_grp)])  3.55 us
  transfers between devices with their start and end apart: 8, of which 6 were waited for; matrix products, arithmetic and copies ran while one was open for 0% of the time, Pallas kernels for 19%

profile of v11, /device:TPU:0, one launch (start us, length us, event | category | flops | bytes accessed | tf_op | source)
XLA Modules:
  0.0 86.4 jit_solution(15433051625270243965)
XLA Ops:
  0.6 1.8 %take_tables.1.mine_t = bf16[8,192,128]{2,1,0:T(8,128)(2,1)} custom-call(s32[1]{0:T(128)} %bitcast.place, bf16[32,192,128]{2,1,0:T(8,128)(2,1)} %bitcast.14), custom_call_target="tpu_custom_call" | custom-call | flops 1000000000 | bytes 100000 | tf_op jit(solution)/shard_map/take_tables/pallas_call | solution.py:448
  2.4 4.0 %collective-permute-start = (bf16[8,192,128]{2,1,0:T(8,128)(2,1)}, bf16[8,192,128]{2,1,0:T(8,128)(2,1)S(1)}, u32[]{:S(2)}, u32[]{:S(2)}) collective-permute-start(bf16[8,192,128]{2,1,0:T(8,128)(2,1)} %take_tables.1.mine_t), channel_id=1, source_target_pairs={{0,4},{4,0},{1,5},{5,1},{2,6},{6,2},{3,7},{7,3},{8,12},{12,8},{9,1... | collective-permute-start | bytes 1179656 | tf_op jit(solution)/shard_map/ppermute | solution.py:663
  6.4 8.7 %layer_backward.1 = bf16[16,352,128]{2,1,0:T(8,128)(2,1)} custom-call(s32[1]{0:T(128)} %bitcast.1.half_ref, bf16[12,192,256]{2,1,0:T(8,128)(2,1)} %bitcast.10, bf16[12,192,256]{2,1,0:T(8,128)(2,1)} %bitcast.11, s32[12,256]{1,0:T(8,128)} %now_ref.1, s32[12,256]{1,0:T(8,128)} %next_ref.1, bf16[256,128]{1,0:T(8,128)(2,1)} %fm_ref.1, bf16[192,128]{1,0:T(8,128)(2,1)} %bitcast.12, ...), custom_call_target="tpu_custom_call" | custom-call | flops 1000000000 | bytes 100000 | tf_op jit(solution)/shard_map/layer_backward/pallas_call | solution.py:318
  15.1 5.0 %all-to-all-start = ((bf16[16,352,128]{2,1,0:T(8,128)(2,1)}), bf16[16,352,128]{2,1,0:T(8,128)(2,1)S(1)}, u32[]{:S(2)}, u32[]{:S(2)}) async-start(bf16[16,352,128]{2,1,0:T(8,128)(2,1)} %layer_backward.1), calls=%async_computation | async-start | bytes 2883584 | tf_op jit(solution)/shard_map/all_to_all | solution.py:61
  20.1 4.2 %collective-permute-done.crossed_t = bf16[8,192,128]{2,1,0:T(8,128)(2,1)S(1)} collective-permute-done((bf16[8,192,128]{2,1,0:T(8,128)(2,1)}, bf16[8,192,128]{2,1,0:T(8,128)(2,1)S(1)}, u32[]{:S(2)}, u32[]{:S(2)}) %collective-permute-start) | collective-permute-done | bytes 393248 | tf_op jit(solution)/shard_map/ppermute | solution.py:663
  24.3 0.3 stack_tables.1.stacked
  24.6 1.0 %copy-done.2 = bf16[2,256,1024]{2,1,0:T(8,128)(2,1)} copy-done((bf16[2,256,1024]{2,1,0:T(8,128)(2,1)}, bf16[2,256,1024]{2,1,0:T(8,128)(2,1)S(1)}, u32[]{:S(2)}) %copy-start.2) | copy-done | bytes 1048600
  25.6 16.9 %all-to-all-done.dense_ref.ids_ref.seen = bf16[16,352,128]{2,1,0:T(8,128)(2,1)S(1)} async-done(((bf16[16,352,128]{2,1,0:T(8,128)(2,1)}), bf16[16,352,128]{2,1,0:T(8,128)(2,1)S(1)}, u32[]{:S(2)}, u32[]{:S(2)}) %all-to-all-start) | async-done | bytes 1441824 | tf_op jit(solution)/shard_map/all_to_all | solution.py:61
  42.4 0.1 half_dense.1
  42.6 0.3 collective-permute-start.1
  42.9 2.2 %part_other.1 = bf16[4,8,48,128]{3,2,1,0:T(8,128)(2,1)} custom-call(s32[1]{0:T(128)} %bitcast.1.half_ref, bf16[16,352,128]{2,1,0:T(8,128)(2,1)S(1)} %all-to-all-done.dense_ref.ids_ref.seen, f32[16,16,128]{2,1,0:T(8,128)S(1)} %get-tuple-element.20.ids_ref.all_ids), custom_call_target="tpu_custom_call" | custom-call | flops 1000000000 | bytes 100000 | tf_op jit(solution)/shard_map/part_other/pallas_call | solution.py:424
  45.1 2.7 %collective-permute-start.2 = (bf16[4,8,48,128]{3,2,1,0:T(8,128)(2,1)}, bf16[4,8,48,128]{3,2,1,0:T(8,128)(2,1)S(1)}, u32[]{:S(2)}, u32[]{:S(2)}) collective-permute-start(bf16[4,8,48,128]{3,2,1,0:T(8,128)(2,1)} %part_other.1), channel_id=1, source_target_pairs={{0,4},{4,0},{1,5},{5,1},{2,6},{6,2},{3,7},{7,3},{8,12},{12,8},{9,1... | collective-permute-start | bytes 1179656 | tf_op jit(solution)/shard_map/ppermute | solution.py:663
  47.8 3.3 %lookup.1.rows = bf16[16,352,128]{2,1,0:T(8,128)(2,1)} custom-call(bf16[2,256,1024]{2,1,0:T(8,128)(2,1)S(1)} %copy-done.3, f32[16,16,128]{2,1,0:T(8,128)S(1)} %get-tuple-element.20.ids_ref.all_ids), custom_call_target="tpu_custom_call" | custom-call | flops 99999997952 | bytes 100000 | tf_op jit(solution)/shard_map/lookup/pallas_call | solution.py:515
  51.1 0.7 fill_dense.1
  51.9 3.8 %all-to-all-start.1 = ((bf16[16,352,128]{2,1,0:T(8,128)(2,1)}), bf16[16,352,128]{2,1,0:T(8,128)(2,1)S(1)}, u32[]{:S(2)}, u32[]{:S(2)}) async-start(bf16[16,352,128]{2,1,0:T(8,128)(2,1)} %get-tuple-element.22), calls=%async_computation.1 | async-start | bytes 2883584 | tf_op jit(solution)/shard_map/all_to_all | solution.py:61
  55.7 1.5 %part_own.1.own = f32[4,8,48,128]{3,2,1,0:T(8,128)S(1)} custom-call(s32[1]{0:T(128)} %bitcast.1.half_ref, bf16[16,352,128]{2,1,0:T(8,128)(2,1)S(1)} %all-to-all-done.dense_ref.ids_ref.seen, f32[16,16,128]{2,1,0:T(8,128)S(1)} %get-tuple-element.20.ids_ref.all_ids, f32[8,128]{1,0:T(8,128)S(1)} %copy-done.1), custom_call_target="tpu_custom_call" | custom-call | flops 1000000000 | bytes 100000 | tf_op jit(solution)/shard_map/part_own/pallas_call | solution.py:424
  57.2 8.4 %collective-permute-done.2.seen = bf16[4,8,48,128]{3,2,1,0:T(8,128)(2,1)S(1)} collective-permute-done((bf16[4,8,48,128]{3,2,1,0:T(8,128)(2,1)}, bf16[4,8,48,128]{3,2,1,0:T(8,128)(2,1)S(1)}, u32[]{:S(2)}, u32[]{:S(2)}) %collective-permute-start.2) | collective-permute-done | bytes 393248 | tf_op jit(solution)/shard_map/ppermute | solution.py:663
  65.7 0.6 collective-permute-start.3
  66.3 1.4 %collective-permute-start.4 = (bf16[8,48,128]{2,1,0:T(8,128)(2,1)S(1)}, bf16[8,48,128]{2,1,0:T(8,128)(2,1)S(1)}, u32[]{:S(2)}, u32[]{:S(2)}) collective-permute-start(bf16[8,48,128]{2,1,0:T(8,128)(2,1)S(1)} %get-tuple-element.26), channel_id=1, source_target_pairs={{0,16},{8,24},{16,0},{24,8},{1,17},{9,25},{17,1},{25,9},{2,18},{10... | collective-permute-start | bytes 294920 | tf_op jit(solution)/shard_map/ppermute | solution.py:689
  67.7 1.6 %collective-permute-start.5 = (bf16[8,48,128]{2,1,0:T(8,128)(2,1)S(1)}, bf16[8,48,128]{2,1,0:T(8,128)(2,1)S(1)}, u32[]{:S(2)}, u32[]{:S(2)}) collective-permute-start(bf16[8,48,128]{2,1,0:T(8,128)(2,1)S(1)} %get-tuple-element.27), channel_id=1, source_target_pairs={{0,24},{8,16},{16,8},{24,0},{1,25},{9,17},{17,9},{25,1},{2,26},{10... | collective-permute-start | bytes 294920 | tf_op jit(solution)/shard_map/ppermute | solution.py:689
  69.2 5.1 %collective-permute-done.3.refs_1_ = bf16[8,48,128]{2,1,0:T(8,128)(2,1)S(1)} collective-permute-done((bf16[8,48,128]{2,1,0:T(8,128)(2,1)S(1)}, bf16[8,48,128]{2,1,0:T(8,128)(2,1)S(1)}, u32[]{:S(2)}, u32[]{:S(2)}) %collective-permute-start.3) | collective-permute-done | bytes 98336 | tf_op jit(solution)/shard_map/ppermute | solution.py:689
  74.3 3.7 %collective-permute-done.5.refs_3_ = bf16[8,48,128]{2,1,0:T(8,128)(2,1)S(1)} collective-permute-done((bf16[8,48,128]{2,1,0:T(8,128)(2,1)S(1)}, bf16[8,48,128]{2,1,0:T(8,128)(2,1)S(1)}, u32[]{:S(2)}, u32[]{:S(2)}) %collective-permute-start.5) | collective-permute-done | bytes 98336 | tf_op jit(solution)/shard_map/ppermute | solution.py:689
  78.0 5.3 %all-to-all-done.1.dense_ref.left0.left1.right0.right1 = bf16[16,352,128]{2,1,0:T(8,128)(2,1)S(1)} async-done(((bf16[16,352,128]{2,1,0:T(8,128)(2,1)}), bf16[16,352,128]{2,1,0:T(8,128)(2,1)S(1)}, u32[]{:S(2)}, u32[]{:S(2)}) %all-to-all-start.1) | async-done | bytes 1441824 | tf_op jit(solution)/shard_map/all_to_all | solution.py:61
  83.4 3.1 %unpack.1 = (bf16[12,192,256]{2,1,0:T(8,128)(2,1)}, f32[32,32,192]{2,1,0:T(8,128)}, f32[256,128]{1,0:T(8,128)}, f32[192,128]{1,0:T(8,128)}, f32[256,256]{1,0:T(8,128)}, /*index=5*/f32[1,192]{1,0:T(1,128)}) custom-call(s32[1]{0:T(128)} %bitcast.place, bf16[16,352,128]{2,1,0:T(8,128)(2,1)S(1)} %all-to-all-done.1.dense_ref.left0.left1.right0.right1, ...), custom_call_target="tpu_custom_call" | custom-call | flops 1000000000 | bytes 100000 | tf_op jit(solution)/shard_map/unpack/pallas_call | solution.py:625
  (10 shorter events, 0.1 us)
Async XLA Ops:
  2.4 21.9 %collective-permute-start = (bf16[8,192,128]{2,1,0:T(8,128)(2,1)}, bf16[8,192,128]{2,1,0:T(8,128)(2,1)S(1)}, u32[]{:S(2)}, u32[]{:S(2)}) collective-permute-start(bf16[8,192,128]{2,1,0:T(8,128)(2,1)} %take_tables.1.mine_t), channel_id=1, source_target_pairs={{0,4},{4,0},{1,5},{5,1},{2,6},{6,2},{3,7},{7,3},{8,12},{12,8},{9,1... | collective-permute-start | bytes 1179656 | tf_op jit(solution)/shard_map/ppermute | solution.py:663
  15.1 9.2 %copy-start = (bf16[8,192,128]{2,1,0:T(8,128)(2,1)S(1)}, bf16[8,192,128]{2,1,0:T(8,128)(2,1)}, u32[]{:S(2)}) copy-start(bf16[8,192,128]{2,1,0:T(8,128)(2,1)} %take_tables.1.mine_t) | copy-start | bytes 1179652
  15.1 27.3 %all-to-all-start = ((bf16[16,352,128]{2,1,0:T(8,128)(2,1)}), bf16[16,352,128]{2,1,0:T(8,128)(2,1)S(1)}, u32[]{:S(2)}, u32[]{:S(2)}) async-start(bf16[16,352,128]{2,1,0:T(8,128)(2,1)} %layer_backward.1), calls=%async_computation | async-start | bytes 2883584 | tf_op jit(solution)/shard_map/all_to_all | solution.py:61
  24.6 1.0 %copy-start.2 = (bf16[2,256,1024]{2,1,0:T(8,128)(2,1)}, bf16[2,256,1024]{2,1,0:T(8,128)(2,1)S(1)}, u32[]{:S(2)}) copy-start(bf16[2,256,1024]{2,1,0:T(8,128)(2,1)S(1)} %stack_tables.1.stacked) | copy-start | bytes 3145732
  42.6 8.6 %collective-permute-start.1 = (f32[64,128]{1,0:T(8,128)S(1)}, f32[64,128]{1,0:T(8,128)S(1)}, u32[]{:S(2)}, u32[]{:S(2)}) collective-permute-start(f32[64,128]{1,0:T(8,128)S(1)} %get-tuple-element.21.own), channel_id=1, source_target_pairs={{0,4},{4,0},{1,5},{5,1},{2,6},{6,2},{3,7},{7,3},{8,12},{12,8},{9,1... | collective-permute-start | bytes 98312 | tf_op jit(solution)/shard_map/ppermute | solution.py:663
  42.9 4.9 %copy-start.3 = (bf16[2,256,1024]{2,1,0:T(8,128)(2,1)S(1)}, bf16[2,256,1024]{2,1,0:T(8,128)(2,1)}, u32[]{:S(2)}) copy-start(bf16[2,256,1024]{2,1,0:T(8,128)(2,1)} %copy-done.2) | copy-start | bytes 3145732
  45.1 20.5 %collective-permute-start.2 = (bf16[4,8,48,128]{3,2,1,0:T(8,128)(2,1)}, bf16[4,8,48,128]{3,2,1,0:T(8,128)(2,1)S(1)}, u32[]{:S(2)}, u32[]{:S(2)}) collective-permute-start(bf16[4,8,48,128]{3,2,1,0:T(8,128)(2,1)} %part_other.1), channel_id=1, source_target_pairs={{0,4},{4,0},{1,5},{5,1},{2,6},{6,2},{3,7},{7,3},{8,12},{12,8},{9,1... | collective-permute-start | bytes 1179656 | tf_op jit(solution)/shard_map/ppermute | solution.py:663
  51.9 3.8 %copy-start.1 = (f32[8,128]{1,0:T(8,128)S(1)}, f32[8,128]{1,0:T(8,128)}, u32[]{:S(2)}) copy-start(f32[8,128]{1,0:T(8,128)} %get-tuple-element.23.refs_0_.after) | copy-start | bytes 12292
  51.9 31.5 %all-to-all-start.1 = ((bf16[16,352,128]{2,1,0:T(8,128)(2,1)}), bf16[16,352,128]{2,1,0:T(8,128)(2,1)S(1)}, u32[]{:S(2)}, u32[]{:S(2)}) async-start(bf16[16,352,128]{2,1,0:T(8,128)(2,1)} %get-tuple-element.22), calls=%async_computation.1 | async-start | bytes 2883584 | tf_op jit(solution)/shard_map/all_to_all | solution.py:61
  65.7 8.7 %collective-permute-start.3 = (bf16[8,48,128]{2,1,0:T(8,128)(2,1)S(1)}, bf16[8,48,128]{2,1,0:T(8,128)(2,1)S(1)}, u32[]{:S(2)}, u32[]{:S(2)}) collective-permute-start(bf16[8,48,128]{2,1,0:T(8,128)(2,1)S(1)} %get-tuple-element.25), channel_id=1, source_target_pairs={{0,8},{8,0},{16,24},{24,16},{1,9},{9,1},{17,25},{25,17},{2,10},{10... | collective-permute-start | bytes 294920 | tf_op jit(solution)/shard_map/ppermute | solution.py:689
  66.3 8.1 %collective-permute-start.4 = (bf16[8,48,128]{2,1,0:T(8,128)(2,1)S(1)}, bf16[8,48,128]{2,1,0:T(8,128)(2,1)S(1)}, u32[]{:S(2)}, u32[]{:S(2)}) collective-permute-start(bf16[8,48,128]{2,1,0:T(8,128)(2,1)S(1)} %get-tuple-element.26), channel_id=1, source_target_pairs={{0,16},{8,24},{16,0},{24,8},{1,17},{9,25},{17,1},{25,9},{2,18},{10... | collective-permute-start | bytes 294920 | tf_op jit(solution)/shard_map/ppermute | solution.py:689
  67.7 10.3 %collective-permute-start.5 = (bf16[8,48,128]{2,1,0:T(8,128)(2,1)S(1)}, bf16[8,48,128]{2,1,0:T(8,128)(2,1)S(1)}, u32[]{:S(2)}, u32[]{:S(2)}) collective-permute-start(bf16[8,48,128]{2,1,0:T(8,128)(2,1)S(1)} %get-tuple-element.27), channel_id=1, source_target_pairs={{0,24},{8,16},{16,8},{24,0},{1,25},{9,17},{17,9},{25,1},{2,26},{10... | collective-permute-start | bytes 294920 | tf_op jit(solution)/shard_map/ppermute | solution.py:689

commit v12 on v11

--- a/solution.py
+++ b/solution.py
@@ -14,7 +14,7 @@
 TILE = 8
 STEP = 4
 LIMIT = 30 * 1024 * 1024
-PEER = ("grp", "lane")
+PEER = ("lane", "grp")
 
 
 BOTH = ("grp", "emb")
@@ -144,8 +144,8 @@
         self.back_right = (self.share + 2 * self.left, self.share + 2 * self.left + self.left // 2)
 
 
-def place_of(n_grp, n_lane, peer):
-    return (peer % n_lane) * n_grp * TILE + (peer // n_lane) * TILE
+def place_of(peer):
+    return peer * TILE
 
 
 def backward_kernel(
@@ -247,7 +247,7 @@
     for group in range(count // STEP):
         for side, base in ((1 - half, 0), (half, wire.half)):
             for peer in range(peers):
-                at = place_of(n_grp, n_lane, peer)
+                at = place_of(peer)
                 line = turned[group, side, at : at + TILE]
                 left = jnp.concatenate([line[:, k * 128 : k * 128 + 128] for k in range(STEP)], axis=0)
                 row = base + group * 32
@@ -287,7 +287,7 @@
         out_ref[peer, at : at + part] = sum_fm[here].astype(BF16)
         out_ref[peer, at + part : at + 2 * part] = sum_lcb[here, 0:128].astype(BF16)
         out_ref[peer, at + 2 * part : at + 3 * part] = sum_lcb[here, 128:256].astype(BF16)
-        place = place_of(n_grp, n_lane, peer)
+        place = place_of(peer)
         lines = []
         for line in spread_ids:
             line = pltpu.roll(line, LANES - place, 1) if place else line
@@ -574,7 +574,7 @@
             for gg in range(n_grp // 2):
                 left, right = [], []
                 for g in (2 * gg, 2 * gg + 1):
-                    peer = g * n_lane + q
+                    peer = q * n_grp + g
                     left.append(left_ref[peer].astype(F32))
                     packed = right_ref[peer].astype(F32)
                     right.append(jnp.concatenate([packed, turn(packed)], axis=0))

time: 86.8 us -> 84 us (0.968)
  waiting for transfers between devices: 43.6 us -> 40.8 us
    all_to_all x2, waiting for transfers between devices: 22.2 us -> 16.1 us  [exchange(): return lax.all_to_all(blocks, axes, split_axis=0, concat_axis=0, tiled=True)]
    ppermute x3, waiting for transfers between devices: 8.76 us -> 11 us  [halves(): lax.ppermute(pieces[k], 'grp', [(g, g ^ k) for g in range(n_grp)])]
    ppermute x3, waiting for transfers between devices: 12.6 us -> 13.7 us  [cross(): return lax.ppermute(array, 'half', [(0, 1), (1, 0)])]
  transfers between devices with their start and end apart: 8 -> 8, of which waited for: 6 -> 7; matrix products, arithmetic and copies ran while one was open for 0% -> 0% of each run, Pallas kernels for 19% -> 20%
where the time goes in v12:
time: 84 us; the launch traced here: 83.6 us
  waiting for transfers between devices  40.8 us (49%)
  Pallas kernels  21.7 us (26%)
  starting transfers between devices  19.4 us (23%)
  local copies, waits for them, and re-layouts  0.98 us (1%)
    all_to_all x2, waiting for transfers between devices, exchange(): return lax.all_to_all(blocks, axes, split_axis=0, concat_axis=0, tiled=True)  16.1 us
    ppermute x3, waiting for transfers between devices, cross(): return lax.ppermute(array, 'half', [(0, 1), (1, 0)])  13.7 us
    ppermute x3, waiting for transfers between devices, halves(): lax.ppermute(pieces[k], 'grp', [(g, g ^ k) for g in range(n_grp)])  11 us
    all_to_all x2, starting transfers between devices, exchange(): return lax.all_to_all(blocks, axes, split_axis=0, concat_axis=0, tiled=True)  8.82 us
    pallas_call x1, Pallas kernels, backward(): pl.pallas_call(functools.partial(backward_kernel, n_grp, n_lane, wire), g...  8.65 us
    ppermute x3, starting transfers between devices, cross(): return lax.ppermute(array, 'half', [(0, 1), (1, 0)])  7.03 us
    pallas_call x2, Pallas kernels, part_sums(): pl.pallas_call(functools.partial(part_kernel, n_grp, wire, other), grid=(...  3.69 us
    ppermute x3, starting transfers between devices, halves(): lax.ppermute(pieces[k], 'grp', [(g, g ^ k) for g in range(n_grp)])  3.55 us
  transfers between devices with their start and end apart: 8, of which 7 were waited for; matrix products, arithmetic and copies ran while one was open for 0% of the time, Pallas kernels for 20%

profile of v12, /device:TPU:0, one launch (start us, length us, event | category | flops | bytes accessed | tf_op | source)
XLA Modules:
  0.0 83.6 jit_solution(5628157630495776791)
XLA Ops:
  0.6 1.8 %take_tables.1.mine_t = bf16[8,192,128]{2,1,0:T(8,128)(2,1)} custom-call(s32[1]{0:T(128)} %bitcast.place, bf16[32,192,128]{2,1,0:T(8,128)(2,1)} %bitcast.14), custom_call_target="tpu_custom_call" | custom-call | flops 1000000000 | bytes 100000 | tf_op jit(solution)/shard_map/take_tables/pallas_call | solution.py:448
  2.4 4.0 %collective-permute-start = (bf16[8,192,128]{2,1,0:T(8,128)(2,1)}, bf16[8,192,128]{2,1,0:T(8,128)(2,1)S(1)}, u32[]{:S(2)}, u32[]{:S(2)}) collective-permute-start(bf16[8,192,128]{2,1,0:T(8,128)(2,1)} %take_tables.1.mine_t), channel_id=1, source_target_pairs={{0,4},{4,0},{1,5},{5,1},{2,6},{6,2},{3,7},{7,3},{8,12},{12,8},{9,1... | collective-permute-start | bytes 1179656 | tf_op jit(solution)/shard_map/ppermute | solution.py:663
  6.4 8.7 %layer_backward.1 = bf16[16,352,128]{2,1,0:T(8,128)(2,1)} custom-call(s32[1]{0:T(128)} %bitcast.1.half_ref, bf16[12,192,256]{2,1,0:T(8,128)(2,1)} %bitcast.10, bf16[12,192,256]{2,1,0:T(8,128)(2,1)} %bitcast.11, s32[12,256]{1,0:T(8,128)} %now_ref.1, s32[12,256]{1,0:T(8,128)} %next_ref.1, bf16[256,128]{1,0:T(8,128)(2,1)} %fm_ref.1, bf16[192,128]{1,0:T(8,128)(2,1)} %bitcast.12, ...), custom_call_target="tpu_custom_call" | custom-call | flops 1000000000 | bytes 100000 | tf_op jit(solution)/shard_map/layer_backward/pallas_call | solution.py:318
  15.1 5.0 %all-to-all-start = ((bf16[16,352,128]{2,1,0:T(8,128)(2,1)}), bf16[16,352,128]{2,1,0:T(8,128)(2,1)S(1)}, u32[]{:S(2)}, u32[]{:S(2)}) async-start(bf16[16,352,128]{2,1,0:T(8,128)(2,1)} %layer_backward.1), calls=%async_computation | async-start | bytes 2883584 | tf_op jit(solution)/shard_map/all_to_all | solution.py:61
  20.1 4.2 %collective-permute-done.crossed_t = bf16[8,192,128]{2,1,0:T(8,128)(2,1)S(1)} collective-permute-done((bf16[8,192,128]{2,1,0:T(8,128)(2,1)}, bf16[8,192,128]{2,1,0:T(8,128)(2,1)S(1)}, u32[]{:S(2)}, u32[]{:S(2)}) %collective-permute-start) | collective-permute-done | bytes 393248 | tf_op jit(solution)/shard_map/ppermute | solution.py:663
  24.3 0.3 stack_tables.1.stacked
  24.6 1.0 %copy-done.2 = bf16[2,256,1024]{2,1,0:T(8,128)(2,1)} copy-done((bf16[2,256,1024]{2,1,0:T(8,128)(2,1)}, bf16[2,256,1024]{2,1,0:T(8,128)(2,1)S(1)}, u32[]{:S(2)}) %copy-start.2) | copy-done | bytes 1048600
  25.6 15.0 %all-to-all-done.dense_ref.ids_ref.seen = bf16[16,352,128]{2,1,0:T(8,128)(2,1)S(1)} async-done(((bf16[16,352,128]{2,1,0:T(8,128)(2,1)}), bf16[16,352,128]{2,1,0:T(8,128)(2,1)S(1)}, u32[]{:S(2)}, u32[]{:S(2)}) %all-to-all-start) | async-done | bytes 1441824 | tf_op jit(solution)/shard_map/all_to_all | solution.py:61
  40.7 1.5 %collective-permute-start.1 = (f32[64,128]{1,0:T(8,128)S(1)}, f32[64,128]{1,0:T(8,128)S(1)}, u32[]{:S(2)}, u32[]{:S(2)}) collective-permute-start(f32[64,128]{1,0:T(8,128)S(1)} %get-tuple-element.21.own), channel_id=1, source_target_pairs={{0,4},{4,0},{1,5},{5,1},{2,6},{6,2},{3,7},{7,3},{8,12},{12,8},{9,1... | collective-permute-start | bytes 98312 | tf_op jit(solution)/shard_map/ppermute | solution.py:663
  42.2 2.2 %part_other.1 = bf16[4,8,48,128]{3,2,1,0:T(8,128)(2,1)} custom-call(s32[1]{0:T(128)} %bitcast.1.half_ref, bf16[16,352,128]{2,1,0:T(8,128)(2,1)S(1)} %all-to-all-done.dense_ref.ids_ref.seen, f32[16,16,128]{2,1,0:T(8,128)S(1)} %get-tuple-element.20.ids_ref.all_ids), custom_call_target="tpu_custom_call" | custom-call | flops 1000000000 | bytes 100000 | tf_op jit(solution)/shard_map/part_other/pallas_call | solution.py:424
  44.4 1.5 %collective-permute-start.2 = (bf16[4,8,48,128]{3,2,1,0:T(8,128)(2,1)}, bf16[4,8,48,128]{3,2,1,0:T(8,128)(2,1)S(1)}, u32[]{:S(2)}, u32[]{:S(2)}) collective-permute-start(bf16[4,8,48,128]{3,2,1,0:T(8,128)(2,1)} %part_other.1), channel_id=1, source_target_pairs={{0,4},{4,0},{1,5},{5,1},{2,6},{6,2},{3,7},{7,3},{8,12},{12,8},{9,1... | collective-permute-start | bytes 1179656 | tf_op jit(solution)/shard_map/ppermute | solution.py:663
  46.0 3.3 %lookup.1.rows = bf16[16,352,128]{2,1,0:T(8,128)(2,1)} custom-call(bf16[2,256,1024]{2,1,0:T(8,128)(2,1)S(1)} %copy-done.3, f32[16,16,128]{2,1,0:T(8,128)S(1)} %get-tuple-element.20.ids_ref.all_ids), custom_call_target="tpu_custom_call" | custom-call | flops 99999997952 | bytes 100000 | tf_op jit(solution)/shard_map/lookup/pallas_call | solution.py:515
  49.3 0.7 fill_dense.1
  50.0 3.8 %all-to-all-start.1 = ((bf16[16,352,128]{2,1,0:T(8,128)(2,1)}), bf16[16,352,128]{2,1,0:T(8,128)(2,1)S(1)}, u32[]{:S(2)}, u32[]{:S(2)}) async-start(bf16[16,352,128]{2,1,0:T(8,128)(2,1)} %get-tuple-element.22), calls=%async_computation.1 | async-start | bytes 2883584 | tf_op jit(solution)/shard_map/all_to_all | solution.py:61
  53.9 1.5 %part_own.1.own = f32[4,8,48,128]{3,2,1,0:T(8,128)S(1)} custom-call(s32[1]{0:T(128)} %bitcast.1.half_ref, bf16[16,352,128]{2,1,0:T(8,128)(2,1)S(1)} %all-to-all-done.dense_ref.ids_ref.seen, f32[16,16,128]{2,1,0:T(8,128)S(1)} %get-tuple-element.20.ids_ref.all_ids, f32[8,128]{1,0:T(8,128)S(1)} %copy-done.1), custom_call_target="tpu_custom_call" | custom-call | flops 1000000000 | bytes 100000 | tf_op jit(solution)/shard_map/part_own/pallas_call | solution.py:424
  55.4 9.5 %collective-permute-done.2.seen = bf16[4,8,48,128]{3,2,1,0:T(8,128)(2,1)S(1)} collective-permute-done((bf16[4,8,48,128]{3,2,1,0:T(8,128)(2,1)}, bf16[4,8,48,128]{3,2,1,0:T(8,128)(2,1)S(1)}, u32[]{:S(2)}, u32[]{:S(2)}) %collective-permute-start.2) | collective-permute-done | bytes 393248 | tf_op jit(solution)/shard_map/ppermute | solution.py:663
  65.0 1.5 %collective-permute-start.3 = (bf16[8,48,128]{2,1,0:T(8,128)(2,1)S(1)}, bf16[8,48,128]{2,1,0:T(8,128)(2,1)S(1)}, u32[]{:S(2)}, u32[]{:S(2)}) collective-permute-start(bf16[8,48,128]{2,1,0:T(8,128)(2,1)S(1)} %get-tuple-element.25), channel_id=1, source_target_pairs={{0,8},{8,0},{16,24},{24,16},{1,9},{9,1},{17,25},{25,17},{2,10},{10... | collective-permute-start | bytes 294920 | tf_op jit(solution)/shard_map/ppermute | solution.py:689
  66.5 0.6 collective-permute-start.4
  67.1 1.5 %collective-permute-start.5 = (bf16[8,48,128]{2,1,0:T(8,128)(2,1)S(1)}, bf16[8,48,128]{2,1,0:T(8,128)(2,1)S(1)}, u32[]{:S(2)}, u32[]{:S(2)}) collective-permute-start(bf16[8,48,128]{2,1,0:T(8,128)(2,1)S(1)} %get-tuple-element.27), channel_id=1, source_target_pairs={{0,24},{8,16},{16,8},{24,0},{1,25},{9,17},{17,9},{25,1},{2,26},{10... | collective-permute-start | bytes 294920 | tf_op jit(solution)/shard_map/ppermute | solution.py:689
  68.5 1.1 %collective-permute-done.3.refs_1_ = bf16[8,48,128]{2,1,0:T(8,128)(2,1)S(1)} collective-permute-done((bf16[8,48,128]{2,1,0:T(8,128)(2,1)S(1)}, bf16[8,48,128]{2,1,0:T(8,128)(2,1)S(1)}, u32[]{:S(2)}, u32[]{:S(2)}) %collective-permute-start.3) | collective-permute-done | bytes 98336 | tf_op jit(solution)/shard_map/ppermute | solution.py:689
  69.7 6.6 %collective-permute-done.4.refs_2_ = bf16[8,48,128]{2,1,0:T(8,128)(2,1)S(1)} collective-permute-done((bf16[8,48,128]{2,1,0:T(8,128)(2,1)S(1)}, bf16[8,48,128]{2,1,0:T(8,128)(2,1)S(1)}, u32[]{:S(2)}, u32[]{:S(2)}) %collective-permute-start.4) | collective-permute-done | bytes 98336 | tf_op jit(solution)/shard_map/ppermute | solution.py:689
  76.3 3.2 %collective-permute-done.5.refs_3_ = bf16[8,48,128]{2,1,0:T(8,128)(2,1)S(1)} collective-permute-done((bf16[8,48,128]{2,1,0:T(8,128)(2,1)S(1)}, bf16[8,48,128]{2,1,0:T(8,128)(2,1)S(1)}, u32[]{:S(2)}, u32[]{:S(2)}) %collective-permute-start.5) | collective-permute-done | bytes 98336 | tf_op jit(solution)/shard_map/ppermute | solution.py:689
  79.5 1.0 %all-to-all-done.1.dense_ref.left0.left1.right0.right1 = bf16[16,352,128]{2,1,0:T(8,128)(2,1)S(1)} async-done(((bf16[16,352,128]{2,1,0:T(8,128)(2,1)}), bf16[16,352,128]{2,1,0:T(8,128)(2,1)S(1)}, u32[]{:S(2)}, u32[]{:S(2)}) %all-to-all-start.1) | async-done | bytes 1441824 | tf_op jit(solution)/shard_map/all_to_all | solution.py:61
  80.5 3.1 %unpack.1 = (bf16[12,192,256]{2,1,0:T(8,128)(2,1)}, f32[32,32,192]{2,1,0:T(8,128)}, f32[256,128]{1,0:T(8,128)}, f32[192,128]{1,0:T(8,128)}, f32[256,256]{1,0:T(8,128)}, /*index=5*/f32[1,192]{1,0:T(1,128)}) custom-call(s32[1]{0:T(128)} %bitcast.place, bf16[16,352,128]{2,1,0:T(8,128)(2,1)S(1)} %all-to-all-done.1.dense_ref.left0.left1.right0.right1, ...), custom_call_target="tpu_custom_call" | custom-call | flops 1000000000 | bytes 100000 | tf_op jit(solution)/shard_map/unpack/pallas_call | solution.py:625
  (10 shorter events, 0.2 us)
Async XLA Ops:
  2.4 21.9 %collective-permute-start = (bf16[8,192,128]{2,1,0:T(8,128)(2,1)}, bf16[8,192,128]{2,1,0:T(8,128)(2,1)S(1)}, u32[]{:S(2)}, u32[]{:S(2)}) collective-permute-start(bf16[8,192,128]{2,1,0:T(8,128)(2,1)} %take_tables.1.mine_t), channel_id=1, source_target_pairs={{0,4},{4,0},{1,5},{5,1},{2,6},{6,2},{3,7},{7,3},{8,12},{12,8},{9,1... | collective-permute-start | bytes 1179656 | tf_op jit(solution)/shard_map/ppermute | solution.py:663
  15.1 9.2 %copy-start = (bf16[8,192,128]{2,1,0:T(8,128)(2,1)S(1)}, bf16[8,192,128]{2,1,0:T(8,128)(2,1)}, u32[]{:S(2)}) copy-start(bf16[8,192,128]{2,1,0:T(8,128)(2,1)} %take_tables.1.mine_t) | copy-start | bytes 1179652
  15.1 25.5 %all-to-all-start = ((bf16[16,352,128]{2,1,0:T(8,128)(2,1)}), bf16[16,352,128]{2,1,0:T(8,128)(2,1)S(1)}, u32[]{:S(2)}, u32[]{:S(2)}) async-start(bf16[16,352,128]{2,1,0:T(8,128)(2,1)} %layer_backward.1), calls=%async_computation | async-start | bytes 2883584 | tf_op jit(solution)/shard_map/all_to_all | solution.py:61
  24.6 1.0 %copy-start.2 = (bf16[2,256,1024]{2,1,0:T(8,128)(2,1)}, bf16[2,256,1024]{2,1,0:T(8,128)(2,1)S(1)}, u32[]{:S(2)}) copy-start(bf16[2,256,1024]{2,1,0:T(8,128)(2,1)S(1)} %stack_tables.1.stacked) | copy-start | bytes 3145732
  40.7 8.6 %collective-permute-start.1 = (f32[64,128]{1,0:T(8,128)S(1)}, f32[64,128]{1,0:T(8,128)S(1)}, u32[]{:S(2)}, u32[]{:S(2)}) collective-permute-start(f32[64,128]{1,0:T(8,128)S(1)} %get-tuple-element.21.own), channel_id=1, source_target_pairs={{0,4},{4,0},{1,5},{5,1},{2,6},{6,2},{3,7},{7,3},{8,12},{12,8},{9,1... | collective-permute-start | bytes 98312 | tf_op jit(solution)/shard_map/ppermute | solution.py:663
  42.2 3.8 %copy-start.3 = (bf16[2,256,1024]{2,1,0:T(8,128)(2,1)S(1)}, bf16[2,256,1024]{2,1,0:T(8,128)(2,1)}, u32[]{:S(2)}) copy-start(bf16[2,256,1024]{2,1,0:T(8,128)(2,1)} %copy-done.2) | copy-start | bytes 3145732
  44.4 20.5 %collective-permute-start.2 = (bf16[4,8,48,128]{3,2,1,0:T(8,128)(2,1)}, bf16[4,8,48,128]{3,2,1,0:T(8,128)(2,1)S(1)}, u32[]{:S(2)}, u32[]{:S(2)}) collective-permute-start(bf16[4,8,48,128]{3,2,1,0:T(8,128)(2,1)} %part_other.1), channel_id=1, source_target_pairs={{0,4},{4,0},{1,5},{5,1},{2,6},{6,2},{3,7},{7,3},{8,12},{12,8},{9,1... | collective-permute-start | bytes 1179656 | tf_op jit(solution)/shard_map/ppermute | solution.py:663
  50.0 3.8 %copy-start.1 = (f32[8,128]{1,0:T(8,128)S(1)}, f32[8,128]{1,0:T(8,128)}, u32[]{:S(2)}) copy-start(f32[8,128]{1,0:T(8,128)} %get-tuple-element.23.refs_0_.after) | copy-start | bytes 12292
  50.0 30.5 %all-to-all-start.1 = ((bf16[16,352,128]{2,1,0:T(8,128)(2,1)}), bf16[16,352,128]{2,1,0:T(8,128)(2,1)S(1)}, u32[]{:S(2)}, u32[]{:S(2)}) async-start(bf16[16,352,128]{2,1,0:T(8,128)(2,1)} %get-tuple-element.22), calls=%async_computation.1 | async-start | bytes 2883584 | tf_op jit(solution)/shard_map/all_to_all | solution.py:61
  65.0 4.7 %collective-permute-start.3 = (bf16[8,48,128]{2,1,0:T(8,128)(2,1)S(1)}, bf16[8,48,128]{2,1,0:T(8,128)(2,1)S(1)}, u32[]{:S(2)}, u32[]{:S(2)}) collective-permute-start(bf16[8,48,128]{2,1,0:T(8,128)(2,1)S(1)} %get-tuple-element.25), channel_id=1, source_target_pairs={{0,8},{8,0},{16,24},{24,16},{1,9},{9,1},{17,25},{25,17},{2,10},{10... | collective-permute-start | bytes 294920 | tf_op jit(solution)/shard_map/ppermute | solution.py:689
  66.5 9.8 %collective-permute-start.4 = (bf16[8,48,128]{2,1,0:T(8,128)(2,1)S(1)}, bf16[8,48,128]{2,1,0:T(8,128)(2,1)S(1)}, u32[]{:S(2)}, u32[]{:S(2)}) collective-permute-start(bf16[8,48,128]{2,1,0:T(8,128)(2,1)S(1)} %get-tuple-element.26), channel_id=1, source_target_pairs={{0,16},{8,24},{16,0},{24,8},{1,17},{9,25},{17,1},{25,9},{2,18},{10... | collective-permute-start | bytes 294920 | tf_op jit(solution)/shard_map/ppermute | solution.py:689
  67.1 12.4 %collective-permute-start.5 = (bf16[8,48,128]{2,1,0:T(8,128)(2,1)S(1)}, bf16[8,48,128]{2,1,0:T(8,128)(2,1)S(1)}, u32[]{:S(2)}, u32[]{:S(2)}) collective-permute-start(bf16[8,48,128]{2,1,0:T(8,128)(2,1)S(1)} %get-tuple-element.27), channel_id=1, source_target_pairs={{0,24},{8,16},{16,8},{24,0},{1,25},{9,17},{17,9},{25,1},{2,26},{10... | collective-permute-start | bytes 294920 | tf_op jit(solution)/shard_map/ppermute | solution.py:689

commit v13 on v11

--- a/solution.py
+++ b/solution.py
@@ -14,7 +14,8 @@
 TILE = 8
 STEP = 4
 LIMIT = 30 * 1024 * 1024
-PEER = ("grp", "lane")
+LANE = ("deep", "core")
+PEER = ("core", "deep", "grp")
 
 
 BOTH = ("grp", "emb")
@@ -145,7 +146,8 @@
 
 
 def place_of(n_grp, n_lane, peer):
-    return (peer % n_lane) * n_grp * TILE + (peer // n_lane) * TILE
+    core, deep, g = peer // (n_grp * n_lane // 2), peer // n_grp % (n_lane // 2), peer % n_grp
+    return ((deep * 2 + core) * n_grp + g) * TILE
 
 
 def backward_kernel(
@@ -574,7 +576,7 @@
             for gg in range(n_grp // 2):
                 left, right = [], []
                 for g in (2 * gg, 2 * gg + 1):
-                    peer = g * n_lane + q
+                    peer = (q % 2 * (n_lane // 2) + q // 2) * n_grp + g
                     left.append(left_ref[peer].astype(F32))
                     packed = right_ref[peer].astype(F32)
                     right.append(jnp.concatenate([packed, turn(packed)], axis=0))
@@ -664,7 +666,7 @@
 
 
 def halves(pooled, upstream, ids_now, ids_next, tables, w_fm, w_proj, w_lcb, gain):
-    n_grp, n_lane = lax.axis_size("grp"), lax.axis_size("lane")
+    n_grp, n_lane = lax.axis_size("grp"), lax.axis_size(LANE)
     count = pooled.shape[0]
     wire = Wire(count, n_grp * n_lane)
     factor = 1.0 / (count * n_grp * 2 * n_lane)
@@ -696,7 +698,7 @@
 
 def solution(mesh):
     n_grp, n_emb = mesh.shape["grp"], mesh.shape["emb"]
-    split = n_emb % 2 == 0 and n_grp * (n_emb // 2) == 16 and n_grp % 2 == 0
+    split = n_emb % 4 == 0 and n_grp * (n_emb // 2) == 16 and n_grp % 2 == 0
 
     def run(*args):
         pooled, _, _, _, tables, w_fm = args[:6]
@@ -711,8 +713,8 @@
             and count <= 12
         )
         if fits:
-            devices = mesh.devices.reshape(n_grp, 2, n_emb // 2)
-            where, emb, body = Mesh(devices, ("grp", "half", "lane")), ("half", "lane"), halves
+            devices = mesh.devices.reshape(n_grp, 2, n_emb // 4, 2)
+            where, emb, body = Mesh(devices, ("grp", "half", "deep", "core")), ("half",) + LANE, halves
         else:
             where, emb, body = mesh, ("emb",), local
         both = ("grp",) + emb

time: 86.8 us -> 84.3 us (0.971)
  waiting for transfers between devices: 43.6 us -> 40.7 us
    all_to_all x2, waiting for transfers between devices: 22.2 us -> 15.3 us  [exchange(): return lax.all_to_all(blocks, axes, split_axis=0, concat_axis=0, tiled=True)]
    ppermute x3, waiting for transfers between devices: 8.76 us -> 12.3 us  [halves(): lax.ppermute(pieces[k], 'grp', [(g, g ^ k) for g in range(n_grp)])]
  transfers between devices with their start and end apart: 8 -> 8, of which waited for: 6 -> 6; matrix products, arithmetic and copies ran while one was open for 0% -> 0% of each run, Pallas kernels for 19% -> 20%
where the time goes in v13:
time: 84.3 us; the launch traced here: 83.9 us
  waiting for transfers between devices  40.7 us (48%)
  Pallas kernels  21.7 us (26%)
  starting transfers between devices  19.7 us (23%)
  local copies, waits for them, and re-layouts  0.98 us (1%)
    all_to_all x2, waiting for transfers between devices, exchange(): return lax.all_to_all(blocks, axes, split_axis=0, concat_axis=0, tiled=True)  15.3 us
    ppermute x3, waiting for transfers between devices, cross(): return lax.ppermute(array, 'half', [(0, 1), (1, 0)])  13.1 us
    ppermute x3, waiting for transfers between devices, halves(): lax.ppermute(pieces[k], 'grp', [(g, g ^ k) for g in range(n_grp)])  12.3 us
    all_to_all x2, starting transfers between devices, exchange(): return lax.all_to_all(blocks, axes, split_axis=0, concat_axis=0, tiled=True)  9.16 us
    pallas_call x1, Pallas kernels, backward(): pl.pallas_call(functools.partial(backward_kernel, n_grp, n_lane, wire), g...  8.65 us
    ppermute x3, starting transfers between devices, cross(): return lax.ppermute(array, 'half', [(0, 1), (1, 0)])  7.03 us
    pallas_call x2, Pallas kernels, part_sums(): pl.pallas_call(functools.partial(part_kernel, n_grp, wire, other), grid=(...  3.69 us
    ppermute x3, starting transfers between devices, halves(): lax.ppermute(pieces[k], 'grp', [(g, g ^ k) for g in range(n_grp)])  3.55 us
  transfers between devices with their start and end apart: 8, of which 6 were waited for; matrix products, arithmetic and copies ran while one was open for 0% of the time, Pallas kernels for 20%

profile of v13, /device:TPU:0, one launch (start us, length us, event | category | flops | bytes accessed | tf_op | source)
XLA Modules:
  0.0 83.9 jit_solution(2364755398562914545)
XLA Ops:
  0.6 1.8 %take_tables.1.mine_t = bf16[8,192,128]{2,1,0:T(8,128)(2,1)} custom-call(s32[1]{0:T(128)} %bitcast.place, bf16[32,192,128]{2,1,0:T(8,128)(2,1)} %bitcast.14), custom_call_target="tpu_custom_call" | custom-call | flops 1000000000 | bytes 100000 | tf_op jit(solution)/shard_map/take_tables/pallas_call | solution.py:450
  2.4 4.0 %collective-permute-start = (bf16[8,192,128]{2,1,0:T(8,128)(2,1)}, bf16[8,192,128]{2,1,0:T(8,128)(2,1)S(1)}, u32[]{:S(2)}, u32[]{:S(2)}) collective-permute-start(bf16[8,192,128]{2,1,0:T(8,128)(2,1)} %take_tables.1.mine_t), channel_id=1, source_target_pairs={{0,4},{4,0},{1,5},{5,1},{2,6},{6,2},{3,7},{7,3},{8,12},{12,8},{9,1... | collective-permute-start | bytes 1179656 | tf_op jit(solution)/shard_map/ppermute | solution.py:665
  6.4 8.7 %layer_backward.1 = bf16[16,352,128]{2,1,0:T(8,128)(2,1)} custom-call(s32[1]{0:T(128)} %bitcast.1.half_ref, bf16[12,192,256]{2,1,0:T(8,128)(2,1)} %bitcast.10, bf16[12,192,256]{2,1,0:T(8,128)(2,1)} %bitcast.11, s32[12,256]{1,0:T(8,128)} %now_ref.1, s32[12,256]{1,0:T(8,128)} %next_ref.1, bf16[256,128]{1,0:T(8,128)(2,1)} %fm_ref.1, bf16[192,128]{1,0:T(8,128)(2,1)} %bitcast.12, ...), custom_call_target="tpu_custom_call" | custom-call | flops 1000000000 | bytes 100000 | tf_op jit(solution)/shard_map/layer_backward/pallas_call | solution.py:320
  15.1 5.0 %all-to-all-start = ((bf16[16,352,128]{2,1,0:T(8,128)(2,1)}), bf16[16,352,128]{2,1,0:T(8,128)(2,1)S(1)}, u32[]{:S(2)}, u32[]{:S(2)}) async-start(bf16[16,352,128]{2,1,0:T(8,128)(2,1)} %layer_backward.1), calls=%async_computation | async-start | bytes 2883584 | tf_op jit(solution)/shard_map/all_to_all | solution.py:62
  20.1 4.2 %collective-permute-done.crossed_t = bf16[8,192,128]{2,1,0:T(8,128)(2,1)S(1)} collective-permute-done((bf16[8,192,128]{2,1,0:T(8,128)(2,1)}, bf16[8,192,128]{2,1,0:T(8,128)(2,1)S(1)}, u32[]{:S(2)}, u32[]{:S(2)}) %collective-permute-start) | collective-permute-done | bytes 393248 | tf_op jit(solution)/shard_map/ppermute | solution.py:665
  24.3 0.3 stack_tables.1.stacked
  24.6 1.0 %copy-done.2 = bf16[2,256,1024]{2,1,0:T(8,128)(2,1)} copy-done((bf16[2,256,1024]{2,1,0:T(8,128)(2,1)}, bf16[2,256,1024]{2,1,0:T(8,128)(2,1)S(1)}, u32[]{:S(2)}) %copy-start.2) | copy-done | bytes 1048600
  25.6 15.3 %all-to-all-done.dense_ref.ids_ref.seen = bf16[16,352,128]{2,1,0:T(8,128)(2,1)S(1)} async-done(((bf16[16,352,128]{2,1,0:T(8,128)(2,1)}), bf16[16,352,128]{2,1,0:T(8,128)(2,1)S(1)}, u32[]{:S(2)}, u32[]{:S(2)}) %all-to-all-start) | async-done | bytes 1441824 | tf_op jit(solution)/shard_map/all_to_all | solution.py:62
  40.9 0.1 half_dense.1
  41.0 1.2 %collective-permute-start.1 = (f32[64,128]{1,0:T(8,128)S(1)}, f32[64,128]{1,0:T(8,128)S(1)}, u32[]{:S(2)}, u32[]{:S(2)}) collective-permute-start(f32[64,128]{1,0:T(8,128)S(1)} %get-tuple-element.21.own), channel_id=1, source_target_pairs={{0,4},{4,0},{1,5},{5,1},{2,6},{6,2},{3,7},{7,3},{8,12},{12,8},{9,1... | collective-permute-start | bytes 98312 | tf_op jit(solution)/shard_map/ppermute | solution.py:665
  42.2 2.2 %part_other.1 = bf16[4,8,48,128]{3,2,1,0:T(8,128)(2,1)} custom-call(s32[1]{0:T(128)} %bitcast.1.half_ref, bf16[16,352,128]{2,1,0:T(8,128)(2,1)S(1)} %all-to-all-done.dense_ref.ids_ref.seen, f32[16,16,128]{2,1,0:T(8,128)S(1)} %get-tuple-element.20.ids_ref.all_ids), custom_call_target="tpu_custom_call" | custom-call | flops 1000000000 | bytes 100000 | tf_op jit(solution)/shard_map/part_other/pallas_call | solution.py:426
  44.4 1.8 %collective-permute-start.2 = (bf16[4,8,48,128]{3,2,1,0:T(8,128)(2,1)}, bf16[4,8,48,128]{3,2,1,0:T(8,128)(2,1)S(1)}, u32[]{:S(2)}, u32[]{:S(2)}) collective-permute-start(bf16[4,8,48,128]{3,2,1,0:T(8,128)(2,1)} %part_other.1), channel_id=1, source_target_pairs={{0,4},{4,0},{1,5},{5,1},{2,6},{6,2},{3,7},{7,3},{8,12},{12,8},{9,1... | collective-permute-start | bytes 1179656 | tf_op jit(solution)/shard_map/ppermute | solution.py:665
  46.3 3.3 %lookup.1.rows = bf16[16,352,128]{2,1,0:T(8,128)(2,1)} custom-call(bf16[2,256,1024]{2,1,0:T(8,128)(2,1)S(1)} %copy-done.3, f32[16,16,128]{2,1,0:T(8,128)S(1)} %get-tuple-element.20.ids_ref.all_ids), custom_call_target="tpu_custom_call" | custom-call | flops 99999997952 | bytes 100000 | tf_op jit(solution)/shard_map/lookup/pallas_call | solution.py:517
  49.6 0.7 fill_dense.1
  50.3 4.2 %all-to-all-start.1 = ((bf16[16,352,128]{2,1,0:T(8,128)(2,1)}), bf16[16,352,128]{2,1,0:T(8,128)(2,1)S(1)}, u32[]{:S(2)}, u32[]{:S(2)}) async-start(bf16[16,352,128]{2,1,0:T(8,128)(2,1)} %get-tuple-element.22), calls=%async_computation.1 | async-start | bytes 2883584 | tf_op jit(solution)/shard_map/all_to_all | solution.py:62
  54.5 1.5 %part_own.1.own = f32[4,8,48,128]{3,2,1,0:T(8,128)S(1)} custom-call(s32[1]{0:T(128)} %bitcast.1.half_ref, bf16[16,352,128]{2,1,0:T(8,128)(2,1)S(1)} %all-to-all-done.dense_ref.ids_ref.seen, f32[16,16,128]{2,1,0:T(8,128)S(1)} %get-tuple-element.20.ids_ref.all_ids, f32[8,128]{1,0:T(8,128)S(1)} %copy-done.1), custom_call_target="tpu_custom_call" | custom-call | flops 1000000000 | bytes 100000 | tf_op jit(solution)/shard_map/part_own/pallas_call | solution.py:426
  56.0 8.9 %collective-permute-done.2.seen = bf16[4,8,48,128]{3,2,1,0:T(8,128)(2,1)S(1)} collective-permute-done((bf16[4,8,48,128]{3,2,1,0:T(8,128)(2,1)}, bf16[4,8,48,128]{3,2,1,0:T(8,128)(2,1)S(1)}, u32[]{:S(2)}, u32[]{:S(2)}) %collective-permute-start.2) | collective-permute-done | bytes 393248 | tf_op jit(solution)/shard_map/ppermute | solution.py:665
  65.0 1.7 %collective-permute-start.3 = (bf16[8,48,128]{2,1,0:T(8,128)(2,1)S(1)}, bf16[8,48,128]{2,1,0:T(8,128)(2,1)S(1)}, u32[]{:S(2)}, u32[]{:S(2)}) collective-permute-start(bf16[8,48,128]{2,1,0:T(8,128)(2,1)S(1)} %get-tuple-element.25), channel_id=1, source_target_pairs={{0,8},{8,0},{16,24},{24,16},{1,9},{9,1},{17,25},{25,17},{2,10},{10... | collective-permute-start | bytes 294920 | tf_op jit(solution)/shard_map/ppermute | solution.py:691
  66.7 1.5 %collective-permute-start.4 = (bf16[8,48,128]{2,1,0:T(8,128)(2,1)S(1)}, bf16[8,48,128]{2,1,0:T(8,128)(2,1)S(1)}, u32[]{:S(2)}, u32[]{:S(2)}) collective-permute-start(bf16[8,48,128]{2,1,0:T(8,128)(2,1)S(1)} %get-tuple-element.26), channel_id=1, source_target_pairs={{0,16},{8,24},{16,0},{24,8},{1,17},{9,25},{17,1},{25,9},{2,18},{10... | collective-permute-start | bytes 294920 | tf_op jit(solution)/shard_map/ppermute | solution.py:691
  68.2 0.3 collective-permute-start.5
  68.5 1.8 %collective-permute-done.3.refs_1_ = bf16[8,48,128]{2,1,0:T(8,128)(2,1)S(1)} collective-permute-done((bf16[8,48,128]{2,1,0:T(8,128)(2,1)S(1)}, bf16[8,48,128]{2,1,0:T(8,128)(2,1)S(1)}, u32[]{:S(2)}, u32[]{:S(2)}) %collective-permute-start.3) | collective-permute-done | bytes 98336 | tf_op jit(solution)/shard_map/ppermute | solution.py:691
  70.3 3.6 %collective-permute-done.4.refs_2_ = bf16[8,48,128]{2,1,0:T(8,128)(2,1)S(1)} collective-permute-done((bf16[8,48,128]{2,1,0:T(8,128)(2,1)S(1)}, bf16[8,48,128]{2,1,0:T(8,128)(2,1)S(1)}, u32[]{:S(2)}, u32[]{:S(2)}) %collective-permute-start.4) | collective-permute-done | bytes 98336 | tf_op jit(solution)/shard_map/ppermute | solution.py:691
  73.9 6.9 %collective-permute-done.5.refs_3_ = bf16[8,48,128]{2,1,0:T(8,128)(2,1)S(1)} collective-permute-done((bf16[8,48,128]{2,1,0:T(8,128)(2,1)S(1)}, bf16[8,48,128]{2,1,0:T(8,128)(2,1)S(1)}, u32[]{:S(2)}, u32[]{:S(2)}) %collective-permute-start.5) | collective-permute-done | bytes 98336 | tf_op jit(solution)/shard_map/ppermute | solution.py:691
  80.8 3.1 %unpack.1 = (bf16[12,192,256]{2,1,0:T(8,128)(2,1)}, f32[32,32,192]{2,1,0:T(8,128)}, f32[256,128]{1,0:T(8,128)}, f32[192,128]{1,0:T(8,128)}, f32[256,256]{1,0:T(8,128)}, /*index=5*/f32[1,192]{1,0:T(1,128)}) custom-call(s32[1]{0:T(128)} %bitcast.place, bf16[16,352,128]{2,1,0:T(8,128)(2,1)S(1)} %all-to-all-done.1.dense_ref.left0.left1.right0.right1, ...), custom_call_target="tpu_custom_call" | custom-call | flops 1000000000 | bytes 100000 | tf_op jit(solution)/shard_map/unpack/pallas_call | solution.py:627
  (10 shorter events, 0.1 us)
Async XLA Ops:
  2.4 21.9 %collective-permute-start = (bf16[8,192,128]{2,1,0:T(8,128)(2,1)}, bf16[8,192,128]{2,1,0:T(8,128)(2,1)S(1)}, u32[]{:S(2)}, u32[]{:S(2)}) collective-permute-start(bf16[8,192,128]{2,1,0:T(8,128)(2,1)} %take_tables.1.mine_t), channel_id=1, source_target_pairs={{0,4},{4,0},{1,5},{5,1},{2,6},{6,2},{3,7},{7,3},{8,12},{12,8},{9,1... | collective-permute-start | bytes 1179656 | tf_op jit(solution)/shard_map/ppermute | solution.py:665
  15.1 9.2 %copy-start = (bf16[8,192,128]{2,1,0:T(8,128)(2,1)S(1)}, bf16[8,192,128]{2,1,0:T(8,128)(2,1)}, u32[]{:S(2)}) copy-start(bf16[8,192,128]{2,1,0:T(8,128)(2,1)} %take_tables.1.mine_t) | copy-start | bytes 1179652
  15.1 25.8 %all-to-all-start = ((bf16[16,352,128]{2,1,0:T(8,128)(2,1)}), bf16[16,352,128]{2,1,0:T(8,128)(2,1)S(1)}, u32[]{:S(2)}, u32[]{:S(2)}) async-start(bf16[16,352,128]{2,1,0:T(8,128)(2,1)} %layer_backward.1), calls=%async_computation | async-start | bytes 2883584 | tf_op jit(solution)/shard_map/all_to_all | solution.py:62
  24.6 1.0 %copy-start.2 = (bf16[2,256,1024]{2,1,0:T(8,128)(2,1)}, bf16[2,256,1024]{2,1,0:T(8,128)(2,1)S(1)}, u32[]{:S(2)}) copy-start(bf16[2,256,1024]{2,1,0:T(8,128)(2,1)S(1)} %stack_tables.1.stacked) | copy-start | bytes 3145732
  41.0 8.6 %collective-permute-start.1 = (f32[64,128]{1,0:T(8,128)S(1)}, f32[64,128]{1,0:T(8,128)S(1)}, u32[]{:S(2)}, u32[]{:S(2)}) collective-permute-start(f32[64,128]{1,0:T(8,128)S(1)} %get-tuple-element.21.own), channel_id=1, source_target_pairs={{0,4},{4,0},{1,5},{5,1},{2,6},{6,2},{3,7},{7,3},{8,12},{12,8},{9,1... | collective-permute-start | bytes 98312 | tf_op jit(solution)/shard_map/ppermute | solution.py:665
  42.2 4.1 %copy-start.3 = (bf16[2,256,1024]{2,1,0:T(8,128)(2,1)S(1)}, bf16[2,256,1024]{2,1,0:T(8,128)(2,1)}, u32[]{:S(2)}) copy-start(bf16[2,256,1024]{2,1,0:T(8,128)(2,1)} %copy-done.2) | copy-start | bytes 3145732
  44.4 20.5 %collective-permute-start.2 = (bf16[4,8,48,128]{3,2,1,0:T(8,128)(2,1)}, bf16[4,8,48,128]{3,2,1,0:T(8,128)(2,1)S(1)}, u32[]{:S(2)}, u32[]{:S(2)}) collective-permute-start(bf16[4,8,48,128]{3,2,1,0:T(8,128)(2,1)} %part_other.1), channel_id=1, source_target_pairs={{0,4},{4,0},{1,5},{5,1},{2,6},{6,2},{3,7},{7,3},{8,12},{12,8},{9,1... | collective-permute-start | bytes 1179656 | tf_op jit(solution)/shard_map/ppermute | solution.py:665
  50.3 4.2 %copy-start.1 = (f32[8,128]{1,0:T(8,128)S(1)}, f32[8,128]{1,0:T(8,128)}, u32[]{:S(2)}) copy-start(f32[8,128]{1,0:T(8,128)} %get-tuple-element.23.refs_0_.after) | copy-start | bytes 12292
  50.3 30.5 %all-to-all-start.1 = ((bf16[16,352,128]{2,1,0:T(8,128)(2,1)}), bf16[16,352,128]{2,1,0:T(8,128)(2,1)S(1)}, u32[]{:S(2)}, u32[]{:S(2)}) async-start(bf16[16,352,128]{2,1,0:T(8,128)(2,1)} %get-tuple-element.22), calls=%async_computation.1 | async-start | bytes 2883584 | tf_op jit(solution)/shard_map/all_to_all | solution.py:62
  65.0 5.3 %collective-permute-start.3 = (bf16[8,48,128]{2,1,0:T(8,128)(2,1)S(1)}, bf16[8,48,128]{2,1,0:T(8,128)(2,1)S(1)}, u32[]{:S(2)}, u32[]{:S(2)}) collective-permute-start(bf16[8,48,128]{2,1,0:T(8,128)(2,1)S(1)} %get-tuple-element.25), channel_id=1, source_target_pairs={{0,8},{8,0},{16,24},{24,16},{1,9},{9,1},{17,25},{25,17},{2,10},{10... | collective-permute-start | bytes 294920 | tf_op jit(solution)/shard_map/ppermute | solution.py:691
  66.7 7.2 %collective-permute-start.4 = (bf16[8,48,128]{2,1,0:T(8,128)(2,1)S(1)}, bf16[8,48,128]{2,1,0:T(8,128)(2,1)S(1)}, u32[]{:S(2)}, u32[]{:S(2)}) collective-permute-start(bf16[8,48,128]{2,1,0:T(8,128)(2,1)S(1)} %get-tuple-element.26), channel_id=1, source_target_pairs={{0,16},{8,24},{16,0},{24,8},{1,17},{9,25},{17,1},{25,9},{2,18},{10... | collective-permute-start | bytes 294920 | tf_op jit(solution)/shard_map/ppermute | solution.py:691
  68.2 12.6 %collective-permute-start.5 = (bf16[8,48,128]{2,1,0:T(8,128)(2,1)S(1)}, bf16[8,48,128]{2,1,0:T(8,128)(2,1)S(1)}, u32[]{:S(2)}, u32[]{:S(2)}) collective-permute-start(bf16[8,48,128]{2,1,0:T(8,128)(2,1)S(1)} %get-tuple-element.27), channel_id=1, source_target_pairs={{0,24},{8,16},{16,8},{24,0},{1,25},{9,17},{17,9},{25,1},{2,26},{10... | collective-permute-start | bytes 294920 | tf_op jit(solution)/shard_map/ppermute | solution.py:691

commit v14 on v13

--- a/solution.py
+++ b/solution.py
@@ -555,9 +555,13 @@
     )(rows, own, seen)
 
 
+def far_first(n_grp):
+    return [0] + list(range(n_grp - 1, 0, -1))
+
+
 def finish_pieces(grp, pieces, out):
     piece = out.shape[1]
-    for k, seen in enumerate(pieces):
+    for k, seen in zip(far_first(len(pieces)), pieces):
         base = jnp.bitwise_xor(grp, k) * TILE
         for f in range(TILE):
             out[base + f, :, 0:128] = seen[f, 0:piece].astype(F32)
@@ -642,7 +646,7 @@
 
 
 def combine_kernel(place, own, seen, after, *outs):
-    for k, out in enumerate(outs):
+    for k, out in zip(far_first(len(outs)), outs):
         g = jnp.bitwise_xor(place[0], k)
         out[...] = (own[g] + seen[g].astype(F32)).astype(BF16)
 
@@ -686,10 +690,9 @@
     rows_wire, token = fill(wire, factor, rows_wire, dense, dense_seen)
     rows = exchange(rows_wire, PEER)
     own = part_sums(n_grp, wire, False, half, seen, ids, token)
-    pieces = combine(grp[None], own, part_seen, token)
-    pieces = [pieces[0]] + [
-        lax.ppermute(pieces[k], "grp", [(g, g ^ k) for g in range(n_grp)]) for k in range(1, n_grp)
-    ]
+    pieces = list(combine(grp[None], own, part_seen, token))
+    for at, k in list(enumerate(far_first(n_grp)))[1:]:
+        pieces[at] = lax.ppermute(pieces[at], "grp", [(g, g ^ k) for g in range(n_grp)])
     next_rows, table_grad, grad_fm, grad_proj_t, grad_lcb, grad_gain = unpack(
         n_grp, n_lane, wire, count, grp[None], rows, pieces
     )

time: 84.3 us -> 83.8 us (level)
  no operation moved by 1% of the time
where the time goes in v14:
time: 83.8 us; the launch traced here: 83.4 us
  waiting for transfers between devices  40.2 us (48%)
  Pallas kernels  21.7 us (26%)
  starting transfers between devices  19.7 us (24%)
  local copies, waits for them, and re-layouts  0.98 us (1%)
    all_to_all x2, waiting for transfers between devices, exchange(): return lax.all_to_all(blocks, axes, split_axis=0, concat_axis=0, tiled=True)  15.3 us
    ppermute x3, waiting for transfers between devices, cross(): return lax.ppermute(array, 'half', [(0, 1), (1, 0)])  13.1 us
    ppermute x3, waiting for transfers between devices, halves(): lax.ppermute(pieces[at], 'grp', [(g, g ^ k) for g in range(n_grp)])  11.8 us
    all_to_all x2, starting transfers between devices, exchange(): return lax.all_to_all(blocks, axes, split_axis=0, concat_axis=0, tiled=True)  9.16 us
    pallas_call x1, Pallas kernels, backward(): pl.pallas_call(functools.partial(backward_kernel, n_grp, n_lane, wire), g...  8.65 us
    ppermute x3, starting transfers between devices, cross(): return lax.ppermute(array, 'half', [(0, 1), (1, 0)])  7.03 us
    pallas_call x2, Pallas kernels, part_sums(): pl.pallas_call(functools.partial(part_kernel, n_grp, wire, other), grid=(...  3.69 us
    ppermute x3, starting transfers between devices, halves(): lax.ppermute(pieces[at], 'grp', [(g, g ^ k) for g in range(n_grp)])  3.55 us
  transfers between devices with their start and end apart: 8, of which 6 were waited for; matrix products, arithmetic and copies ran while one was open for 0% of the time, Pallas kernels for 20%

profile of v14, /device:TPU:0, one launch (start us, length us, event | category | flops | bytes accessed | tf_op | source)
XLA Modules:
  0.0 83.4 jit_solution(1273604056074517796)
XLA Ops:
  0.6 1.8 %take_tables.1.mine_t = bf16[8,192,128]{2,1,0:T(8,128)(2,1)} custom-call(s32[1]{0:T(128)} %bitcast.place, bf16[32,192,128]{2,1,0:T(8,128)(2,1)} %bitcast.14), custom_call_target="tpu_custom_call" | custom-call | flops 1000000000 | bytes 100000 | tf_op jit(solution)/shard_map/take_tables/pallas_call | solution.py:450
  2.4 4.0 %collective-permute-start = (bf16[8,192,128]{2,1,0:T(8,128)(2,1)}, bf16[8,192,128]{2,1,0:T(8,128)(2,1)S(1)}, u32[]{:S(2)}, u32[]{:S(2)}) collective-permute-start(bf16[8,192,128]{2,1,0:T(8,128)(2,1)} %take_tables.1.mine_t), channel_id=1, source_target_pairs={{0,4},{4,0},{1,5},{5,1},{2,6},{6,2},{3,7},{7,3},{8,12},{12,8},{9,1... | collective-permute-start | bytes 1179656 | tf_op jit(solution)/shard_map/ppermute | solution.py:669
  6.4 8.7 %layer_backward.1 = bf16[16,352,128]{2,1,0:T(8,128)(2,1)} custom-call(s32[1]{0:T(128)} %bitcast.1.half_ref, bf16[12,192,256]{2,1,0:T(8,128)(2,1)} %bitcast.10, bf16[12,192,256]{2,1,0:T(8,128)(2,1)} %bitcast.11, s32[12,256]{1,0:T(8,128)} %now_ref.1, s32[12,256]{1,0:T(8,128)} %next_ref.1, bf16[256,128]{1,0:T(8,128)(2,1)} %fm_ref.1, bf16[192,128]{1,0:T(8,128)(2,1)} %bitcast.12, ...), custom_call_target="tpu_custom_call" | custom-call | flops 1000000000 | bytes 100000 | tf_op jit(solution)/shard_map/layer_backward/pallas_call | solution.py:320
  15.1 5.0 %all-to-all-start = ((bf16[16,352,128]{2,1,0:T(8,128)(2,1)}), bf16[16,352,128]{2,1,0:T(8,128)(2,1)S(1)}, u32[]{:S(2)}, u32[]{:S(2)}) async-start(bf16[16,352,128]{2,1,0:T(8,128)(2,1)} %layer_backward.1), calls=%async_computation | async-start | bytes 2883584 | tf_op jit(solution)/shard_map/all_to_all | solution.py:62
  20.1 4.2 %collective-permute-done.crossed_t = bf16[8,192,128]{2,1,0:T(8,128)(2,1)S(1)} collective-permute-done((bf16[8,192,128]{2,1,0:T(8,128)(2,1)}, bf16[8,192,128]{2,1,0:T(8,128)(2,1)S(1)}, u32[]{:S(2)}, u32[]{:S(2)}) %collective-permute-start) | collective-permute-done | bytes 393248 | tf_op jit(solution)/shard_map/ppermute | solution.py:669
  24.3 0.3 stack_tables.1.stacked
  24.6 1.0 %copy-done.2 = bf16[2,256,1024]{2,1,0:T(8,128)(2,1)} copy-done((bf16[2,256,1024]{2,1,0:T(8,128)(2,1)}, bf16[2,256,1024]{2,1,0:T(8,128)(2,1)S(1)}, u32[]{:S(2)}) %copy-start.2) | copy-done | bytes 1048600
  25.6 15.3 %all-to-all-done.dense_ref.ids_ref.seen = bf16[16,352,128]{2,1,0:T(8,128)(2,1)S(1)} async-done(((bf16[16,352,128]{2,1,0:T(8,128)(2,1)}), bf16[16,352,128]{2,1,0:T(8,128)(2,1)S(1)}, u32[]{:S(2)}, u32[]{:S(2)}) %all-to-all-start) | async-done | bytes 1441824 | tf_op jit(solution)/shard_map/all_to_all | solution.py:62
  40.9 0.1 half_dense.1
  41.0 1.2 %collective-permute-start.1 = (f32[64,128]{1,0:T(8,128)S(1)}, f32[64,128]{1,0:T(8,128)S(1)}, u32[]{:S(2)}, u32[]{:S(2)}) collective-permute-start(f32[64,128]{1,0:T(8,128)S(1)} %get-tuple-element.21.own), channel_id=1, source_target_pairs={{0,4},{4,0},{1,5},{5,1},{2,6},{6,2},{3,7},{7,3},{8,12},{12,8},{9,1... | collective-permute-start | bytes 98312 | tf_op jit(solution)/shard_map/ppermute | solution.py:669
  42.2 2.2 %part_other.1 = bf16[4,8,48,128]{3,2,1,0:T(8,128)(2,1)} custom-call(s32[1]{0:T(128)} %bitcast.1.half_ref, bf16[16,352,128]{2,1,0:T(8,128)(2,1)S(1)} %all-to-all-done.dense_ref.ids_ref.seen, f32[16,16,128]{2,1,0:T(8,128)S(1)} %get-tuple-element.20.ids_ref.all_ids), custom_call_target="tpu_custom_call" | custom-call | flops 1000000000 | bytes 100000 | tf_op jit(solution)/shard_map/part_other/pallas_call | solution.py:426
  44.4 1.8 %collective-permute-start.2 = (bf16[4,8,48,128]{3,2,1,0:T(8,128)(2,1)}, bf16[4,8,48,128]{3,2,1,0:T(8,128)(2,1)S(1)}, u32[]{:S(2)}, u32[]{:S(2)}) collective-permute-start(bf16[4,8,48,128]{3,2,1,0:T(8,128)(2,1)} %part_other.1), channel_id=1, source_target_pairs={{0,4},{4,0},{1,5},{5,1},{2,6},{6,2},{3,7},{7,3},{8,12},{12,8},{9,1... | collective-permute-start | bytes 1179656 | tf_op jit(solution)/shard_map/ppermute | solution.py:669
  46.3 3.3 %lookup.1.rows = bf16[16,352,128]{2,1,0:T(8,128)(2,1)} custom-call(bf16[2,256,1024]{2,1,0:T(8,128)(2,1)S(1)} %copy-done.3, f32[16,16,128]{2,1,0:T(8,128)S(1)} %get-tuple-element.20.ids_ref.all_ids), custom_call_target="tpu_custom_call" | custom-call | flops 99999997952 | bytes 100000 | tf_op jit(solution)/shard_map/lookup/pallas_call | solution.py:517
  49.6 0.7 fill_dense.1
  50.3 4.2 %all-to-all-start.1 = ((bf16[16,352,128]{2,1,0:T(8,128)(2,1)}), bf16[16,352,128]{2,1,0:T(8,128)(2,1)S(1)}, u32[]{:S(2)}, u32[]{:S(2)}) async-start(bf16[16,352,128]{2,1,0:T(8,128)(2,1)} %get-tuple-element.22), calls=%async_computation.1 | async-start | bytes 2883584 | tf_op jit(solution)/shard_map/all_to_all | solution.py:62
  54.5 1.5 %part_own.1.own = f32[4,8,48,128]{3,2,1,0:T(8,128)S(1)} custom-call(s32[1]{0:T(128)} %bitcast.1.half_ref, bf16[16,352,128]{2,1,0:T(8,128)(2,1)S(1)} %all-to-all-done.dense_ref.ids_ref.seen, f32[16,16,128]{2,1,0:T(8,128)S(1)} %get-tuple-element.20.ids_ref.all_ids, f32[8,128]{1,0:T(8,128)S(1)} %copy-done.1), custom_call_target="tpu_custom_call" | custom-call | flops 1000000000 | bytes 100000 | tf_op jit(solution)/shard_map/part_own/pallas_call | solution.py:426
  56.0 8.9 %collective-permute-done.2.seen = bf16[4,8,48,128]{3,2,1,0:T(8,128)(2,1)S(1)} collective-permute-done((bf16[4,8,48,128]{3,2,1,0:T(8,128)(2,1)}, bf16[4,8,48,128]{3,2,1,0:T(8,128)(2,1)S(1)}, u32[]{:S(2)}, u32[]{:S(2)}) %collective-permute-start.2) | collective-permute-done | bytes 393248 | tf_op jit(solution)/shard_map/ppermute | solution.py:669
  65.0 2.7 %collective-permute-start.3 = (bf16[8,48,128]{2,1,0:T(8,128)(2,1)S(1)}, bf16[8,48,128]{2,1,0:T(8,128)(2,1)S(1)}, u32[]{:S(2)}, u32[]{:S(2)}) collective-permute-start(bf16[8,48,128]{2,1,0:T(8,128)(2,1)S(1)} %get-tuple-element.25), channel_id=1, source_target_pairs={{0,24},{8,16},{16,8},{24,0},{1,25},{9,17},{17,9},{25,1},{2,26},{10... | collective-permute-start | bytes 294920 | tf_op jit(solution)/shard_map/ppermute | solution.py:695
  67.7 0.5 collective-permute-start.4
  68.2 0.3 collective-permute-start.5
  68.5 2.6 %collective-permute-done.3.refs_1_ = bf16[8,48,128]{2,1,0:T(8,128)(2,1)S(1)} collective-permute-done((bf16[8,48,128]{2,1,0:T(8,128)(2,1)S(1)}, bf16[8,48,128]{2,1,0:T(8,128)(2,1)S(1)}, u32[]{:S(2)}, u32[]{:S(2)}) %collective-permute-start.3) | collective-permute-done | bytes 98336 | tf_op jit(solution)/shard_map/ppermute | solution.py:695
  71.2 2.2 %collective-permute-done.4.refs_2_ = bf16[8,48,128]{2,1,0:T(8,128)(2,1)S(1)} collective-permute-done((bf16[8,48,128]{2,1,0:T(8,128)(2,1)S(1)}, bf16[8,48,128]{2,1,0:T(8,128)(2,1)S(1)}, u32[]{:S(2)}, u32[]{:S(2)}) %collective-permute-start.4) | collective-permute-done | bytes 98336 | tf_op jit(solution)/shard_map/ppermute | solution.py:695
  73.4 6.9 %collective-permute-done.5.refs_3_ = bf16[8,48,128]{2,1,0:T(8,128)(2,1)S(1)} collective-permute-done((bf16[8,48,128]{2,1,0:T(8,128)(2,1)S(1)}, bf16[8,48,128]{2,1,0:T(8,128)(2,1)S(1)}, u32[]{:S(2)}, u32[]{:S(2)}) %collective-permute-start.5) | collective-permute-done | bytes 98336 | tf_op jit(solution)/shard_map/ppermute | solution.py:695
  80.3 3.1 %unpack.1 = (bf16[12,192,256]{2,1,0:T(8,128)(2,1)}, f32[32,32,192]{2,1,0:T(8,128)}, f32[256,128]{1,0:T(8,128)}, f32[192,128]{1,0:T(8,128)}, f32[256,256]{1,0:T(8,128)}, /*index=5*/f32[1,192]{1,0:T(1,128)}) custom-call(s32[1]{0:T(128)} %bitcast.place, bf16[16,352,128]{2,1,0:T(8,128)(2,1)S(1)} %all-to-all-done.1.dense_ref.left0.left1.right0.right1, ...), custom_call_target="tpu_custom_call" | custom-call | flops 1000000000 | bytes 100000 | tf_op jit(solution)/shard_map/unpack/pallas_call | solution.py:631
  (10 shorter events, 0.1 us)
Async XLA Ops:
  2.4 21.9 %collective-permute-start = (bf16[8,192,128]{2,1,0:T(8,128)(2,1)}, bf16[8,192,128]{2,1,0:T(8,128)(2,1)S(1)}, u32[]{:S(2)}, u32[]{:S(2)}) collective-permute-start(bf16[8,192,128]{2,1,0:T(8,128)(2,1)} %take_tables.1.mine_t), channel_id=1, source_target_pairs={{0,4},{4,0},{1,5},{5,1},{2,6},{6,2},{3,7},{7,3},{8,12},{12,8},{9,1... | collective-permute-start | bytes 1179656 | tf_op jit(solution)/shard_map/ppermute | solution.py:669
  15.1 9.2 %copy-start = (bf16[8,192,128]{2,1,0:T(8,128)(2,1)S(1)}, bf16[8,192,128]{2,1,0:T(8,128)(2,1)}, u32[]{:S(2)}) copy-start(bf16[8,192,128]{2,1,0:T(8,128)(2,1)} %take_tables.1.mine_t) | copy-start | bytes 1179652
  15.1 25.8 %all-to-all-start = ((bf16[16,352,128]{2,1,0:T(8,128)(2,1)}), bf16[16,352,128]{2,1,0:T(8,128)(2,1)S(1)}, u32[]{:S(2)}, u32[]{:S(2)}) async-start(bf16[16,352,128]{2,1,0:T(8,128)(2,1)} %layer_backward.1), calls=%async_computation | async-start | bytes 2883584 | tf_op jit(solution)/shard_map/all_to_all | solution.py:62
  24.6 1.0 %copy-start.2 = (bf16[2,256,1024]{2,1,0:T(8,128)(2,1)}, bf16[2,256,1024]{2,1,0:T(8,128)(2,1)S(1)}, u32[]{:S(2)}) copy-start(bf16[2,256,1024]{2,1,0:T(8,128)(2,1)S(1)} %stack_tables.1.stacked) | copy-start | bytes 3145732
  41.0 8.6 %collective-permute-start.1 = (f32[64,128]{1,0:T(8,128)S(1)}, f32[64,128]{1,0:T(8,128)S(1)}, u32[]{:S(2)}, u32[]{:S(2)}) collective-permute-start(f32[64,128]{1,0:T(8,128)S(1)} %get-tuple-element.21.own), channel_id=1, source_target_pairs={{0,4},{4,0},{1,5},{5,1},{2,6},{6,2},{3,7},{7,3},{8,12},{12,8},{9,1... | collective-permute-start | bytes 98312 | tf_op jit(solution)/shard_map/ppermute | solution.py:669
  42.2 4.1 %copy-start.3 = (bf16[2,256,1024]{2,1,0:T(8,128)(2,1)S(1)}, bf16[2,256,1024]{2,1,0:T(8,128)(2,1)}, u32[]{:S(2)}) copy-start(bf16[2,256,1024]{2,1,0:T(8,128)(2,1)} %copy-done.2) | copy-start | bytes 3145732
  44.4 20.5 %collective-permute-start.2 = (bf16[4,8,48,128]{3,2,1,0:T(8,128)(2,1)}, bf16[4,8,48,128]{3,2,1,0:T(8,128)(2,1)S(1)}, u32[]{:S(2)}, u32[]{:S(2)}) collective-permute-start(bf16[4,8,48,128]{3,2,1,0:T(8,128)(2,1)} %part_other.1), channel_id=1, source_target_pairs={{0,4},{4,0},{1,5},{5,1},{2,6},{6,2},{3,7},{7,3},{8,12},{12,8},{9,1... | collective-permute-start | bytes 1179656 | tf_op jit(solution)/shard_map/ppermute | solution.py:669
  50.3 4.2 %copy-start.1 = (f32[8,128]{1,0:T(8,128)S(1)}, f32[8,128]{1,0:T(8,128)}, u32[]{:S(2)}) copy-start(f32[8,128]{1,0:T(8,128)} %get-tuple-element.23.refs_0_.after) | copy-start | bytes 12292
  50.3 30.0 %all-to-all-start.1 = ((bf16[16,352,128]{2,1,0:T(8,128)(2,1)}), bf16[16,352,128]{2,1,0:T(8,128)(2,1)S(1)}, u32[]{:S(2)}, u32[]{:S(2)}) async-start(bf16[16,352,128]{2,1,0:T(8,128)(2,1)} %get-tuple-element.22), calls=%async_computation.1 | async-start | bytes 2883584 | tf_op jit(solution)/shard_map/all_to_all | solution.py:62
  65.0 6.2 %collective-permute-start.3 = (bf16[8,48,128]{2,1,0:T(8,128)(2,1)S(1)}, bf16[8,48,128]{2,1,0:T(8,128)(2,1)S(1)}, u32[]{:S(2)}, u32[]{:S(2)}) collective-permute-start(bf16[8,48,128]{2,1,0:T(8,128)(2,1)S(1)} %get-tuple-element.25), channel_id=1, source_target_pairs={{0,24},{8,16},{16,8},{24,0},{1,25},{9,17},{17,9},{25,1},{2,26},{10... | collective-permute-start | bytes 294920 | tf_op jit(solution)/shard_map/ppermute | solution.py:695
  67.7 5.7 %collective-permute-start.4 = (bf16[8,48,128]{2,1,0:T(8,128)(2,1)S(1)}, bf16[8,48,128]{2,1,0:T(8,128)(2,1)S(1)}, u32[]{:S(2)}, u32[]{:S(2)}) collective-permute-start(bf16[8,48,128]{2,1,0:T(8,128)(2,1)S(1)} %get-tuple-element.26), channel_id=1, source_target_pairs={{0,16},{8,24},{16,0},{24,8},{1,17},{9,25},{17,1},{25,9},{2,18},{10... | collective-permute-start | bytes 294920 | tf_op jit(solution)/shard_map/ppermute | solution.py:695
  68.2 12.1 %collective-permute-start.5 = (bf16[8,48,128]{2,1,0:T(8,128)(2,1)S(1)}, bf16[8,48,128]{2,1,0:T(8,128)(2,1)S(1)}, u32[]{:S(2)}, u32[]{:S(2)}) collective-permute-start(bf16[8,48,128]{2,1,0:T(8,128)(2,1)S(1)} %get-tuple-element.27), channel_id=1, source_target_pairs={{0,8},{8,0},{16,24},{24,16},{1,9},{9,1},{17,25},{25,17},{2,10},{10... | collective-permute-start | bytes 294920 | tf_op jit(solution)/shard_map/ppermute | solution.py:695

commit v15 on v14

--- a/solution.py
+++ b/solution.py
@@ -15,7 +15,7 @@
 STEP = 4
 LIMIT = 30 * 1024 * 1024
 LANE = ("deep", "core")
-PEER = ("core", "deep", "grp")
+PEER = ("deep", "grp", "core")
 
 
 BOTH = ("grp", "emb")
@@ -146,7 +146,7 @@
 
 
 def place_of(n_grp, n_lane, peer):
-    core, deep, g = peer // (n_grp * n_lane // 2), peer // n_grp % (n_lane // 2), peer % n_grp
+    deep, g, core = peer // (2 * n_grp), peer // 2 % n_grp, peer % 2
     return ((deep * 2 + core) * n_grp + g) * TILE
 
 
@@ -580,7 +580,7 @@
             for gg in range(n_grp // 2):
                 left, right = [], []
                 for g in (2 * gg, 2 * gg + 1):
-                    peer = (q % 2 * (n_lane // 2) + q // 2) * n_grp + g
+                    peer = (q // 2 * n_grp + g) * 2 + q % 2
                     left.append(left_ref[peer].astype(F32))
                     packed = right_ref[peer].astype(F32)
                     right.append(jnp.concatenate([packed, turn(packed)], axis=0))

time: 83.8 us -> 86.7 us (1.035)
  starting transfers between devices: 19.7 us -> 21.3 us
  waiting for transfers between devices: 40.2 us -> 41.6 us
    all_to_all x2, waiting for transfers between devices: 15.3 us -> 20.6 us  [exchange(): return lax.all_to_all(blocks, axes, split_axis=0, concat_axis=0, tiled=True)]
    ppermute x3, waiting for transfers between devices: 11.8 us -> 9.53 us  [halves(): lax.ppermute(pieces[at], 'grp', [(g, g ^ k) for g in range(n_grp)])]
    ppermute x3, waiting for transfers between devices: 13.1 us -> 11.4 us  [cross(): return lax.ppermute(array, 'half', [(0, 1), (1, 0)])]
    all_to_all x2, starting transfers between devices: 9.16 us -> 10 us  [exchange(): return lax.all_to_all(blocks, axes, split_axis=0, concat_axis=0, tiled=True)]
  transfers between devices with their start and end apart: 8 -> 8, of which waited for: 6 -> 7; matrix products, arithmetic and copies ran while one was open for 0% -> 0% of each run, Pallas kernels for 20% -> 19%
where the time goes in v15:
time: 86.7 us; the launch traced here: 86.3 us
  waiting for transfers between devices  41.6 us (48%)
  Pallas kernels  21.8 us (25%)
  starting transfers between devices  21.3 us (25%)
  local copies, waits for them, and re-layouts  0.98 us (1%)
    all_to_all x2, waiting for transfers between devices, exchange(): return lax.all_to_all(blocks, axes, split_axis=0, concat_axis=0, tiled=True)  20.6 us
    ppermute x3, waiting for transfers between devices, cross(): return lax.ppermute(array, 'half', [(0, 1), (1, 0)])  11.4 us
    all_to_all x2, starting transfers between devices, exchange(): return lax.all_to_all(blocks, axes, split_axis=0, concat_axis=0, tiled=True)  10 us
    ppermute x3, waiting for transfers between devices, halves(): lax.ppermute(pieces[at], 'grp', [(g, g ^ k) for g in range(n_grp)])  9.53 us
    pallas_call x1, Pallas kernels, backward(): pl.pallas_call(functools.partial(backward_kernel, n_grp, n_lane, wire), g...  8.65 us
    ppermute x3, starting transfers between devices, cross(): return lax.ppermute(array, 'half', [(0, 1), (1, 0)])  7 us
    ppermute x3, starting transfers between devices, halves(): lax.ppermute(pieces[at], 'grp', [(g, g ^ k) for g in range(n_grp)])  4.22 us
    pallas_call x2, Pallas kernels, part_sums(): pl.pallas_call(functools.partial(part_kernel, n_grp, wire, other), grid=(...  3.69 us
  transfers between devices with their start and end apart: 8, of which 7 were waited for; matrix products, arithmetic and copies ran while one was open for 0% of the time, Pallas kernels for 19%

profile of v15, /device:TPU:0, one launch (start us, length us, event | category | flops | bytes accessed | tf_op | source)
XLA Modules:
  0.0 86.3 jit_solution(1644407298805758102)
XLA Ops:
  0.6 1.8 %take_tables.1.mine_t = bf16[8,192,128]{2,1,0:T(8,128)(2,1)} custom-call(s32[1]{0:T(128)} %bitcast.place, bf16[32,192,128]{2,1,0:T(8,128)(2,1)} %bitcast.14), custom_call_target="tpu_custom_call" | custom-call | flops 1000000000 | bytes 100000 | tf_op jit(solution)/shard_map/take_tables/pallas_call | solution.py:450
  2.4 4.0 %collective-permute-start = (bf16[8,192,128]{2,1,0:T(8,128)(2,1)}, bf16[8,192,128]{2,1,0:T(8,128)(2,1)S(1)}, u32[]{:S(2)}, u32[]{:S(2)}) collective-permute-start(bf16[8,192,128]{2,1,0:T(8,128)(2,1)} %take_tables.1.mine_t), channel_id=1, source_target_pairs={{0,4},{4,0},{1,5},{5,1},{2,6},{6,2},{3,7},{7,3},{8,12},{12,8},{9,1... | collective-permute-start | bytes 1179656 | tf_op jit(solution)/shard_map/ppermute | solution.py:669
  6.4 8.7 %layer_backward.1 = bf16[16,352,128]{2,1,0:T(8,128)(2,1)} custom-call(s32[1]{0:T(128)} %bitcast.1.half_ref, bf16[12,192,256]{2,1,0:T(8,128)(2,1)} %bitcast.10, bf16[12,192,256]{2,1,0:T(8,128)(2,1)} %bitcast.11, s32[12,256]{1,0:T(8,128)} %now_ref.1, s32[12,256]{1,0:T(8,128)} %next_ref.1, bf16[256,128]{1,0:T(8,128)(2,1)} %fm_ref.1, bf16[192,128]{1,0:T(8,128)(2,1)} %bitcast.12, ...), custom_call_target="tpu_custom_call" | custom-call | flops 1000000000 | bytes 100000 | tf_op jit(solution)/shard_map/layer_backward/pallas_call | solution.py:320
  15.1 5.0 %all-to-all-start = ((bf16[16,352,128]{2,1,0:T(8,128)(2,1)}), bf16[16,352,128]{2,1,0:T(8,128)(2,1)S(1)}, u32[]{:S(2)}, u32[]{:S(2)}) async-start(bf16[16,352,128]{2,1,0:T(8,128)(2,1)} %layer_backward.1), calls=%async_computation | async-start | bytes 2883584 | tf_op jit(solution)/shard_map/all_to_all | solution.py:62
  20.1 4.2 %collective-permute-done.crossed_t = bf16[8,192,128]{2,1,0:T(8,128)(2,1)S(1)} collective-permute-done((bf16[8,192,128]{2,1,0:T(8,128)(2,1)}, bf16[8,192,128]{2,1,0:T(8,128)(2,1)S(1)}, u32[]{:S(2)}, u32[]{:S(2)}) %collective-permute-start) | collective-permute-done | bytes 393248 | tf_op jit(solution)/shard_map/ppermute | solution.py:669
  24.3 0.3 stack_tables.1.stacked
  24.6 1.0 %copy-done.2 = bf16[2,256,1024]{2,1,0:T(8,128)(2,1)} copy-done((bf16[2,256,1024]{2,1,0:T(8,128)(2,1)}, bf16[2,256,1024]{2,1,0:T(8,128)(2,1)S(1)}, u32[]{:S(2)}) %copy-start.2) | copy-done | bytes 1048600
  25.6 16.3 %all-to-all-done.dense_ref.ids_ref.seen = bf16[16,352,128]{2,1,0:T(8,128)(2,1)S(1)} async-done(((bf16[16,352,128]{2,1,0:T(8,128)(2,1)}), bf16[16,352,128]{2,1,0:T(8,128)(2,1)S(1)}, u32[]{:S(2)}, u32[]{:S(2)}) %all-to-all-start) | async-done | bytes 1441824 | tf_op jit(solution)/shard_map/all_to_all | solution.py:62
  41.8 0.1 half_dense.1
  42.0 0.1 collective-permute-start.1
  42.1 2.2 %part_other.1 = bf16[4,8,48,128]{3,2,1,0:T(8,128)(2,1)} custom-call(s32[1]{0:T(128)} %bitcast.1.half_ref, bf16[16,352,128]{2,1,0:T(8,128)(2,1)S(1)} %all-to-all-done.dense_ref.ids_ref.seen, f32[16,16,128]{2,1,0:T(8,128)S(1)} %get-tuple-element.20.ids_ref.all_ids), custom_call_target="tpu_custom_call" | custom-call | flops 1000000000 | bytes 100000 | tf_op jit(solution)/shard_map/part_other/pallas_call | solution.py:426
  44.3 2.9 %collective-permute-start.2 = (bf16[4,8,48,128]{3,2,1,0:T(8,128)(2,1)}, bf16[4,8,48,128]{3,2,1,0:T(8,128)(2,1)S(1)}, u32[]{:S(2)}, u32[]{:S(2)}) collective-permute-start(bf16[4,8,48,128]{3,2,1,0:T(8,128)(2,1)} %part_other.1), channel_id=1, source_target_pairs={{0,4},{4,0},{1,5},{5,1},{2,6},{6,2},{3,7},{7,3},{8,12},{12,8},{9,1... | collective-permute-start | bytes 1179656 | tf_op jit(solution)/shard_map/ppermute | solution.py:669
  47.2 3.3 %lookup.1.rows = bf16[16,352,128]{2,1,0:T(8,128)(2,1)} custom-call(bf16[2,256,1024]{2,1,0:T(8,128)(2,1)S(1)} %copy-done.3, f32[16,16,128]{2,1,0:T(8,128)S(1)} %get-tuple-element.20.ids_ref.all_ids), custom_call_target="tpu_custom_call" | custom-call | flops 99999997952 | bytes 100000 | tf_op jit(solution)/shard_map/lookup/pallas_call | solution.py:517
  50.5 0.7 fill_dense.1
  51.3 5.1 %all-to-all-start.1 = ((bf16[16,352,128]{2,1,0:T(8,128)(2,1)}), bf16[16,352,128]{2,1,0:T(8,128)(2,1)S(1)}, u32[]{:S(2)}, u32[]{:S(2)}) async-start(bf16[16,352,128]{2,1,0:T(8,128)(2,1)} %get-tuple-element.22), calls=%async_computation.1 | async-start | bytes 2883584 | tf_op jit(solution)/shard_map/all_to_all | solution.py:62
  56.3 1.5 %part_own.1.own = f32[4,8,48,128]{3,2,1,0:T(8,128)S(1)} custom-call(s32[1]{0:T(128)} %bitcast.1.half_ref, bf16[16,352,128]{2,1,0:T(8,128)(2,1)S(1)} %all-to-all-done.dense_ref.ids_ref.seen, f32[16,16,128]{2,1,0:T(8,128)S(1)} %get-tuple-element.20.ids_ref.all_ids, f32[8,128]{1,0:T(8,128)S(1)} %copy-done.1), custom_call_target="tpu_custom_call" | custom-call | flops 1000000000 | bytes 100000 | tf_op jit(solution)/shard_map/part_own/pallas_call | solution.py:426
  57.8 7.2 %collective-permute-done.2.seen = bf16[4,8,48,128]{3,2,1,0:T(8,128)(2,1)S(1)} collective-permute-done((bf16[4,8,48,128]{3,2,1,0:T(8,128)(2,1)}, bf16[4,8,48,128]{3,2,1,0:T(8,128)(2,1)S(1)}, u32[]{:S(2)}, u32[]{:S(2)}) %collective-permute-start.2) | collective-permute-done | bytes 393248 | tf_op jit(solution)/shard_map/ppermute | solution.py:669
  65.1 3.6 %collective-permute-start.3 = (bf16[8,48,128]{2,1,0:T(8,128)(2,1)S(1)}, bf16[8,48,128]{2,1,0:T(8,128)(2,1)S(1)}, u32[]{:S(2)}, u32[]{:S(2)}) collective-permute-start(bf16[8,48,128]{2,1,0:T(8,128)(2,1)S(1)} %get-tuple-element.25), channel_id=1, source_target_pairs={{0,24},{8,16},{16,8},{24,0},{1,25},{9,17},{17,9},{25,1},{2,26},{10... | collective-permute-start | bytes 294920 | tf_op jit(solution)/shard_map/ppermute | solution.py:695
  68.7 0.6 collective-permute-start.5
  69.3 7.1 %collective-permute-done.3.refs_1_ = bf16[8,48,128]{2,1,0:T(8,128)(2,1)S(1)} collective-permute-done((bf16[8,48,128]{2,1,0:T(8,128)(2,1)S(1)}, bf16[8,48,128]{2,1,0:T(8,128)(2,1)S(1)}, u32[]{:S(2)}, u32[]{:S(2)}) %collective-permute-start.3) | collective-permute-done | bytes 98336 | tf_op jit(solution)/shard_map/ppermute | solution.py:695
  76.5 1.5 %collective-permute-done.4.refs_2_ = bf16[8,48,128]{2,1,0:T(8,128)(2,1)S(1)} collective-permute-done((bf16[8,48,128]{2,1,0:T(8,128)(2,1)S(1)}, bf16[8,48,128]{2,1,0:T(8,128)(2,1)S(1)}, u32[]{:S(2)}, u32[]{:S(2)}) %collective-permute-start.4) | collective-permute-done | bytes 98336 | tf_op jit(solution)/shard_map/ppermute | solution.py:695
  77.9 0.9 %collective-permute-done.5.refs_3_ = bf16[8,48,128]{2,1,0:T(8,128)(2,1)S(1)} collective-permute-done((bf16[8,48,128]{2,1,0:T(8,128)(2,1)S(1)}, bf16[8,48,128]{2,1,0:T(8,128)(2,1)S(1)}, u32[]{:S(2)}, u32[]{:S(2)}) %collective-permute-start.5) | collective-permute-done | bytes 98336 | tf_op jit(solution)/shard_map/ppermute | solution.py:695
  78.9 4.4 %all-to-all-done.1.dense_ref.left0.left1.right0.right1 = bf16[16,352,128]{2,1,0:T(8,128)(2,1)S(1)} async-done(((bf16[16,352,128]{2,1,0:T(8,128)(2,1)}), bf16[16,352,128]{2,1,0:T(8,128)(2,1)S(1)}, u32[]{:S(2)}, u32[]{:S(2)}) %all-to-all-start.1) | async-done | bytes 1441824 | tf_op jit(solution)/shard_map/all_to_all | solution.py:62
  83.2 3.1 %unpack.1 = (bf16[12,192,256]{2,1,0:T(8,128)(2,1)}, f32[32,32,192]{2,1,0:T(8,128)}, f32[256,128]{1,0:T(8,128)}, f32[192,128]{1,0:T(8,128)}, f32[256,256]{1,0:T(8,128)}, /*index=5*/f32[1,192]{1,0:T(1,128)}) custom-call(s32[1]{0:T(128)} %bitcast.place, bf16[16,352,128]{2,1,0:T(8,128)(2,1)S(1)} %all-to-all-done.1.dense_ref.left0.left1.right0.right1, ...), custom_call_target="tpu_custom_call" | custom-call | flops 1000000000 | bytes 100000 | tf_op jit(solution)/shard_map/unpack/pallas_call | solution.py:631
  (10 shorter events, 0.1 us)
Async XLA Ops:
  2.4 21.9 %collective-permute-start = (bf16[8,192,128]{2,1,0:T(8,128)(2,1)}, bf16[8,192,128]{2,1,0:T(8,128)(2,1)S(1)}, u32[]{:S(2)}, u32[]{:S(2)}) collective-permute-start(bf16[8,192,128]{2,1,0:T(8,128)(2,1)} %take_tables.1.mine_t), channel_id=1, source_target_pairs={{0,4},{4,0},{1,5},{5,1},{2,6},{6,2},{3,7},{7,3},{8,12},{12,8},{9,1... | collective-permute-start | bytes 1179656 | tf_op jit(solution)/shard_map/ppermute | solution.py:669
  15.1 9.2 %copy-start = (bf16[8,192,128]{2,1,0:T(8,128)(2,1)S(1)}, bf16[8,192,128]{2,1,0:T(8,128)(2,1)}, u32[]{:S(2)}) copy-start(bf16[8,192,128]{2,1,0:T(8,128)(2,1)} %take_tables.1.mine_t) | copy-start | bytes 1179652
  15.1 26.7 %all-to-all-start = ((bf16[16,352,128]{2,1,0:T(8,128)(2,1)}), bf16[16,352,128]{2,1,0:T(8,128)(2,1)S(1)}, u32[]{:S(2)}, u32[]{:S(2)}) async-start(bf16[16,352,128]{2,1,0:T(8,128)(2,1)} %layer_backward.1), calls=%async_computation | async-start | bytes 2883584 | tf_op jit(solution)/shard_map/all_to_all | solution.py:62
  24.6 1.0 %copy-start.2 = (bf16[2,256,1024]{2,1,0:T(8,128)(2,1)}, bf16[2,256,1024]{2,1,0:T(8,128)(2,1)S(1)}, u32[]{:S(2)}) copy-start(bf16[2,256,1024]{2,1,0:T(8,128)(2,1)S(1)} %stack_tables.1.stacked) | copy-start | bytes 3145732
  42.0 8.5 %collective-permute-start.1 = (f32[64,128]{1,0:T(8,128)S(1)}, f32[64,128]{1,0:T(8,128)S(1)}, u32[]{:S(2)}, u32[]{:S(2)}) collective-permute-start(f32[64,128]{1,0:T(8,128)S(1)} %get-tuple-element.21.own), channel_id=1, source_target_pairs={{0,4},{4,0},{1,5},{5,1},{2,6},{6,2},{3,7},{7,3},{8,12},{12,8},{9,1... | collective-permute-start | bytes 98312 | tf_op jit(solution)/shard_map/ppermute | solution.py:669
  42.0 5.1 %copy-start.3 = (bf16[2,256,1024]{2,1,0:T(8,128)(2,1)S(1)}, bf16[2,256,1024]{2,1,0:T(8,128)(2,1)}, u32[]{:S(2)}) copy-start(bf16[2,256,1024]{2,1,0:T(8,128)(2,1)} %copy-done.2) | copy-start | bytes 3145732
  44.3 20.7 %collective-permute-start.2 = (bf16[4,8,48,128]{3,2,1,0:T(8,128)(2,1)}, bf16[4,8,48,128]{3,2,1,0:T(8,128)(2,1)S(1)}, u32[]{:S(2)}, u32[]{:S(2)}) collective-permute-start(bf16[4,8,48,128]{3,2,1,0:T(8,128)(2,1)} %part_other.1), channel_id=1, source_target_pairs={{0,4},{4,0},{1,5},{5,1},{2,6},{6,2},{3,7},{7,3},{8,12},{12,8},{9,1... | collective-permute-start | bytes 1179656 | tf_op jit(solution)/shard_map/ppermute | solution.py:669
  51.3 5.1 %copy-start.1 = (f32[8,128]{1,0:T(8,128)S(1)}, f32[8,128]{1,0:T(8,128)}, u32[]{:S(2)}) copy-start(f32[8,128]{1,0:T(8,128)} %get-tuple-element.23.refs_0_.after) | copy-start | bytes 12292
  51.3 32.0 %all-to-all-start.1 = ((bf16[16,352,128]{2,1,0:T(8,128)(2,1)}), bf16[16,352,128]{2,1,0:T(8,128)(2,1)S(1)}, u32[]{:S(2)}, u32[]{:S(2)}) async-start(bf16[16,352,128]{2,1,0:T(8,128)(2,1)} %get-tuple-element.22), calls=%async_computation.1 | async-start | bytes 2883584 | tf_op jit(solution)/shard_map/all_to_all | solution.py:62
  65.1 11.4 %collective-permute-start.3 = (bf16[8,48,128]{2,1,0:T(8,128)(2,1)S(1)}, bf16[8,48,128]{2,1,0:T(8,128)(2,1)S(1)}, u32[]{:S(2)}, u32[]{:S(2)}) collective-permute-start(bf16[8,48,128]{2,1,0:T(8,128)(2,1)S(1)} %get-tuple-element.25), channel_id=1, source_target_pairs={{0,24},{8,16},{16,8},{24,0},{1,25},{9,17},{17,9},{25,1},{2,26},{10... | collective-permute-start | bytes 294920 | tf_op jit(solution)/shard_map/ppermute | solution.py:695
  68.7 9.2 %collective-permute-start.4 = (bf16[8,48,128]{2,1,0:T(8,128)(2,1)S(1)}, bf16[8,48,128]{2,1,0:T(8,128)(2,1)S(1)}, u32[]{:S(2)}, u32[]{:S(2)}) collective-permute-start(bf16[8,48,128]{2,1,0:T(8,128)(2,1)S(1)} %get-tuple-element.26), channel_id=1, source_target_pairs={{0,16},{8,24},{16,0},{24,8},{1,17},{9,25},{17,1},{25,9},{2,18},{10... | collective-permute-start | bytes 294920 | tf_op jit(solution)/shard_map/ppermute | solution.py:695
  68.7 10.2 %collective-permute-start.5 = (bf16[8,48,128]{2,1,0:T(8,128)(2,1)S(1)}, bf16[8,48,128]{2,1,0:T(8,128)(2,1)S(1)}, u32[]{:S(2)}, u32[]{:S(2)}) collective-permute-start(bf16[8,48,128]{2,1,0:T(8,128)(2,1)S(1)} %get-tuple-element.27), channel_id=1, source_target_pairs={{0,8},{8,0},{16,24},{24,16},{1,9},{9,1},{17,25},{25,17},{2,10},{10... | collective-permute-start | bytes 294920 | tf_op jit(solution)/shard_map/ppermute | solution.py:695
